TPU v7x, 128 devices: a whole 4x4x4 slice. The times are simulated.
128 devices in a mesh: outer: 8 (over y, core), inner: 16 (over x, z).
Axes of the slice: x: 4, y: 4, z: 4, core: 2. Of those that a mesh axis runs over, the one named last changes fastest.
Arguments:
- images: bfloat16 [20480, 768], P(('outer', 'inner')), may hold values from -16 to 16
- texts: bfloat16 [20480, 768], P(('outer', 'inner')), may hold values from -16 to 16
Outputs:
- image_grad: float32 [20480, 768], P(('outer', 'inner'))
- text_grad: float32 [20480, 768], P(('outer', 'inner'))
All inputs are finite; a program needn't handle non-finite values.
Results may differ from a plain program's by a relative error of at most 0.0016.
Values may be sent and summed in bfloat16 or wider, within the bound.
No kernel may reach another device: no remote copies, remote signals or barrier semaphores. Data moves between devices by JAX's collectives and lax.ppermute only.
A program may use at most 64 MiB of HBM per device.

v0:
```python
import math

import jax
import jax.numpy as jnp
from jax import lax
from jax.sharding import PartitionSpec as P


def joined(part, axis, combine):
    gathered = jax.tree.map(lambda a: lax.all_gather(a, axis), part)

    def take(source):
        return jax.tree.map(lambda a: lax.dynamic_index_in_dim(a, source, 0, False), gathered)

    return lax.fori_loop(
        1, lax.axis_size(axis), lambda source, state: combine(state, take(source)), take(0)
    )


def choose_block(total_rows):
    block_count = max(1, total_rows // 512)
    while total_rows % block_count:
        block_count = block_count - 1
    return total_rows // block_count


def merge_pair(earlier, latter):
    highest = jnp.maximum(earlier[0], latter[0])
    return (
        highest,
        earlier[1] * jnp.exp(earlier[0] - highest) + latter[1] * jnp.exp(latter[0] - highest),
    )


def weights_for(scores, lse_rows, lse_cols):
    return (jnp.exp(scores - lse_rows[:, None]) + jnp.exp(scores - lse_cols[None, :])).astype(
        jnp.bfloat16
    )


def body(images, texts):
    features = images.shape[1]
    score_scale = 4.0 / math.sqrt(features)
    text_group = lax.all_gather(texts, "inner", axis=0, tiled=True)
    image_group = lax.all_gather(images, "outer", axis=0, tiled=True)
    group_rows = image_group.shape[0]
    text_rows = text_group.shape[0]
    block_size = choose_block(group_rows)
    block_count = group_rows // block_size
    image_blocks = image_group.reshape(block_count, block_size, features)

    def forward(running, img_blk):
        scores = jnp.dot(img_blk, text_group.T, preferred_element_type=jnp.float32) * score_scale
        row_max = jnp.max(scores, axis=1)
        row_sum = jnp.sum(jnp.exp(scores - row_max[:, None]), axis=1)
        blk_max = jnp.max(scores, axis=0)
        blk_sum = jnp.sum(jnp.exp(scores - blk_max[None, :]), axis=0)
        return (merge_pair(running, (blk_max, blk_sum)), (row_max, row_sum))

    initial = (jnp.full((text_rows,), -jnp.inf, jnp.float32), jnp.zeros((text_rows,), jnp.float32))
    column_part, row_part = lax.scan(forward, initial, image_blocks)
    row_max, row_sum = joined(
        (row_part[0].reshape(group_rows), row_part[1].reshape(group_rows)), "outer", merge_pair
    )
    row_lse = row_max + jnp.log(row_sum)
    col_max, col_sum = joined((column_part[0], column_part[1]), "inner", merge_pair)
    col_lse = col_max + jnp.log(col_sum)
    row_blocks = row_lse.reshape(block_count, block_size)

    def both_sides(text_acc, inputs):
        img_blk, lse_blk = inputs
        scores = jnp.dot(img_blk, text_group.T, preferred_element_type=jnp.float32) * score_scale
        weights = weights_for(scores, lse_blk, col_lse)
        text_acc = text_acc + jnp.einsum(
            "rt,re->te", weights, img_blk, preferred_element_type=jnp.float32
        )
        return (text_acc, 0.5 * jnp.dot(weights, text_group, preferred_element_type=jnp.float32))

    text_acc, image_parts = lax.scan(
        both_sides, jnp.zeros((text_rows, features), jnp.float32), (image_blocks, row_blocks)
    )
    text_sum = lax.psum_scatter(0.5 * text_acc, "inner", scatter_dimension=0, tiled=True)
    image_sum = lax.psum_scatter(
        image_parts.reshape(group_rows, features), "outer", scatter_dimension=0, tiled=True
    )
    return (image_sum - texts.astype(jnp.float32), text_sum - images.astype(jnp.float32))


def solution(mesh):
    placed = (P(("outer", "inner"), None), P(("outer", "inner"), None))
    return jax.shard_map(
        body,
        mesh=mesh,
        in_specs=placed,
        out_specs=(P(("outer", "inner"), None), P(("outer", "inner"), None)),
        check_vma=False,
    )
```

profile of v0, /device:TPU:1, one launch (start us, length us, event | category | flops | bytes accessed | tf_op | source)
XLA Modules:
  0.0 344.9 jit_solution(15437299294469001791)
XLA Ops:
  7.2 0.0 all-gather.9.cloned.1.call-start
  7.2 0.7 all-gather.9.cloned.1.call-update
  7.9 0.0 all-gather.11.cloned.1.call-start
  7.9 0.7 all-gather.11.cloned.1.call-update
  8.6 0.0 reduce-scatter.3.cloned.1.call-start
  8.8 29.6 %all-gather.9.cloned.1.call-done = bf16[1280,768]{1,0:T(8,128)(2,1)} async-done(((bf16[160,768]{1,0:T(8,128)(2,1)}), bf16[1280,768]{1,0:T(8,128)(2,1)}) %all-gather.9.cloned.1.call-update) | async-done | bytes 1966096 | tf_op jit(solution)/shard_map/all_gather | solution.py:45
  38.3 52.5 %all-gather.11.cloned.1.call-done = bf16[2560,768]{1,0:T(8,128)(2,1)} async-done(((bf16[160,768]{1,0:T(8,128)(2,1)}), bf16[2560,768]{1,0:T(8,128)(2,1)}) %all-gather.11.cloned.1.call-update) | async-done | bytes 3932176 | tf_op jit(solution)/shard_map/all_gather | solution.py:44
  90.8 14.9 %while.66 = (s32[]{:T(128)}, f32[2560]{0:T(1024)S(1)}, f32[2560]{0:T(1024)S(1)}, f32[2,640]{1,0:T(2,128)S(1)}, f32[2,640]{1,0:T(2,128)S(1)}, /*index=5*/bf16[2,6...) while((s32[]{:T(128)}, f32[2560]{0:T(1024)S(1)}, f32[2560]{0:T(1024)S(1)}, ...), condition=%wide.region_5.6_spmd.clone, body=%wide.region_0.5_spmd.clone.sunk | while | flops 2528065536 | bytes 18142840 | solution.py:61
  90.8 5.2 %fusion.26 = (f32[640]{0:T(1024)S(1)}, f32[2560]{0:T(1024)S(1)}, f32[640,2560]{1,0:T(8,128)S(1)}) fusion(bf16[2560,768]{1,0:T(8,128)(2,1)} %get-tuple-element.669, bf16[2,640,768]{2,1,0:T(8,128)(2,1)} %get-tuple-element.668, s32[]{:T(128)S(6)} %copy.26), kind=kOutput, calls=%fused_computation.38.clone.1 | convolution fusion | flops 2521494528 | bytes 11481604 | tf_op jit(solution)/shard_map/while/body/eval_jaxpr/dot_general | solution.py:53
  96.0 2.0 exponential_reduce_fusion.3
  98.2 5.2 %fusion.26 = (f32[640]{0:T(1024)S(1)}, f32[2560]{0:T(1024)S(1)}, f32[640,2560]{1,0:T(8,128)S(1)}) fusion(bf16[2560,768]{1,0:T(8,128)(2,1)} %get-tuple-element.669, bf16[2,640,768]{2,1,0:T(8,128)(2,1)} %get-tuple-element.668, s32[]{:T(128)S(6)} %copy.26), kind=kOutput, calls=%fused_computation.38.clone.1 | convolution fusion | flops 2521494528 | bytes 11481604 | tf_op jit(solution)/shard_map/while/body/eval_jaxpr/dot_general | solution.py:53
  103.5 2.0 exponential_reduce_fusion.3
  105.7 13.8 %all-gather.2 = f32[8,1,1280]{2,1,0:T(1,128)S(1)} all-gather(f32[1,1,1280]{2,1,0:T(1,128)S(1)} %reshape.27), channel_id=1, replica_groups=mesh['outer'=8,'inner'=16] {'outer'}, dimensions={0}, use_global_device_ids=true | all-gather | bytes 46080 | tf_op jit(solution)/shard_map/all_gather | solution.py:10
  119.5 12.8 %all-gather.3 = f32[8,1,1280]{2,1,0:T(1,128)S(1)} all-gather(f32[1,1,1280]{2,1,0:T(1,128)S(1)} %reshape.29), channel_id=1, replica_groups=mesh['outer'=8,'inner'=16] {'outer'}, dimensions={0}, use_global_device_ids=true | all-gather | bytes 46080 | tf_op jit(solution)/shard_map/all_gather | solution.py:10
  132.4 17.7 %all-gather.5 = f32[16,1,2560]{2,1,0:T(1,128)S(1)} all-gather(f32[1,1,2560]{2,1,0:T(1,128)S(1)} %reshape.33), channel_id=3, replica_groups=mesh['outer'=8,'inner'=16] {'inner'}, dimensions={0}, use_global_device_ids=true | all-gather | bytes 174080 | tf_op jit(solution)/shard_map/all_gather | solution.py:10
  150.2 16.5 %all-gather.4 = f32[16,1,2560]{2,1,0:T(1,128)S(1)} all-gather(f32[1,1,2560]{2,1,0:T(1,128)S(1)} %reshape.31), channel_id=2, replica_groups=mesh['outer'=8,'inner'=16] {'inner'}, dimensions={0}, use_global_device_ids=true | all-gather | bytes 174080 | tf_op jit(solution)/shard_map/all_gather | solution.py:10
  166.8 0.6 while.64
  167.4 1.7 while.65
  167.4 0.1 dynamic-slice_reduce_fusion.9
  167.5 0.1 dynamic-slice_reduce_fusion.9
  167.7 0.1 dynamic-slice_reduce_fusion.9
  167.8 0.1 dynamic-slice_reduce_fusion.9
  167.9 0.1 dynamic-slice_reduce_fusion.9
  168.0 0.1 dynamic-slice_reduce_fusion.9
  168.1 0.1 dynamic-slice_reduce_fusion.9
  168.2 0.1 dynamic-slice_reduce_fusion.9
  168.3 0.1 dynamic-slice_reduce_fusion.9
  168.4 0.1 dynamic-slice_reduce_fusion.9
  168.6 0.1 dynamic-slice_reduce_fusion.9
  168.7 0.1 dynamic-slice_reduce_fusion.9
  168.8 0.1 dynamic-slice_reduce_fusion.9
  168.9 0.1 dynamic-slice_reduce_fusion.9
  169.0 0.1 dynamic-slice_reduce_fusion.9
  169.1 36.2 %while.67 = (s32[]{:T(128)}, f32[2560,768]{1,0:T(8,128)}, f32[2,640,768]{2,1,0:T(8,128)}, bf16[2,640,768]{2,1,0:T(8,128)(2,1)}, bf16[2560,768]{1,0:T(8,128)(2,1)...) while((s32[]{:T(128)}, f32[2560,768]{1,0:T(8,128)}, ...), condition=%wide.region_11.12_spmd.clone, body=%wide.region_10.11_spmd.clone.sunk | while | flops 7562362880 | bytes 155338544 | solution.py:79
  169.2 0.0 copy-start.3
  169.2 0.0 copy-start.7
  169.2 6.0 %add_convert_fusion.2 = bf16[640,2560]{1,0:T(8,128)(2,1)S(1)} fusion(bf16[2560,768]{1,0:T(8,128)(2,1)} %get-tuple-element.742, f32[2560]{0:T(1024)S(1)} %get-tuple-element.744, f32[640]{0:T(1024)S(1)} %dynamic-slice_reduce_fusion.10, bf16[2,640,768]{2,1,0:T(8,128)(2,1)} %get-tuple-element.741, s32[]{:T(128)S(6)} %copy.57), kind=kOutput, calls=%fused_computation.16.clone.1 | convolution fusion | flops 2524774400 | bytes 8204804 | tf_op jit(solution)/shard_map/while/body/eval_jaxpr/dot_general | solution.py:72
  175.2 0.0 copy-done.3
  175.2 0.0 copy-done.7
  175.2 0.0 copy-start
  175.2 0.0 copy-start.2
  175.3 2.7 bitcast_dynamic-update-slice_fusion.2
  178.0 0.5 copy-done
  178.5 0.5 copy-done.2
  179.0 5.1 %select_add_fusion.2 = f32[2560,768]{1,0:T(8,128)S(1)} fusion(f32[2560,768]{1,0:T(8,128)S(1)} %copy-done, bf16[640,2560]{1,0:T(8,128)(2,1)S(1)} %add_convert_fusion.2, pred[]{:T(512)S(6)} %compare.7, bf16[2,640,768]{2,1,0:T(8,128)(2,1)S(1)} %copy-done.2, s32[]{:T(128)S(6)} %copy.57), kind=kOutput, calls=%fused_computation.15.clone.1 | convolution fusion | flops 2520514560 | bytes 19988484 | tf_op jit(solution)/shard_map/while/body/eval_jaxpr/rt,re->te/dot_general | solution.py:74
  184.2 0.0 copy-done.4
  184.2 0.0 copy-start.1
  184.2 3.1 copy-done.1
  187.3 6.0 %add_convert_fusion.2 = bf16[640,2560]{1,0:T(8,128)(2,1)S(1)} fusion(bf16[2560,768]{1,0:T(8,128)(2,1)} %get-tuple-element.742, f32[2560]{0:T(1024)S(1)} %get-tuple-element.744, f32[640]{0:T(1024)S(1)} %dynamic-slice_reduce_fusion.10, bf16[2,640,768]{2,1,0:T(8,128)(2,1)} %get-tuple-element.741, s32[]{:T(128)S(6)} %copy.57), kind=kOutput, calls=%fused_computation.16.clone.1 | convolution fusion | flops 2524774400 | bytes 8204804 | tf_op jit(solution)/shard_map/while/body/eval_jaxpr/dot_general | solution.py:72
  193.3 2.7 bitcast_dynamic-update-slice_fusion.2
  196.1 0.5 copy-done
  196.6 0.5 copy-done.2
  197.1 5.1 %select_add_fusion.2 = f32[2560,768]{1,0:T(8,128)S(1)} fusion(f32[2560,768]{1,0:T(8,128)S(1)} %copy-done, bf16[640,2560]{1,0:T(8,128)(2,1)S(1)} %add_convert_fusion.2, pred[]{:T(512)S(6)} %compare.7, bf16[2,640,768]{2,1,0:T(8,128)(2,1)S(1)} %copy-done.2, s32[]{:T(128)S(6)} %copy.57), kind=kOutput, calls=%fused_computation.15.clone.1 | convolution fusion | flops 2520514560 | bytes 19988484 | tf_op jit(solution)/shard_map/while/body/eval_jaxpr/rt,re->te/dot_general | solution.py:74
  202.3 3.1 copy-done.1
  205.3 0.0 reduce-scatter.3.cloned.1.call-update
  205.4 0.0 reduce-scatter.5.cloned.1.call-start
  205.4 6.9 %broadcast_multiply_fusion = f32[2560,768]{1,0:T(8,128)} fusion(f32[2560,768]{1,0:T(8,128)} %get-tuple-element.355), kind=kLoop, calls=%fused_computation.25 | loop fusion | flops 1966080 | bytes 15728640 | tf_op jit(solution)/shard_map/mul | solution.py:82
  212.3 0.0 reduce-scatter.5.cloned.1.call-update
  212.3 36.3 %reduce-scatter.3.cloned.1.call-done = f32[160,768]{1,0:T(8,128)} async-done(((f32[1280,768]{1,0:T(8,128)}), f32[160,768]{1,0:T(8,128)}) %reduce-scatter.3.cloned.1.call-update) | async-done | bytes 491536 | tf_op jit(solution)/shard_map/reduce_scatter | solution.py:83
  248.6 0.0 copy-done.5
  248.6 1.8 convert_subtract_fusion.1
  250.5 86.1 %reduce-scatter.5.cloned.1.call-done = f32[160,768]{1,0:T(8,128)} async-done(((f32[2560,768]{1,0:T(8,128)}), f32[160,768]{1,0:T(8,128)}) %reduce-scatter.5.cloned.1.call-update) | async-done | bytes 491536 | tf_op jit(solution)/shard_map/reduce_scatter | solution.py:82
  336.6 0.0 copy-done.6
  336.6 1.8 convert_subtract_fusion
  (74 shorter events, 1.1 us)
Async XLA Ops:
  7.2 31.2 %all-gather.9.cloned.1.call-start = ((), (), s32[]{:S(2)}) async-start(), calls=%async_computation.2 | async-start | bytes 2211840 | tf_op jit(solution)/shard_map/all_gather | solution.py:45
  7.9 82.9 %all-gather.11.cloned.1.call-start = ((), (), s32[]{:S(2)}) async-start(), calls=%async_computation.3 | async-start | bytes 4177920 | tf_op jit(solution)/shard_map/all_gather | solution.py:44
  8.6 240.0 %reduce-scatter.3.cloned.1.call-start = ((), (), s32[]{:S(2)}) async-start(), calls=%async_computation.4 | async-start | bytes 4423680 | tf_op jit(solution)/shard_map/reduce_scatter | solution.py:83
  169.2 6.0 %copy-start.3 = (f32[2,640,768]{2,1,0:T(8,128)S(1)}, f32[2,640,768]{2,1,0:T(8,128)}, u32[]{:S(2)}) copy-start(f32[2,640,768]{2,1,0:T(8,128)} %get-tuple-element.731) | copy-start | bytes 11796484 | tf_op jit(solution)/shard_map/while
  169.2 6.0 %copy-start.7 = (bf16[2560,768]{1,0:T(8,128)(2,1)S(1)}, bf16[2560,768]{1,0:T(8,128)(2,1)}, u32[]{:S(2)}) copy-start(bf16[2560,768]{1,0:T(8,128)(2,1)} %get-tuple-element.742) | copy-start | bytes 11796484 | tf_op jit(solution)/shard_map/while
  175.2 3.2 copy-start
  175.2 3.8 %copy-start.2 = (bf16[2,640,768]{2,1,0:T(8,128)(2,1)S(1)}, bf16[2,640,768]{2,1,0:T(8,128)(2,1)}, u32[]{:S(2)}) copy-start(bf16[2,640,768]{2,1,0:T(8,128)(2,1)} %get-tuple-element.741) | copy-start | bytes 5898244 | tf_op jit(solution)/shard_map/while
  179.0 5.1 %copy-start.4 = (f32[2,640,768]{2,1,0:T(8,128)}, f32[2,640,768]{2,1,0:T(8,128)S(1)}, u32[]{:S(2)}) copy-start(f32[2,640,768]{2,1,0:T(8,128)S(1)} %bitcast_dynamic-update-slice_fusion.2) | copy-start | bytes 11796484 | tf_op jit(solution)/shard_map/while
  184.2 3.1 copy-start.1
  187.3 6.0 %copy-start.3 = (f32[2,640,768]{2,1,0:T(8,128)S(1)}, f32[2,640,768]{2,1,0:T(8,128)}, u32[]{:S(2)}) copy-start(f32[2,640,768]{2,1,0:T(8,128)} %get-tuple-element.731) | copy-start | bytes 11796484 | tf_op jit(solution)/shard_map/while
  187.3 6.0 %copy-start.7 = (bf16[2560,768]{1,0:T(8,128)(2,1)S(1)}, bf16[2560,768]{1,0:T(8,128)(2,1)}, u32[]{:S(2)}) copy-start(bf16[2560,768]{1,0:T(8,128)(2,1)} %get-tuple-element.742) | copy-start | bytes 11796484 | tf_op jit(solution)/shard_map/while
  193.3 3.2 copy-start
  193.3 3.8 %copy-start.2 = (bf16[2,640,768]{2,1,0:T(8,128)(2,1)S(1)}, bf16[2,640,768]{2,1,0:T(8,128)(2,1)}, u32[]{:S(2)}) copy-start(bf16[2,640,768]{2,1,0:T(8,128)(2,1)} %get-tuple-element.741) | copy-start | bytes 5898244 | tf_op jit(solution)/shard_map/while
  197.1 5.1 %copy-start.4 = (f32[2,640,768]{2,1,0:T(8,128)}, f32[2,640,768]{2,1,0:T(8,128)S(1)}, u32[]{:S(2)}) copy-start(f32[2,640,768]{2,1,0:T(8,128)S(1)} %bitcast_dynamic-update-slice_fusion.2) | copy-start | bytes 11796484 | tf_op jit(solution)/shard_map/while
  202.3 3.1 copy-start.1
  205.4 131.2 %reduce-scatter.5.cloned.1.call-start = ((), (), s32[]{:S(2)}) async-start(), calls=%async_computation.5 | async-start | bytes 8355840 | tf_op jit(solution)/shard_map/reduce_scatter | solution.py:82
  212.3 36.3 %copy-start.5 = (bf16[160,768]{1,0:T(8,128)(2,1)S(1)}, bf16[160,768]{1,0:T(8,128)(2,1)}, u32[]{:S(2)}) copy-start(bf16[160,768]{1,0:T(8,128)(2,1)} %param.11) | copy-start | bytes 737284
  212.3 124.3 %copy-start.6 = (bf16[160,768]{1,0:T(8,128)(2,1)S(1)}, bf16[160,768]{1,0:T(8,128)(2,1)}, u32[]{:S(2)}) copy-start(bf16[160,768]{1,0:T(8,128)(2,1)} %param.10) | copy-start | bytes 737284
Sparse Core Ops, SparseCore 0:
  9.7 28.5 all-gather.8
  40.5 50.2 all-gather.10
  205.5 43.1 reduce-scatter.2
  252.0 84.5 reduce-scatter.4
where the time goes:
time: 346 us; the launch traced here: 345 us
  waiting for transfers between devices  206 us (60%)
  blocking collectives  60.9 us (18%)
  matrix products  38.2 us (11%)
  other arithmetic  15 us (4%)
  between operations  13.9 us (4%)
  local copies, waits for them, and re-layouts  9.94 us (3%)
    reduce_scatter x1, waiting for transfers between devices, body(): lax.psum_scatter(0.5 * text_acc, 'inner', scatter_dimension=0, tiled=True)  86.1 us
    all_gather x4, blocking collectives, joined(): gathered = jax.tree.map(lambda a: lax.all_gather(a, axis), part)  60.9 us
    all_gather x1, waiting for transfers between devices, body(): text_group = lax.all_gather(texts, 'inner', axis=0, tiled=True)  52.5 us
    reduce_scatter x1, waiting for transfers between devices, body(): lax.psum_scatter(image_parts.reshape(group_rows, features), 'outer', scat...  36.3 us
    all_gather x1, waiting for transfers between devices, body(): image_group = lax.all_gather(images, 'outer', axis=0, tiled=True)  29.6 us
    dot_general x2, matrix products, both_sides(): jnp.dot(img_blk, text_group.T, preferred_element_type=jnp.float32)  12 us
    dot_general x2, matrix products, forward(): jnp.dot(img_blk, text_group.T, preferred_element_type=jnp.float32)  10.5 us
    dot_general x2, matrix products, both_sides(): jnp.einsum('rt,re->te', weights, img_blk, preferred_element_type=jnp.floa...  10.3 us
  transfers between devices with their start and end apart: 4, of which 4 were waited for; matrix products, arithmetic and copies ran while one was open for 3% of the time, Pallas kernels for 0%

commit v1 on v0

v1 whole, which is shorter than its diff:
```python
import functools
import math

import jax
import jax.numpy as jnp
from jax import lax
from jax.experimental import pallas as pl
from jax.experimental.pallas import tpu as pltpu
from jax.sharding import Mesh, PartitionSpec as P

AXES = ("y", "core", "x", "z")
SIZES = (4, 2, 4, 4)
ORDER = (0, 1, 2, 4, 3, 5, 6, 7)
PLACE = tuple(ORDER.index(m) for m in range(8))
LOG2E = 1.4426950408889634
VMEM_LIMIT = 56 * 1024 * 1024


def flat(y, c, x, z):
    return ((y * 2 + c) * 4 + x) * 4 + z


def coords():
    for y in range(4):
        for c in range(2):
            for x in range(4):
                for z in range(4):
                    yield y, c, x, z


def partner(v, c):
    return v ^ 1 if c == 0 else 3 - v


def across(m):
    pairs = []
    for y, c, x, z in coords():
        target = (
            partner(y, c) if m & 2 else y,
            c,
            partner(x, c) if m & 1 else x,
            partner(z, c) if m & 4 else z,
        )
        pairs.append((flat(y, c, x, z), flat(*target)))
    return pairs


SWAP = [(flat(y, c, x, z), flat(y, 1 - c, x, z)) for y, c, x, z in coords()]


def cube_groups():
    groups = []
    seen = set()
    for y, c, x, z in coords():
        members = []
        for m in range(8):
            yy = partner(y, c) if m & 2 else y
            xx = partner(x, c) if m & 1 else x
            zz = partner(z, c) if m & 4 else z
            place = (xx & 1) | ((yy & 1) << 1) | ((zz & 1) << 2)
            members.append((place, flat(yy, c, xx, zz)))
        key = tuple(d for _, d in sorted(members))
        if key not in seen:
            seen.add(key)
            groups.append(list(key))
    return groups


GROUPS = cube_groups()


def to_cube(a, m):
    return lax.ppermute(a, AXES, across(m))


def swap(a):
    return lax.ppermute(a, AXES, SWAP)


def column_of(row, rows):
    padded = -(-rows // 128) * 128
    wide = jnp.broadcast_to(row, (128, rows))
    if padded != rows:
        wide = jnp.concatenate([wide, jnp.zeros((128, padded - rows), jnp.float32)], axis=1)
    return wide.T[:rows, :1]


def row_of(column, rows):
    padded = -(-rows // 128) * 128
    wide = jnp.broadcast_to(column, (rows, 128))
    if padded != rows:
        wide = jnp.concatenate([wide, jnp.zeros((padded - rows, 128), jnp.float32)], axis=0)
    return wide.T[:1, :rows]


def load_blocks(core, a_refs, b_refs, a_s, b_s, a_sem, b_sem):
    rows = a_refs[0].shape[0]
    for k in range(8):
        pltpu.make_async_copy(a_refs[k], a_s.at[pl.ds(k * rows, rows)], a_sem.at[k]).start()
        stage = (k // 4) ^ core
        start = pl.multiple_of((stage * 4 + k % 4) * rows, 16)
        pltpu.make_async_copy(b_refs[k], b_s.at[pl.ds(start, rows)], b_sem.at[stage * 4 + k % 4]).start()


def wait_half(h, a_refs, b_refs, a_s, b_s, a_sem, b_sem):
    rows = a_refs[0].shape[0]
    for j in range(4):
        k = h * 4 + j
        pltpu.make_async_copy(a_refs[k], a_s.at[pl.ds(k * rows, rows)], a_sem.at[k]).wait()
        pltpu.make_async_copy(b_refs[k], b_s.at[pl.ds(k * rows, rows)], b_sem.at[k]).wait()


def scores_kernel(scale, core_ref, *refs):
    a_refs, b_refs = refs[:8], refs[8:16]
    s_ref, a_stat, b_stat = refs[16:19]
    a_s, b_s, col_m, col_s, a_sem, b_sem = refs[19:]
    rows = a_refs[0].shape[0]
    half = 4 * rows
    core = core_ref[0]
    step = pl.program_id(0)

    @pl.when(step == 0)
    def _():
        load_blocks(core, a_refs, b_refs, a_s, b_s, a_sem, b_sem)
        wait_half(0, a_refs, b_refs, a_s, b_s, a_sem, b_sem)

    @pl.when(step == 4)
    def _():
        wait_half(1, a_refs, b_refs, a_s, b_s, a_sem, b_sem)

    quadrant = step // 4
    a_blk = a_s[pl.ds(pl.multiple_of(step * rows, 16), rows), :]
    b_half = b_s[pl.ds(pl.multiple_of(quadrant * half, 16), half), :]
    s = lax.dot_general(a_blk, b_half, (((1,), (1,)), ((), ())), preferred_element_type=jnp.float32) * scale
    s_ref[0] = s
    row_m = jnp.max(s, axis=1, keepdims=True)
    row_sum = jnp.sum(jnp.exp2(s - row_m), axis=1, keepdims=True)
    a_stat[pl.ds(step, 1), :] = row_of(row_m + jnp.log2(row_sum), rows)
    blk_m = jnp.max(s, axis=0, keepdims=True)
    blk_s = jnp.sum(jnp.exp2(s - blk_m), axis=0, keepdims=True)

    @pl.when(step % 4 == 0)
    def _():
        col_m[...] = blk_m
        col_s[...] = blk_s

    @pl.when(step % 4 != 0)
    def _():
        before = col_m[...]
        top = jnp.maximum(before, blk_m)
        col_s[...] = col_s[...] * jnp.exp2(before - top) + blk_s * jnp.exp2(blk_m - top)
        col_m[...] = top

    @pl.when(step % 4 == 3)
    def _():
        lse = col_m[...] + jnp.log2(col_s[...])
        for j in range(4):
            b_stat[pl.ds((quadrant ^ core) * 4 + j, 1), :] = lse[:, j * rows : (j + 1) * rows]


def any_spec():
    return pl.BlockSpec(memory_space=pl.ANY)


def scores_call(core, a_blocks, b_blocks, scale):
    rows, features = a_blocks[0].shape
    half = 4 * rows
    stat = jax.ShapeDtypeStruct((8, rows), jnp.float32)
    return pl.pallas_call(
        functools.partial(scores_kernel, scale),
        grid=(8,),
        in_specs=[pl.BlockSpec(memory_space=pltpu.SMEM)] + [any_spec()] * 16,
        out_specs=[
            pl.BlockSpec((1, rows, half), lambda i: (i, 0, 0)),
            pl.BlockSpec((8, rows), lambda i: (0, 0)),
            pl.BlockSpec((8, rows), lambda i: (0, 0)),
        ],
        out_shape=[jax.ShapeDtypeStruct((8, rows, half), jnp.float32), stat, stat],
        scratch_shapes=[
            pltpu.VMEM((8 * rows, features), jnp.bfloat16),
            pltpu.VMEM((8 * rows, features), jnp.bfloat16),
            pltpu.VMEM((1, half), jnp.float32),
            pltpu.VMEM((1, half), jnp.float32),
            pltpu.SemaphoreType.DMA((8,)),
            pltpu.SemaphoreType.DMA((8,)),
        ],
        compiler_params=pltpu.CompilerParams(vmem_limit_bytes=VMEM_LIMIT),
        cost_estimate=pl.CostEstimate(
            flops=2 * 8 * rows * half * features, bytes_accessed=32 * rows * half, transcendentals=16 * rows * half
        ),
        name="scores",
    )(core, *a_blocks, *b_blocks)


def merge_kernel(place_ref, got_ref, out_ref):
    me = place_ref[0]
    for m in range(8):
        parts = []
        for k in range(8):
            offset = (me ^ k) ^ m
            row = jnp.int32(0)
            for n in range(8):
                row = jnp.where(offset == n, PLACE[n], row)
            parts.append(got_ref[k, pl.ds(row, 1), :])
        top = functools.reduce(jnp.maximum, parts)
        total = functools.reduce(jnp.add, [jnp.exp2(p - top) for p in parts])
        out_ref[PLACE[m] : PLACE[m] + 1, :] = top + jnp.log2(total)


def merge_call(place, got):
    return pl.pallas_call(
        merge_kernel,
        in_specs=[pl.BlockSpec(memory_space=pltpu.SMEM), pl.BlockSpec(memory_space=pltpu.VMEM)],
        out_specs=pl.BlockSpec(memory_space=pltpu.VMEM),
        out_shape=jax.ShapeDtypeStruct(got.shape[1:], jnp.float32),
        name="merge",
    )(place, got)


def grads_kernel(core_ref, *refs):
    s_ref, a_lse, b_lse = refs[:3]
    a_refs, b_refs = refs[3:11], refs[11:19]
    ga, gb, gb0 = refs[19:22]
    a_s, b_s, w_s, col, a_sem, b_sem = refs[22:]
    rows = a_refs[0].shape[0]
    half = 4 * rows
    core = core_ref[0]
    step = pl.program_id(0)
    quadrant = step // 4

    @pl.when(step == 0)
    def _():
        load_blocks(core, a_refs, b_refs, a_s, b_s, a_sem, b_sem)
        wait_half(0, a_refs, b_refs, a_s, b_s, a_sem, b_sem)

    @pl.when(step == 4)
    def _():
        wait_half(1, a_refs, b_refs, a_s, b_s, a_sem, b_sem)

    @pl.when(step % 4 == 0)
    def _():
        col[...] = jnp.concatenate(
            [b_lse[pl.ds((quadrant ^ core) * 4 + j, 1), :] for j in range(4)], axis=1
        )

    s = s_ref[0]
    lse = column_of(a_lse[pl.ds(step, 1), :], rows)
    w = (jnp.exp2(s - lse) + jnp.exp2(s - col[...])).astype(jnp.bfloat16)
    w_s[pl.ds(pl.multiple_of((step % 4) * rows, 16), rows), :] = w
    b_half = b_s[pl.ds(pl.multiple_of(quadrant * half, 16), half), :]
    ga[0] = 0.5 * jnp.dot(w, b_half, preferred_element_type=jnp.float32)

    @pl.when(step % 4 == 3)
    def _():
        a_half = a_s[pl.ds(pl.multiple_of(quadrant * half, 16), half), :]
        for j in range(4):
            g = 0.5 * lax.dot_general(
                w_s[:, j * rows : (j + 1) * rows],
                a_half,
                (((0,), (0,)), ((), ())),
                preferred_element_type=jnp.float32,
            )
            gb[pl.ds((quadrant ^ core) * 4 + j, 1)] = g.astype(jnp.bfloat16)[None]
            if j == 0:

                @pl.when(quadrant == core)
                def _():
                    gb0[...] = g


def grads_call(core, s, a_lse, b_lse, a_blocks, b_blocks):
    rows, features = a_blocks[0].shape
    half = 4 * rows
    return pl.pallas_call(
        grads_kernel,
        grid=(8,),
        in_specs=[
            pl.BlockSpec(memory_space=pltpu.SMEM),
            pl.BlockSpec((1, rows, half), lambda i: (i, 0, 0)),
            pl.BlockSpec((8, rows), lambda i: (0, 0)),
            pl.BlockSpec((8, rows), lambda i: (0, 0)),
        ]
        + [any_spec()] * 16,
        out_specs=[
            pl.BlockSpec((1, rows, features), lambda i: (i, 0, 0)),
            pl.BlockSpec((8, rows, features), lambda i: (0, 0, 0)),
            pl.BlockSpec((rows, features), lambda i: (0, 0)),
        ],
        out_shape=[
            jax.ShapeDtypeStruct((8, rows, features), jnp.float32),
            jax.ShapeDtypeStruct((8, rows, features), jnp.bfloat16),
            jax.ShapeDtypeStruct((rows, features), jnp.float32),
        ],
        scratch_shapes=[
            pltpu.VMEM((8 * rows, features), jnp.bfloat16),
            pltpu.VMEM((8 * rows, features), jnp.bfloat16),
            pltpu.VMEM((half, half), jnp.bfloat16),
            pltpu.VMEM((1, half), jnp.float32),
            pltpu.SemaphoreType.DMA((8,)),
            pltpu.SemaphoreType.DMA((8,)),
        ],
        compiler_params=pltpu.CompilerParams(vmem_limit_bytes=VMEM_LIMIT),
        cost_estimate=pl.CostEstimate(
            flops=4 * 8 * rows * half * features, bytes_accessed=32 * rows * half, transcendentals=16 * rows * half
        ),
        name="grads",
    )(core, s, a_lse, b_lse, *a_blocks, *b_blocks)


def body(images, texts):
    rows, features = images.shape
    scale = 4.0 / math.sqrt(features) * LOG2E
    core = lax.axis_index("core")
    first = core == 0
    core_arr = core.astype(jnp.int32).reshape(1)
    place = (
        (lax.axis_index("x") & 1) | ((lax.axis_index("y") & 1) << 1) | ((lax.axis_index("z") & 1) << 2)
    ).astype(jnp.int32).reshape(1)

    mine = jnp.where(first, images, texts)
    other = swap(jnp.where(first, texts, images))
    own = jnp.concatenate([mine, other], axis=0)
    near = {m: to_cube(own, m) for m in (1, 2, 4)}
    blocks = {0: own, **near}
    blocks[3] = to_cube(near[2], 1)
    blocks[6] = to_cube(near[4], 2)
    blocks[5] = to_cube(near[1], 4)
    blocks[7] = to_cube(near[1], 6)
    a_blocks = [blocks[m] for m in ORDER]
    b_blocks = [swap(blocks[m]) for m in ORDER]

    s, a_stat, b_stat = scores_call(core_arr, a_blocks, b_blocks, scale)
    chip_stat = jnp.logaddexp2(a_stat, swap(b_stat))
    got = lax.all_to_all(
        jnp.broadcast_to(chip_stat[None], (8,) + chip_stat.shape), AXES, 0, 0, axis_index_groups=GROUPS
    )
    a_lse = merge_call(place, got)
    b_lse = swap(a_lse)

    ga, gb, gb0 = grads_call(core_arr, s, a_lse, b_lse, a_blocks, b_blocks)
    gb_other = {m: swap(gb[PLACE[m]]) for m in range(1, 8)}
    gb0_other = swap(gb0)

    def chip_part(m):
        return ga[PLACE[m]] + gb_other[m].astype(jnp.float32)

    def narrow(a):
        return a.astype(jnp.bfloat16)

    from_xy = to_cube(narrow(chip_part(3)), 1)
    from_yz = to_cube(narrow(chip_part(6)), 2)
    from_xz = to_cube(narrow(chip_part(5)), 4)
    from_xyz = to_cube(narrow(chip_part(7)), 6)
    wide = lambda a: a.astype(jnp.float32)
    from_x = to_cube(narrow(chip_part(1) + wide(from_xz) + wide(from_xyz)), 1)
    from_y = to_cube(narrow(chip_part(2) + wide(from_xy)), 2)
    from_z = to_cube(narrow(chip_part(4) + wide(from_yz)), 4)
    total = ga[0] + gb0_other + wide(from_x) + wide(from_y) + wide(from_z)
    kept, sent = total[:rows], total[rows:]
    got_sum = swap(sent)
    image_sum = jnp.where(first, kept, got_sum)
    text_sum = jnp.where(first, got_sum, kept)
    return (image_sum - wide(texts), text_sum - wide(images))


def solution(mesh):
    chips = Mesh(mesh.devices.reshape(SIZES), AXES)
    spec = P(AXES, None)
    return jax.shard_map(
        body,
        mesh=chips,
        in_specs=(spec, spec),
        out_specs=(spec, spec),
        check_vma=False,
    )
```

time: 346 us -> 150 us (0.43)
  waiting for transfers between devices: 206 us -> 55.6 us
  blocking collectives: 60.9 us -> 0 us
  Pallas kernels: 0 us -> 44.8 us
  matrix products: 38.2 us -> 0 us
  starting transfers between devices: 0.16 us -> 37.5 us
  between operations: 13.9 us -> 0.99 us
  other arithmetic: 15 us -> 5.65 us
  local copies, waits for them, and re-layouts: 9.94 us -> 4.94 us
    reduce_scatter x2 -> x0, waiting for transfers between devices: 122 us -> none  [the longest x1 86.1 us: body(): lax.psum_scatter(0.5 * text_acc, 'inner', scatter_dimension=0, tiled=True)]
    all_gather x2 -> x0, waiting for transfers between devices: 82 us -> none  [the longest x1 52.5 us: body(): text_group = lax.all_gather(texts, 'inner', axis=0, tiled=True)]
    all_gather x4 -> x0, blocking collectives: 60.9 us -> none  [joined(): gathered = jax.tree.map(lambda a: lax.all_gather(a, axis), part)]
    ppermute x0 -> x34, waiting for transfers between devices: none -> 47 us  [the longest x14 38 us: to_cube(): return lax.ppermute(a, AXES, across(m))]
    pallas_call x0 -> x3, Pallas kernels: none -> 44.8 us  [the longest x1 26.5 us: grads_call(): pl.pallas_call(grads_kernel, grid=(8,), in_specs=[pl.BlockSpec(memory_spa...]
    dot_general x8 -> x0, matrix products: 38.2 us -> none  [the longest x2 12 us: both_sides(): jnp.dot(img_blk, text_group.T, preferred_element_type=jnp.float32)]
    ppermute x0 -> x34, starting transfers between devices: none -> 32 us  [the longest x14 27.9 us: to_cube(): return lax.ppermute(a, AXES, across(m))]
    all_to_all x0 -> x1, waiting for transfers between devices: none -> 8.58 us  [body(): lax.all_to_all(jnp.broadcast_to(chip_stat[None], (8,) + chip_stat.shape),...]
  transfers between devices with their start and end apart: 4 -> 35, of which waited for: 4 -> 19; matrix products, arithmetic and copies ran while one was open for 3% -> 2% of each run, Pallas kernels for 0% -> 0%
where the time goes in v1:
time: 150 us; the launch traced here: 149 us
  waiting for transfers between devices  55.6 us (37%)
  Pallas kernels  44.8 us (30%)
  starting transfers between devices  37.5 us (25%)
  other arithmetic  5.65 us (4%)
  local copies, waits for them, and re-layouts  4.94 us (3%)
    ppermute x14, waiting for transfers between devices, to_cube(): return lax.ppermute(a, AXES, across(m))  38 us
    ppermute x14, starting transfers between devices, to_cube(): return lax.ppermute(a, AXES, across(m))  27.9 us
    pallas_call x1, Pallas kernels, grads_call(): pl.pallas_call(grads_kernel, grid=(8,), in_specs=[pl.BlockSpec(memory_spa...  26.5 us
    pallas_call x1, Pallas kernels, scores_call(): pl.pallas_call(functools.partial(scores_kernel, scale), grid=(8,), in_spe...  16.7 us
    ppermute x20, waiting for transfers between devices, swap(): return lax.ppermute(a, AXES, SWAP)  9.02 us
    all_to_all x1, waiting for transfers between devices, body(): lax.all_to_all(jnp.broadcast_to(chip_stat[None], (8,) + chip_stat.shape),...  8.58 us
    all_to_all x1, starting transfers between devices, body(): lax.all_to_all(jnp.broadcast_to(chip_stat[None], (8,) + chip_stat.shape),...  5.55 us
    ppermute x20, starting transfers between devices, swap(): return lax.ppermute(a, AXES, SWAP)  4.07 us
  transfers between devices with their start and end apart: 35, of which 19 were waited for; matrix products, arithmetic and copies ran while one was open for 2% of the time, Pallas kernels for 0%

profile of v1, /device:TPU:1, one launch (start us, length us, event | category | flops | bytes accessed | tf_op | source)
XLA Modules:
  0.0 149.4 jit_solution(1835484874890597351)
XLA Ops:
  0.6 1.1 broadcast_select_fusion.1
  1.7 1.5 %collective-permute-start = (bf16[160,768]{1,0:T(8,128)(2,1)S(1)}, bf16[160,768]{1,0:T(8,128)(2,1)S(1)}, u32[]{:S(2)}, u32[]{:S(2)}) collective-permute-start(bf16[160,768]{1,0:T(8,128)(2,1)S(1)} %get-tuple-element.31), channel_id=1, source_target_pairs={{0,16},{1,17},{2,18},{3,19},{4,20},{5,21},{6,22},{7,23},{8,24},{9,... | collective-permute-start | bytes 737288 | tf_op jit(solution)/shard_map/ppermute | solution.py:77
  3.2 1.1 collective-permute-done
  4.4 0.0 copy-start.3
  4.4 3.9 %collective-permute-start.3 = (bf16[320,768]{1,0:T(8,128)(2,1)S(1)}, bf16[320,768]{1,0:T(8,128)(2,1)S(1)}, u32[]{:S(2)}, u32[]{:S(2)}) collective-permute-start(bf16[320,768]{1,0:T(8,128)(2,1)S(1)} %pad_maximum_fusion.refs_0_.refs_3_), channel_id=1, source_target_pairs={{0,1},{1,0},{2,3},{3,2},{4,5},{5,4},{6,7},{7,6},{8,9},{9,8},{10,11... | collective-permute-start | bytes 1474568 | tf_op jit(solution)/shard_map/ppermute | solution.py:73
  8.3 2.7 %collective-permute-start.2 = (bf16[320,768]{1,0:T(8,128)(2,1)S(1)}, bf16[320,768]{1,0:T(8,128)(2,1)S(1)}, u32[]{:S(2)}, u32[]{:S(2)}) collective-permute-start(bf16[320,768]{1,0:T(8,128)(2,1)S(1)} %pad_maximum_fusion.refs_0_.refs_3_), channel_id=1, source_target_pairs={{0,32},{1,33},{2,34},{3,35},{4,36},{5,37},{6,38},{7,39},{8,40},{9,... | collective-permute-start | bytes 1474568 | tf_op jit(solution)/shard_map/ppermute | solution.py:73
  11.1 2.5 %collective-permute-start.1 = (bf16[320,768]{1,0:T(8,128)(2,1)S(1)}, bf16[320,768]{1,0:T(8,128)(2,1)S(1)}, u32[]{:S(2)}, u32[]{:S(2)}) collective-permute-start(bf16[320,768]{1,0:T(8,128)(2,1)S(1)} %pad_maximum_fusion.refs_0_.refs_3_), channel_id=1, source_target_pairs={{0,4},{1,5},{2,6},{3,7},{4,0},{5,1},{6,2},{7,3},{8,12},{9,13},{10,... | collective-permute-start | bytes 1474568 | tf_op jit(solution)/shard_map/ppermute | solution.py:73
  13.6 1.0 collective-permute-done.3.refs_3_.refs_6_
  14.6 0.0 collective-permute-start.11
  14.6 2.7 %collective-permute-start.6 = (bf16[320,768]{1,0:T(8,128)(2,1)S(1)}, bf16[320,768]{1,0:T(8,128)(2,1)S(1)}, u32[]{:S(2)}, u32[]{:S(2)}) collective-permute-start(bf16[320,768]{1,0:T(8,128)(2,1)S(1)} %collective-permute-done.3.refs_3_.refs_6_), channel_id=1, source_target_pairs={{0,32},{1,33},{2,34},{3,35},{4,36},{5,37},{6,38},{7,39},{8,40},{9,... | collective-permute-start | bytes 1474568 | tf_op jit(solution)/shard_map/ppermute | solution.py:73
  17.3 2.6 %collective-permute-start.4 = (bf16[320,768]{1,0:T(8,128)(2,1)S(1)}, bf16[320,768]{1,0:T(8,128)(2,1)S(1)}, u32[]{:S(2)}, u32[]{:S(2)}) collective-permute-start(bf16[320,768]{1,0:T(8,128)(2,1)S(1)} %collective-permute-done.2.refs_2_.refs_5_), channel_id=1, source_target_pairs={{0,4},{1,5},{2,6},{3,7},{4,0},{5,1},{6,2},{7,3},{8,12},{9,13},{10,... | collective-permute-start | bytes 1474568 | tf_op jit(solution)/shard_map/ppermute | solution.py:73
  19.9 0.1 collective-permute-done.1.refs_1_.refs_4_
  20.0 3.5 %collective-permute-start.7 = (bf16[320,768]{1,0:T(8,128)(2,1)S(1)}, bf16[320,768]{1,0:T(8,128)(2,1)S(1)}, u32[]{:S(2)}, u32[]{:S(2)}) collective-permute-start(bf16[320,768]{1,0:T(8,128)(2,1)S(1)} %collective-permute-done.1.refs_1_.refs_4_), channel_id=1, source_target_pairs={{0,33},{1,32},{2,35},{3,34},{4,37},{5,36},{6,39},{7,38},{8,41},{9,... | collective-permute-start | bytes 1474568 | tf_op jit(solution)/shard_map/ppermute | solution.py:73
  23.5 1.5 %collective-permute-start.5 = (bf16[320,768]{1,0:T(8,128)(2,1)S(1)}, bf16[320,768]{1,0:T(8,128)(2,1)S(1)}, u32[]{:S(2)}, u32[]{:S(2)}) collective-permute-start(bf16[320,768]{1,0:T(8,128)(2,1)S(1)} %collective-permute-done.1.refs_1_.refs_4_), channel_id=1, source_target_pairs={{0,1},{1,0},{2,3},{3,2},{4,5},{5,4},{6,7},{7,6},{8,9},{9,8},{10,11... | collective-permute-start | bytes 1474568 | tf_op jit(solution)/shard_map/ppermute | solution.py:73
  25.0 0.5 collective-permute-start.14
  25.5 1.0 collective-permute-done.4.refs_4_.refs_7_
  26.5 0.2 collective-permute-start.12
  26.7 4.9 %collective-permute-done.7.refs_7_.refs_10_ = bf16[320,768]{1,0:T(8,128)(2,1)S(1)} collective-permute-done((bf16[320,768]{1,0:T(8,128)(2,1)S(1)}, bf16[320,768]{1,0:T(8,128)(2,1)S(1)}, u32[]{:S(2)}, u32[]{:S(2)}) %collective-permute-start.7) | collective-permute-done | bytes 491552 | tf_op jit(solution)/shard_map/ppermute | solution.py:73
  31.6 5.2 %collective-permute-done.5.refs_5_.refs_8_ = bf16[320,768]{1,0:T(8,128)(2,1)S(1)} collective-permute-done((bf16[320,768]{1,0:T(8,128)(2,1)S(1)}, bf16[320,768]{1,0:T(8,128)(2,1)S(1)}, u32[]{:S(2)}, u32[]{:S(2)}) %collective-permute-start.5) | collective-permute-done | bytes 491552 | tf_op jit(solution)/shard_map/ppermute | solution.py:73
  36.8 1.8 %collective-permute-done.13.refs_13_.refs_16_ = bf16[320,768]{1,0:T(8,128)(2,1)S(1)} collective-permute-done((bf16[320,768]{1,0:T(8,128)(2,1)S(1)}, bf16[320,768]{1,0:T(8,128)(2,1)S(1)}, u32[]{:S(2)}, u32[]{:S(2)}) %collective-permute-start.13) | collective-permute-done | bytes 491552 | tf_op jit(solution)/shard_map/ppermute | solution.py:77
  38.8 0.7 copy-done.20
  39.4 16.7 %scores.1 = (f32[8,320,1280]{2,1,0:T(8,128)}, f32[8,320]{1,0:T(8,128)}, f32[8,320]{1,0:T(8,128)}) custom-call(s32[1]{0:T(128)} %bitcast.core_ref, bf16[320,768]{1,0:T(8,128)(2,1)} %copy-done.3, bf16[320,768]{1,0:T(8,128)(2,1)} %copy-done.9, bf16[320,768]{1,0:T(8,128)(2,1)} %copy-done.7, bf16[320,768]{1,0:T(8,128)(2,1)} %copy-done.6, ...), custom_call_target="tpu_custom_call" | custom-call | flops 5033164800 | bytes 13107200 | tf_op jit(solution)/shard_map/scores/pallas_call | solution.py:169
  56.1 0.1 collective-permute-start.16
  56.2 1.4 collective-permute-done.16
  57.6 0.7 add_select_fusion
  58.3 0.6 broadcast_in_dim.2
  59.0 5.6 %all-to-all-start = ((f32[8,8,320]{2,1,0:T(8,128)}), f32[8,8,320]{2,1,0:T(8,128)S(1)}, u32[]{:S(2)}, u32[]{:S(2)}) async-start(f32[8,8,320]{2,1,0:T(8,128)} %broadcast_in_dim.2), calls=%async_computation | async-start | bytes 196608 | tf_op jit(solution)/shard_map/all_to_all | solution.py:334
  64.5 8.6 %all-to-all-done.got_ref = f32[8,8,320]{2,1,0:T(8,128)S(1)} async-done(((f32[8,8,320]{2,1,0:T(8,128)}), f32[8,8,320]{2,1,0:T(8,128)S(1)}, u32[]{:S(2)}, u32[]{:S(2)}) %all-to-all-start) | async-done | bytes 81952 | tf_op jit(solution)/shard_map/all_to_all | solution.py:334
  73.1 0.6 copy-done.4
  73.7 1.6 %merge.1.refs_1_ = f32[8,320]{1,0:T(8,128)} custom-call(s32[1]{0:T(128)} %bitcast.1.place_ref, f32[8,8,320]{2,1,0:T(8,128)} %copy-done.4), custom_call_target="tpu_custom_call" | custom-call | tf_op jit(solution)/shard_map/merge/pallas_call | solution.py:211
  75.3 1.4 collective-permute-done.17.refs_2_
  76.7 0.6 copy-done.21
  77.3 26.5 %grads.1 = (f32[8,320,768]{2,1,0:T(8,128)}, bf16[8,320,768]{2,1,0:T(8,128)(2,1)}, f32[320,768]{1,0:T(8,128)}) custom-call(s32[1]{0:T(128)} %bitcast.core_ref, f32[8,320,1280]{2,1,0:T(8,128)} %get-tuple-element.8.refs_0_, f32[8,320]{1,0:T(8,128)} %merge.1.refs_1_, f32[8,320]{1,0:T(8,128)} %copy-done.21, bf16[320,768]{1,0:T(8,128)(2,1)} %copy-done.3, ...), custom_call_target="tpu_custom_call" | custom-call | flops 10066329600 | bytes 13107200 | tf_op jit(solution)/shard_map/grads/pallas_call | solution.py:274
  103.8 2.3 %slice_bitcast_fusion.6 = (bf16[320,768]{1,0:T(8,128)(2,1)S(1)}, bf16[320,768]{1,0:T(8,128)(2,1)S(1)}, bf16[320,768]{1,0:T(8,128)(2,1)S(1)}, bf16[320,768]{1,0:T...) fusion(bf16[8,320,768]{2,1,0:T(8,128)(2,1)} %get-tuple-element.13), kind=kLoop, calls=%fused_computation.31 | loop fusion | bytes 6881280 | tf_op jit(solution)/shard_map/squeeze | solution.py:341
  106.1 0.1 collective-permute-start.22
  106.2 0.5 collective-permute-start.20
  106.7 0.1 collective-permute-start.19
  106.8 0.4 collective-permute-start.30
  107.2 0.1 collective-permute-start.26
  107.3 0.7 collective-permute-done.22
  108.1 0.7 collective-permute-done.20
  108.8 1.8 %fusion.7 = (bf16[320,768]{1,0:T(8,128)(2,1)S(1)}, bf16[320,768]{1,0:T(8,128)(2,1)S(1)}) fusion(bf16[320,768]{1,0:T(8,128)(2,1)S(1)} %collective-permute-done.20, f32[8,320,768]{2,1,0:T(8,128)} %get-tuple-element.11, bf16[320,768]{1,0:T(8,128)(2,1)S(1)} %collective-permute-done.22), kind=kLoop, calls=%fused_computation.13 | loop fusion | flops 1474560 | bytes 3932160 | tf_op jit(solution)/shard_map/convert_element_type | solution.py:348
  110.5 0.4 collective-permute-start.21
  110.9 2.3 %collective-permute-start.23 = (bf16[320,768]{1,0:T(8,128)(2,1)S(1)}, bf16[320,768]{1,0:T(8,128)(2,1)S(1)}, u32[]{:S(2)}, u32[]{:S(2)}) collective-permute-start(bf16[320,768]{1,0:T(8,128)(2,1)S(1)} %get-tuple-element.18), channel_id=1, source_target_pairs={{0,33},{1,32},{2,35},{3,34},{4,37},{5,36},{6,39},{7,38},{8,41},{9,... | collective-permute-start | bytes 1474568 | tf_op jit(solution)/shard_map/ppermute | solution.py:73
  113.2 0.0 copy-start.1
  113.2 0.0 copy-start.2
  113.2 0.5 collective-permute-start.25
  113.7 11.1 %collective-permute-done.21 = bf16[320,768]{1,0:T(8,128)(2,1)S(1)} collective-permute-done((bf16[320,768]{1,0:T(8,128)(2,1)S(1)}, bf16[320,768]{1,0:T(8,128)(2,1)S(1)}, u32[]{:S(2)}, u32[]{:S(2)}) %collective-permute-start.21) | collective-permute-done | bytes 491552 | tf_op jit(solution)/shard_map/ppermute | solution.py:73
  124.8 0.4 fusion.10
  125.2 0.2 collective-permute-start.31
  125.4 0.4 collective-permute-start.27
  125.9 2.3 %collective-permute-start.24 = (bf16[320,768]{1,0:T(8,128)(2,1)S(1)}, bf16[320,768]{1,0:T(8,128)(2,1)S(1)}, u32[]{:S(2)}, u32[]{:S(2)}) collective-permute-start(bf16[320,768]{1,0:T(8,128)(2,1)S(1)} %get-tuple-element.14), channel_id=1, source_target_pairs={{0,4},{1,5},{2,6},{3,7},{4,0},{5,1},{6,2},{7,3},{8,12},{9,13},{10,... | collective-permute-start | bytes 1474568 | tf_op jit(solution)/shard_map/ppermute | solution.py:73
  128.2 6.0 %collective-permute-done.31 = bf16[320,768]{1,0:T(8,128)(2,1)S(1)} collective-permute-done((bf16[320,768]{1,0:T(8,128)(2,1)S(1)}, bf16[320,768]{1,0:T(8,128)(2,1)S(1)}, u32[]{:S(2)}, u32[]{:S(2)}) %collective-permute-start.31) | collective-permute-done | bytes 491552 | tf_op jit(solution)/shard_map/ppermute | solution.py:73
  134.2 0.2 collective-permute-done.27
  134.3 0.3 fusion.5
  134.6 2.6 %collective-permute-start.28 = (bf16[320,768]{1,0:T(8,128)(2,1)S(1)}, bf16[320,768]{1,0:T(8,128)(2,1)S(1)}, u32[]{:S(2)}, u32[]{:S(2)}) collective-permute-start(bf16[320,768]{1,0:T(8,128)(2,1)S(1)} %get-tuple-element.19), channel_id=1, source_target_pairs={{0,32},{1,33},{2,34},{3,35},{4,36},{5,37},{6,38},{7,39},{8,40},{9,... | collective-permute-start | bytes 1474568 | tf_op jit(solution)/shard_map/ppermute | solution.py:73
  137.2 0.3 collective-permute-start.32
  137.5 2.1 %collective-permute-done.24 = bf16[320,768]{1,0:T(8,128)(2,1)S(1)} collective-permute-done((bf16[320,768]{1,0:T(8,128)(2,1)S(1)}, bf16[320,768]{1,0:T(8,128)(2,1)S(1)}, u32[]{:S(2)}, u32[]{:S(2)}) %collective-permute-start.24) | collective-permute-done | bytes 491552 | tf_op jit(solution)/shard_map/ppermute | solution.py:73
  139.6 4.0 %collective-permute-done.28 = bf16[320,768]{1,0:T(8,128)(2,1)S(1)} collective-permute-done((bf16[320,768]{1,0:T(8,128)(2,1)S(1)}, bf16[320,768]{1,0:T(8,128)(2,1)S(1)}, u32[]{:S(2)}, u32[]{:S(2)}) %collective-permute-start.28) | collective-permute-done | bytes 491552 | tf_op jit(solution)/shard_map/ppermute | solution.py:73
  143.6 2.5 %collective-permute-done.32 = bf16[320,768]{1,0:T(8,128)(2,1)S(1)} collective-permute-done((bf16[320,768]{1,0:T(8,128)(2,1)S(1)}, bf16[320,768]{1,0:T(8,128)(2,1)S(1)}, u32[]{:S(2)}, u32[]{:S(2)}) %collective-permute-start.32) | collective-permute-done | bytes 491552 | tf_op jit(solution)/shard_map/ppermute | solution.py:73
  146.1 0.2 fusion.13
  146.4 0.1 collective-permute-start.33
  146.5 1.9 %collective-permute-done.33 = f32[160,768]{1,0:T(8,128)S(1)} collective-permute-done((f32[160,768]{1,0:T(8,128)S(1)}, f32[160,768]{1,0:T(8,128)S(1)}, u32[]{:S(2)}, u32[]{:S(2)}) %collective-permute-start.33) | collective-permute-done | bytes 491552 | tf_op jit(solution)/shard_map/ppermute | solution.py:77
  148.4 1.1 convert_subtract_fusion
  (64 shorter events, 0.2 us)
Async XLA Ops:
  1.7 2.6 %collective-permute-start = (bf16[160,768]{1,0:T(8,128)(2,1)S(1)}, bf16[160,768]{1,0:T(8,128)(2,1)S(1)}, u32[]{:S(2)}, u32[]{:S(2)}) collective-permute-start(bf16[160,768]{1,0:T(8,128)(2,1)S(1)} %get-tuple-element.31), channel_id=1, source_target_pairs={{0,16},{1,17},{2,18},{3,19},{4,20},{5,21},{6,22},{7,23},{8,24},{9,... | collective-permute-start | bytes 737288 | tf_op jit(solution)/shard_map/ppermute | solution.py:77
  4.4 34.2 %copy-start.3 = (bf16[320,768]{1,0:T(8,128)(2,1)}, bf16[320,768]{1,0:T(8,128)(2,1)S(1)}, u32[]{:S(2)}) copy-start(bf16[320,768]{1,0:T(8,128)(2,1)S(1)} %pad_maximum_fusion.refs_0_.refs_3_) | copy-start | bytes 1474564
  4.4 10.1 %collective-permute-start.3 = (bf16[320,768]{1,0:T(8,128)(2,1)S(1)}, bf16[320,768]{1,0:T(8,128)(2,1)S(1)}, u32[]{:S(2)}, u32[]{:S(2)}) collective-permute-start(bf16[320,768]{1,0:T(8,128)(2,1)S(1)} %pad_maximum_fusion.refs_0_.refs_3_), channel_id=1, source_target_pairs={{0,1},{1,0},{2,3},{3,2},{4,5},{5,4},{6,7},{7,6},{8,9},{9,8},{10,11... | collective-permute-start | bytes 1474568 | tf_op jit(solution)/shard_map/ppermute | solution.py:73
  8.3 9.0 %collective-permute-start.2 = (bf16[320,768]{1,0:T(8,128)(2,1)S(1)}, bf16[320,768]{1,0:T(8,128)(2,1)S(1)}, u32[]{:S(2)}, u32[]{:S(2)}) collective-permute-start(bf16[320,768]{1,0:T(8,128)(2,1)S(1)} %pad_maximum_fusion.refs_0_.refs_3_), channel_id=1, source_target_pairs={{0,32},{1,33},{2,34},{3,35},{4,36},{5,37},{6,38},{7,39},{8,40},{9,... | collective-permute-start | bytes 1474568 | tf_op jit(solution)/shard_map/ppermute | solution.py:73
  11.1 6.2 %collective-permute-start.8 = (bf16[320,768]{1,0:T(8,128)(2,1)S(1)}, bf16[320,768]{1,0:T(8,128)(2,1)S(1)}, u32[]{:S(2)}, u32[]{:S(2)}) collective-permute-start(bf16[320,768]{1,0:T(8,128)(2,1)S(1)} %pad_maximum_fusion.refs_0_.refs_3_), channel_id=1, source_target_pairs={{0,16},{1,17},{2,18},{3,19},{4,20},{5,21},{6,22},{7,23},{8,24},{9,... | collective-permute-start | bytes 1474568 | tf_op jit(solution)/shard_map/ppermute | solution.py:77
  11.1 8.9 %collective-permute-start.1 = (bf16[320,768]{1,0:T(8,128)(2,1)S(1)}, bf16[320,768]{1,0:T(8,128)(2,1)S(1)}, u32[]{:S(2)}, u32[]{:S(2)}) collective-permute-start(bf16[320,768]{1,0:T(8,128)(2,1)S(1)} %pad_maximum_fusion.refs_0_.refs_3_), channel_id=1, source_target_pairs={{0,4},{1,5},{2,6},{3,7},{4,0},{5,1},{6,2},{7,3},{8,12},{9,13},{10,... | collective-permute-start | bytes 1474568 | tf_op jit(solution)/shard_map/ppermute | solution.py:73
  14.6 24.1 %copy-start.6 = (bf16[320,768]{1,0:T(8,128)(2,1)}, bf16[320,768]{1,0:T(8,128)(2,1)S(1)}, u32[]{:S(2)}) copy-start(bf16[320,768]{1,0:T(8,128)(2,1)S(1)} %collective-permute-done.3.refs_3_.refs_6_) | copy-start | bytes 1474564
  14.6 8.9 %collective-permute-start.11 = (bf16[320,768]{1,0:T(8,128)(2,1)S(1)}, bf16[320,768]{1,0:T(8,128)(2,1)S(1)}, u32[]{:S(2)}, u32[]{:S(2)}) collective-permute-start(bf16[320,768]{1,0:T(8,128)(2,1)S(1)} %collective-permute-done.3.refs_3_.refs_6_), channel_id=1, source_target_pairs={{0,16},{1,17},{2,18},{3,19},{4,20},{5,21},{6,22},{7,23},{8,24},{9,... | collective-permute-start | bytes 1474568 | tf_op jit(solution)/shard_map/ppermute | solution.py:77
  14.6 10.4 %collective-permute-start.6 = (bf16[320,768]{1,0:T(8,128)(2,1)S(1)}, bf16[320,768]{1,0:T(8,128)(2,1)S(1)}, u32[]{:S(2)}, u32[]{:S(2)}) collective-permute-start(bf16[320,768]{1,0:T(8,128)(2,1)S(1)} %collective-permute-done.3.refs_3_.refs_6_), channel_id=1, source_target_pairs={{0,32},{1,33},{2,34},{3,35},{4,36},{5,37},{6,38},{7,39},{8,40},{9,... | collective-permute-start | bytes 1474568 | tf_op jit(solution)/shard_map/ppermute | solution.py:73
  17.3 21.3 %copy-start.7 = (bf16[320,768]{1,0:T(8,128)(2,1)}, bf16[320,768]{1,0:T(8,128)(2,1)S(1)}, u32[]{:S(2)}) copy-start(bf16[320,768]{1,0:T(8,128)(2,1)S(1)} %collective-permute-done.2.refs_2_.refs_5_) | copy-start | bytes 1474564
  17.3 7.7 %collective-permute-start.10 = (bf16[320,768]{1,0:T(8,128)(2,1)S(1)}, bf16[320,768]{1,0:T(8,128)(2,1)S(1)}, u32[]{:S(2)}, u32[]{:S(2)}) collective-permute-start(bf16[320,768]{1,0:T(8,128)(2,1)S(1)} %collective-permute-done.2.refs_2_.refs_5_), channel_id=1, source_target_pairs={{0,16},{1,17},{2,18},{3,19},{4,20},{5,21},{6,22},{7,23},{8,24},{9,... | collective-permute-start | bytes 1474568 | tf_op jit(solution)/shard_map/ppermute | solution.py:77
  17.3 21.3 %copy-start.8 = (bf16[320,768]{1,0:T(8,128)(2,1)}, bf16[320,768]{1,0:T(8,128)(2,1)S(1)}, u32[]{:S(2)}) copy-start(bf16[320,768]{1,0:T(8,128)(2,1)S(1)} %collective-permute-done.8.refs_8_.refs_11_) | copy-start | bytes 1474564
  17.3 9.1 %collective-permute-start.4 = (bf16[320,768]{1,0:T(8,128)(2,1)S(1)}, bf16[320,768]{1,0:T(8,128)(2,1)S(1)}, u32[]{:S(2)}, u32[]{:S(2)}) collective-permute-start(bf16[320,768]{1,0:T(8,128)(2,1)S(1)} %collective-permute-done.2.refs_2_.refs_5_), channel_id=1, source_target_pairs={{0,4},{1,5},{2,6},{3,7},{4,0},{5,1},{6,2},{7,3},{8,12},{9,13},{10,... | collective-permute-start | bytes 1474568 | tf_op jit(solution)/shard_map/ppermute | solution.py:73
  20.0 18.7 %copy-start.9 = (bf16[320,768]{1,0:T(8,128)(2,1)}, bf16[320,768]{1,0:T(8,128)(2,1)S(1)}, u32[]{:S(2)}) copy-start(bf16[320,768]{1,0:T(8,128)(2,1)S(1)} %collective-permute-done.1.refs_1_.refs_4_) | copy-start | bytes 1474564
  20.0 11.6 %collective-permute-start.7 = (bf16[320,768]{1,0:T(8,128)(2,1)S(1)}, bf16[320,768]{1,0:T(8,128)(2,1)S(1)}, u32[]{:S(2)}, u32[]{:S(2)}) collective-permute-start(bf16[320,768]{1,0:T(8,128)(2,1)S(1)} %collective-permute-done.1.refs_1_.refs_4_), channel_id=1, source_target_pairs={{0,33},{1,32},{2,35},{3,34},{4,37},{5,36},{6,39},{7,38},{8,41},{9,... | collective-permute-start | bytes 1474568 | tf_op jit(solution)/shard_map/ppermute | solution.py:73
  23.4 15.2 %copy-start.10 = (bf16[320,768]{1,0:T(8,128)(2,1)}, bf16[320,768]{1,0:T(8,128)(2,1)S(1)}, u32[]{:S(2)}) copy-start(bf16[320,768]{1,0:T(8,128)(2,1)S(1)} %collective-permute-done.11.refs_11_.refs_14_) | copy-start | bytes 1474564
  23.5 13.3 %collective-permute-start.5 = (bf16[320,768]{1,0:T(8,128)(2,1)S(1)}, bf16[320,768]{1,0:T(8,128)(2,1)S(1)}, u32[]{:S(2)}, u32[]{:S(2)}) collective-permute-start(bf16[320,768]{1,0:T(8,128)(2,1)S(1)} %collective-permute-done.1.refs_1_.refs_4_), channel_id=1, source_target_pairs={{0,1},{1,0},{2,3},{3,2},{4,5},{5,4},{6,7},{7,6},{8,9},{9,8},{10,11... | collective-permute-start | bytes 1474568 | tf_op jit(solution)/shard_map/ppermute | solution.py:73
  25.0 13.7 %copy-start.11 = (bf16[320,768]{1,0:T(8,128)(2,1)}, bf16[320,768]{1,0:T(8,128)(2,1)S(1)}, u32[]{:S(2)}) copy-start(bf16[320,768]{1,0:T(8,128)(2,1)S(1)} %collective-permute-done.6.refs_6_.refs_9_) | copy-start | bytes 1474564
  25.0 11.8 %collective-permute-start.9 = (bf16[320,768]{1,0:T(8,128)(2,1)S(1)}, bf16[320,768]{1,0:T(8,128)(2,1)S(1)}, u32[]{:S(2)}, u32[]{:S(2)}) collective-permute-start(bf16[320,768]{1,0:T(8,128)(2,1)S(1)} %collective-permute-done.1.refs_1_.refs_4_), channel_id=1, source_target_pairs={{0,16},{1,17},{2,18},{3,19},{4,20},{5,21},{6,22},{7,23},{8,24},{9,... | collective-permute-start | bytes 1474568 | tf_op jit(solution)/shard_map/ppermute | solution.py:77
  25.0 13.7 %copy-start.12 = (bf16[320,768]{1,0:T(8,128)(2,1)}, bf16[320,768]{1,0:T(8,128)(2,1)S(1)}, u32[]{:S(2)}) copy-start(bf16[320,768]{1,0:T(8,128)(2,1)S(1)} %collective-permute-done.10.refs_10_.refs_13_) | copy-start | bytes 1474564
  25.0 11.8 %collective-permute-start.14 = (bf16[320,768]{1,0:T(8,128)(2,1)S(1)}, bf16[320,768]{1,0:T(8,128)(2,1)S(1)}, u32[]{:S(2)}, u32[]{:S(2)}) collective-permute-start(bf16[320,768]{1,0:T(8,128)(2,1)S(1)} %collective-permute-done.6.refs_6_.refs_9_), channel_id=1, source_target_pairs={{0,16},{1,17},{2,18},{3,19},{4,20},{5,21},{6,22},{7,23},{8,24},{9,... | collective-permute-start | bytes 1474568 | tf_op jit(solution)/shard_map/ppermute | solution.py:77
  26.5 12.2 %copy-start.13 = (bf16[320,768]{1,0:T(8,128)(2,1)}, bf16[320,768]{1,0:T(8,128)(2,1)S(1)}, u32[]{:S(2)}) copy-start(bf16[320,768]{1,0:T(8,128)(2,1)S(1)} %collective-permute-done.4.refs_4_.refs_7_) | copy-start | bytes 1474564
  26.5 10.3 %collective-permute-start.12 = (bf16[320,768]{1,0:T(8,128)(2,1)S(1)}, bf16[320,768]{1,0:T(8,128)(2,1)S(1)}, u32[]{:S(2)}, u32[]{:S(2)}) collective-permute-start(bf16[320,768]{1,0:T(8,128)(2,1)S(1)} %collective-permute-done.4.refs_4_.refs_7_), channel_id=1, source_target_pairs={{0,16},{1,17},{2,18},{3,19},{4,20},{5,21},{6,22},{7,23},{8,24},{9,... | collective-permute-start | bytes 1474568 | tf_op jit(solution)/shard_map/ppermute | solution.py:77
  31.6 7.1 %copy-start.14 = (bf16[320,768]{1,0:T(8,128)(2,1)}, bf16[320,768]{1,0:T(8,128)(2,1)S(1)}, u32[]{:S(2)}) copy-start(bf16[320,768]{1,0:T(8,128)(2,1)S(1)} %collective-permute-done.7.refs_7_.refs_10_) | copy-start | bytes 1474564
  31.6 5.2 %collective-permute-start.15 = (bf16[320,768]{1,0:T(8,128)(2,1)S(1)}, bf16[320,768]{1,0:T(8,128)(2,1)S(1)}, u32[]{:S(2)}, u32[]{:S(2)}) collective-permute-start(bf16[320,768]{1,0:T(8,128)(2,1)S(1)} %collective-permute-done.7.refs_7_.refs_10_), channel_id=1, source_target_pairs={{0,16},{1,17},{2,18},{3,19},{4,20},{5,21},{6,22},{7,23},{8,24},{9,... | collective-permute-start | bytes 1474568 | tf_op jit(solution)/shard_map/ppermute | solution.py:77
  36.8 2.0 %copy-start.15 = (bf16[320,768]{1,0:T(8,128)(2,1)}, bf16[320,768]{1,0:T(8,128)(2,1)S(1)}, u32[]{:S(2)}) copy-start(bf16[320,768]{1,0:T(8,128)(2,1)S(1)} %collective-permute-done.5.refs_5_.refs_8_) | copy-start | bytes 1474564
  36.8 1.9 %collective-permute-start.13 = (bf16[320,768]{1,0:T(8,128)(2,1)S(1)}, bf16[320,768]{1,0:T(8,128)(2,1)S(1)}, u32[]{:S(2)}, u32[]{:S(2)}) collective-permute-start(bf16[320,768]{1,0:T(8,128)(2,1)S(1)} %collective-permute-done.5.refs_5_.refs_8_), channel_id=1, source_target_pairs={{0,16},{1,17},{2,18},{3,19},{4,20},{5,21},{6,22},{7,23},{8,24},{9,... | collective-permute-start | bytes 1474568 | tf_op jit(solution)/shard_map/ppermute | solution.py:77
  36.8 2.0 %copy-start.16 = (bf16[320,768]{1,0:T(8,128)(2,1)}, bf16[320,768]{1,0:T(8,128)(2,1)S(1)}, u32[]{:S(2)}) copy-start(bf16[320,768]{1,0:T(8,128)(2,1)S(1)} %collective-permute-done.9.refs_9_.refs_12_) | copy-start | bytes 1474564
  36.8 1.9 %copy-start.17 = (bf16[320,768]{1,0:T(8,128)(2,1)}, bf16[320,768]{1,0:T(8,128)(2,1)S(1)}, u32[]{:S(2)}) copy-start(bf16[320,768]{1,0:T(8,128)(2,1)S(1)} %collective-permute-done.14.refs_14_.refs_17_) | copy-start | bytes 1474564
  36.8 1.9 %copy-start.18 = (bf16[320,768]{1,0:T(8,128)(2,1)}, bf16[320,768]{1,0:T(8,128)(2,1)S(1)}, u32[]{:S(2)}) copy-start(bf16[320,768]{1,0:T(8,128)(2,1)S(1)} %collective-permute-done.12.refs_12_.refs_15_) | copy-start | bytes 1474564
  36.8 1.9 %copy-start.19 = (bf16[320,768]{1,0:T(8,128)(2,1)}, bf16[320,768]{1,0:T(8,128)(2,1)S(1)}, u32[]{:S(2)}) copy-start(bf16[320,768]{1,0:T(8,128)(2,1)S(1)} %collective-permute-done.15.refs_15_.refs_18_) | copy-start | bytes 1474564
  38.6 0.8 copy-start.20
  56.1 1.5 collective-permute-start.16
  59.0 14.1 %all-to-all-start = ((f32[8,8,320]{2,1,0:T(8,128)}), f32[8,8,320]{2,1,0:T(8,128)S(1)}, u32[]{:S(2)}, u32[]{:S(2)}) async-start(f32[8,8,320]{2,1,0:T(8,128)} %broadcast_in_dim.2), calls=%async_computation | async-start | bytes 196608 | tf_op jit(solution)/shard_map/all_to_all | solution.py:334
  73.1 0.6 copy-start.4
  75.3 1.4 collective-permute-start.17
  76.7 0.6 copy-start.21
  103.8 21.0 %copy-start = (f32[8,320,768]{2,1,0:T(8,128)S(1)}, f32[8,320,768]{2,1,0:T(8,128)}, u32[]{:S(2)}) copy-start(f32[8,320,768]{2,1,0:T(8,128)} %get-tuple-element.11) | copy-start | bytes 23592964
  103.8 22.0 %copy-start.5 = (f32[320,768]{1,0:T(8,128)S(1)}, f32[320,768]{1,0:T(8,128)}, u32[]{:S(2)}) copy-start(f32[320,768]{1,0:T(8,128)} %get-tuple-element.12) | copy-start | bytes 2949124
  106.1 1.9 %collective-permute-start.22 = (bf16[320,768]{1,0:T(8,128)(2,1)S(1)}, bf16[320,768]{1,0:T(8,128)(2,1)S(1)}, u32[]{:S(2)}, u32[]{:S(2)}) collective-permute-start(bf16[320,768]{1,0:T(8,128)(2,1)S(1)} %get-tuple-element.26), channel_id=1, source_target_pairs={{0,16},{1,17},{2,18},{3,19},{4,20},{5,21},{6,22},{7,23},{8,24},{9,... | collective-permute-start | bytes 1474568 | tf_op jit(solution)/shard_map/ppermute | solution.py:77
  106.2 2.6 %collective-permute-start.20 = (bf16[320,768]{1,0:T(8,128)(2,1)S(1)}, bf16[320,768]{1,0:T(8,128)(2,1)S(1)}, u32[]{:S(2)}, u32[]{:S(2)}) collective-permute-start(bf16[320,768]{1,0:T(8,128)(2,1)S(1)} %get-tuple-element.27), channel_id=1, source_target_pairs={{0,16},{1,17},{2,18},{3,19},{4,20},{5,21},{6,22},{7,23},{8,24},{9,... | collective-permute-start | bytes 1474568 | tf_op jit(solution)/shard_map/ppermute | solution.py:77
  106.7 6.4 %collective-permute-start.19 = (bf16[320,768]{1,0:T(8,128)(2,1)S(1)}, bf16[320,768]{1,0:T(8,128)(2,1)S(1)}, u32[]{:S(2)}, u32[]{:S(2)}) collective-permute-start(bf16[320,768]{1,0:T(8,128)(2,1)S(1)} %get-tuple-element.21), channel_id=1, source_target_pairs={{0,16},{1,17},{2,18},{3,19},{4,20},{5,21},{6,22},{7,23},{8,24},{9,... | collective-permute-start | bytes 1474568 | tf_op jit(solution)/shard_map/ppermute | solution.py:77
  106.8 6.4 %collective-permute-start.30 = (bf16[320,768]{1,0:T(8,128)(2,1)S(1)}, bf16[320,768]{1,0:T(8,128)(2,1)S(1)}, u32[]{:S(2)}, u32[]{:S(2)}) collective-permute-start(bf16[320,768]{1,0:T(8,128)(2,1)S(1)} %get-tuple-element.22), channel_id=1, source_target_pairs={{0,16},{1,17},{2,18},{3,19},{4,20},{5,21},{6,22},{7,23},{8,24},{9,... | collective-permute-start | bytes 1474568 | tf_op jit(solution)/shard_map/ppermute | solution.py:77
  107.2 6.5 %collective-permute-start.26 = (bf16[320,768]{1,0:T(8,128)(2,1)S(1)}, bf16[320,768]{1,0:T(8,128)(2,1)S(1)}, u32[]{:S(2)}, u32[]{:S(2)}) collective-permute-start(bf16[320,768]{1,0:T(8,128)(2,1)S(1)} %get-tuple-element.24), channel_id=1, source_target_pairs={{0,16},{1,17},{2,18},{3,19},{4,20},{5,21},{6,22},{7,23},{8,24},{9,... | collective-permute-start | bytes 1474568 | tf_op jit(solution)/shard_map/ppermute | solution.py:77
  110.5 14.2 %collective-permute-start.21 = (bf16[320,768]{1,0:T(8,128)(2,1)S(1)}, bf16[320,768]{1,0:T(8,128)(2,1)S(1)}, u32[]{:S(2)}, u32[]{:S(2)}) collective-permute-start(bf16[320,768]{1,0:T(8,128)(2,1)S(1)} %get-tuple-element.17), channel_id=1, source_target_pairs={{0,1},{1,0},{2,3},{3,2},{4,5},{5,4},{6,7},{7,6},{8,9},{9,8},{10,11... | collective-permute-start | bytes 1474568 | tf_op jit(solution)/shard_map/ppermute | solution.py:73
  110.9 13.9 %collective-permute-start.23 = (bf16[320,768]{1,0:T(8,128)(2,1)S(1)}, bf16[320,768]{1,0:T(8,128)(2,1)S(1)}, u32[]{:S(2)}, u32[]{:S(2)}) collective-permute-start(bf16[320,768]{1,0:T(8,128)(2,1)S(1)} %get-tuple-element.18), channel_id=1, source_target_pairs={{0,33},{1,32},{2,35},{3,34},{4,37},{5,36},{6,39},{7,38},{8,41},{9,... | collective-permute-start | bytes 1474568 | tf_op jit(solution)/shard_map/ppermute | solution.py:73
  113.2 12.7 %collective-permute-start.29 = (bf16[320,768]{1,0:T(8,128)(2,1)S(1)}, bf16[320,768]{1,0:T(8,128)(2,1)S(1)}, u32[]{:S(2)}, u32[]{:S(2)}) collective-permute-start(bf16[320,768]{1,0:T(8,128)(2,1)S(1)} %get-tuple-element.23), channel_id=1, source_target_pairs={{0,16},{1,17},{2,18},{3,19},{4,20},{5,21},{6,22},{7,23},{8,24},{9,... | collective-permute-start | bytes 1474568 | tf_op jit(solution)/shard_map/ppermute | solution.py:77
  113.2 35.2 %copy-start.1 = (bf16[160,768]{1,0:T(8,128)(2,1)S(1)}, bf16[160,768]{1,0:T(8,128)(2,1)}, u32[]{:S(2)}) copy-start(bf16[160,768]{1,0:T(8,128)(2,1)} %param.2) | copy-start | bytes 737284
  113.2 35.2 %copy-start.2 = (bf16[160,768]{1,0:T(8,128)(2,1)S(1)}, bf16[160,768]{1,0:T(8,128)(2,1)}, u32[]{:S(2)}) copy-start(bf16[160,768]{1,0:T(8,128)(2,1)} %param.3) | copy-start | bytes 737284
  113.2 15.0 %collective-permute-start.25 = (bf16[320,768]{1,0:T(8,128)(2,1)S(1)}, bf16[320,768]{1,0:T(8,128)(2,1)S(1)}, u32[]{:S(2)}, u32[]{:S(2)}) collective-permute-start(bf16[320,768]{1,0:T(8,128)(2,1)S(1)} %get-tuple-element.25), channel_id=1, source_target_pairs={{0,16},{1,17},{2,18},{3,19},{4,20},{5,21},{6,22},{7,23},{8,24},{9,... | collective-permute-start | bytes 1474568 | tf_op jit(solution)/shard_map/ppermute | solution.py:77
  125.2 9.0 %collective-permute-start.31 = (bf16[320,768]{1,0:T(8,128)(2,1)S(1)}, bf16[320,768]{1,0:T(8,128)(2,1)S(1)}, u32[]{:S(2)}, u32[]{:S(2)}) collective-permute-start(bf16[320,768]{1,0:T(8,128)(2,1)S(1)} %get-tuple-element.15), channel_id=1, source_target_pairs={{0,32},{1,33},{2,34},{3,35},{4,36},{5,37},{6,38},{7,39},{8,40},{9,... | collective-permute-start | bytes 1474568 | tf_op jit(solution)/shard_map/ppermute | solution.py:73
  125.4 8.9 %collective-permute-start.27 = (bf16[320,768]{1,0:T(8,128)(2,1)S(1)}, bf16[320,768]{1,0:T(8,128)(2,1)S(1)}, u32[]{:S(2)}, u32[]{:S(2)}) collective-permute-start(bf16[320,768]{1,0:T(8,128)(2,1)S(1)} %get-tuple-element.16), channel_id=1, source_target_pairs={{0,4},{1,5},{2,6},{3,7},{4,0},{5,1},{6,2},{7,3},{8,12},{9,13},{10,... | collective-permute-start | bytes 1474568 | tf_op jit(solution)/shard_map/ppermute | solution.py:73
  125.9 11.7 %collective-permute-start.18 = (f32[320,768]{1,0:T(8,128)S(1)}, f32[320,768]{1,0:T(8,128)S(1)}, u32[]{:S(2)}, u32[]{:S(2)}) collective-permute-start(f32[320,768]{1,0:T(8,128)S(1)} %copy-done.5), channel_id=1, source_target_pairs={{0,16},{1,17},{2,18},{3,19},{4,20},{5,21},{6,22},{7,23},{8,24},{9,... | collective-permute-start | bytes 2949128 | tf_op jit(solution)/shard_map/ppermute | solution.py:77
  125.9 13.7 %collective-permute-start.24 = (bf16[320,768]{1,0:T(8,128)(2,1)S(1)}, bf16[320,768]{1,0:T(8,128)(2,1)S(1)}, u32[]{:S(2)}, u32[]{:S(2)}) collective-permute-start(bf16[320,768]{1,0:T(8,128)(2,1)S(1)} %get-tuple-element.14), channel_id=1, source_target_pairs={{0,4},{1,5},{2,6},{3,7},{4,0},{5,1},{6,2},{7,3},{8,12},{9,13},{10,... | collective-permute-start | bytes 1474568 | tf_op jit(solution)/shard_map/ppermute | solution.py:73
  134.6 9.0 %collective-permute-start.28 = (bf16[320,768]{1,0:T(8,128)(2,1)S(1)}, bf16[320,768]{1,0:T(8,128)(2,1)S(1)}, u32[]{:S(2)}, u32[]{:S(2)}) collective-permute-start(bf16[320,768]{1,0:T(8,128)(2,1)S(1)} %get-tuple-element.19), channel_id=1, source_target_pairs={{0,32},{1,33},{2,34},{3,35},{4,36},{5,37},{6,38},{7,39},{8,40},{9,... | collective-permute-start | bytes 1474568 | tf_op jit(solution)/shard_map/ppermute | solution.py:73
  137.2 8.9 %collective-permute-start.32 = (bf16[320,768]{1,0:T(8,128)(2,1)S(1)}, bf16[320,768]{1,0:T(8,128)(2,1)S(1)}, u32[]{:S(2)}, u32[]{:S(2)}) collective-permute-start(bf16[320,768]{1,0:T(8,128)(2,1)S(1)} %get-tuple-element.20), channel_id=1, source_target_pairs={{0,1},{1,0},{2,3},{3,2},{4,5},{5,4},{6,7},{7,6},{8,9},{9,8},{10,11... | collective-permute-start | bytes 1474568 | tf_op jit(solution)/shard_map/ppermute | solution.py:73
  146.4 1.9 %collective-permute-start.33 = (f32[160,768]{1,0:T(8,128)S(1)}, f32[160,768]{1,0:T(8,128)S(1)}, u32[]{:S(2)}, u32[]{:S(2)}) collective-permute-start(f32[160,768]{1,0:T(8,128)S(1)} %slice.69), channel_id=1, source_target_pairs={{0,16},{1,17},{2,18},{3,19},{4,20},{5,21},{6,22},{7,23},{8,24},{9,... | collective-permute-start | bytes 1474568 | tf_op jit(solution)/shard_map/ppermute | solution.py:77

commit v2 on v1

v2 whole, which is shorter than its diff:
```python
import functools
import math

import jax
import jax.numpy as jnp
from jax import lax
from jax.experimental import pallas as pl
from jax.experimental.pallas import tpu as pltpu
from jax.sharding import Mesh, PartitionSpec as P

AXES = ("y", "core", "x", "z")
SIZES = (4, 2, 4, 4)
ORDER = (0, 1, 2, 4, 3, 5, 6, 7)
PLACE = tuple(ORDER.index(m) for m in range(8))
LOG2E = 1.4426950408889634
VMEM_LIMIT = 36 * 1024 * 1024
RANGE = 60.0


def flat(y, c, x, z):
    return ((y * 2 + c) * 4 + x) * 4 + z


def coords():
    for y in range(4):
        for c in range(2):
            for x in range(4):
                for z in range(4):
                    yield y, c, x, z


def partner(v, c):
    return v ^ 1 if c == 0 else 3 - v


def across(m):
    pairs = []
    for y, c, x, z in coords():
        target = (
            partner(y, c) if m & 2 else y,
            c,
            partner(x, c) if m & 1 else x,
            partner(z, c) if m & 4 else z,
        )
        pairs.append((flat(y, c, x, z), flat(*target)))
    return pairs


SWAP = [(flat(y, c, x, z), flat(y, 1 - c, x, z)) for y, c, x, z in coords()]


def cube_groups():
    groups = []
    seen = set()
    for y, c, x, z in coords():
        members = []
        for m in range(8):
            yy = partner(y, c) if m & 2 else y
            xx = partner(x, c) if m & 1 else x
            zz = partner(z, c) if m & 4 else z
            place = (xx & 1) | ((yy & 1) << 1) | ((zz & 1) << 2)
            members.append((place, flat(yy, c, xx, zz)))
        key = tuple(d for _, d in sorted(members))
        if key not in seen:
            seen.add(key)
            groups.append(list(key))
    return groups


GROUPS = cube_groups()


def to_cube(a, m):
    return lax.ppermute(a, AXES, across(m))


def swap(a):
    return lax.ppermute(a, AXES, SWAP)


def column_of(row, rows):
    padded = -(-rows // 128) * 128
    wide = jnp.broadcast_to(row, (128, rows))
    if padded != rows:
        wide = jnp.concatenate([wide, jnp.zeros((128, padded - rows), jnp.float32)], axis=1)
    return wide.T[:rows, :1]


def row_of(column, rows):
    padded = -(-rows // 128) * 128
    wide = jnp.broadcast_to(column, (rows, 128))
    if padded != rows:
        wide = jnp.concatenate([wide, jnp.zeros((padded - rows, 128), jnp.float32)], axis=0)
    return wide.T[:1, :rows]


def any_spec():
    return pl.BlockSpec(memory_space=pl.ANY)


def vmem_spec():
    return pl.BlockSpec(memory_space=pltpu.VMEM)


def smem_spec():
    return pl.BlockSpec(memory_space=pltpu.SMEM)


def cost(matmuls, rows, cols, depth, passes=0):
    return pl.CostEstimate(
        flops=2 * matmuls * rows * cols * depth, bytes_accessed=passes * rows * cols, transcendentals=0
    )


def params():
    return pltpu.CompilerParams(vmem_limit_bytes=VMEM_LIMIT)


def dot_nt(a, b):
    return lax.dot_general(a, b, (((1,), (1,)), ((), ())), preferred_element_type=jnp.float32)


def dot_tn(a, b):
    return lax.dot_general(a, b, (((0,), (0,)), ((), ())), preferred_element_type=jnp.float32)


def join_kernel(b0, b1, b2, b3, out, sem):
    rows = b0.shape[0]
    copies = [
        pltpu.make_async_copy(b, out.at[pl.ds(j * rows, rows)], sem.at[j]) for j, b in enumerate((b0, b1, b2, b3))
    ]
    for c in copies:
        c.start()
    for c in copies:
        c.wait()


def join_call(blocks):
    rows, features = blocks[0].shape
    return pl.pallas_call(
        join_kernel,
        in_specs=[any_spec()] * 4,
        out_specs=any_spec(),
        out_shape=jax.ShapeDtypeStruct((4 * rows, features), blocks[0].dtype),
        scratch_shapes=[pltpu.SemaphoreType.DMA((4,))],
        name="join",
    )(*blocks)


def scores_kernel(scale, core_ref, a_lo, b_lo, *refs):
    a_hi, b_hi = refs[:4], refs[4:8]
    e_ref, a_cat, b_cat, a_stat, b_stat, flags, col_m, col_s, sem = refs[8:]
    rows = a_hi[0].shape[0]
    half = 4 * rows
    core = core_ref[0]

    def copies_a(h):
        if h == 0:
            return [pltpu.make_async_copy(a_lo, a_cat.at[0], sem.at[0])]
        return [pltpu.make_async_copy(a_hi[j], a_cat.at[1, pl.ds(j * rows, rows)], sem.at[1 + j]) for j in range(4)]

    def copies_b(h):
        place = core if h == 0 else 1 - core
        if h == 0:
            return [pltpu.make_async_copy(b_lo, b_cat.at[place], sem.at[5])]
        return [
            pltpu.make_async_copy(b_hi[j], b_cat.at[place, pl.ds(j * rows, rows)], sem.at[6 + j]) for j in range(4)
        ]

    for c in copies_b(0) + copies_a(0) + copies_b(1) + copies_a(1):
        c.start()

    def quadrant(q):
        for c in copies_a(q):
            c.wait()
        for h in range(2):

            @pl.when((h ^ core) == q)
            def _():
                for c in copies_b(h):
                    c.wait()

        b_half = b_cat[q]
        sums = []
        col = None
        for r in range(4):
            sl = slice(r * rows, (r + 1) * rows)
            e = jnp.exp2(dot_nt(a_cat[q, sl, :], b_half) * scale)
            e_ref[q, sl, :] = e
            sums.append(jnp.sum(e, axis=1, keepdims=True))
            part = jnp.sum(e, axis=0, keepdims=True)
            col = part if col is None else col + part
        row_lse = jnp.log2(row_of(jnp.concatenate(sums, axis=0), half))
        col_lse = jnp.log2(col)
        for j in range(4):
            sl = slice(j * rows, (j + 1) * rows)
            a_stat[4 * q + j : 4 * q + j + 1, :] = row_lse[:, sl]
            b_stat[pl.ds((q ^ core) * 4 + j, 1), :] = col_lse[:, sl]
        reach = jnp.max(jnp.maximum(jnp.abs(row_lse), jnp.abs(col_lse)))
        bad = jnp.logical_not(reach <= RANGE)
        flags[q] = bad.astype(jnp.int32)

        @pl.when(bad)
        def _():
            col_m[...] = jnp.full_like(col_m, -jnp.inf)
            col_s[...] = jnp.zeros_like(col_s)

            @pl.loop(0, 4)
            def _(r):
                sl = pl.ds(pl.multiple_of(r * rows, 16), rows)
                s = dot_nt(a_cat[q, sl, :], b_cat[q]) * scale
                e_ref[q, sl, :] = s
                row_m = jnp.max(s, axis=1, keepdims=True)
                row_s = jnp.sum(jnp.exp2(s - row_m), axis=1, keepdims=True)
                a_stat[pl.ds(4 * q + r, 1), :] = row_of(row_m + jnp.log2(row_s), rows)
                blk_m = jnp.max(s, axis=0, keepdims=True)
                blk_s = jnp.sum(jnp.exp2(s - blk_m), axis=0, keepdims=True)
                before = col_m[...]
                top = jnp.maximum(before, blk_m)
                col_s[...] = col_s[...] * jnp.exp2(before - top) + blk_s * jnp.exp2(blk_m - top)
                col_m[...] = top

            lse = col_m[...] + jnp.log2(col_s[...])
            for j in range(4):
                b_stat[pl.ds((q ^ core) * 4 + j, 1), :] = lse[:, j * rows : (j + 1) * rows]

    quadrant(0)
    quadrant(1)


def scores_call(core, a_lo, b_lo, a_hi, b_hi, scale):
    rows, features = a_hi[0].shape
    half = 4 * rows
    stat = jax.ShapeDtypeStruct((8, rows), jnp.float32)
    return pl.pallas_call(
        functools.partial(scores_kernel, scale),
        in_specs=[smem_spec()] + [any_spec()] * 10,
        out_specs=[vmem_spec()] * 5 + [smem_spec()],
        out_shape=[
            pltpu.VMEM((2, half, half), jnp.float32),
            pltpu.VMEM((2, half, features), jnp.bfloat16),
            pltpu.VMEM((2, half, features), jnp.bfloat16),
            stat,
            stat,
            jax.ShapeDtypeStruct((2,), jnp.int32),
        ],
        scratch_shapes=[
            pltpu.VMEM((1, half), jnp.float32),
            pltpu.VMEM((1, half), jnp.float32),
            pltpu.SemaphoreType.DMA((10,)),
        ],
        compiler_params=params(),
        cost_estimate=cost(2, half, half, features),
        name="scores",
    )(core, a_lo, b_lo, *a_hi, *b_hi)


def merge_kernel(place_ref, got_ref, out_ref):
    me = place_ref[0]
    for m in range(8):
        parts = []
        for k in range(8):
            offset = (me ^ k) ^ m
            row = jnp.int32(0)
            for n in range(8):
                row = jnp.where(offset == n, PLACE[n], row)
            parts.append(got_ref[k, pl.ds(row, 1), :])
        top = functools.reduce(jnp.maximum, parts)
        total = functools.reduce(jnp.add, [jnp.exp2(p - top) for p in parts])
        out_ref[PLACE[m] : PLACE[m] + 1, :] = top + jnp.log2(total)


def merge_call(place, got):
    return pl.pallas_call(
        merge_kernel,
        in_specs=[pl.BlockSpec(memory_space=pltpu.SMEM), pl.BlockSpec(memory_space=pltpu.VMEM)],
        out_specs=pl.BlockSpec(memory_space=pltpu.VMEM),
        out_shape=jax.ShapeDtypeStruct(got.shape[1:], jnp.float32),
        name="merge",
    )(place, got)


def weights_kernel(core_ref, flags, e_ref, a_lse, b_lse, a_cat, w_ref, gb_hi):
    rows = a_lse.shape[1]
    half = 4 * rows
    core = core_ref[0]
    for q in range(2):
        a_row = jnp.concatenate([a_lse[4 * q + j : 4 * q + j + 1, :] for j in range(4)], axis=1)
        b_row = jnp.concatenate([b_lse[pl.ds((q ^ core) * 4 + j, 1), :] for j in range(4)], axis=1)

        @pl.when(flags[q] == 0)
        def _():
            a_col = column_of(jnp.exp2(-a_row), half)
            b_exp = jnp.exp2(-b_row)
            for r in range(4):
                sl = slice(r * rows, (r + 1) * rows)
                w_ref[q, sl, :] = (e_ref[q, sl, :] * (a_col[sl, :] + b_exp)).astype(jnp.bfloat16)

        @pl.when(flags[q] != 0)
        def _():
            a_col = column_of(a_row, half)
            for r in range(4):
                sl = slice(r * rows, (r + 1) * rows)
                s = e_ref[q, sl, :]
                w_ref[q, sl, :] = (jnp.exp2(s - a_col[sl, :]) + jnp.exp2(s - b_row)).astype(jnp.bfloat16)

    q = 1 - core
    gb_hi[...] = (0.5 * dot_tn(w_ref[q], a_cat[q])).astype(jnp.bfloat16)


def weights_call(core, flags, e, a_lse, b_lse, a_cat):
    _, half, features = a_cat.shape
    return pl.pallas_call(
        weights_kernel,
        in_specs=[smem_spec()] * 2 + [vmem_spec()] * 4,
        out_specs=[vmem_spec()] * 2,
        out_shape=[
            pltpu.VMEM((2, half, half), jnp.bfloat16),
            jax.ShapeDtypeStruct((half, features), jnp.bfloat16),
        ],
        compiler_params=params(),
        cost_estimate=cost(1, half, half, features, 12),
        name="weights",
    )(core, flags, e, a_lse, b_lse, a_cat)


def middle_kernel(core_ref, w_ref, a_cat, b_cat, ga_hi, gb0, gb_lo):
    rows = gb0.shape[0]
    q = core_ref[0]
    g = 0.5 * dot_tn(w_ref[q], a_cat[q])
    gb0[...] = g[:rows]
    gb_lo[...] = g[rows:].astype(jnp.bfloat16)
    ga_hi[...] = 0.5 * jnp.dot(w_ref[1], b_cat[1], preferred_element_type=jnp.float32)


def middle_call(core, w, a_cat, b_cat):
    _, half, features = a_cat.shape
    rows = half // 4
    return pl.pallas_call(
        middle_kernel,
        in_specs=[smem_spec()] + [vmem_spec()] * 3,
        out_specs=[vmem_spec()] * 3,
        out_shape=[
            pltpu.VMEM((half, features), jnp.float32),
            jax.ShapeDtypeStruct((rows, features), jnp.float32),
            jax.ShapeDtypeStruct((half - rows, features), jnp.bfloat16),
        ],
        compiler_params=params(),
        cost_estimate=cost(2, half, half, features),
        name="middle",
    )(core, w, a_cat, b_cat)


def far_kernel(ga_hi, got, *outs):
    rows = outs[0].shape[0]
    for j in range(4):
        sl = slice(j * rows, (j + 1) * rows)
        outs[j][...] = (ga_hi[sl, :] + got[sl, :].astype(jnp.float32)).astype(jnp.bfloat16)


def far_call(ga_hi, got):
    half, features = ga_hi.shape
    rows = half // 4
    return pl.pallas_call(
        far_kernel,
        in_specs=[vmem_spec()] * 2,
        out_specs=[vmem_spec()] * 4,
        out_shape=[jax.ShapeDtypeStruct((rows, features), jnp.bfloat16)] * 4,
        compiler_params=params(),
        cost_estimate=cost(0, half, features, 1, 8),
        name="far",
    )(ga_hi, got)


def last_kernel(w_ref, b_cat, ga_lo):
    ga_lo[...] = 0.5 * jnp.dot(w_ref[0], b_cat[0], preferred_element_type=jnp.float32)


def last_call(w, b_cat):
    _, half, features = b_cat.shape
    return pl.pallas_call(
        last_kernel,
        in_specs=[vmem_spec()] * 2,
        out_specs=vmem_spec(),
        out_shape=pltpu.VMEM((half, features), jnp.float32),
        compiler_params=params(),
        cost_estimate=cost(1, half, half, features),
        name="last",
    )(w, b_cat)


def near_kernel(ga_lo, got0, got_lo, r_xy, r_yz, r_xz, r_xyz, p0, p1, p2, p4):
    rows = p0.shape[0]
    wide = lambda ref: ref[...].astype(jnp.float32)
    p0[...] = ga_lo[:rows] + got0[...]
    part = lambda j: ga_lo[j * rows : (j + 1) * rows, :] + got_lo[(j - 1) * rows : j * rows, :].astype(jnp.float32)
    p1[...] = (part(1) + wide(r_xz) + wide(r_xyz)).astype(jnp.bfloat16)
    p2[...] = (part(2) + wide(r_xy)).astype(jnp.bfloat16)
    p4[...] = (part(3) + wide(r_yz)).astype(jnp.bfloat16)


def near_call(ga_lo, got0, got_lo, *received):
    rows, features = got0.shape
    narrow = jax.ShapeDtypeStruct((rows, features), jnp.bfloat16)
    return pl.pallas_call(
        near_kernel,
        in_specs=[vmem_spec()] * 7,
        out_specs=[vmem_spec()] * 4,
        out_shape=[pltpu.VMEM((rows, features), jnp.float32)] + [narrow] * 3,
        compiler_params=params(),
        cost_estimate=cost(0, 4 * rows, features, 1, 12),
        name="near",
    )(ga_lo, got0, got_lo, *received)


def body(images, texts):
    rows, features = images.shape
    scale = 4.0 / math.sqrt(features) * LOG2E
    core = lax.axis_index("core")
    first = core == 0
    core_arr = core.astype(jnp.int32).reshape(1)
    place = (
        (lax.axis_index("x") & 1) | ((lax.axis_index("y") & 1) << 1) | ((lax.axis_index("z") & 1) << 2)
    ).astype(jnp.int32).reshape(1)

    mine = jnp.where(first, images, texts)
    other = swap(jnp.where(first, texts, images))
    own = jnp.concatenate([mine, other], axis=0)
    near = {m: to_cube(own, m) for m in (1, 2, 4)}
    far = {3: to_cube(near[2], 1), 6: to_cube(near[4], 2), 5: to_cube(near[1], 4), 7: to_cube(near[1], 6)}
    a_lo = join_call([own, near[1], near[2], near[4]])
    b_lo = swap(a_lo)
    a_hi = [far[m] for m in ORDER[4:]]
    b_hi = [swap(a) for a in a_hi]

    e, a_cat, b_cat, a_stat, b_stat, flags = scores_call(core_arr, a_lo, b_lo, a_hi, b_hi, scale)
    chip_stat = jnp.logaddexp2(a_stat, swap(b_stat))
    got = lax.all_to_all(
        jnp.broadcast_to(chip_stat[None], (8,) + chip_stat.shape), AXES, 0, 0, axis_index_groups=GROUPS
    )
    a_lse = merge_call(place, got)
    b_lse = swap(a_lse)

    w, gb_hi = weights_call(core_arr, flags, e, a_lse, b_lse, a_cat)
    got_hi = swap(gb_hi)
    ga_hi, gb0, gb_lo = middle_call(core_arr, w, a_cat, b_cat)
    got0, got_lo = swap(gb0), swap(gb_lo)
    p = dict(zip(ORDER[4:], far_call(ga_hi, got_hi)))
    from_xyz = to_cube(p[7], 6)
    from_xy = to_cube(p[3], 1)
    from_yz = to_cube(p[6], 2)
    from_xz = to_cube(p[5], 4)
    ga_lo = last_call(w, b_cat)
    p0, p1, p2, p4 = near_call(ga_lo, got0, got_lo, from_xy, from_yz, from_xz, from_xyz)
    wide = lambda a: a.astype(jnp.float32)
    total = p0 + wide(to_cube(p1, 1)) + wide(to_cube(p2, 2)) + wide(to_cube(p4, 4))
    kept, sent = total[:rows], total[rows:]
    got_sum = swap(sent)
    image_sum = jnp.where(first, kept, got_sum)
    text_sum = jnp.where(first, got_sum, kept)
    return (image_sum - wide(texts), text_sum - wide(images))


def solution(mesh):
    chips = Mesh(mesh.devices.reshape(SIZES), AXES)
    spec = P(AXES, None)
    return jax.shard_map(
        body,
        mesh=chips,
        in_specs=(spec, spec),
        out_specs=(spec, spec),
        check_vma=False,
    )
```

time: 150 us -> 213 us (1.42)
  Pallas kernels: 44.8 us -> 107 us
  local copies, waits for them, and re-layouts: 4.94 us -> 18.2 us
  starting transfers between devices: 37.5 us -> 31.7 us
  waiting for transfers between devices: 55.6 us -> 52.1 us
  other arithmetic: 5.65 us -> 3.1 us
    pallas_call x2 -> x7, Pallas kernels: 43.2 us -> 105 us  [the longest x1 60.7 us: join_call(): pl.pallas_call(join_kernel, in_specs=[any_spec()] * 4, out_specs=any_spec...]
    unnamed x44 -> x52, local copies, waits for them, and re-layouts: 1.97 us -> 17.5 us
    ppermute x14, waiting for transfers between devices: 38 us -> 33.2 us  [to_cube(): return lax.ppermute(a, AXES, across(m))]
    ppermute x14, starting transfers between devices: 27.9 us -> 24.6 us  [to_cube(): return lax.ppermute(a, AXES, across(m))]
    convert_element_type x3 -> x0, other arithmetic: 2.51 us -> none  [narrow(): return a.astype(jnp.bfloat16)]
    squeeze x1 -> x0, local copies, waits for them, and re-layouts: 2.29 us -> none  [body(): gb_other = {m: swap(gb[PLACE[m]]) for m in range(1, 8)}]
    ppermute x20 -> x12, waiting for transfers between devices: 9.02 us -> 10.3 us  [swap(): return lax.ppermute(a, AXES, SWAP)]
  transfers between devices with their start and end apart: 35 -> 27, of which waited for: 19 -> 20; matrix products, arithmetic and copies ran while one was open for 2% -> 0% of each run, Pallas kernels for 0% -> 5%
where the time goes in v2:
time: 213 us
  Pallas kernels  107 us (50%)
  waiting for transfers between devices  52.1 us (24%)
  starting transfers between devices  31.7 us (15%)
  local copies, waits for them, and re-layouts  18.2 us (9%)
  other arithmetic  3.1 us (1%)
    pallas_call x1, Pallas kernels, join_call(): pl.pallas_call(join_kernel, in_specs=[any_spec()] * 4, out_specs=any_spec...  60.7 us
    ppermute x14, waiting for transfers between devices, to_cube(): return lax.ppermute(a, AXES, across(m))  33.2 us
    ppermute x14, starting transfers between devices, to_cube(): return lax.ppermute(a, AXES, across(m))  24.6 us
    pallas_call x1, Pallas kernels, scores_call(): pl.pallas_call(functools.partial(scores_kernel, scale), in_specs=[smem_sp...  20.9 us
    unnamed x52, local copies, waits for them, and re-layouts  17.5 us
    pallas_call x1, Pallas kernels, weights_call(): pl.pallas_call(weights_kernel, in_specs=[smem_spec()] * 2 + [vmem_spec()]...  11.6 us
    ppermute x12, waiting for transfers between devices, swap(): return lax.ppermute(a, AXES, SWAP)  10.3 us
    all_to_all x1, waiting for transfers between devices, body(): lax.all_to_all(jnp.broadcast_to(chip_stat[None], (8,) + chip_stat.shape),...  8.58 us
  transfers between devices with their start and end apart: 27, of which 20 were waited for; matrix products, arithmetic and copies ran while one was open for 0% of the time, Pallas kernels for 5%

profile of v2, /device:TPU:1, one launch (start us, length us, event | category | flops | bytes accessed | tf_op | source)
XLA Modules:
  0.0 212.7 jit_solution(12627390849370298229)
XLA Ops:
  0.6 1.1 broadcast_select_fusion.1
  1.7 1.5 collective-permute-start
  3.2 1.1 collective-permute-done
  4.4 3.9 %collective-permute-start.3 = (bf16[320,768]{1,0:T(8,128)(2,1)S(1)}, bf16[320,768]{1,0:T(8,128)(2,1)S(1)}, u32[]{:S(2)}, u32[]{:S(2)}) collective-permute-start(bf16[320,768]{1,0:T(8,128)(2,1)S(1)} %pad_maximum_fusion.b0), channel_id=1, source_target_pairs={{0,1},{1,0},{2,3},{3,2},{4,5},{5,4},{6,7},{7,6},{8,9},{9,8},{10,11... | collective-permute-start | bytes 1474568 | tf_op jit(solution)/shard_map/ppermute | solution.py:74
  8.3 2.7 %collective-permute-start.2 = (bf16[320,768]{1,0:T(8,128)(2,1)S(1)}, bf16[320,768]{1,0:T(8,128)(2,1)S(1)}, u32[]{:S(2)}, u32[]{:S(2)}) collective-permute-start(bf16[320,768]{1,0:T(8,128)(2,1)S(1)} %pad_maximum_fusion.b0), channel_id=1, source_target_pairs={{0,32},{1,33},{2,34},{3,35},{4,36},{5,37},{6,38},{7,39},{8,40},{9,... | collective-permute-start | bytes 1474568 | tf_op jit(solution)/shard_map/ppermute | solution.py:74
  11.1 2.5 %collective-permute-start.1 = (bf16[320,768]{1,0:T(8,128)(2,1)S(1)}, bf16[320,768]{1,0:T(8,128)(2,1)S(1)}, u32[]{:S(2)}, u32[]{:S(2)}) collective-permute-start(bf16[320,768]{1,0:T(8,128)(2,1)S(1)} %pad_maximum_fusion.b0), channel_id=1, source_target_pairs={{0,4},{1,5},{2,6},{3,7},{4,0},{5,1},{6,2},{7,3},{8,12},{9,13},{10,... | collective-permute-start | bytes 1474568 | tf_op jit(solution)/shard_map/ppermute | solution.py:74
  13.6 1.0 collective-permute-done.3.b3
  14.6 2.7 %collective-permute-done.2.b2 = bf16[320,768]{1,0:T(8,128)(2,1)S(1)} collective-permute-done((bf16[320,768]{1,0:T(8,128)(2,1)S(1)}, bf16[320,768]{1,0:T(8,128)(2,1)S(1)}, u32[]{:S(2)}, u32[]{:S(2)}) %collective-permute-start.2) | collective-permute-done | bytes 491552 | tf_op jit(solution)/shard_map/ppermute | solution.py:74
  17.3 2.7 %collective-permute-done.1.b1 = bf16[320,768]{1,0:T(8,128)(2,1)S(1)} collective-permute-done((bf16[320,768]{1,0:T(8,128)(2,1)S(1)}, bf16[320,768]{1,0:T(8,128)(2,1)S(1)}, u32[]{:S(2)}, u32[]{:S(2)}) %collective-permute-start.1) | collective-permute-done | bytes 491552 | tf_op jit(solution)/shard_map/ppermute | solution.py:74
  20.0 0.8 copy-done.11
  20.8 60.7 %join.1.a_lo = bf16[1280,768]{1,0:T(8,128)(2,1)} custom-call(bf16[320,768]{1,0:T(8,128)(2,1)} %copy-done.8, bf16[320,768]{1,0:T(8,128)(2,1)} %copy-done.11, bf16[320,768]{1,0:T(8,128)(2,1)} %copy-done.12, bf16[320,768]{1,0:T(8,128)(2,1)} %copy-done.13), custom_call_target="tpu_custom_call" | custom-call | tf_op jit(solution)/shard_map/join/pallas_call | solution.py:140
  81.6 0.8 collective-permute-start.7
  82.4 2.5 %collective-permute-start.5 = (bf16[320,768]{1,0:T(8,128)(2,1)}, bf16[320,768]{1,0:T(8,128)(2,1)S(1)}, u32[]{:S(2)}, u32[]{:S(2)}) collective-permute-start(bf16[320,768]{1,0:T(8,128)(2,1)} %copy-done.12), channel_id=1, source_target_pairs={{0,4},{1,5},{2,6},{3,7},{4,0},{5,1},{6,2},{7,3},{8,12},{9,13},{10,... | collective-permute-start | bytes 1474568 | tf_op jit(solution)/shard_map/ppermute | solution.py:74
  84.9 1.7 collective-permute-start.8
  86.6 2.6 %collective-permute-start.6 = (bf16[320,768]{1,0:T(8,128)(2,1)}, bf16[320,768]{1,0:T(8,128)(2,1)S(1)}, u32[]{:S(2)}, u32[]{:S(2)}) collective-permute-start(bf16[320,768]{1,0:T(8,128)(2,1)} %copy-done.11), channel_id=1, source_target_pairs={{0,1},{1,0},{2,3},{3,2},{4,5},{5,4},{6,7},{7,6},{8,9},{9,8},{10,11... | collective-permute-start | bytes 1474568 | tf_op jit(solution)/shard_map/ppermute | solution.py:74
  89.2 1.7 collective-permute-done.7.refs_2_
  90.9 0.2 collective-permute-start.11
  91.1 0.5 collective-permute-done.5.refs_0_
  91.7 4.6 %collective-permute-done.8.refs_3_ = bf16[320,768]{1,0:T(8,128)(2,1)S(1)} collective-permute-done((bf16[320,768]{1,0:T(8,128)(2,1)}, bf16[320,768]{1,0:T(8,128)(2,1)S(1)}, u32[]{:S(2)}, u32[]{:S(2)}) %collective-permute-start.8) | collective-permute-done | bytes 491552 | tf_op jit(solution)/shard_map/ppermute | solution.py:74
  96.2 4.8 %collective-permute-done.6.refs_1_ = bf16[320,768]{1,0:T(8,128)(2,1)S(1)} collective-permute-done((bf16[320,768]{1,0:T(8,128)(2,1)}, bf16[320,768]{1,0:T(8,128)(2,1)S(1)}, u32[]{:S(2)}, u32[]{:S(2)}) %collective-permute-start.6) | collective-permute-done | bytes 491552 | tf_op jit(solution)/shard_map/ppermute | solution.py:74
  101.0 1.8 collective-permute-done.10.refs_5_
  102.9 0.7 copy-done.23
  103.7 0.6 copy-done.15
  104.3 20.9 %scores.1 = (f32[2,1280,1280]{2,1,0:T(8,128)S(1)}, bf16[2,1280,768]{2,1,0:T(8,128)(2,1)S(1)}, bf16[2,1280,768]{2,1,0:T(8,128)(2,1)S(1)}, f32[8,320]{1,0:T(8,128)}, f32[8,320]{1,0:T(8,128)}, /*index=5*/s32[2]{0:T(128)}) custom-call(s32[1]{0:T(128)} %bitcast.core_ref, bf16[1280,768]{1,0:T(8,128)(2,1)} %join.1.a_lo, bf16[1280,768]{1,0:T(8,128)(2,1)} %copy-done.15, ...), custom_call_target="tpu_custom_call" | custom-call | flops 5033164800 | tf_op jit(solution)/shard_map/scores/pallas_call | solution.py:235
  125.2 4.7 %copy-done = f32[2,1280,1280]{2,1,0:T(8,128)} copy-done((f32[2,1280,1280]{2,1,0:T(8,128)}, f32[2,1280,1280]{2,1,0:T(8,128)S(1)}, u32[]{:S(2)}) %copy-start) | copy-done | bytes 13107224
  130.0 1.9 copy-done.2
  131.8 1.9 copy-done.4
  133.8 1.4 collective-permute-done.13
  135.2 0.7 add_select_fusion
  135.9 0.6 broadcast_in_dim.2
  136.5 4.3 %all-to-all-start = ((f32[8,8,320]{2,1,0:T(8,128)}), f32[8,8,320]{2,1,0:T(8,128)S(1)}, u32[]{:S(2)}, u32[]{:S(2)}) async-start(f32[8,8,320]{2,1,0:T(8,128)} %broadcast_in_dim.2), calls=%async_computation | async-start | bytes 196608 | tf_op jit(solution)/shard_map/all_to_all | solution.py:438
  140.9 8.6 %all-to-all-done.got_ref = f32[8,8,320]{2,1,0:T(8,128)S(1)} async-done(((f32[8,8,320]{2,1,0:T(8,128)}), f32[8,8,320]{2,1,0:T(8,128)S(1)}, u32[]{:S(2)}, u32[]{:S(2)}) %all-to-all-start) | async-done | bytes 81952 | tf_op jit(solution)/shard_map/all_to_all | solution.py:438
  149.5 0.6 copy-done.14
  150.1 1.6 merge.1.a_lse
  151.7 1.4 collective-permute-done.14.b_lse
  153.0 2.1 copy-done.5
  155.2 0.7 copy-done.6
  155.9 0.6 copy-done.7
  156.5 11.6 %weights.1 = (bf16[2,1280,1280]{2,1,0:T(8,128)(2,1)S(1)}, bf16[1280,768]{1,0:T(8,128)(2,1)S(1)}) custom-call(s32[1]{0:T(128)} %bitcast.core_ref, s32[2]{0:T(128)S(1)} %copy-done.7, f32[2,1280,1280]{2,1,0:T(8,128)} %copy-done, f32[8,320]{1,0:T(8,128)S(1)} %copy-done.6, f32[8,320]{1,0:T(8,128)S(1)} %collective-permute-done.14.b_lse, ...), custom_call_target="tpu_custom_call" | custom-call | flops 2516582400 | bytes 19660800 | tf_op jit(solution)/shard_map/weights/pallas_call | solution.py:313
  168.0 2.7 %copy-done.1 = bf16[2,1280,1280]{2,1,0:T(8,128)(2,1)} copy-done((bf16[2,1280,1280]{2,1,0:T(8,128)(2,1)}, bf16[2,1280,1280]{2,1,0:T(8,128)(2,1)S(1)}, u32[]{:S(2)}) %copy-start.1) | copy-done | bytes 6553624
  170.7 0.2 collective-permute-start.17
  170.9 8.3 %middle.1 = (f32[1280,768]{1,0:T(8,128)S(1)}, f32[320,768]{1,0:T(8,128)S(1)}, bf16[960,768]{1,0:T(8,128)(2,1)S(1)}) custom-call(s32[1]{0:T(128)} %bitcast.core_ref, bf16[2,1280,1280]{2,1,0:T(8,128)(2,1)} %copy-done.1, bf16[2,1280,768]{2,1,0:T(8,128)(2,1)S(1)} %copy-done.5, bf16[2,1280,768]{2,1,0:T(8,128)(2,1)S(1)} %copy-done.3), custom_call_target="tpu_custom_call" | custom-call | flops 5033164800 | tf_op jit(solution)/shard_map/middle/pallas_call | solution.py:339
  179.2 0.4 collective-permute-start.16
  179.6 0.3 collective-permute-start.15
  180.0 0.3 far.1
  180.3 0.4 collective-permute-start.18
  180.6 0.3 collective-permute-start.19
  180.9 0.3 collective-permute-start.20
  181.2 2.8 %collective-permute-done.15.got0 = f32[320,768]{1,0:T(8,128)S(1)} collective-permute-done((f32[320,768]{1,0:T(8,128)S(1)}, f32[320,768]{1,0:T(8,128)S(1)}, u32[]{:S(2)}, u32[]{:S(2)}) %collective-permute-start.15) | collective-permute-done | bytes 983072 | tf_op jit(solution)/shard_map/ppermute | solution.py:78
  184.0 1.7 collective-permute-start.21
  185.7 2.7 %last.1.ga_lo = f32[1280,768]{1,0:T(8,128)S(1)} custom-call(bf16[2,1280,1280]{2,1,0:T(8,128)(2,1)S(1)} %bitcast.3, bf16[2,1280,768]{2,1,0:T(8,128)(2,1)S(1)} %copy-done.3), custom_call_target="tpu_custom_call" | custom-call | flops 2516582400 | tf_op jit(solution)/shard_map/last/pallas_call | solution.py:381
  188.5 0.9 collective-permute-done.18.r_xy
  189.4 0.3 collective-permute-done.19.r_yz
  189.7 5.4 %collective-permute-done.20.r_xz = bf16[320,768]{1,0:T(8,128)(2,1)S(1)} collective-permute-done((bf16[320,768]{1,0:T(8,128)(2,1)S(1)}, bf16[320,768]{1,0:T(8,128)(2,1)S(1)}, u32[]{:S(2)}, u32[]{:S(2)}) %collective-permute-start.20) | collective-permute-done | bytes 491552 | tf_op jit(solution)/shard_map/ppermute | solution.py:74
  195.1 0.6 near.1
  195.7 2.3 %collective-permute-start.22 = (bf16[320,768]{1,0:T(8,128)(2,1)S(1)}, bf16[320,768]{1,0:T(8,128)(2,1)S(1)}, u32[]{:S(2)}, u32[]{:S(2)}) collective-permute-start(bf16[320,768]{1,0:T(8,128)(2,1)S(1)} %get-tuple-element.37), channel_id=1, source_target_pairs={{0,4},{1,5},{2,6},{3,7},{4,0},{5,1},{6,2},{7,3},{8,12},{9,13},{10,... | collective-permute-start | bytes 1474568 | tf_op jit(solution)/shard_map/ppermute | solution.py:74
  198.1 2.5 %collective-permute-start.23 = (bf16[320,768]{1,0:T(8,128)(2,1)S(1)}, bf16[320,768]{1,0:T(8,128)(2,1)S(1)}, u32[]{:S(2)}, u32[]{:S(2)}) collective-permute-start(bf16[320,768]{1,0:T(8,128)(2,1)S(1)} %get-tuple-element.38), channel_id=1, source_target_pairs={{0,32},{1,33},{2,34},{3,35},{4,36},{5,37},{6,38},{7,39},{8,40},{9,... | collective-permute-start | bytes 1474568 | tf_op jit(solution)/shard_map/ppermute | solution.py:74
  200.6 0.3 collective-permute-start.24
  200.9 3.8 %collective-permute-done.22 = bf16[320,768]{1,0:T(8,128)(2,1)S(1)} collective-permute-done((bf16[320,768]{1,0:T(8,128)(2,1)S(1)}, bf16[320,768]{1,0:T(8,128)(2,1)S(1)}, u32[]{:S(2)}, u32[]{:S(2)}) %collective-permute-start.22) | collective-permute-done | bytes 491552 | tf_op jit(solution)/shard_map/ppermute | solution.py:74
  204.7 2.3 %collective-permute-done.23 = bf16[320,768]{1,0:T(8,128)(2,1)S(1)} collective-permute-done((bf16[320,768]{1,0:T(8,128)(2,1)S(1)}, bf16[320,768]{1,0:T(8,128)(2,1)S(1)}, u32[]{:S(2)}, u32[]{:S(2)}) %collective-permute-start.23) | collective-permute-done | bytes 491552 | tf_op jit(solution)/shard_map/ppermute | solution.py:74
  206.9 2.5 %collective-permute-done.24 = bf16[320,768]{1,0:T(8,128)(2,1)S(1)} collective-permute-done((bf16[320,768]{1,0:T(8,128)(2,1)S(1)}, bf16[320,768]{1,0:T(8,128)(2,1)S(1)}, u32[]{:S(2)}, u32[]{:S(2)}) %collective-permute-start.24) | collective-permute-done | bytes 491552 | tf_op jit(solution)/shard_map/ppermute | solution.py:74
  209.5 0.2 convert_add_fusion
  209.8 1.9 collective-permute-done.25
  211.7 1.0 convert_subtract_fusion
  (58 shorter events, 0.4 us)
Async XLA Ops:
  1.7 2.6 %collective-permute-start = (bf16[160,768]{1,0:T(8,128)(2,1)S(1)}, bf16[160,768]{1,0:T(8,128)(2,1)S(1)}, u32[]{:S(2)}, u32[]{:S(2)}) collective-permute-start(bf16[160,768]{1,0:T(8,128)(2,1)S(1)} %get-tuple-element.43), channel_id=1, source_target_pairs={{0,16},{1,17},{2,18},{3,19},{4,20},{5,21},{6,22},{7,23},{8,24},{9,... | collective-permute-start | bytes 737288 | tf_op jit(solution)/shard_map/ppermute | solution.py:78
  4.4 15.6 %copy-start.8 = (bf16[320,768]{1,0:T(8,128)(2,1)}, bf16[320,768]{1,0:T(8,128)(2,1)S(1)}, u32[]{:S(2)}) copy-start(bf16[320,768]{1,0:T(8,128)(2,1)S(1)} %pad_maximum_fusion.b0) | copy-start | bytes 1474564
  4.4 10.1 %collective-permute-start.3 = (bf16[320,768]{1,0:T(8,128)(2,1)S(1)}, bf16[320,768]{1,0:T(8,128)(2,1)S(1)}, u32[]{:S(2)}, u32[]{:S(2)}) collective-permute-start(bf16[320,768]{1,0:T(8,128)(2,1)S(1)} %pad_maximum_fusion.b0), channel_id=1, source_target_pairs={{0,1},{1,0},{2,3},{3,2},{4,5},{5,4},{6,7},{7,6},{8,9},{9,8},{10,11... | collective-permute-start | bytes 1474568 | tf_op jit(solution)/shard_map/ppermute | solution.py:74
  8.3 9.0 %collective-permute-start.2 = (bf16[320,768]{1,0:T(8,128)(2,1)S(1)}, bf16[320,768]{1,0:T(8,128)(2,1)S(1)}, u32[]{:S(2)}, u32[]{:S(2)}) collective-permute-start(bf16[320,768]{1,0:T(8,128)(2,1)S(1)} %pad_maximum_fusion.b0), channel_id=1, source_target_pairs={{0,32},{1,33},{2,34},{3,35},{4,36},{5,37},{6,38},{7,39},{8,40},{9,... | collective-permute-start | bytes 1474568 | tf_op jit(solution)/shard_map/ppermute | solution.py:74
  11.1 8.9 %collective-permute-start.1 = (bf16[320,768]{1,0:T(8,128)(2,1)S(1)}, bf16[320,768]{1,0:T(8,128)(2,1)S(1)}, u32[]{:S(2)}, u32[]{:S(2)}) collective-permute-start(bf16[320,768]{1,0:T(8,128)(2,1)S(1)} %pad_maximum_fusion.b0), channel_id=1, source_target_pairs={{0,4},{1,5},{2,6},{3,7},{4,0},{5,1},{6,2},{7,3},{8,12},{9,13},{10,... | collective-permute-start | bytes 1474568 | tf_op jit(solution)/shard_map/ppermute | solution.py:74
  14.6 5.4 %copy-start.13 = (bf16[320,768]{1,0:T(8,128)(2,1)}, bf16[320,768]{1,0:T(8,128)(2,1)S(1)}, u32[]{:S(2)}) copy-start(bf16[320,768]{1,0:T(8,128)(2,1)S(1)} %collective-permute-done.3.b3) | copy-start | bytes 1474564
  17.3 2.7 %copy-start.12 = (bf16[320,768]{1,0:T(8,128)(2,1)}, bf16[320,768]{1,0:T(8,128)(2,1)S(1)}, u32[]{:S(2)}) copy-start(bf16[320,768]{1,0:T(8,128)(2,1)S(1)} %collective-permute-done.2.b2) | copy-start | bytes 1474564
  20.0 0.8 copy-start.11
  81.5 21.4 %collective-permute-start.4 = (bf16[1280,768]{1,0:T(8,128)(2,1)}, bf16[1280,768]{1,0:T(8,128)(2,1)S(1)}, u32[]{:S(2)}, u32[]{:S(2)}) collective-permute-start(bf16[1280,768]{1,0:T(8,128)(2,1)} %join.1.a_lo), channel_id=1, source_target_pairs={{0,16},{1,17},{2,18},{3,19},{4,20},{5,21},{6,22},{7,23},{8,24},{9,... | collective-permute-start | bytes 5898248 | tf_op jit(solution)/shard_map/ppermute | solution.py:78
  81.6 9.3 %collective-permute-start.7 = (bf16[320,768]{1,0:T(8,128)(2,1)}, bf16[320,768]{1,0:T(8,128)(2,1)S(1)}, u32[]{:S(2)}, u32[]{:S(2)}) collective-permute-start(bf16[320,768]{1,0:T(8,128)(2,1)} %copy-done.13), channel_id=1, source_target_pairs={{0,32},{1,33},{2,34},{3,35},{4,36},{5,37},{6,38},{7,39},{8,40},{9,... | collective-permute-start | bytes 1474568 | tf_op jit(solution)/shard_map/ppermute | solution.py:74
  82.4 9.2 %collective-permute-start.5 = (bf16[320,768]{1,0:T(8,128)(2,1)}, bf16[320,768]{1,0:T(8,128)(2,1)S(1)}, u32[]{:S(2)}, u32[]{:S(2)}) collective-permute-start(bf16[320,768]{1,0:T(8,128)(2,1)} %copy-done.12), channel_id=1, source_target_pairs={{0,4},{1,5},{2,6},{3,7},{4,0},{5,1},{6,2},{7,3},{8,12},{9,13},{10,... | collective-permute-start | bytes 1474568 | tf_op jit(solution)/shard_map/ppermute | solution.py:74
  84.9 11.3 %collective-permute-start.8 = (bf16[320,768]{1,0:T(8,128)(2,1)}, bf16[320,768]{1,0:T(8,128)(2,1)S(1)}, u32[]{:S(2)}, u32[]{:S(2)}) collective-permute-start(bf16[320,768]{1,0:T(8,128)(2,1)} %copy-done.11), channel_id=1, source_target_pairs={{0,33},{1,32},{2,35},{3,34},{4,37},{5,36},{6,39},{7,38},{8,41},{9,... | collective-permute-start | bytes 1474568 | tf_op jit(solution)/shard_map/ppermute | solution.py:74
  86.6 14.4 %collective-permute-start.6 = (bf16[320,768]{1,0:T(8,128)(2,1)}, bf16[320,768]{1,0:T(8,128)(2,1)S(1)}, u32[]{:S(2)}, u32[]{:S(2)}) collective-permute-start(bf16[320,768]{1,0:T(8,128)(2,1)} %copy-done.11), channel_id=1, source_target_pairs={{0,1},{1,0},{2,3},{3,2},{4,5},{5,4},{6,7},{7,6},{8,9},{9,8},{10,11... | collective-permute-start | bytes 1474568 | tf_op jit(solution)/shard_map/ppermute | solution.py:74
  90.9 12.0 %copy-start.16 = (bf16[320,768]{1,0:T(8,128)(2,1)}, bf16[320,768]{1,0:T(8,128)(2,1)S(1)}, u32[]{:S(2)}) copy-start(bf16[320,768]{1,0:T(8,128)(2,1)S(1)} %collective-permute-done.7.refs_2_) | copy-start | bytes 1474564
  90.9 10.1 %collective-permute-start.11 = (bf16[320,768]{1,0:T(8,128)(2,1)S(1)}, bf16[320,768]{1,0:T(8,128)(2,1)S(1)}, u32[]{:S(2)}, u32[]{:S(2)}) collective-permute-start(bf16[320,768]{1,0:T(8,128)(2,1)S(1)} %collective-permute-done.7.refs_2_), channel_id=1, source_target_pairs={{0,16},{1,17},{2,18},{3,19},{4,20},{5,21},{6,22},{7,23},{8,24},{9,... | collective-permute-start | bytes 1474568 | tf_op jit(solution)/shard_map/ppermute | solution.py:78
  91.6 11.2 %copy-start.17 = (bf16[320,768]{1,0:T(8,128)(2,1)}, bf16[320,768]{1,0:T(8,128)(2,1)S(1)}, u32[]{:S(2)}) copy-start(bf16[320,768]{1,0:T(8,128)(2,1)S(1)} %collective-permute-done.5.refs_0_) | copy-start | bytes 1474564
  91.7 9.3 %collective-permute-start.9 = (bf16[320,768]{1,0:T(8,128)(2,1)S(1)}, bf16[320,768]{1,0:T(8,128)(2,1)S(1)}, u32[]{:S(2)}, u32[]{:S(2)}) collective-permute-start(bf16[320,768]{1,0:T(8,128)(2,1)S(1)} %collective-permute-done.5.refs_0_), channel_id=1, source_target_pairs={{0,16},{1,17},{2,18},{3,19},{4,20},{5,21},{6,22},{7,23},{8,24},{9,... | collective-permute-start | bytes 1474568 | tf_op jit(solution)/shard_map/ppermute | solution.py:78
  96.2 6.7 %copy-start.18 = (bf16[320,768]{1,0:T(8,128)(2,1)}, bf16[320,768]{1,0:T(8,128)(2,1)S(1)}, u32[]{:S(2)}) copy-start(bf16[320,768]{1,0:T(8,128)(2,1)S(1)} %collective-permute-done.8.refs_3_) | copy-start | bytes 1474564
  96.2 4.8 %collective-permute-start.12 = (bf16[320,768]{1,0:T(8,128)(2,1)S(1)}, bf16[320,768]{1,0:T(8,128)(2,1)S(1)}, u32[]{:S(2)}, u32[]{:S(2)}) collective-permute-start(bf16[320,768]{1,0:T(8,128)(2,1)S(1)} %collective-permute-done.8.refs_3_), channel_id=1, source_target_pairs={{0,16},{1,17},{2,18},{3,19},{4,20},{5,21},{6,22},{7,23},{8,24},{9,... | collective-permute-start | bytes 1474568 | tf_op jit(solution)/shard_map/ppermute | solution.py:78
  101.0 1.9 copy-start.19
  101.0 1.9 collective-permute-start.10
  101.0 1.9 copy-start.20
  101.0 1.9 copy-start.21
  101.0 1.9 copy-start.22
  102.8 0.8 copy-start.23
  102.8 1.4 copy-start.15
  125.2 4.7 %copy-start = (f32[2,1280,1280]{2,1,0:T(8,128)}, f32[2,1280,1280]{2,1,0:T(8,128)S(1)}, u32[]{:S(2)}) copy-start(f32[2,1280,1280]{2,1,0:T(8,128)S(1)} %get-tuple-element.22.e_ref) | copy-start | bytes 39321604
  130.0 1.9 copy-start.2
  131.8 1.9 copy-start.4
  133.8 1.4 collective-permute-start.13
  136.5 12.9 %all-to-all-start = ((f32[8,8,320]{2,1,0:T(8,128)}), f32[8,8,320]{2,1,0:T(8,128)S(1)}, u32[]{:S(2)}, u32[]{:S(2)}) async-start(f32[8,8,320]{2,1,0:T(8,128)} %broadcast_in_dim.2), calls=%async_computation | async-start | bytes 196608 | tf_op jit(solution)/shard_map/all_to_all | solution.py:438
  149.5 0.6 copy-start.14
  151.7 1.4 collective-permute-start.14
  153.0 2.1 copy-start.5
  155.2 0.7 copy-start.6
  155.9 0.6 copy-start.7
  156.5 14.5 %copy-start.3 = (bf16[2,1280,768]{2,1,0:T(8,128)(2,1)S(1)}, bf16[2,1280,768]{2,1,0:T(8,128)(2,1)}, u32[]{:S(2)}) copy-start(bf16[2,1280,768]{2,1,0:T(8,128)(2,1)} %copy-done.2) | copy-start | bytes 11796484
  168.0 2.7 %copy-start.1 = (bf16[2,1280,1280]{2,1,0:T(8,128)(2,1)}, bf16[2,1280,1280]{2,1,0:T(8,128)(2,1)S(1)}, u32[]{:S(2)}) copy-start(bf16[2,1280,1280]{2,1,0:T(8,128)(2,1)S(1)} %get-tuple-element.26.w_ref) | copy-start | bytes 19660804
  170.7 9.2 %collective-permute-start.17 = (bf16[1280,768]{1,0:T(8,128)(2,1)S(1)}, bf16[1280,768]{1,0:T(8,128)(2,1)S(1)}, u32[]{:S(2)}, u32[]{:S(2)}) collective-permute-start(bf16[1280,768]{1,0:T(8,128)(2,1)S(1)} %get-tuple-element.31), channel_id=1, source_target_pairs={{0,16},{1,17},{2,18},{3,19},{4,20},{5,21},{6,22},{7,23},{8,24},{9,... | collective-permute-start | bytes 5898248 | tf_op jit(solution)/shard_map/ppermute | solution.py:78
  170.9 14.8 %slice-start = ((s8[6553600]{0:T(1024)(128)(4,1)}), s8[4194304]{0:T(1024)(128)(4,1)S(1)}, s32[]{:S(2)}) async-start(s8[6553600]{0:T(1024)(128)(4,1)} %bitcast.2), calls=%async_computation.1 | async-start | bytes 8388608
  170.9 14.8 %slice-start.1 = ((s8[6553600]{0:T(1024)(128)(4,1)}), s8[2359296]{0:T(1024)(128)(4,1)S(1)}, s32[]{:S(2)}) async-start(s8[6553600]{0:T(1024)(128)(4,1)} %bitcast.2), calls=%async_computation.2 | async-start | bytes 4718592
  179.2 9.2 %collective-permute-start.16 = (bf16[960,768]{1,0:T(8,128)(2,1)S(1)}, bf16[960,768]{1,0:T(8,128)(2,1)S(1)}, u32[]{:S(2)}, u32[]{:S(2)}) collective-permute-start(bf16[960,768]{1,0:T(8,128)(2,1)S(1)} %get-tuple-element.29), channel_id=1, source_target_pairs={{0,16},{1,17},{2,18},{3,19},{4,20},{5,21},{6,22},{7,23},{8,24},{9,... | collective-permute-start | bytes 4423688 | tf_op jit(solution)/shard_map/ppermute | solution.py:78
  179.6 4.3 %collective-permute-start.15 = (f32[320,768]{1,0:T(8,128)S(1)}, f32[320,768]{1,0:T(8,128)S(1)}, u32[]{:S(2)}, u32[]{:S(2)}) collective-permute-start(f32[320,768]{1,0:T(8,128)S(1)} %get-tuple-element.28), channel_id=1, source_target_pairs={{0,16},{1,17},{2,18},{3,19},{4,20},{5,21},{6,22},{7,23},{8,24},{9,... | collective-permute-start | bytes 2949128 | tf_op jit(solution)/shard_map/ppermute | solution.py:78
  180.3 9.1 %collective-permute-start.18 = (bf16[320,768]{1,0:T(8,128)(2,1)S(1)}, bf16[320,768]{1,0:T(8,128)(2,1)S(1)}, u32[]{:S(2)}, u32[]{:S(2)}) collective-permute-start(bf16[320,768]{1,0:T(8,128)(2,1)S(1)} %get-tuple-element.32), channel_id=1, source_target_pairs={{0,4},{1,5},{2,6},{3,7},{4,0},{5,1},{6,2},{7,3},{8,12},{9,13},{10,... | collective-permute-start | bytes 1474568 | tf_op jit(solution)/shard_map/ppermute | solution.py:74
  180.6 9.0 %collective-permute-start.19 = (bf16[320,768]{1,0:T(8,128)(2,1)S(1)}, bf16[320,768]{1,0:T(8,128)(2,1)S(1)}, u32[]{:S(2)}, u32[]{:S(2)}) collective-permute-start(bf16[320,768]{1,0:T(8,128)(2,1)S(1)} %get-tuple-element.33), channel_id=1, source_target_pairs={{0,32},{1,33},{2,34},{3,35},{4,36},{5,37},{6,38},{7,39},{8,40},{9,... | collective-permute-start | bytes 1474568 | tf_op jit(solution)/shard_map/ppermute | solution.py:74
  180.9 14.2 %collective-permute-start.20 = (bf16[320,768]{1,0:T(8,128)(2,1)S(1)}, bf16[320,768]{1,0:T(8,128)(2,1)S(1)}, u32[]{:S(2)}, u32[]{:S(2)}) collective-permute-start(bf16[320,768]{1,0:T(8,128)(2,1)S(1)} %get-tuple-element.34), channel_id=1, source_target_pairs={{0,1},{1,0},{2,3},{3,2},{4,5},{5,4},{6,7},{7,6},{8,9},{9,8},{10,11... | collective-permute-start | bytes 1474568 | tf_op jit(solution)/shard_map/ppermute | solution.py:74
  184.0 11.1 %collective-permute-start.21 = (bf16[320,768]{1,0:T(8,128)(2,1)S(1)}, bf16[320,768]{1,0:T(8,128)(2,1)S(1)}, u32[]{:S(2)}, u32[]{:S(2)}) collective-permute-start(bf16[320,768]{1,0:T(8,128)(2,1)S(1)} %get-tuple-element.35), channel_id=1, source_target_pairs={{0,33},{1,32},{2,35},{3,34},{4,37},{5,36},{6,39},{7,38},{8,41},{9,... | collective-permute-start | bytes 1474568 | tf_op jit(solution)/shard_map/ppermute | solution.py:74
  195.7 16.0 %copy-start.9 = (bf16[160,768]{1,0:T(8,128)(2,1)S(1)}, bf16[160,768]{1,0:T(8,128)(2,1)}, u32[]{:S(2)}) copy-start(bf16[160,768]{1,0:T(8,128)(2,1)} %param.2) | copy-start | bytes 737284
  195.7 16.0 %copy-start.10 = (bf16[160,768]{1,0:T(8,128)(2,1)S(1)}, bf16[160,768]{1,0:T(8,128)(2,1)}, u32[]{:S(2)}) copy-start(bf16[160,768]{1,0:T(8,128)(2,1)} %param.3) | copy-start | bytes 737284
  195.7 9.0 %collective-permute-start.22 = (bf16[320,768]{1,0:T(8,128)(2,1)S(1)}, bf16[320,768]{1,0:T(8,128)(2,1)S(1)}, u32[]{:S(2)}, u32[]{:S(2)}) collective-permute-start(bf16[320,768]{1,0:T(8,128)(2,1)S(1)} %get-tuple-element.37), channel_id=1, source_target_pairs={{0,4},{1,5},{2,6},{3,7},{4,0},{5,1},{6,2},{7,3},{8,12},{9,13},{10,... | collective-permute-start | bytes 1474568 | tf_op jit(solution)/shard_map/ppermute | solution.py:74
  198.1 8.9 %collective-permute-start.23 = (bf16[320,768]{1,0:T(8,128)(2,1)S(1)}, bf16[320,768]{1,0:T(8,128)(2,1)S(1)}, u32[]{:S(2)}, u32[]{:S(2)}) collective-permute-start(bf16[320,768]{1,0:T(8,128)(2,1)S(1)} %get-tuple-element.38), channel_id=1, source_target_pairs={{0,32},{1,33},{2,34},{3,35},{4,36},{5,37},{6,38},{7,39},{8,40},{9,... | collective-permute-start | bytes 1474568 | tf_op jit(solution)/shard_map/ppermute | solution.py:74
  200.6 8.9 %collective-permute-start.24 = (bf16[320,768]{1,0:T(8,128)(2,1)S(1)}, bf16[320,768]{1,0:T(8,128)(2,1)S(1)}, u32[]{:S(2)}, u32[]{:S(2)}) collective-permute-start(bf16[320,768]{1,0:T(8,128)(2,1)S(1)} %get-tuple-element.39), channel_id=1, source_target_pairs={{0,1},{1,0},{2,3},{3,2},{4,5},{5,4},{6,7},{7,6},{8,9},{9,8},{10,11... | collective-permute-start | bytes 1474568 | tf_op jit(solution)/shard_map/ppermute | solution.py:74
  209.7 1.9 collective-permute-start.25

commit v3 on v2

--- a/solution.py
+++ b/solution.py
@@ -13,7 +13,7 @@
 ORDER = (0, 1, 2, 4, 3, 5, 6, 7)
 PLACE = tuple(ORDER.index(m) for m in range(8))
 LOG2E = 1.4426950408889634
-VMEM_LIMIT = 36 * 1024 * 1024
+VMEM_LIMIT = 20 * 1024 * 1024
 RANGE = 60.0
 
 
@@ -124,47 +124,24 @@
     return lax.dot_general(a, b, (((0,), (0,)), ((), ())), preferred_element_type=jnp.float32)
 
 
-def join_kernel(b0, b1, b2, b3, out, sem):
-    rows = b0.shape[0]
-    copies = [
-        pltpu.make_async_copy(b, out.at[pl.ds(j * rows, rows)], sem.at[j]) for j, b in enumerate((b0, b1, b2, b3))
-    ]
-    for c in copies:
-        c.start()
-    for c in copies:
-        c.wait()
-
-
-def join_call(blocks):
-    rows, features = blocks[0].shape
-    return pl.pallas_call(
-        join_kernel,
-        in_specs=[any_spec()] * 4,
-        out_specs=any_spec(),
-        out_shape=jax.ShapeDtypeStruct((4 * rows, features), blocks[0].dtype),
-        scratch_shapes=[pltpu.SemaphoreType.DMA((4,))],
-        name="join",
-    )(*blocks)
-
-
-def scores_kernel(scale, core_ref, a_lo, b_lo, *refs):
-    a_hi, b_hi = refs[:4], refs[4:8]
-    e_ref, a_cat, b_cat, a_stat, b_stat, flags, col_m, col_s, sem = refs[8:]
-    rows = a_hi[0].shape[0]
+def scores_kernel(scale, core_ref, *refs):
+    a_refs, b_refs = refs[:8], refs[8:16]
+    e_ref, a_stat, b_stat, flags, a_cat, b_cat, col_m, col_s, sem = refs[16:]
+    rows = a_refs[0].shape[0]
     half = 4 * rows
     core = core_ref[0]
 
     def copies_a(h):
-        if h == 0:
-            return [pltpu.make_async_copy(a_lo, a_cat.at[0], sem.at[0])]
-        return [pltpu.make_async_copy(a_hi[j], a_cat.at[1, pl.ds(j * rows, rows)], sem.at[1 + j]) for j in range(4)]
+        return [
+            pltpu.make_async_copy(a_refs[4 * h + j], a_cat.at[h, pl.ds(j * rows, rows)], sem.at[4 * h + j])
+            for j in range(4)
+        ]
 
     def copies_b(h):
-        place = core if h == 0 else 1 - core
-        if h == 0:
-            return [pltpu.make_async_copy(b_lo, b_cat.at[place], sem.at[5])]
+        place = h ^ core
         return [
-            pltpu.make_async_copy(b_hi[j], b_cat.at[place, pl.ds(j * rows, rows)], sem.at[6 + j]) for j in range(4)
+            pltpu.make_async_copy(b_refs[4 * h + j], b_cat.at[place, pl.ds(j * rows, rows)], sem.at[8 + 4 * h + j])
+            for j in range(4)
         ]
 
     for c in copies_b(0) + copies_a(0) + copies_b(1) + copies_a(1):
@@ -228,31 +205,31 @@
     quadrant(1)
 
 
-def scores_call(core, a_lo, b_lo, a_hi, b_hi, scale):
-    rows, features = a_hi[0].shape
+def scores_call(core, a_blocks, b_blocks, scale):
+    rows, features = a_blocks[0].shape
     half = 4 * rows
     stat = jax.ShapeDtypeStruct((8, rows), jnp.float32)
     return pl.pallas_call(
         functools.partial(scores_kernel, scale),
-        in_specs=[smem_spec()] + [any_spec()] * 10,
-        out_specs=[vmem_spec()] * 5 + [smem_spec()],
+        in_specs=[smem_spec()] + [any_spec()] * 16,
+        out_specs=[vmem_spec()] * 3 + [smem_spec()],
         out_shape=[
             pltpu.VMEM((2, half, half), jnp.float32),
-            pltpu.VMEM((2, half, features), jnp.bfloat16),
-            pltpu.VMEM((2, half, features), jnp.bfloat16),
             stat,
             stat,
             jax.ShapeDtypeStruct((2,), jnp.int32),
         ],
         scratch_shapes=[
+            pltpu.VMEM((2, half, features), jnp.bfloat16),
+            pltpu.VMEM((2, half, features), jnp.bfloat16),
             pltpu.VMEM((1, half), jnp.float32),
             pltpu.VMEM((1, half), jnp.float32),
-            pltpu.SemaphoreType.DMA((10,)),
+            pltpu.SemaphoreType.DMA((16,)),
         ],
         compiler_params=params(),
         cost_estimate=cost(2, half, half, features),
         name="scores",
-    )(core, a_lo, b_lo, *a_hi, *b_hi)
+    )(core, *a_blocks, *b_blocks)
 
 
 def merge_kernel(place_ref, got_ref, out_ref):
@@ -280,10 +257,37 @@
     )(place, got)
 
 
-def weights_kernel(core_ref, flags, e_ref, a_lse, b_lse, a_cat, w_ref, gb_hi):
+def half_copies(refs, h, out, sem):
+    rows = refs[0].shape[0]
+    return [
+        pltpu.make_async_copy(refs[4 * h + j], out.at[pl.ds(j * rows, rows)], sem.at[j]) for j in range(4)
+    ]
+
+
+def start_half(core, refs, shift, out, sem):
+    for c in range(2):
+
+        @pl.when(core == c)
+        def _():
+            for copy in half_copies(refs, c ^ shift, out, sem):
+                copy.start()
+
+
+def wait_half(refs, out, sem):
+    for copy in half_copies(refs, 0, out, sem):
+        copy.wait()
+
+
+def half_scratch(block):
+    return [pltpu.VMEM((4 * block.shape[0], block.shape[1]), block.dtype), pltpu.SemaphoreType.DMA((4,))]
+
+
+def weights_kernel(core_ref, flags, e_ref, a_lse, b_lse, *refs):
+    a_refs, (w_ref, gb_hi, a_half, a_sem) = refs[:8], refs[8:]
     rows = a_lse.shape[1]
     half = 4 * rows
     core = core_ref[0]
+    start_half(core, a_refs, 1, a_half, a_sem)
     for q in range(2):
         a_row = jnp.concatenate([a_lse[4 * q + j : 4 * q + j + 1, :] for j in range(4)], axis=1)
         b_row = jnp.concatenate([b_lse[pl.ds((q ^ core) * 4 + j, 1), :] for j in range(4)], axis=1)
@@ -304,51 +308,60 @@
                 s = e_ref[q, sl, :]
                 w_ref[q, sl, :] = (jnp.exp2(s - a_col[sl, :]) + jnp.exp2(s - b_row)).astype(jnp.bfloat16)
 
-    q = 1 - core
-    gb_hi[...] = (0.5 * dot_tn(w_ref[q], a_cat[q])).astype(jnp.bfloat16)
-
-
-def weights_call(core, flags, e, a_lse, b_lse, a_cat):
-    _, half, features = a_cat.shape
+    wait_half(a_refs, a_half, a_sem)
+    gb_hi[...] = (0.5 * dot_tn(w_ref[1 - core], a_half[...])).astype(jnp.bfloat16)
+
+
+def weights_call(core, flags, e, a_lse, b_lse, a_blocks):
+    rows, features = a_blocks[0].shape
+    half = 4 * rows
     return pl.pallas_call(
         weights_kernel,
-        in_specs=[smem_spec()] * 2 + [vmem_spec()] * 4,
+        in_specs=[smem_spec()] * 2 + [vmem_spec()] * 3 + [any_spec()] * 8,
         out_specs=[vmem_spec()] * 2,
         out_shape=[
             pltpu.VMEM((2, half, half), jnp.bfloat16),
             jax.ShapeDtypeStruct((half, features), jnp.bfloat16),
         ],
+        scratch_shapes=half_scratch(a_blocks[0]),
         compiler_params=params(),
         cost_estimate=cost(1, half, half, features, 12),
         name="weights",
-    )(core, flags, e, a_lse, b_lse, a_cat)
-
-
-def middle_kernel(core_ref, w_ref, a_cat, b_cat, ga_hi, gb0, gb_lo):
+    )(core, flags, e, a_lse, b_lse, *a_blocks)
+
+
+def middle_kernel(core_ref, w_ref, *refs):
+    a_refs, b_refs = refs[:8], refs[8:16]
+    ga_hi, gb0, gb_lo, a_half, a_sem, b_half, b_sem = refs[16:]
     rows = gb0.shape[0]
-    q = core_ref[0]
-    g = 0.5 * dot_tn(w_ref[q], a_cat[q])
+    core = core_ref[0]
+    start_half(core, a_refs, 0, a_half, a_sem)
+    start_half(core, b_refs, 1, b_half, b_sem)
+    wait_half(a_refs, a_half, a_sem)
+    g = 0.5 * dot_tn(w_ref[core], a_half[...])
     gb0[...] = g[:rows]
     gb_lo[...] = g[rows:].astype(jnp.bfloat16)
-    ga_hi[...] = 0.5 * jnp.dot(w_ref[1], b_cat[1], preferred_element_type=jnp.float32)
-
-
-def middle_call(core, w, a_cat, b_cat):
-    _, half, features = a_cat.shape
-    rows = half // 4
+    wait_half(b_refs, b_half, b_sem)
+    ga_hi[...] = 0.5 * jnp.dot(w_ref[1], b_half[...], preferred_element_type=jnp.float32)
+
+
+def middle_call(core, w, a_blocks, b_blocks):
+    rows, features = a_blocks[0].shape
+    half = 4 * rows
     return pl.pallas_call(
         middle_kernel,
-        in_specs=[smem_spec()] + [vmem_spec()] * 3,
+        in_specs=[smem_spec(), vmem_spec()] + [any_spec()] * 16,
         out_specs=[vmem_spec()] * 3,
         out_shape=[
             pltpu.VMEM((half, features), jnp.float32),
             jax.ShapeDtypeStruct((rows, features), jnp.float32),
             jax.ShapeDtypeStruct((half - rows, features), jnp.bfloat16),
         ],
+        scratch_shapes=half_scratch(a_blocks[0]) + half_scratch(b_blocks[0]),
         compiler_params=params(),
         cost_estimate=cost(2, half, half, features),
         name="middle",
-    )(core, w, a_cat, b_cat)
+    )(core, w, *a_blocks, *b_blocks)
 
 
 def far_kernel(ga_hi, got, *outs):
@@ -372,29 +385,34 @@
     )(ga_hi, got)
 
 
-def last_kernel(w_ref, b_cat, ga_lo):
-    ga_lo[...] = 0.5 * jnp.dot(w_ref[0], b_cat[0], preferred_element_type=jnp.float32)
-
-
-def last_call(w, b_cat):
-    _, half, features = b_cat.shape
+def last_kernel(core_ref, w_ref, *refs):
+    b_refs, (ga_lo, b_half, b_sem) = refs[:8], refs[8:]
+    start_half(core_ref[0], b_refs, 0, b_half, b_sem)
+    wait_half(b_refs, b_half, b_sem)
+    ga_lo[...] = 0.5 * jnp.dot(w_ref[0], b_half[...], preferred_element_type=jnp.float32)
+
+
+def last_call(core, w, b_blocks):
+    rows, features = b_blocks[0].shape
+    half = 4 * rows
     return pl.pallas_call(
         last_kernel,
-        in_specs=[vmem_spec()] * 2,
+        in_specs=[smem_spec(), vmem_spec()] + [any_spec()] * 8,
         out_specs=vmem_spec(),
         out_shape=pltpu.VMEM((half, features), jnp.float32),
+        scratch_shapes=half_scratch(b_blocks[0]),
         compiler_params=params(),
         cost_estimate=cost(1, half, half, features),
         name="last",
-    )(w, b_cat)
-
-
-def near_kernel(ga_lo, got0, got_lo, r_xy, r_yz, r_xz, r_xyz, p0, p1, p2, p4):
+    )(core, w, *b_blocks)
+
+
+def near_kernel(ga_lo, got0, got_lo, r_xy, r_yz, r_xz, p0, p1, p2, p4):
     rows = p0.shape[0]
     wide = lambda ref: ref[...].astype(jnp.float32)
     p0[...] = ga_lo[:rows] + got0[...]
     part = lambda j: ga_lo[j * rows : (j + 1) * rows, :] + got_lo[(j - 1) * rows : j * rows, :].astype(jnp.float32)
-    p1[...] = (part(1) + wide(r_xz) + wide(r_xyz)).astype(jnp.bfloat16)
+    p1[...] = (part(1) + wide(r_xz)).astype(jnp.bfloat16)
     p2[...] = (part(2) + wide(r_xy)).astype(jnp.bfloat16)
     p4[...] = (part(3) + wide(r_yz)).astype(jnp.bfloat16)
 
@@ -404,7 +422,7 @@
     narrow = jax.ShapeDtypeStruct((rows, features), jnp.bfloat16)
     return pl.pallas_call(
         near_kernel,
-        in_specs=[vmem_spec()] * 7,
+        in_specs=[vmem_spec()] * 6,
         out_specs=[vmem_spec()] * 4,
         out_shape=[pltpu.VMEM((rows, features), jnp.float32)] + [narrow] * 3,
         compiler_params=params(),
@@ -426,14 +444,14 @@
     mine = jnp.where(first, images, texts)
     other = swap(jnp.where(first, texts, images))
     own = jnp.concatenate([mine, other], axis=0)
-    near = {m: to_cube(own, m) for m in (1, 2, 4)}
-    far = {3: to_cube(near[2], 1), 6: to_cube(near[4], 2), 5: to_cube(near[1], 4), 7: to_cube(near[1], 6)}
-    a_lo = join_call([own, near[1], near[2], near[4]])
-    b_lo = swap(a_lo)
-    a_hi = [far[m] for m in ORDER[4:]]
-    b_hi = [swap(a) for a in a_hi]
-
-    e, a_cat, b_cat, a_stat, b_stat, flags = scores_call(core_arr, a_lo, b_lo, a_hi, b_hi, scale)
+    blocks = {0: own, 1: to_cube(own, 1), 2: to_cube(own, 2), 4: to_cube(own, 4), 7: to_cube(own, 7)}
+    blocks[5] = to_cube(blocks[1], 4)
+    blocks[3] = to_cube(blocks[2], 1)
+    blocks[6] = to_cube(blocks[4], 2)
+    a_blocks = [blocks[m] for m in ORDER]
+    b_blocks = [swap(a) for a in a_blocks]
+
+    e, a_stat, b_stat, flags = scores_call(core_arr, a_blocks, b_blocks, scale)
     chip_stat = jnp.logaddexp2(a_stat, swap(b_stat))
     got = lax.all_to_all(
         jnp.broadcast_to(chip_stat[None], (8,) + chip_stat.shape), AXES, 0, 0, axis_index_groups=GROUPS
@@ -441,19 +459,19 @@
     a_lse = merge_call(place, got)
     b_lse = swap(a_lse)
 
-    w, gb_hi = weights_call(core_arr, flags, e, a_lse, b_lse, a_cat)
+    w, gb_hi = weights_call(core_arr, flags, e, a_lse, b_lse, a_blocks)
     got_hi = swap(gb_hi)
-    ga_hi, gb0, gb_lo = middle_call(core_arr, w, a_cat, b_cat)
+    ga_hi, gb0, gb_lo = middle_call(core_arr, w, a_blocks, b_blocks)
     got0, got_lo = swap(gb0), swap(gb_lo)
     p = dict(zip(ORDER[4:], far_call(ga_hi, got_hi)))
-    from_xyz = to_cube(p[7], 6)
     from_xy = to_cube(p[3], 1)
     from_yz = to_cube(p[6], 2)
     from_xz = to_cube(p[5], 4)
-    ga_lo = last_call(w, b_cat)
-    p0, p1, p2, p4 = near_call(ga_lo, got0, got_lo, from_xy, from_yz, from_xz, from_xyz)
+    from_xyz = to_cube(p[7], 7)
+    ga_lo = last_call(core_arr, w, b_blocks)
+    p0, p1, p2, p4 = near_call(ga_lo, got0, got_lo, from_xy, from_yz, from_xz)
     wide = lambda a: a.astype(jnp.float32)
-    total = p0 + wide(to_cube(p1, 1)) + wide(to_cube(p2, 2)) + wide(to_cube(p4, 4))
+    total = p0 + wide(from_xyz) + wide(to_cube(p1, 1)) + wide(to_cube(p2, 2)) + wide(to_cube(p4, 4))
     kept, sent = total[:rows], total[rows:]
     got_sum = swap(sent)
     image_sum = jnp.where(first, kept, got_sum)

time: 213 us -> 144 us (0.68)
  Pallas kernels: 107 us -> 49.1 us
  waiting for transfers between devices: 52.1 us -> 41.6 us
  local copies, waits for them, and re-layouts: 18.2 us -> 15.7 us
    pallas_call x4 -> x3, Pallas kernels: 72.3 us -> 14.5 us  [the longest x1 9.98 us: middle_call(): pl.pallas_call(middle_kernel, in_specs=[smem_spec(), vmem_spec()] + [any_...]
    ppermute x14, waiting for transfers between devices: 33.2 us -> 25.8 us  [to_cube(): return lax.ppermute(a, AXES, across(m))]
    pallas_call x1, Pallas kernels: 20.9 us -> 24.1 us  [scores_call(): pl.pallas_call(functools.partial(scores_kernel, scale), in_specs=[smem_sp...]
    ppermute x12 -> x15, waiting for transfers between devices: 10.3 us -> 7.24 us  [swap(): return lax.ppermute(a, AXES, SWAP)]
    pallas_call x1, Pallas kernels: 11.6 us -> 8.53 us  [weights_call(): pl.pallas_call(weights_kernel, in_specs=[smem_spec()] * 2 + [vmem_spec()]...]
    unnamed x52 -> x48, local copies, waits for them, and re-layouts: 17.5 us -> 15 us
  transfers between devices with their start and end apart: 27 -> 30, of which waited for: 20 -> 15; matrix products, arithmetic and copies ran while one was open for 0% -> 0% of each run, Pallas kernels for 5% -> 10%
where the time goes in v3:
time: 144 us; the launch traced here: 143 us
  Pallas kernels  49.1 us (34%)
  waiting for transfers between devices  41.6 us (29%)
  starting transfers between devices  33.6 us (23%)
  local copies, waits for them, and re-layouts  15.7 us (11%)
  other arithmetic  2.45 us (2%)
    ppermute x14, waiting for transfers between devices, to_cube(): return lax.ppermute(a, AXES, across(m))  25.8 us
    ppermute x14, starting transfers between devices, to_cube(): return lax.ppermute(a, AXES, across(m))  24.5 us
    pallas_call x1, Pallas kernels, scores_call(): pl.pallas_call(functools.partial(scores_kernel, scale), in_specs=[smem_sp...  24.1 us
    unnamed x48, local copies, waits for them, and re-layouts  15 us
    pallas_call x1, Pallas kernels, middle_call(): pl.pallas_call(middle_kernel, in_specs=[smem_spec(), vmem_spec()] + [any_...  9.98 us
    all_to_all x1, waiting for transfers between devices, body(): lax.all_to_all(jnp.broadcast_to(chip_stat[None], (8,) + chip_stat.shape),...  8.58 us
    pallas_call x1, Pallas kernels, weights_call(): pl.pallas_call(weights_kernel, in_specs=[smem_spec()] * 2 + [vmem_spec()]...  8.53 us
    ppermute x15, waiting for transfers between devices, swap(): return lax.ppermute(a, AXES, SWAP)  7.24 us
  transfers between devices with their start and end apart: 30, of which 15 were waited for; matrix products, arithmetic and copies ran while one was open for 0% of the time, Pallas kernels for 10%

profile of v3, /device:TPU:1, one launch (start us, length us, event | category | flops | bytes accessed | tf_op | source)
XLA Modules:
  0.0 143.4 jit_solution(5841548832622704270)
XLA Ops:
  0.6 1.1 broadcast_select_fusion.1
  1.7 1.5 %collective-permute-start = (bf16[160,768]{1,0:T(8,128)(2,1)S(1)}, bf16[160,768]{1,0:T(8,128)(2,1)S(1)}, u32[]{:S(2)}, u32[]{:S(2)}) collective-permute-start(bf16[160,768]{1,0:T(8,128)(2,1)S(1)} %get-tuple-element.39), channel_id=1, source_target_pairs={{0,16},{1,17},{2,18},{3,19},{4,20},{5,21},{6,22},{7,23},{8,24},{9,... | collective-permute-start | bytes 737288 | tf_op jit(solution)/shard_map/ppermute | solution.py:78
  3.2 1.1 collective-permute-done
  4.4 8.6 %collective-permute-start.7 = (bf16[320,768]{1,0:T(8,128)(2,1)S(1)}, bf16[320,768]{1,0:T(8,128)(2,1)S(1)}, u32[]{:S(2)}, u32[]{:S(2)}) collective-permute-start(bf16[320,768]{1,0:T(8,128)(2,1)S(1)} %pad_maximum_fusion.refs_0_), channel_id=1, source_target_pairs={{0,37},{1,36},{2,39},{3,38},{4,33},{5,32},{6,35},{7,34},{8,45},{9,... | collective-permute-start | bytes 1474568 | tf_op jit(solution)/shard_map/ppermute | solution.py:74
  13.0 0.0 collective-permute-start.2
  13.0 0.6 collective-permute-start.1
  13.6 5.7 %collective-permute-done.7.refs_7_ = bf16[320,768]{1,0:T(8,128)(2,1)S(1)} collective-permute-done((bf16[320,768]{1,0:T(8,128)(2,1)S(1)}, bf16[320,768]{1,0:T(8,128)(2,1)S(1)}, u32[]{:S(2)}, u32[]{:S(2)}) %collective-permute-start.7) | collective-permute-done | bytes 491552 | tf_op jit(solution)/shard_map/ppermute | solution.py:74
  19.3 5.2 %collective-permute-done.3.refs_3_ = bf16[320,768]{1,0:T(8,128)(2,1)S(1)} collective-permute-done((bf16[320,768]{1,0:T(8,128)(2,1)S(1)}, bf16[320,768]{1,0:T(8,128)(2,1)S(1)}, u32[]{:S(2)}, u32[]{:S(2)}) %collective-permute-start.3) | collective-permute-done | bytes 491552 | tf_op jit(solution)/shard_map/ppermute | solution.py:74
  24.5 0.0 collective-permute-start.11
  24.5 0.0 collective-permute-done.8.refs_8_.refs_0_
  24.5 1.2 collective-permute-start.6
  25.7 0.0 collective-permute-done.2.refs_2_
  25.7 1.6 %collective-permute-start.4 = (bf16[320,768]{1,0:T(8,128)(2,1)S(1)}, bf16[320,768]{1,0:T(8,128)(2,1)S(1)}, u32[]{:S(2)}, u32[]{:S(2)}) collective-permute-start(bf16[320,768]{1,0:T(8,128)(2,1)S(1)} %collective-permute-done.2.refs_2_), channel_id=1, source_target_pairs={{0,4},{1,5},{2,6},{3,7},{4,0},{5,1},{6,2},{7,3},{8,12},{9,13},{10,... | collective-permute-start | bytes 1474568 | tf_op jit(solution)/shard_map/ppermute | solution.py:74
  27.3 0.0 collective-permute-done.1.refs_1_
  27.3 1.6 %collective-permute-start.5 = (bf16[320,768]{1,0:T(8,128)(2,1)S(1)}, bf16[320,768]{1,0:T(8,128)(2,1)S(1)}, u32[]{:S(2)}, u32[]{:S(2)}) collective-permute-start(bf16[320,768]{1,0:T(8,128)(2,1)S(1)} %collective-permute-done.1.refs_1_), channel_id=1, source_target_pairs={{0,1},{1,0},{2,3},{3,2},{4,5},{5,4},{6,7},{7,6},{8,9},{9,8},{10,11... | collective-permute-start | bytes 1474568 | tf_op jit(solution)/shard_map/ppermute | solution.py:74
  28.9 0.0 collective-permute-done.15.refs_15_.refs_7_
  28.9 0.5 collective-permute-start.9
  29.4 4.0 %collective-permute-done.6.refs_6_ = bf16[320,768]{1,0:T(8,128)(2,1)S(1)} collective-permute-done((bf16[320,768]{1,0:T(8,128)(2,1)S(1)}, bf16[320,768]{1,0:T(8,128)(2,1)S(1)}, u32[]{:S(2)}, u32[]{:S(2)}) %collective-permute-start.6) | collective-permute-done | bytes 491552 | tf_op jit(solution)/shard_map/ppermute | solution.py:74
  33.4 0.4 collective-permute-start.14
  33.8 0.8 collective-permute-done.4.refs_4_
  34.6 1.6 %collective-permute-done.5.refs_5_ = bf16[320,768]{1,0:T(8,128)(2,1)S(1)} collective-permute-done((bf16[320,768]{1,0:T(8,128)(2,1)S(1)}, bf16[320,768]{1,0:T(8,128)(2,1)S(1)}, u32[]{:S(2)}, u32[]{:S(2)}) %collective-permute-start.5) | collective-permute-done | bytes 491552 | tf_op jit(solution)/shard_map/ppermute | solution.py:74
  36.2 0.0 collective-permute-done.9.refs_9_.refs_1_
  36.3 0.2 collective-permute-done.12.refs_12_.refs_4_
  36.5 1.6 %collective-permute-done.13.refs_13_.refs_5_ = bf16[320,768]{1,0:T(8,128)(2,1)S(1)} collective-permute-done((bf16[320,768]{1,0:T(8,128)(2,1)S(1)}, bf16[320,768]{1,0:T(8,128)(2,1)S(1)}, u32[]{:S(2)}, u32[]{:S(2)}) %collective-permute-start.13) | collective-permute-done | bytes 491552 | tf_op jit(solution)/shard_map/ppermute | solution.py:78
  38.1 24.1 %scores.1 = (f32[2,1280,1280]{2,1,0:T(8,128)S(1)}, f32[8,320]{1,0:T(8,128)S(1)}, f32[8,320]{1,0:T(8,128)S(1)}, s32[2]{0:T(128)S(1)}) custom-call(s32[1]{0:T(128)} %bitcast.core_ref, bf16[320,768]{1,0:T(8,128)(2,1)S(1)} %pad_maximum_fusion.refs_0_, bf16[320,768]{1,0:T(8,128)(2,1)S(1)} %collective-permute-done.1.refs_1_, ...), custom_call_target="tpu_custom_call" | custom-call | flops 5033164800 | tf_op jit(solution)/shard_map/scores/pallas_call | solution.py:212
  62.3 4.7 %copy-done = f32[2,1280,1280]{2,1,0:T(8,128)} copy-done((f32[2,1280,1280]{2,1,0:T(8,128)}, f32[2,1280,1280]{2,1,0:T(8,128)S(1)}, u32[]{:S(2)}) %copy-start) | copy-done | bytes 13107224
  67.1 0.1 collective-permute-start.16
  67.2 1.0 collective-permute-done.16
  68.3 0.6 broadcast_in_dim.2
  68.9 5.5 %all-to-all-start = ((f32[8,8,320]{2,1,0:T(8,128)}), f32[8,8,320]{2,1,0:T(8,128)S(1)}, u32[]{:S(2)}, u32[]{:S(2)}) async-start(f32[8,8,320]{2,1,0:T(8,128)} %broadcast_in_dim.2), calls=%async_computation | async-start | bytes 196608 | tf_op jit(solution)/shard_map/all_to_all | solution.py:456
  74.4 8.6 %all-to-all-done.got_ref = f32[8,8,320]{2,1,0:T(8,128)S(1)} async-done(((f32[8,8,320]{2,1,0:T(8,128)}), f32[8,8,320]{2,1,0:T(8,128)S(1)}, u32[]{:S(2)}, u32[]{:S(2)}) %all-to-all-start) | async-done | bytes 81952 | tf_op jit(solution)/shard_map/all_to_all | solution.py:456
  83.0 0.6 copy-done.23
  83.6 1.6 %merge.1.a_lse = f32[8,320]{1,0:T(8,128)} custom-call(s32[1]{0:T(128)} %bitcast.1.place_ref, f32[8,8,320]{2,1,0:T(8,128)} %copy-done.23), custom_call_target="tpu_custom_call" | custom-call | tf_op jit(solution)/shard_map/merge/pallas_call | solution.py:251
  85.1 1.4 collective-permute-done.17.b_lse
  86.5 4.7 %copy-done.1 = f32[2,1280,1280]{2,1,0:T(8,128)S(1)} copy-done((f32[2,1280,1280]{2,1,0:T(8,128)S(1)}, f32[2,1280,1280]{2,1,0:T(8,128)}, u32[]{:S(2)}) %copy-start.1) | copy-done | bytes 13107224
  91.3 1.0 copy-done.3
  92.3 1.0 copy-done.13
  93.3 1.0 copy-done.17
  94.4 1.0 copy-done.19
  95.4 0.7 copy-done.20
  96.1 8.5 %weights.1 = (bf16[2,1280,1280]{2,1,0:T(8,128)(2,1)S(1)}, bf16[1280,768]{1,0:T(8,128)(2,1)S(1)}) custom-call(s32[1]{0:T(128)} %bitcast.core_ref, s32[2]{0:T(128)S(1)} %get-tuple-element.19.flags, f32[2,1280,1280]{2,1,0:T(8,128)S(1)} %copy-done.1, f32[8,320]{1,0:T(8,128)S(1)} %copy-done.20, f32[8,320]{1,0:T(8,128)S(1)} %collective-permute-done.17.b_lse, ...), custom_call_target="tpu_custom_call" | custom-call | flops 2516582400 | bytes 19660800 | tf_op jit(solution)/shard_map/weights/pallas_call | solution.py:318
  104.7 0.2 collective-permute-start.20
  104.9 10.0 %middle.1 = (f32[1280,768]{1,0:T(8,128)S(1)}, f32[320,768]{1,0:T(8,128)S(1)}, bf16[960,768]{1,0:T(8,128)(2,1)S(1)}) custom-call(s32[1]{0:T(128)} %bitcast.core_ref, bf16[2,1280,1280]{2,1,0:T(8,128)(2,1)S(1)} %get-tuple-element.23.w_ref, bf16[320,768]{1,0:T(8,128)(2,1)S(1)} %pad_maximum_fusion.refs_0_, bf16[320,768]{1,0:T(8,128)(2,1)S(1)} %copy-done.3, ...), custom_call_target="tpu_custom_call" | custom-call | flops 5033164800 | tf_op jit(solution)/shard_map/middle/pallas_call | solution.py:351
  114.9 0.6 collective-permute-start.19
  115.5 0.1 collective-permute-start.18
  115.6 0.3 far.1
  115.9 0.4 collective-permute-start.21
  116.3 0.3 collective-permute-start.22
  116.6 0.3 collective-permute-start.23
  116.9 4.0 %last.1.ga_lo = f32[1280,768]{1,0:T(8,128)S(1)} custom-call(s32[1]{0:T(128)} %bitcast.core_ref, bf16[2,1280,1280]{2,1,0:T(8,128)(2,1)S(1)} %get-tuple-element.23.w_ref, bf16[320,768]{1,0:T(8,128)(2,1)S(1)} %collective-permute-done.8.refs_8_.refs_0_, bf16[320,768]{1,0:T(8,128)(2,1)S(1)} %copy-done.7, bf16[320,768]{1,0:T(8,128)(2,1)S(1)} %copy-done.5, ...), custom_call_target="tpu_custom_call" | custom-call | flops 2516582400 | tf_op jit(solution)/shard_map/last/pallas_call | solution.py:398
  120.9 6.7 %collective-permute-start.24 = (bf16[320,768]{1,0:T(8,128)(2,1)S(1)}, bf16[320,768]{1,0:T(8,128)(2,1)S(1)}, u32[]{:S(2)}, u32[]{:S(2)}) collective-permute-start(bf16[320,768]{1,0:T(8,128)(2,1)S(1)} %get-tuple-element.32), channel_id=1, source_target_pairs={{0,37},{1,36},{2,39},{3,38},{4,33},{5,32},{6,35},{7,34},{8,45},{9,... | collective-permute-start | bytes 1474568 | tf_op jit(solution)/shard_map/ppermute | solution.py:74
  127.6 0.5 near.1
  128.1 0.0 copy-start.21
  128.1 0.0 copy-start.22
  128.2 0.5 collective-permute-start.25
  128.7 2.5 %collective-permute-start.26 = (bf16[320,768]{1,0:T(8,128)(2,1)S(1)}, bf16[320,768]{1,0:T(8,128)(2,1)S(1)}, u32[]{:S(2)}, u32[]{:S(2)}) collective-permute-start(bf16[320,768]{1,0:T(8,128)(2,1)S(1)} %get-tuple-element.34), channel_id=1, source_target_pairs={{0,32},{1,33},{2,34},{3,35},{4,36},{5,37},{6,38},{7,39},{8,40},{9,... | collective-permute-start | bytes 1474568 | tf_op jit(solution)/shard_map/ppermute | solution.py:74
  131.2 0.3 collective-permute-start.27
  131.5 2.7 %collective-permute-done.24 = bf16[320,768]{1,0:T(8,128)(2,1)S(1)} collective-permute-done((bf16[320,768]{1,0:T(8,128)(2,1)S(1)}, bf16[320,768]{1,0:T(8,128)(2,1)S(1)}, u32[]{:S(2)}, u32[]{:S(2)}) %collective-permute-start.24) | collective-permute-done | bytes 491552 | tf_op jit(solution)/shard_map/ppermute | solution.py:74
  134.2 5.2 %collective-permute-done.25 = bf16[320,768]{1,0:T(8,128)(2,1)S(1)} collective-permute-done((bf16[320,768]{1,0:T(8,128)(2,1)S(1)}, bf16[320,768]{1,0:T(8,128)(2,1)S(1)}, u32[]{:S(2)}, u32[]{:S(2)}) %collective-permute-start.25) | collective-permute-done | bytes 491552 | tf_op jit(solution)/shard_map/ppermute | solution.py:74
  139.3 0.7 collective-permute-done.27
  140.1 0.3 convert_add_fusion
  140.4 0.1 collective-permute-start.28
  140.5 1.9 %collective-permute-done.28 = f32[160,768]{1,0:T(8,128)S(1)} collective-permute-done((f32[160,768]{1,0:T(8,128)S(1)}, f32[160,768]{1,0:T(8,128)S(1)}, u32[]{:S(2)}, u32[]{:S(2)}) %collective-permute-start.28) | collective-permute-done | bytes 491552 | tf_op jit(solution)/shard_map/ppermute | solution.py:78
  142.3 1.0 convert_subtract_fusion
  (58 shorter events, 0.2 us)
Async XLA Ops:
  1.7 2.6 %collective-permute-start = (bf16[160,768]{1,0:T(8,128)(2,1)S(1)}, bf16[160,768]{1,0:T(8,128)(2,1)S(1)}, u32[]{:S(2)}, u32[]{:S(2)}) collective-permute-start(bf16[160,768]{1,0:T(8,128)(2,1)S(1)} %get-tuple-element.39), channel_id=1, source_target_pairs={{0,16},{1,17},{2,18},{3,19},{4,20},{5,21},{6,22},{7,23},{8,24},{9,... | collective-permute-start | bytes 737288 | tf_op jit(solution)/shard_map/ppermute | solution.py:78
  4.4 14.9 %collective-permute-start.7 = (bf16[320,768]{1,0:T(8,128)(2,1)S(1)}, bf16[320,768]{1,0:T(8,128)(2,1)S(1)}, u32[]{:S(2)}, u32[]{:S(2)}) collective-permute-start(bf16[320,768]{1,0:T(8,128)(2,1)S(1)} %pad_maximum_fusion.refs_0_), channel_id=1, source_target_pairs={{0,37},{1,36},{2,39},{3,38},{4,33},{5,32},{6,35},{7,34},{8,45},{9,... | collective-permute-start | bytes 1474568 | tf_op jit(solution)/shard_map/ppermute | solution.py:74
  13.0 11.5 %collective-permute-start.3 = (bf16[320,768]{1,0:T(8,128)(2,1)S(1)}, bf16[320,768]{1,0:T(8,128)(2,1)S(1)}, u32[]{:S(2)}, u32[]{:S(2)}) collective-permute-start(bf16[320,768]{1,0:T(8,128)(2,1)S(1)} %pad_maximum_fusion.refs_0_), channel_id=1, source_target_pairs={{0,1},{1,0},{2,3},{3,2},{4,5},{5,4},{6,7},{7,6},{8,9},{9,8},{10,11... | collective-permute-start | bytes 1474568 | tf_op jit(solution)/shard_map/ppermute | solution.py:74
  13.0 11.5 %collective-permute-start.8 = (bf16[320,768]{1,0:T(8,128)(2,1)S(1)}, bf16[320,768]{1,0:T(8,128)(2,1)S(1)}, u32[]{:S(2)}, u32[]{:S(2)}) collective-permute-start(bf16[320,768]{1,0:T(8,128)(2,1)S(1)} %pad_maximum_fusion.refs_0_), channel_id=1, source_target_pairs={{0,16},{1,17},{2,18},{3,19},{4,20},{5,21},{6,22},{7,23},{8,24},{9,... | collective-permute-start | bytes 1474568 | tf_op jit(solution)/shard_map/ppermute | solution.py:78
  13.0 12.7 %collective-permute-start.2 = (bf16[320,768]{1,0:T(8,128)(2,1)S(1)}, bf16[320,768]{1,0:T(8,128)(2,1)S(1)}, u32[]{:S(2)}, u32[]{:S(2)}) collective-permute-start(bf16[320,768]{1,0:T(8,128)(2,1)S(1)} %pad_maximum_fusion.refs_0_), channel_id=1, source_target_pairs={{0,32},{1,33},{2,34},{3,35},{4,36},{5,37},{6,38},{7,39},{8,40},{9,... | collective-permute-start | bytes 1474568 | tf_op jit(solution)/shard_map/ppermute | solution.py:74
  13.0 14.3 %collective-permute-start.1 = (bf16[320,768]{1,0:T(8,128)(2,1)S(1)}, bf16[320,768]{1,0:T(8,128)(2,1)S(1)}, u32[]{:S(2)}, u32[]{:S(2)}) collective-permute-start(bf16[320,768]{1,0:T(8,128)(2,1)S(1)} %pad_maximum_fusion.refs_0_), channel_id=1, source_target_pairs={{0,4},{1,5},{2,6},{3,7},{4,0},{5,1},{6,2},{7,3},{8,12},{9,13},{10,... | collective-permute-start | bytes 1474568 | tf_op jit(solution)/shard_map/ppermute | solution.py:74
  19.3 9.6 %collective-permute-start.15 = (bf16[320,768]{1,0:T(8,128)(2,1)S(1)}, bf16[320,768]{1,0:T(8,128)(2,1)S(1)}, u32[]{:S(2)}, u32[]{:S(2)}) collective-permute-start(bf16[320,768]{1,0:T(8,128)(2,1)S(1)} %collective-permute-done.7.refs_7_), channel_id=1, source_target_pairs={{0,16},{1,17},{2,18},{3,19},{4,20},{5,21},{6,22},{7,23},{8,24},{9,... | collective-permute-start | bytes 1474568 | tf_op jit(solution)/shard_map/ppermute | solution.py:78
  24.5 4.4 %collective-permute-start.11 = (bf16[320,768]{1,0:T(8,128)(2,1)S(1)}, bf16[320,768]{1,0:T(8,128)(2,1)S(1)}, u32[]{:S(2)}, u32[]{:S(2)}) collective-permute-start(bf16[320,768]{1,0:T(8,128)(2,1)S(1)} %collective-permute-done.3.refs_3_), channel_id=1, source_target_pairs={{0,16},{1,17},{2,18},{3,19},{4,20},{5,21},{6,22},{7,23},{8,24},{9,... | collective-permute-start | bytes 1474568 | tf_op jit(solution)/shard_map/ppermute | solution.py:78
  24.5 8.9 %collective-permute-start.6 = (bf16[320,768]{1,0:T(8,128)(2,1)S(1)}, bf16[320,768]{1,0:T(8,128)(2,1)S(1)}, u32[]{:S(2)}, u32[]{:S(2)}) collective-permute-start(bf16[320,768]{1,0:T(8,128)(2,1)S(1)} %collective-permute-done.3.refs_3_), channel_id=1, source_target_pairs={{0,32},{1,33},{2,34},{3,35},{4,36},{5,37},{6,38},{7,39},{8,40},{9,... | collective-permute-start | bytes 1474568 | tf_op jit(solution)/shard_map/ppermute | solution.py:74
  25.7 8.9 %collective-permute-start.4 = (bf16[320,768]{1,0:T(8,128)(2,1)S(1)}, bf16[320,768]{1,0:T(8,128)(2,1)S(1)}, u32[]{:S(2)}, u32[]{:S(2)}) collective-permute-start(bf16[320,768]{1,0:T(8,128)(2,1)S(1)} %collective-permute-done.2.refs_2_), channel_id=1, source_target_pairs={{0,4},{1,5},{2,6},{3,7},{4,0},{5,1},{6,2},{7,3},{8,12},{9,13},{10,... | collective-permute-start | bytes 1474568 | tf_op jit(solution)/shard_map/ppermute | solution.py:74
  27.3 34.9 %copy-start.2 = (bf16[320,768]{1,0:T(8,128)(2,1)}, bf16[320,768]{1,0:T(8,128)(2,1)S(1)}, u32[]{:S(2)}) copy-start(bf16[320,768]{1,0:T(8,128)(2,1)S(1)} %collective-permute-done.1.refs_1_) | copy-start | bytes 1474564
  27.3 8.9 %collective-permute-start.5 = (bf16[320,768]{1,0:T(8,128)(2,1)S(1)}, bf16[320,768]{1,0:T(8,128)(2,1)S(1)}, u32[]{:S(2)}, u32[]{:S(2)}) collective-permute-start(bf16[320,768]{1,0:T(8,128)(2,1)S(1)} %collective-permute-done.1.refs_1_), channel_id=1, source_target_pairs={{0,1},{1,0},{2,3},{3,2},{4,5},{5,4},{6,7},{7,6},{8,9},{9,8},{10,11... | collective-permute-start | bytes 1474568 | tf_op jit(solution)/shard_map/ppermute | solution.py:74
  28.9 7.3 %collective-permute-start.10 = (bf16[320,768]{1,0:T(8,128)(2,1)S(1)}, bf16[320,768]{1,0:T(8,128)(2,1)S(1)}, u32[]{:S(2)}, u32[]{:S(2)}) collective-permute-start(bf16[320,768]{1,0:T(8,128)(2,1)S(1)} %collective-permute-done.2.refs_2_), channel_id=1, source_target_pairs={{0,16},{1,17},{2,18},{3,19},{4,20},{5,21},{6,22},{7,23},{8,24},{9,... | collective-permute-start | bytes 1474568 | tf_op jit(solution)/shard_map/ppermute | solution.py:78
  28.9 7.3 %collective-permute-start.9 = (bf16[320,768]{1,0:T(8,128)(2,1)S(1)}, bf16[320,768]{1,0:T(8,128)(2,1)S(1)}, u32[]{:S(2)}, u32[]{:S(2)}) collective-permute-start(bf16[320,768]{1,0:T(8,128)(2,1)S(1)} %collective-permute-done.1.refs_1_), channel_id=1, source_target_pairs={{0,16},{1,17},{2,18},{3,19},{4,20},{5,21},{6,22},{7,23},{8,24},{9,... | collective-permute-start | bytes 1474568 | tf_op jit(solution)/shard_map/ppermute | solution.py:78
  33.4 28.9 %copy-start.12 = (bf16[320,768]{1,0:T(8,128)(2,1)}, bf16[320,768]{1,0:T(8,128)(2,1)S(1)}, u32[]{:S(2)}) copy-start(bf16[320,768]{1,0:T(8,128)(2,1)S(1)} %collective-permute-done.6.refs_6_) | copy-start | bytes 1474564
  33.4 2.9 %collective-permute-start.14 = (bf16[320,768]{1,0:T(8,128)(2,1)S(1)}, bf16[320,768]{1,0:T(8,128)(2,1)S(1)}, u32[]{:S(2)}, u32[]{:S(2)}) collective-permute-start(bf16[320,768]{1,0:T(8,128)(2,1)S(1)} %collective-permute-done.6.refs_6_), channel_id=1, source_target_pairs={{0,16},{1,17},{2,18},{3,19},{4,20},{5,21},{6,22},{7,23},{8,24},{9,... | collective-permute-start | bytes 1474568 | tf_op jit(solution)/shard_map/ppermute | solution.py:78
  34.6 27.6 %copy-start.16 = (bf16[320,768]{1,0:T(8,128)(2,1)}, bf16[320,768]{1,0:T(8,128)(2,1)S(1)}, u32[]{:S(2)}) copy-start(bf16[320,768]{1,0:T(8,128)(2,1)S(1)} %collective-permute-done.4.refs_4_) | copy-start | bytes 1474564
  34.6 1.9 %collective-permute-start.12 = (bf16[320,768]{1,0:T(8,128)(2,1)S(1)}, bf16[320,768]{1,0:T(8,128)(2,1)S(1)}, u32[]{:S(2)}, u32[]{:S(2)}) collective-permute-start(bf16[320,768]{1,0:T(8,128)(2,1)S(1)} %collective-permute-done.4.refs_4_), channel_id=1, source_target_pairs={{0,16},{1,17},{2,18},{3,19},{4,20},{5,21},{6,22},{7,23},{8,24},{9,... | collective-permute-start | bytes 1474568 | tf_op jit(solution)/shard_map/ppermute | solution.py:78
  36.2 26.1 %copy-start.18 = (bf16[320,768]{1,0:T(8,128)(2,1)}, bf16[320,768]{1,0:T(8,128)(2,1)S(1)}, u32[]{:S(2)}) copy-start(bf16[320,768]{1,0:T(8,128)(2,1)S(1)} %collective-permute-done.5.refs_5_) | copy-start | bytes 1474564
  36.2 1.9 %collective-permute-start.13 = (bf16[320,768]{1,0:T(8,128)(2,1)S(1)}, bf16[320,768]{1,0:T(8,128)(2,1)S(1)}, u32[]{:S(2)}, u32[]{:S(2)}) collective-permute-start(bf16[320,768]{1,0:T(8,128)(2,1)S(1)} %collective-permute-done.5.refs_5_), channel_id=1, source_target_pairs={{0,16},{1,17},{2,18},{3,19},{4,20},{5,21},{6,22},{7,23},{8,24},{9,... | collective-permute-start | bytes 1474568 | tf_op jit(solution)/shard_map/ppermute | solution.py:78
  36.2 26.0 %copy-start.4 = (bf16[320,768]{1,0:T(8,128)(2,1)}, bf16[320,768]{1,0:T(8,128)(2,1)S(1)}, u32[]{:S(2)}) copy-start(bf16[320,768]{1,0:T(8,128)(2,1)S(1)} %collective-permute-done.10.refs_10_.refs_2_) | copy-start | bytes 1474564
  36.2 26.0 %copy-start.6 = (bf16[320,768]{1,0:T(8,128)(2,1)}, bf16[320,768]{1,0:T(8,128)(2,1)S(1)}, u32[]{:S(2)}) copy-start(bf16[320,768]{1,0:T(8,128)(2,1)S(1)} %collective-permute-done.9.refs_9_.refs_1_) | copy-start | bytes 1474564
  36.2 26.0 %copy-start.8 = (bf16[320,768]{1,0:T(8,128)(2,1)}, bf16[320,768]{1,0:T(8,128)(2,1)S(1)}, u32[]{:S(2)}) copy-start(bf16[320,768]{1,0:T(8,128)(2,1)S(1)} %collective-permute-done.14.refs_14_.refs_6_) | copy-start | bytes 1474564
  36.5 25.8 %copy-start.10 = (bf16[320,768]{1,0:T(8,128)(2,1)}, bf16[320,768]{1,0:T(8,128)(2,1)S(1)}, u32[]{:S(2)}) copy-start(bf16[320,768]{1,0:T(8,128)(2,1)S(1)} %collective-permute-done.12.refs_12_.refs_4_) | copy-start | bytes 1474564
  38.1 24.2 %copy-start.14 = (bf16[320,768]{1,0:T(8,128)(2,1)}, bf16[320,768]{1,0:T(8,128)(2,1)S(1)}, u32[]{:S(2)}) copy-start(bf16[320,768]{1,0:T(8,128)(2,1)S(1)} %collective-permute-done.13.refs_13_.refs_5_) | copy-start | bytes 1474564
  62.3 4.7 %copy-start = (f32[2,1280,1280]{2,1,0:T(8,128)}, f32[2,1280,1280]{2,1,0:T(8,128)S(1)}, u32[]{:S(2)}) copy-start(f32[2,1280,1280]{2,1,0:T(8,128)S(1)} %get-tuple-element.20.e_ref) | copy-start | bytes 39321604
  67.1 1.2 collective-permute-start.16
  68.9 14.1 %all-to-all-start = ((f32[8,8,320]{2,1,0:T(8,128)}), f32[8,8,320]{2,1,0:T(8,128)S(1)}, u32[]{:S(2)}, u32[]{:S(2)}) async-start(f32[8,8,320]{2,1,0:T(8,128)} %broadcast_in_dim.2), calls=%async_computation | async-start | bytes 196608 | tf_op jit(solution)/shard_map/all_to_all | solution.py:456
  83.0 0.6 copy-start.23
  85.1 1.4 collective-permute-start.17
  86.5 4.7 %copy-start.1 = (f32[2,1280,1280]{2,1,0:T(8,128)S(1)}, f32[2,1280,1280]{2,1,0:T(8,128)}, u32[]{:S(2)}) copy-start(f32[2,1280,1280]{2,1,0:T(8,128)} %copy-done) | copy-start | bytes 39321604
  91.3 1.0 copy-start.3
  92.3 1.0 copy-start.13
  93.3 1.0 copy-start.17
  94.4 1.0 copy-start.19
  95.4 0.7 copy-start.20
  96.1 8.8 %copy-start.5 = (bf16[320,768]{1,0:T(8,128)(2,1)S(1)}, bf16[320,768]{1,0:T(8,128)(2,1)}, u32[]{:S(2)}) copy-start(bf16[320,768]{1,0:T(8,128)(2,1)} %copy-done.4) | copy-start | bytes 1474564
  96.1 8.8 %copy-start.7 = (bf16[320,768]{1,0:T(8,128)(2,1)S(1)}, bf16[320,768]{1,0:T(8,128)(2,1)}, u32[]{:S(2)}) copy-start(bf16[320,768]{1,0:T(8,128)(2,1)} %copy-done.6) | copy-start | bytes 1474564
  96.1 8.8 %copy-start.9 = (bf16[320,768]{1,0:T(8,128)(2,1)S(1)}, bf16[320,768]{1,0:T(8,128)(2,1)}, u32[]{:S(2)}) copy-start(bf16[320,768]{1,0:T(8,128)(2,1)} %copy-done.8) | copy-start | bytes 1474564
  96.1 8.8 %copy-start.11 = (bf16[320,768]{1,0:T(8,128)(2,1)S(1)}, bf16[320,768]{1,0:T(8,128)(2,1)}, u32[]{:S(2)}) copy-start(bf16[320,768]{1,0:T(8,128)(2,1)} %copy-done.10) | copy-start | bytes 1474564
  96.1 8.8 %copy-start.15 = (bf16[320,768]{1,0:T(8,128)(2,1)S(1)}, bf16[320,768]{1,0:T(8,128)(2,1)}, u32[]{:S(2)}) copy-start(bf16[320,768]{1,0:T(8,128)(2,1)} %copy-done.14) | copy-start | bytes 1474564
  104.7 11.0 %collective-permute-start.20 = (bf16[1280,768]{1,0:T(8,128)(2,1)S(1)}, bf16[1280,768]{1,0:T(8,128)(2,1)S(1)}, u32[]{:S(2)}, u32[]{:S(2)}) collective-permute-start(bf16[1280,768]{1,0:T(8,128)(2,1)S(1)} %get-tuple-element.27), channel_id=1, source_target_pairs={{0,16},{1,17},{2,18},{3,19},{4,20},{5,21},{6,22},{7,23},{8,24},{9,... | collective-permute-start | bytes 5898248 | tf_op jit(solution)/shard_map/ppermute | solution.py:78
  114.9 12.7 %collective-permute-start.19 = (bf16[960,768]{1,0:T(8,128)(2,1)S(1)}, bf16[960,768]{1,0:T(8,128)(2,1)S(1)}, u32[]{:S(2)}, u32[]{:S(2)}) collective-permute-start(bf16[960,768]{1,0:T(8,128)(2,1)S(1)} %get-tuple-element.25), channel_id=1, source_target_pairs={{0,16},{1,17},{2,18},{3,19},{4,20},{5,21},{6,22},{7,23},{8,24},{9,... | collective-permute-start | bytes 4423688 | tf_op jit(solution)/shard_map/ppermute | solution.py:78
  115.5 5.4 %collective-permute-start.18 = (f32[320,768]{1,0:T(8,128)S(1)}, f32[320,768]{1,0:T(8,128)S(1)}, u32[]{:S(2)}, u32[]{:S(2)}) collective-permute-start(f32[320,768]{1,0:T(8,128)S(1)} %get-tuple-element.24), channel_id=1, source_target_pairs={{0,16},{1,17},{2,18},{3,19},{4,20},{5,21},{6,22},{7,23},{8,24},{9,... | collective-permute-start | bytes 2949128 | tf_op jit(solution)/shard_map/ppermute | solution.py:78
  115.9 11.7 %collective-permute-start.21 = (bf16[320,768]{1,0:T(8,128)(2,1)S(1)}, bf16[320,768]{1,0:T(8,128)(2,1)S(1)}, u32[]{:S(2)}, u32[]{:S(2)}) collective-permute-start(bf16[320,768]{1,0:T(8,128)(2,1)S(1)} %get-tuple-element.28), channel_id=1, source_target_pairs={{0,4},{1,5},{2,6},{3,7},{4,0},{5,1},{6,2},{7,3},{8,12},{9,13},{10,... | collective-permute-start | bytes 1474568 | tf_op jit(solution)/shard_map/ppermute | solution.py:74
  116.3 11.3 %collective-permute-start.22 = (bf16[320,768]{1,0:T(8,128)(2,1)S(1)}, bf16[320,768]{1,0:T(8,128)(2,1)S(1)}, u32[]{:S(2)}, u32[]{:S(2)}) collective-permute-start(bf16[320,768]{1,0:T(8,128)(2,1)S(1)} %get-tuple-element.29), channel_id=1, source_target_pairs={{0,32},{1,33},{2,34},{3,35},{4,36},{5,37},{6,38},{7,39},{8,40},{9,... | collective-permute-start | bytes 1474568 | tf_op jit(solution)/shard_map/ppermute | solution.py:74
  116.6 11.0 %collective-permute-start.23 = (bf16[320,768]{1,0:T(8,128)(2,1)S(1)}, bf16[320,768]{1,0:T(8,128)(2,1)S(1)}, u32[]{:S(2)}, u32[]{:S(2)}) collective-permute-start(bf16[320,768]{1,0:T(8,128)(2,1)S(1)} %get-tuple-element.30), channel_id=1, source_target_pairs={{0,1},{1,0},{2,3},{3,2},{4,5},{5,4},{6,7},{7,6},{8,9},{9,8},{10,11... | collective-permute-start | bytes 1474568 | tf_op jit(solution)/shard_map/ppermute | solution.py:74
  120.9 13.3 %collective-permute-start.24 = (bf16[320,768]{1,0:T(8,128)(2,1)S(1)}, bf16[320,768]{1,0:T(8,128)(2,1)S(1)}, u32[]{:S(2)}, u32[]{:S(2)}) collective-permute-start(bf16[320,768]{1,0:T(8,128)(2,1)S(1)} %get-tuple-element.32), channel_id=1, source_target_pairs={{0,37},{1,36},{2,39},{3,38},{4,33},{5,32},{6,35},{7,34},{8,45},{9,... | collective-permute-start | bytes 1474568 | tf_op jit(solution)/shard_map/ppermute | solution.py:74
  128.1 14.2 %copy-start.21 = (bf16[160,768]{1,0:T(8,128)(2,1)S(1)}, bf16[160,768]{1,0:T(8,128)(2,1)}, u32[]{:S(2)}) copy-start(bf16[160,768]{1,0:T(8,128)(2,1)} %param.2) | copy-start | bytes 737284
  128.1 14.2 %copy-start.22 = (bf16[160,768]{1,0:T(8,128)(2,1)S(1)}, bf16[160,768]{1,0:T(8,128)(2,1)}, u32[]{:S(2)}) copy-start(bf16[160,768]{1,0:T(8,128)(2,1)} %param.3) | copy-start | bytes 737284
  128.2 11.2 %collective-permute-start.25 = (bf16[320,768]{1,0:T(8,128)(2,1)S(1)}, bf16[320,768]{1,0:T(8,128)(2,1)S(1)}, u32[]{:S(2)}, u32[]{:S(2)}) collective-permute-start(bf16[320,768]{1,0:T(8,128)(2,1)S(1)} %get-tuple-element.33), channel_id=1, source_target_pairs={{0,4},{1,5},{2,6},{3,7},{4,0},{5,1},{6,2},{7,3},{8,12},{9,13},{10,... | collective-permute-start | bytes 1474568 | tf_op jit(solution)/shard_map/ppermute | solution.py:74
  128.7 10.7 %collective-permute-start.26 = (bf16[320,768]{1,0:T(8,128)(2,1)S(1)}, bf16[320,768]{1,0:T(8,128)(2,1)S(1)}, u32[]{:S(2)}, u32[]{:S(2)}) collective-permute-start(bf16[320,768]{1,0:T(8,128)(2,1)S(1)} %get-tuple-element.34), channel_id=1, source_target_pairs={{0,32},{1,33},{2,34},{3,35},{4,36},{5,37},{6,38},{7,39},{8,40},{9,... | collective-permute-start | bytes 1474568 | tf_op jit(solution)/shard_map/ppermute | solution.py:74
  131.2 8.9 %collective-permute-start.27 = (bf16[320,768]{1,0:T(8,128)(2,1)S(1)}, bf16[320,768]{1,0:T(8,128)(2,1)S(1)}, u32[]{:S(2)}, u32[]{:S(2)}) collective-permute-start(bf16[320,768]{1,0:T(8,128)(2,1)S(1)} %get-tuple-element.35), channel_id=1, source_target_pairs={{0,1},{1,0},{2,3},{3,2},{4,5},{5,4},{6,7},{7,6},{8,9},{9,8},{10,11... | collective-permute-start | bytes 1474568 | tf_op jit(solution)/shard_map/ppermute | solution.py:74
  140.4 1.9 %collective-permute-start.28 = (f32[160,768]{1,0:T(8,128)S(1)}, f32[160,768]{1,0:T(8,128)S(1)}, u32[]{:S(2)}, u32[]{:S(2)}) collective-permute-start(f32[160,768]{1,0:T(8,128)S(1)} %slice.9), channel_id=1, source_target_pairs={{0,16},{1,17},{2,18},{3,19},{4,20},{5,21},{6,22},{7,23},{8,24},{9,... | collective-permute-start | bytes 1474568 | tf_op jit(solution)/shard_map/ppermute | solution.py:78

commit v4 on v3

--- a/solution.py
+++ b/solution.py
@@ -13,7 +13,7 @@
 ORDER = (0, 1, 2, 4, 3, 5, 6, 7)
 PLACE = tuple(ORDER.index(m) for m in range(8))
 LOG2E = 1.4426950408889634
-VMEM_LIMIT = 20 * 1024 * 1024
+VMEM_LIMIT = 12 * 1024 * 1024
 RANGE = 60.0
 
 
@@ -253,6 +253,7 @@
         in_specs=[pl.BlockSpec(memory_space=pltpu.SMEM), pl.BlockSpec(memory_space=pltpu.VMEM)],
         out_specs=pl.BlockSpec(memory_space=pltpu.VMEM),
         out_shape=jax.ShapeDtypeStruct(got.shape[1:], jnp.float32),
+        compiler_params=pltpu.CompilerParams(vmem_limit_bytes=2 * 1024 * 1024),
         name="merge",
     )(place, got)
 
@@ -441,15 +442,21 @@
         (lax.axis_index("x") & 1) | ((lax.axis_index("y") & 1) << 1) | ((lax.axis_index("z") & 1) << 2)
     ).astype(jnp.int32).reshape(1)
 
-    mine = jnp.where(first, images, texts)
-    other = swap(jnp.where(first, texts, images))
-    own = jnp.concatenate([mine, other], axis=0)
-    blocks = {0: own, 1: to_cube(own, 1), 2: to_cube(own, 2), 4: to_cube(own, 4), 7: to_cube(own, 7)}
-    blocks[5] = to_cube(blocks[1], 4)
-    blocks[3] = to_cube(blocks[2], 1)
-    blocks[6] = to_cube(blocks[4], 2)
+    theirs = swap(jnp.concatenate([images, texts], axis=0))
+    joined = lambda lead, follow: jnp.concatenate([lead, follow], axis=0)
+    own = jnp.where(first, joined(images, theirs[:rows]), joined(texts, theirs[rows:]))
+    other = jnp.where(first, joined(theirs[rows:], texts), joined(theirs[:rows], images))
+    near = {m: to_cube(own, m) for m in (1, 2, 4)}
+    far = {7: to_cube(own, 7), 5: to_cube(near[1], 4), 3: to_cube(near[2], 1), 6: to_cube(near[4], 2)}
+    blocks = {0: own, **near, **far}
+    held = lax.optimization_barrier(tuple(blocks[m] for m in (1, 2, 4, 7)))
+    swapped = {0: other}
+    for m, a in zip((1, 2, 4, 7), held):
+        swapped[m] = swap(a)
+    for m in (5, 3, 6):
+        swapped[m] = swap(blocks[m])
     a_blocks = [blocks[m] for m in ORDER]
-    b_blocks = [swap(a) for a in a_blocks]
+    b_blocks = [swapped[m] for m in ORDER]
 
     e, a_stat, b_stat, flags = scores_call(core_arr, a_blocks, b_blocks, scale)
     chip_stat = jnp.logaddexp2(a_stat, swap(b_stat))

time: 144 us -> 144 us (level)
  starting transfers between devices: 33.6 us -> 44.5 us
  waiting for transfers between devices: 41.6 us -> 31.9 us
  other arithmetic: 2.45 us -> 3.99 us
  Pallas kernels: 49.1 us -> 47.6 us
    ppermute x14, waiting for transfers between devices: 25.8 us -> 16 us  [to_cube(): return lax.ppermute(a, AXES, across(m))]
    ppermute x14, starting transfers between devices: 24.5 us -> 32.5 us  [to_cube(): return lax.ppermute(a, AXES, across(m))]
    all_to_all x1, starting transfers between devices: 5.48 us -> 8.07 us  [body(): lax.all_to_all(jnp.broadcast_to(chip_stat[None], (8,) + chip_stat.shape),...]
    pallas_call x1, Pallas kernels: 1.55 us -> 0.07 us  [merge_call(): pl.pallas_call(merge_kernel, in_specs=[pl.BlockSpec(memory_space=pltpu.SM...]
    unnamed x48 -> x44, local copies, waits for them, and re-layouts: 15 us -> 13.7 us
    ppermute x15 -> x14, starting transfers between devices: 3.63 us -> 3.9 us  [swap(): return lax.ppermute(a, AXES, SWAP)]
    ppermute x15 -> x14, waiting for transfers between devices: 7.24 us -> 7.37 us  [swap(): return lax.ppermute(a, AXES, SWAP)]
  transfers between devices with their start and end apart: 30 -> 29, of which waited for: 15 -> 14; matrix products, arithmetic and copies ran while one was open for 0% -> 0% of each run, Pallas kernels for 10% -> 10%
where the time goes in v4:
time: 144 us; the launch traced here: 143 us
  Pallas kernels  47.6 us (33%)
  starting transfers between devices  44.5 us (31%)
  waiting for transfers between devices  31.9 us (22%)
  local copies, waits for them, and re-layouts  14.4 us (10%)
  other arithmetic  3.99 us (3%)
    ppermute x14, starting transfers between devices, to_cube(): return lax.ppermute(a, AXES, across(m))  32.5 us
    pallas_call x1, Pallas kernels, scores_call(): pl.pallas_call(functools.partial(scores_kernel, scale), in_specs=[smem_sp...  24.2 us
    ppermute x14, waiting for transfers between devices, to_cube(): return lax.ppermute(a, AXES, across(m))  16 us
    unnamed x44, local copies, waits for them, and re-layouts  13.7 us
    pallas_call x1, Pallas kernels, middle_call(): pl.pallas_call(middle_kernel, in_specs=[smem_spec(), vmem_spec()] + [any_...  9.98 us
    all_to_all x1, waiting for transfers between devices, body(): lax.all_to_all(jnp.broadcast_to(chip_stat[None], (8,) + chip_stat.shape),...  8.58 us
    pallas_call x1, Pallas kernels, weights_call(): pl.pallas_call(weights_kernel, in_specs=[smem_spec()] * 2 + [vmem_spec()]...  8.53 us
    all_to_all x1, starting transfers between devices, body(): lax.all_to_all(jnp.broadcast_to(chip_stat[None], (8,) + chip_stat.shape),...  8.07 us
  transfers between devices with their start and end apart: 29, of which 14 were waited for; matrix products, arithmetic and copies ran while one was open for 0% of the time, Pallas kernels for 10%

profile of v4, /device:TPU:1, one launch (start us, length us, event | category | flops | bytes accessed | tf_op | source)
XLA Modules:
  0.0 143.3 jit_solution(12624244145851390084)
XLA Ops:
  0.6 1.1 pad_maximum_fusion.1
  1.7 1.5 %collective-permute-start = (bf16[320,768]{1,0:T(8,128)(2,1)S(1)}, bf16[320,768]{1,0:T(8,128)(2,1)S(1)}, u32[]{:S(2)}, u32[]{:S(2)}) collective-permute-start(bf16[320,768]{1,0:T(8,128)(2,1)S(1)} %pad_maximum_fusion.1), channel_id=1, source_target_pairs={{0,16},{1,17},{2,18},{3,19},{4,20},{5,21},{6,22},{7,23},{8,24},{9,... | collective-permute-start | bytes 1474568 | tf_op jit(solution)/shard_map/ppermute | solution.py:78
  3.2 1.5 %collective-permute-done = bf16[320,768]{1,0:T(8,128)(2,1)S(1)} collective-permute-done((bf16[320,768]{1,0:T(8,128)(2,1)S(1)}, bf16[320,768]{1,0:T(8,128)(2,1)S(1)}, u32[]{:S(2)}, u32[]{:S(2)}) %collective-permute-start) | collective-permute-done | bytes 491552 | tf_op jit(solution)/shard_map/ppermute | solution.py:78
  4.8 1.5 %fusion.1 = (bf16[320,768]{1,0:T(8,128)(2,1)S(1)}, bf16[320,768]{1,0:T(8,128)(2,1)S(1)}) fusion(bf16[160,768]{1,0:T(8,128)(2,1)} %param.3, bf16[160,768]{1,0:T(8,128)(2,1)S(1)} %get-tuple-element.48, bf16[160,768]{1,0:T(8,128)(2,1)} %param.2, bf16[160,768]{1,0:T(8,128)(2,1)S(1)} %get-tuple-element.49, pred[]{:T(512)S(6)} %eq.3), kind=kLoop, calls=%fused_computation.5 | loop fusion | flops 4423680 | bytes 1966081 | tf_op jit(solution)/shard_map/jit(_where)/select_n | solution.py:448
  6.3 3.9 %collective-permute-start.3 = (bf16[320,768]{1,0:T(8,128)(2,1)S(1)}, bf16[320,768]{1,0:T(8,128)(2,1)S(1)}, u32[]{:S(2)}, u32[]{:S(2)}) collective-permute-start(bf16[320,768]{1,0:T(8,128)(2,1)S(1)} %get-tuple-element.47.refs_0_), channel_id=1, source_target_pairs={{0,1},{1,0},{2,3},{3,2},{4,5},{5,4},{6,7},{7,6},{8,9},{9,8},{10,11... | collective-permute-start | bytes 1474568 | tf_op jit(solution)/shard_map/ppermute | solution.py:74
  10.2 2.7 %collective-permute-start.2 = (bf16[320,768]{1,0:T(8,128)(2,1)S(1)}, bf16[320,768]{1,0:T(8,128)(2,1)S(1)}, u32[]{:S(2)}, u32[]{:S(2)}) collective-permute-start(bf16[320,768]{1,0:T(8,128)(2,1)S(1)} %get-tuple-element.47.refs_0_), channel_id=1, source_target_pairs={{0,32},{1,33},{2,34},{3,35},{4,36},{5,37},{6,38},{7,39},{8,40},{9,... | collective-permute-start | bytes 1474568 | tf_op jit(solution)/shard_map/ppermute | solution.py:74
  13.0 2.1 %collective-permute-start.7 = (bf16[320,768]{1,0:T(8,128)(2,1)S(1)}, bf16[320,768]{1,0:T(8,128)(2,1)S(1)}, u32[]{:S(2)}, u32[]{:S(2)}) collective-permute-start(bf16[320,768]{1,0:T(8,128)(2,1)S(1)} %get-tuple-element.47.refs_0_), channel_id=1, source_target_pairs={{0,37},{1,36},{2,39},{3,38},{4,33},{5,32},{6,35},{7,34},{8,45},{9,... | collective-permute-start | bytes 1474568 | tf_op jit(solution)/shard_map/ppermute | solution.py:74
  15.1 0.4 collective-permute-start.1
  15.4 1.3 collective-permute-done.3.refs_3_
  16.7 7.3 %collective-permute-start.6 = (bf16[320,768]{1,0:T(8,128)(2,1)S(1)}, bf16[320,768]{1,0:T(8,128)(2,1)S(1)}, u32[]{:S(2)}, u32[]{:S(2)}) collective-permute-start(bf16[320,768]{1,0:T(8,128)(2,1)S(1)} %collective-permute-done.3.refs_3_), channel_id=1, source_target_pairs={{0,32},{1,33},{2,34},{3,35},{4,36},{5,37},{6,38},{7,39},{8,40},{9,... | collective-permute-start | bytes 1474568 | tf_op jit(solution)/shard_map/ppermute | solution.py:74
  24.0 0.4 collective-permute-done.2.refs_2_
  24.4 2.5 %collective-permute-start.4 = (bf16[320,768]{1,0:T(8,128)(2,1)S(1)}, bf16[320,768]{1,0:T(8,128)(2,1)S(1)}, u32[]{:S(2)}, u32[]{:S(2)}) collective-permute-start(bf16[320,768]{1,0:T(8,128)(2,1)S(1)} %collective-permute-done.2.refs_2_), channel_id=1, source_target_pairs={{0,4},{1,5},{2,6},{3,7},{4,0},{5,1},{6,2},{7,3},{8,12},{9,13},{10,... | collective-permute-start | bytes 1474568 | tf_op jit(solution)/shard_map/ppermute | solution.py:74
  26.9 0.0 collective-permute-done.7.refs_7_
  26.9 0.0 collective-permute-done.1.refs_1_
  27.0 0.1 collective-permute-start.8
  27.0 0.5 collective-permute-start.9
  27.5 2.7 %collective-permute-start.5 = (bf16[320,768]{1,0:T(8,128)(2,1)S(1)}, bf16[320,768]{1,0:T(8,128)(2,1)S(1)}, u32[]{:S(2)}, u32[]{:S(2)}) collective-permute-start(bf16[320,768]{1,0:T(8,128)(2,1)S(1)} %collective-permute-done.1.refs_1_), channel_id=1, source_target_pairs={{0,1},{1,0},{2,3},{3,2},{4,5},{5,4},{6,7},{7,6},{8,9},{9,8},{10,11... | collective-permute-start | bytes 1474568 | tf_op jit(solution)/shard_map/ppermute | solution.py:74
  30.2 0.0 collective-permute-done.6.refs_6_
  30.2 3.1 %collective-permute-done.4.refs_4_ = bf16[320,768]{1,0:T(8,128)(2,1)S(1)} collective-permute-done((bf16[320,768]{1,0:T(8,128)(2,1)S(1)}, bf16[320,768]{1,0:T(8,128)(2,1)S(1)}, u32[]{:S(2)}, u32[]{:S(2)}) %collective-permute-start.4) | collective-permute-done | bytes 491552 | tf_op jit(solution)/shard_map/ppermute | solution.py:74
  33.3 0.5 collective-permute-start.13
  33.9 0.1 collective-permute-start.11
  33.9 2.5 %collective-permute-done.5.refs_5_ = bf16[320,768]{1,0:T(8,128)(2,1)S(1)} collective-permute-done((bf16[320,768]{1,0:T(8,128)(2,1)S(1)}, bf16[320,768]{1,0:T(8,128)(2,1)S(1)}, u32[]{:S(2)}, u32[]{:S(2)}) %collective-permute-start.5) | collective-permute-done | bytes 491552 | tf_op jit(solution)/shard_map/ppermute | solution.py:74
  36.4 0.0 collective-permute-start.12
  36.5 0.1 collective-permute-done.11.refs_12_.refs_4_
  36.6 1.7 %collective-permute-done.12.refs_13_.refs_5_ = bf16[320,768]{1,0:T(8,128)(2,1)S(1)} collective-permute-done((bf16[320,768]{1,0:T(8,128)(2,1)S(1)}, bf16[320,768]{1,0:T(8,128)(2,1)S(1)}, u32[]{:S(2)}, u32[]{:S(2)}) %collective-permute-start.12) | collective-permute-done | bytes 491552 | tf_op jit(solution)/shard_map/ppermute | solution.py:78
  38.3 24.2 %scores.1 = (f32[2,1280,1280]{2,1,0:T(8,128)S(1)}, f32[8,320]{1,0:T(8,128)S(1)}, f32[8,320]{1,0:T(8,128)S(1)}, s32[2]{0:T(128)S(1)}) custom-call(s32[1]{0:T(128)} %bitcast.core_ref, bf16[320,768]{1,0:T(8,128)(2,1)S(1)} %get-tuple-element.47.refs_0_, bf16[320,768]{1,0:T(8,128)(2,1)S(1)} %collective-permute-done.1.refs_1_, ...), custom_call_target="tpu_custom_call" | custom-call | flops 5033164800 | tf_op jit(solution)/shard_map/scores/pallas_call | solution.py:212
  62.6 4.7 %copy-done = f32[2,1280,1280]{2,1,0:T(8,128)} copy-done((f32[2,1280,1280]{2,1,0:T(8,128)}, f32[2,1280,1280]{2,1,0:T(8,128)S(1)}, u32[]{:S(2)}) %copy-start) | copy-done | bytes 13107224
  67.3 0.1 collective-permute-start.15
  67.4 1.1 collective-permute-done.15
  68.5 0.6 broadcast_in_dim.2
  69.1 8.1 %all-to-all-start = ((f32[8,8,320]{2,1,0:T(8,128)}), f32[8,8,320]{2,1,0:T(8,128)S(1)}, u32[]{:S(2)}, u32[]{:S(2)}) async-start(f32[8,8,320]{2,1,0:T(8,128)} %broadcast_in_dim.2), calls=%async_computation | async-start | bytes 196608 | tf_op jit(solution)/shard_map/all_to_all | solution.py:463
  77.2 8.6 %all-to-all-done.got_ref = f32[8,8,320]{2,1,0:T(8,128)S(1)} async-done(((f32[8,8,320]{2,1,0:T(8,128)}), f32[8,8,320]{2,1,0:T(8,128)S(1)}, u32[]{:S(2)}, u32[]{:S(2)}) %all-to-all-start) | async-done | bytes 81952 | tf_op jit(solution)/shard_map/all_to_all | solution.py:463
  85.8 0.1 merge.1.a_lse
  85.9 0.1 collective-permute-start.16
  86.0 1.2 collective-permute-done.16.b_lse
  87.1 4.7 %copy-done.1 = f32[2,1280,1280]{2,1,0:T(8,128)S(1)} copy-done((f32[2,1280,1280]{2,1,0:T(8,128)S(1)}, f32[2,1280,1280]{2,1,0:T(8,128)}, u32[]{:S(2)}) %copy-start.1) | copy-done | bytes 13107224
  91.9 1.0 copy-done.5
  92.9 1.0 copy-done.9
  93.9 1.0 copy-done.13
  95.0 1.0 copy-done.19
  96.0 8.5 %weights.1 = (bf16[2,1280,1280]{2,1,0:T(8,128)(2,1)S(1)}, bf16[1280,768]{1,0:T(8,128)(2,1)S(1)}) custom-call(s32[1]{0:T(128)} %bitcast.core_ref, s32[2]{0:T(128)S(1)} %get-tuple-element.27.flags, f32[2,1280,1280]{2,1,0:T(8,128)S(1)} %copy-done.1, f32[8,320]{1,0:T(8,128)S(1)} %merge.1.a_lse, f32[8,320]{1,0:T(8,128)S(1)} %collective-permute-done.16.b_lse, ...), custom_call_target="tpu_custom_call" | custom-call | flops 2516582400 | bytes 19660800 | tf_op jit(solution)/shard_map/weights/pallas_call | solution.py:319
  104.5 0.2 collective-permute-start.19
  104.8 10.0 %middle.1 = (f32[1280,768]{1,0:T(8,128)S(1)}, f32[320,768]{1,0:T(8,128)S(1)}, bf16[960,768]{1,0:T(8,128)(2,1)S(1)}) custom-call(s32[1]{0:T(128)} %bitcast.core_ref, bf16[2,1280,1280]{2,1,0:T(8,128)(2,1)S(1)} %get-tuple-element.31.w_ref, bf16[320,768]{1,0:T(8,128)(2,1)S(1)} %get-tuple-element.47.refs_0_, bf16[320,768]{1,0:T(8,128)(2,1)S(1)} %copy-done.5, ...), custom_call_target="tpu_custom_call" | custom-call | flops 5033164800 | tf_op jit(solution)/shard_map/middle/pallas_call | solution.py:352
  114.8 0.6 collective-permute-start.18
  115.4 0.1 collective-permute-start.17
  115.5 0.3 far.1
  115.8 0.4 collective-permute-start.20
  116.2 0.3 collective-permute-start.21
  116.5 0.3 collective-permute-start.22
  116.7 4.0 %last.1.ga_lo = f32[1280,768]{1,0:T(8,128)S(1)} custom-call(s32[1]{0:T(128)} %bitcast.core_ref, bf16[2,1280,1280]{2,1,0:T(8,128)(2,1)S(1)} %get-tuple-element.31.w_ref, bf16[320,768]{1,0:T(8,128)(2,1)S(1)} %get-tuple-element.46.refs_8_.refs_0_, bf16[320,768]{1,0:T(8,128)(2,1)S(1)} %collective-permute-done.8.refs_9_.refs_1_, ...), custom_call_target="tpu_custom_call" | custom-call | flops 2516582400 | tf_op jit(solution)/shard_map/last/pallas_call | solution.py:399
  120.8 6.7 %collective-permute-start.23 = (bf16[320,768]{1,0:T(8,128)(2,1)S(1)}, bf16[320,768]{1,0:T(8,128)(2,1)S(1)}, u32[]{:S(2)}, u32[]{:S(2)}) collective-permute-start(bf16[320,768]{1,0:T(8,128)(2,1)S(1)} %get-tuple-element.40), channel_id=1, source_target_pairs={{0,37},{1,36},{2,39},{3,38},{4,33},{5,32},{6,35},{7,34},{8,45},{9,... | collective-permute-start | bytes 1474568 | tf_op jit(solution)/shard_map/ppermute | solution.py:74
  127.5 0.5 near.1
  128.0 0.0 copy-start.20
  128.0 0.0 copy-start.21
  128.0 0.5 collective-permute-start.24
  128.5 2.5 %collective-permute-start.25 = (bf16[320,768]{1,0:T(8,128)(2,1)S(1)}, bf16[320,768]{1,0:T(8,128)(2,1)S(1)}, u32[]{:S(2)}, u32[]{:S(2)}) collective-permute-start(bf16[320,768]{1,0:T(8,128)(2,1)S(1)} %get-tuple-element.42), channel_id=1, source_target_pairs={{0,32},{1,33},{2,34},{3,35},{4,36},{5,37},{6,38},{7,39},{8,40},{9,... | collective-permute-start | bytes 1474568 | tf_op jit(solution)/shard_map/ppermute | solution.py:74
  131.1 0.3 collective-permute-start.26
  131.4 2.7 %collective-permute-done.23 = bf16[320,768]{1,0:T(8,128)(2,1)S(1)} collective-permute-done((bf16[320,768]{1,0:T(8,128)(2,1)S(1)}, bf16[320,768]{1,0:T(8,128)(2,1)S(1)}, u32[]{:S(2)}, u32[]{:S(2)}) %collective-permute-start.23) | collective-permute-done | bytes 491552 | tf_op jit(solution)/shard_map/ppermute | solution.py:74
  134.1 5.2 %collective-permute-done.24 = bf16[320,768]{1,0:T(8,128)(2,1)S(1)} collective-permute-done((bf16[320,768]{1,0:T(8,128)(2,1)S(1)}, bf16[320,768]{1,0:T(8,128)(2,1)S(1)}, u32[]{:S(2)}, u32[]{:S(2)}) %collective-permute-start.24) | collective-permute-done | bytes 491552 | tf_op jit(solution)/shard_map/ppermute | solution.py:74
  139.2 0.7 collective-permute-done.26
  140.0 0.3 convert_add_fusion
  140.3 0.1 collective-permute-start.27
  140.4 1.9 %collective-permute-done.27 = f32[160,768]{1,0:T(8,128)S(1)} collective-permute-done((f32[160,768]{1,0:T(8,128)S(1)}, f32[160,768]{1,0:T(8,128)S(1)}, u32[]{:S(2)}, u32[]{:S(2)}) %collective-permute-start.27) | collective-permute-done | bytes 491552 | tf_op jit(solution)/shard_map/ppermute | solution.py:78
  142.2 1.0 convert_subtract_fusion
  (53 shorter events, 0.2 us)
Async XLA Ops:
  1.7 3.0 %collective-permute-start = (bf16[320,768]{1,0:T(8,128)(2,1)S(1)}, bf16[320,768]{1,0:T(8,128)(2,1)S(1)}, u32[]{:S(2)}, u32[]{:S(2)}) collective-permute-start(bf16[320,768]{1,0:T(8,128)(2,1)S(1)} %pad_maximum_fusion.1), channel_id=1, source_target_pairs={{0,16},{1,17},{2,18},{3,19},{4,20},{5,21},{6,22},{7,23},{8,24},{9,... | collective-permute-start | bytes 1474568 | tf_op jit(solution)/shard_map/ppermute | solution.py:78
  6.3 10.4 %collective-permute-start.3 = (bf16[320,768]{1,0:T(8,128)(2,1)S(1)}, bf16[320,768]{1,0:T(8,128)(2,1)S(1)}, u32[]{:S(2)}, u32[]{:S(2)}) collective-permute-start(bf16[320,768]{1,0:T(8,128)(2,1)S(1)} %get-tuple-element.47.refs_0_), channel_id=1, source_target_pairs={{0,1},{1,0},{2,3},{3,2},{4,5},{5,4},{6,7},{7,6},{8,9},{9,8},{10,11... | collective-permute-start | bytes 1474568 | tf_op jit(solution)/shard_map/ppermute | solution.py:74
  10.2 14.2 %collective-permute-start.2 = (bf16[320,768]{1,0:T(8,128)(2,1)S(1)}, bf16[320,768]{1,0:T(8,128)(2,1)S(1)}, u32[]{:S(2)}, u32[]{:S(2)}) collective-permute-start(bf16[320,768]{1,0:T(8,128)(2,1)S(1)} %get-tuple-element.47.refs_0_), channel_id=1, source_target_pairs={{0,32},{1,33},{2,34},{3,35},{4,36},{5,37},{6,38},{7,39},{8,40},{9,... | collective-permute-start | bytes 1474568 | tf_op jit(solution)/shard_map/ppermute | solution.py:74
  13.0 14.0 %collective-permute-start.7 = (bf16[320,768]{1,0:T(8,128)(2,1)S(1)}, bf16[320,768]{1,0:T(8,128)(2,1)S(1)}, u32[]{:S(2)}, u32[]{:S(2)}) collective-permute-start(bf16[320,768]{1,0:T(8,128)(2,1)S(1)} %get-tuple-element.47.refs_0_), channel_id=1, source_target_pairs={{0,37},{1,36},{2,39},{3,38},{4,33},{5,32},{6,35},{7,34},{8,45},{9,... | collective-permute-start | bytes 1474568 | tf_op jit(solution)/shard_map/ppermute | solution.py:74
  15.1 11.9 %collective-permute-start.1 = (bf16[320,768]{1,0:T(8,128)(2,1)S(1)}, bf16[320,768]{1,0:T(8,128)(2,1)S(1)}, u32[]{:S(2)}, u32[]{:S(2)}) collective-permute-start(bf16[320,768]{1,0:T(8,128)(2,1)S(1)} %get-tuple-element.47.refs_0_), channel_id=1, source_target_pairs={{0,4},{1,5},{2,6},{3,7},{4,0},{5,1},{6,2},{7,3},{8,12},{9,13},{10,... | collective-permute-start | bytes 1474568 | tf_op jit(solution)/shard_map/ppermute | solution.py:74
  16.7 13.5 %collective-permute-start.6 = (bf16[320,768]{1,0:T(8,128)(2,1)S(1)}, bf16[320,768]{1,0:T(8,128)(2,1)S(1)}, u32[]{:S(2)}, u32[]{:S(2)}) collective-permute-start(bf16[320,768]{1,0:T(8,128)(2,1)S(1)} %collective-permute-done.3.refs_3_), channel_id=1, source_target_pairs={{0,32},{1,33},{2,34},{3,35},{4,36},{5,37},{6,38},{7,39},{8,40},{9,... | collective-permute-start | bytes 1474568 | tf_op jit(solution)/shard_map/ppermute | solution.py:74
  24.4 8.9 %collective-permute-start.4 = (bf16[320,768]{1,0:T(8,128)(2,1)S(1)}, bf16[320,768]{1,0:T(8,128)(2,1)S(1)}, u32[]{:S(2)}, u32[]{:S(2)}) collective-permute-start(bf16[320,768]{1,0:T(8,128)(2,1)S(1)} %collective-permute-done.2.refs_2_), channel_id=1, source_target_pairs={{0,4},{1,5},{2,6},{3,7},{4,0},{5,1},{6,2},{7,3},{8,12},{9,13},{10,... | collective-permute-start | bytes 1474568 | tf_op jit(solution)/shard_map/ppermute | solution.py:74
  27.0 35.5 %copy-start.4 = (bf16[320,768]{1,0:T(8,128)(2,1)}, bf16[320,768]{1,0:T(8,128)(2,1)S(1)}, u32[]{:S(2)}) copy-start(bf16[320,768]{1,0:T(8,128)(2,1)S(1)} %collective-permute-done.1.refs_1_) | copy-start | bytes 1474564
  27.0 6.4 %collective-permute-start.8 = (bf16[320,768]{1,0:T(8,128)(2,1)S(1)}, bf16[320,768]{1,0:T(8,128)(2,1)S(1)}, u32[]{:S(2)}, u32[]{:S(2)}) collective-permute-start(bf16[320,768]{1,0:T(8,128)(2,1)S(1)} %collective-permute-done.1.refs_1_), channel_id=1, source_target_pairs={{0,16},{1,17},{2,18},{3,19},{4,20},{5,21},{6,22},{7,23},{8,24},{9,... | collective-permute-start | bytes 1474568 | tf_op jit(solution)/shard_map/ppermute | solution.py:78
  27.0 6.8 %collective-permute-start.9 = (bf16[320,768]{1,0:T(8,128)(2,1)S(1)}, bf16[320,768]{1,0:T(8,128)(2,1)S(1)}, u32[]{:S(2)}, u32[]{:S(2)}) collective-permute-start(bf16[320,768]{1,0:T(8,128)(2,1)S(1)} %collective-permute-done.2.refs_2_), channel_id=1, source_target_pairs={{0,16},{1,17},{2,18},{3,19},{4,20},{5,21},{6,22},{7,23},{8,24},{9,... | collective-permute-start | bytes 1474568 | tf_op jit(solution)/shard_map/ppermute | solution.py:78
  27.5 8.9 %collective-permute-start.5 = (bf16[320,768]{1,0:T(8,128)(2,1)S(1)}, bf16[320,768]{1,0:T(8,128)(2,1)S(1)}, u32[]{:S(2)}, u32[]{:S(2)}) collective-permute-start(bf16[320,768]{1,0:T(8,128)(2,1)S(1)} %collective-permute-done.1.refs_1_), channel_id=1, source_target_pairs={{0,1},{1,0},{2,3},{3,2},{4,5},{5,4},{6,7},{7,6},{8,9},{9,8},{10,11... | collective-permute-start | bytes 1474568 | tf_op jit(solution)/shard_map/ppermute | solution.py:74
  30.2 32.3 %copy-start.8 = (bf16[320,768]{1,0:T(8,128)(2,1)}, bf16[320,768]{1,0:T(8,128)(2,1)S(1)}, u32[]{:S(2)}) copy-start(bf16[320,768]{1,0:T(8,128)(2,1)S(1)} %collective-permute-done.6.refs_6_) | copy-start | bytes 1474564
  30.2 6.2 %collective-permute-start.10 = (bf16[320,768]{1,0:T(8,128)(2,1)S(1)}, bf16[320,768]{1,0:T(8,128)(2,1)S(1)}, u32[]{:S(2)}, u32[]{:S(2)}) collective-permute-start(bf16[320,768]{1,0:T(8,128)(2,1)S(1)} %collective-permute-done.3.refs_3_), channel_id=1, source_target_pairs={{0,16},{1,17},{2,18},{3,19},{4,20},{5,21},{6,22},{7,23},{8,24},{9,... | collective-permute-start | bytes 1474568 | tf_op jit(solution)/shard_map/ppermute | solution.py:78
  33.3 29.1 %copy-start.12 = (bf16[320,768]{1,0:T(8,128)(2,1)}, bf16[320,768]{1,0:T(8,128)(2,1)S(1)}, u32[]{:S(2)}) copy-start(bf16[320,768]{1,0:T(8,128)(2,1)S(1)} %collective-permute-done.4.refs_4_) | copy-start | bytes 1474564
  33.3 3.1 %collective-permute-start.14 = (bf16[320,768]{1,0:T(8,128)(2,1)S(1)}, bf16[320,768]{1,0:T(8,128)(2,1)S(1)}, u32[]{:S(2)}, u32[]{:S(2)}) collective-permute-start(bf16[320,768]{1,0:T(8,128)(2,1)S(1)} %collective-permute-done.7.refs_7_), channel_id=1, source_target_pairs={{0,16},{1,17},{2,18},{3,19},{4,20},{5,21},{6,22},{7,23},{8,24},{9,... | collective-permute-start | bytes 1474568 | tf_op jit(solution)/shard_map/ppermute | solution.py:78
  33.3 3.1 %collective-permute-start.13 = (bf16[320,768]{1,0:T(8,128)(2,1)S(1)}, bf16[320,768]{1,0:T(8,128)(2,1)S(1)}, u32[]{:S(2)}, u32[]{:S(2)}) collective-permute-start(bf16[320,768]{1,0:T(8,128)(2,1)S(1)} %collective-permute-done.6.refs_6_), channel_id=1, source_target_pairs={{0,16},{1,17},{2,18},{3,19},{4,20},{5,21},{6,22},{7,23},{8,24},{9,... | collective-permute-start | bytes 1474568 | tf_op jit(solution)/shard_map/ppermute | solution.py:78
  33.9 2.8 %collective-permute-start.11 = (bf16[320,768]{1,0:T(8,128)(2,1)S(1)}, bf16[320,768]{1,0:T(8,128)(2,1)S(1)}, u32[]{:S(2)}, u32[]{:S(2)}) collective-permute-start(bf16[320,768]{1,0:T(8,128)(2,1)S(1)} %collective-permute-done.4.refs_4_), channel_id=1, source_target_pairs={{0,16},{1,17},{2,18},{3,19},{4,20},{5,21},{6,22},{7,23},{8,24},{9,... | collective-permute-start | bytes 1474568 | tf_op jit(solution)/shard_map/ppermute | solution.py:78
  36.4 26.1 %copy-start.18 = (bf16[320,768]{1,0:T(8,128)(2,1)}, bf16[320,768]{1,0:T(8,128)(2,1)S(1)}, u32[]{:S(2)}) copy-start(bf16[320,768]{1,0:T(8,128)(2,1)S(1)} %collective-permute-done.5.refs_5_) | copy-start | bytes 1474564
  36.4 1.9 %collective-permute-start.12 = (bf16[320,768]{1,0:T(8,128)(2,1)S(1)}, bf16[320,768]{1,0:T(8,128)(2,1)S(1)}, u32[]{:S(2)}, u32[]{:S(2)}) collective-permute-start(bf16[320,768]{1,0:T(8,128)(2,1)S(1)} %collective-permute-done.5.refs_5_), channel_id=1, source_target_pairs={{0,16},{1,17},{2,18},{3,19},{4,20},{5,21},{6,22},{7,23},{8,24},{9,... | collective-permute-start | bytes 1474568 | tf_op jit(solution)/shard_map/ppermute | solution.py:78
  36.5 26.0 %copy-start.2 = (bf16[320,768]{1,0:T(8,128)(2,1)}, bf16[320,768]{1,0:T(8,128)(2,1)S(1)}, u32[]{:S(2)}) copy-start(bf16[320,768]{1,0:T(8,128)(2,1)S(1)} %collective-permute-done.10.refs_11_.refs_3_) | copy-start | bytes 1474564
  36.5 26.1 %copy-start.6 = (bf16[320,768]{1,0:T(8,128)(2,1)}, bf16[320,768]{1,0:T(8,128)(2,1)S(1)}, u32[]{:S(2)}) copy-start(bf16[320,768]{1,0:T(8,128)(2,1)S(1)} %collective-permute-done.14.refs_15_.refs_7_) | copy-start | bytes 1474564
  36.5 26.0 %copy-start.10 = (bf16[320,768]{1,0:T(8,128)(2,1)}, bf16[320,768]{1,0:T(8,128)(2,1)S(1)}, u32[]{:S(2)}) copy-start(bf16[320,768]{1,0:T(8,128)(2,1)S(1)} %collective-permute-done.13.refs_14_.refs_6_) | copy-start | bytes 1474564
  36.6 25.9 %copy-start.14 = (bf16[320,768]{1,0:T(8,128)(2,1)}, bf16[320,768]{1,0:T(8,128)(2,1)S(1)}, u32[]{:S(2)}) copy-start(bf16[320,768]{1,0:T(8,128)(2,1)S(1)} %collective-permute-done.11.refs_12_.refs_4_) | copy-start | bytes 1474564
  38.3 24.3 %copy-start.16 = (bf16[320,768]{1,0:T(8,128)(2,1)}, bf16[320,768]{1,0:T(8,128)(2,1)S(1)}, u32[]{:S(2)}) copy-start(bf16[320,768]{1,0:T(8,128)(2,1)S(1)} %collective-permute-done.12.refs_13_.refs_5_) | copy-start | bytes 1474564
  62.6 4.8 %copy-start = (f32[2,1280,1280]{2,1,0:T(8,128)}, f32[2,1280,1280]{2,1,0:T(8,128)S(1)}, u32[]{:S(2)}) copy-start(f32[2,1280,1280]{2,1,0:T(8,128)S(1)} %get-tuple-element.28.e_ref) | copy-start | bytes 39321604
  67.3 1.2 collective-permute-start.15
  69.1 16.6 %all-to-all-start = ((f32[8,8,320]{2,1,0:T(8,128)}), f32[8,8,320]{2,1,0:T(8,128)S(1)}, u32[]{:S(2)}, u32[]{:S(2)}) async-start(f32[8,8,320]{2,1,0:T(8,128)} %broadcast_in_dim.2), calls=%async_computation | async-start | bytes 196608 | tf_op jit(solution)/shard_map/all_to_all | solution.py:463
  85.9 1.3 collective-permute-start.16
  87.1 4.7 %copy-start.1 = (f32[2,1280,1280]{2,1,0:T(8,128)S(1)}, f32[2,1280,1280]{2,1,0:T(8,128)}, u32[]{:S(2)}) copy-start(f32[2,1280,1280]{2,1,0:T(8,128)} %copy-done) | copy-start | bytes 39321604
  91.9 1.0 copy-start.5
  92.9 1.0 copy-start.9
  93.9 1.0 copy-start.13
  94.9 1.0 copy-start.19
  96.0 8.8 %copy-start.3 = (bf16[320,768]{1,0:T(8,128)(2,1)S(1)}, bf16[320,768]{1,0:T(8,128)(2,1)}, u32[]{:S(2)}) copy-start(bf16[320,768]{1,0:T(8,128)(2,1)} %copy-done.2) | copy-start | bytes 1474564
  96.0 8.8 %copy-start.7 = (bf16[320,768]{1,0:T(8,128)(2,1)S(1)}, bf16[320,768]{1,0:T(8,128)(2,1)}, u32[]{:S(2)}) copy-start(bf16[320,768]{1,0:T(8,128)(2,1)} %copy-done.6) | copy-start | bytes 1474564
  96.0 8.8 %copy-start.11 = (bf16[320,768]{1,0:T(8,128)(2,1)S(1)}, bf16[320,768]{1,0:T(8,128)(2,1)}, u32[]{:S(2)}) copy-start(bf16[320,768]{1,0:T(8,128)(2,1)} %copy-done.10) | copy-start | bytes 1474564
  96.0 8.8 %copy-start.15 = (bf16[320,768]{1,0:T(8,128)(2,1)S(1)}, bf16[320,768]{1,0:T(8,128)(2,1)}, u32[]{:S(2)}) copy-start(bf16[320,768]{1,0:T(8,128)(2,1)} %copy-done.14) | copy-start | bytes 1474564
  96.0 8.8 %copy-start.17 = (bf16[320,768]{1,0:T(8,128)(2,1)S(1)}, bf16[320,768]{1,0:T(8,128)(2,1)}, u32[]{:S(2)}) copy-start(bf16[320,768]{1,0:T(8,128)(2,1)} %copy-done.16) | copy-start | bytes 1474564
  104.5 11.0 %collective-permute-start.19 = (bf16[1280,768]{1,0:T(8,128)(2,1)S(1)}, bf16[1280,768]{1,0:T(8,128)(2,1)S(1)}, u32[]{:S(2)}, u32[]{:S(2)}) collective-permute-start(bf16[1280,768]{1,0:T(8,128)(2,1)S(1)} %get-tuple-element.35), channel_id=1, source_target_pairs={{0,16},{1,17},{2,18},{3,19},{4,20},{5,21},{6,22},{7,23},{8,24},{9,... | collective-permute-start | bytes 5898248 | tf_op jit(solution)/shard_map/ppermute | solution.py:78
  114.8 12.7 %collective-permute-start.18 = (bf16[960,768]{1,0:T(8,128)(2,1)S(1)}, bf16[960,768]{1,0:T(8,128)(2,1)S(1)}, u32[]{:S(2)}, u32[]{:S(2)}) collective-permute-start(bf16[960,768]{1,0:T(8,128)(2,1)S(1)} %get-tuple-element.33), channel_id=1, source_target_pairs={{0,16},{1,17},{2,18},{3,19},{4,20},{5,21},{6,22},{7,23},{8,24},{9,... | collective-permute-start | bytes 4423688 | tf_op jit(solution)/shard_map/ppermute | solution.py:78
  115.4 5.4 %collective-permute-start.17 = (f32[320,768]{1,0:T(8,128)S(1)}, f32[320,768]{1,0:T(8,128)S(1)}, u32[]{:S(2)}, u32[]{:S(2)}) collective-permute-start(f32[320,768]{1,0:T(8,128)S(1)} %get-tuple-element.32), channel_id=1, source_target_pairs={{0,16},{1,17},{2,18},{3,19},{4,20},{5,21},{6,22},{7,23},{8,24},{9,... | collective-permute-start | bytes 2949128 | tf_op jit(solution)/shard_map/ppermute | solution.py:78
  115.8 11.7 %collective-permute-start.20 = (bf16[320,768]{1,0:T(8,128)(2,1)S(1)}, bf16[320,768]{1,0:T(8,128)(2,1)S(1)}, u32[]{:S(2)}, u32[]{:S(2)}) collective-permute-start(bf16[320,768]{1,0:T(8,128)(2,1)S(1)} %get-tuple-element.36), channel_id=1, source_target_pairs={{0,4},{1,5},{2,6},{3,7},{4,0},{5,1},{6,2},{7,3},{8,12},{9,13},{10,... | collective-permute-start | bytes 1474568 | tf_op jit(solution)/shard_map/ppermute | solution.py:74
  116.2 11.3 %collective-permute-start.21 = (bf16[320,768]{1,0:T(8,128)(2,1)S(1)}, bf16[320,768]{1,0:T(8,128)(2,1)S(1)}, u32[]{:S(2)}, u32[]{:S(2)}) collective-permute-start(bf16[320,768]{1,0:T(8,128)(2,1)S(1)} %get-tuple-element.37), channel_id=1, source_target_pairs={{0,32},{1,33},{2,34},{3,35},{4,36},{5,37},{6,38},{7,39},{8,40},{9,... | collective-permute-start | bytes 1474568 | tf_op jit(solution)/shard_map/ppermute | solution.py:74
  116.5 11.0 %collective-permute-start.22 = (bf16[320,768]{1,0:T(8,128)(2,1)S(1)}, bf16[320,768]{1,0:T(8,128)(2,1)S(1)}, u32[]{:S(2)}, u32[]{:S(2)}) collective-permute-start(bf16[320,768]{1,0:T(8,128)(2,1)S(1)} %get-tuple-element.38), channel_id=1, source_target_pairs={{0,1},{1,0},{2,3},{3,2},{4,5},{5,4},{6,7},{7,6},{8,9},{9,8},{10,11... | collective-permute-start | bytes 1474568 | tf_op jit(solution)/shard_map/ppermute | solution.py:74
  120.8 13.3 %collective-permute-start.23 = (bf16[320,768]{1,0:T(8,128)(2,1)S(1)}, bf16[320,768]{1,0:T(8,128)(2,1)S(1)}, u32[]{:S(2)}, u32[]{:S(2)}) collective-permute-start(bf16[320,768]{1,0:T(8,128)(2,1)S(1)} %get-tuple-element.40), channel_id=1, source_target_pairs={{0,37},{1,36},{2,39},{3,38},{4,33},{5,32},{6,35},{7,34},{8,45},{9,... | collective-permute-start | bytes 1474568 | tf_op jit(solution)/shard_map/ppermute | solution.py:74
  128.0 14.2 %copy-start.20 = (bf16[160,768]{1,0:T(8,128)(2,1)S(1)}, bf16[160,768]{1,0:T(8,128)(2,1)}, u32[]{:S(2)}) copy-start(bf16[160,768]{1,0:T(8,128)(2,1)} %param.2) | copy-start | bytes 737284
  128.0 14.2 %copy-start.21 = (bf16[160,768]{1,0:T(8,128)(2,1)S(1)}, bf16[160,768]{1,0:T(8,128)(2,1)}, u32[]{:S(2)}) copy-start(bf16[160,768]{1,0:T(8,128)(2,1)} %param.3) | copy-start | bytes 737284
  128.0 11.2 %collective-permute-start.24 = (bf16[320,768]{1,0:T(8,128)(2,1)S(1)}, bf16[320,768]{1,0:T(8,128)(2,1)S(1)}, u32[]{:S(2)}, u32[]{:S(2)}) collective-permute-start(bf16[320,768]{1,0:T(8,128)(2,1)S(1)} %get-tuple-element.41), channel_id=1, source_target_pairs={{0,4},{1,5},{2,6},{3,7},{4,0},{5,1},{6,2},{7,3},{8,12},{9,13},{10,... | collective-permute-start | bytes 1474568 | tf_op jit(solution)/shard_map/ppermute | solution.py:74
  128.5 10.7 %collective-permute-start.25 = (bf16[320,768]{1,0:T(8,128)(2,1)S(1)}, bf16[320,768]{1,0:T(8,128)(2,1)S(1)}, u32[]{:S(2)}, u32[]{:S(2)}) collective-permute-start(bf16[320,768]{1,0:T(8,128)(2,1)S(1)} %get-tuple-element.42), channel_id=1, source_target_pairs={{0,32},{1,33},{2,34},{3,35},{4,36},{5,37},{6,38},{7,39},{8,40},{9,... | collective-permute-start | bytes 1474568 | tf_op jit(solution)/shard_map/ppermute | solution.py:74
  131.1 8.9 %collective-permute-start.26 = (bf16[320,768]{1,0:T(8,128)(2,1)S(1)}, bf16[320,768]{1,0:T(8,128)(2,1)S(1)}, u32[]{:S(2)}, u32[]{:S(2)}) collective-permute-start(bf16[320,768]{1,0:T(8,128)(2,1)S(1)} %get-tuple-element.43), channel_id=1, source_target_pairs={{0,1},{1,0},{2,3},{3,2},{4,5},{5,4},{6,7},{7,6},{8,9},{9,8},{10,11... | collective-permute-start | bytes 1474568 | tf_op jit(solution)/shard_map/ppermute | solution.py:74
  140.3 1.9 %collective-permute-start.27 = (f32[160,768]{1,0:T(8,128)S(1)}, f32[160,768]{1,0:T(8,128)S(1)}, u32[]{:S(2)}, u32[]{:S(2)}) collective-permute-start(f32[160,768]{1,0:T(8,128)S(1)} %slice.21), channel_id=1, source_target_pairs={{0,16},{1,17},{2,18},{3,19},{4,20},{5,21},{6,22},{7,23},{8,24},{9,... | collective-permute-start | bytes 1474568 | tf_op jit(solution)/shard_map/ppermute | solution.py:78

commit v5 on v4

--- a/solution.py
+++ b/solution.py
@@ -47,27 +47,6 @@
 
 
 SWAP = [(flat(y, c, x, z), flat(y, 1 - c, x, z)) for y, c, x, z in coords()]
-
-
-def cube_groups():
-    groups = []
-    seen = set()
-    for y, c, x, z in coords():
-        members = []
-        for m in range(8):
-            yy = partner(y, c) if m & 2 else y
-            xx = partner(x, c) if m & 1 else x
-            zz = partner(z, c) if m & 4 else z
-            place = (xx & 1) | ((yy & 1) << 1) | ((zz & 1) << 2)
-            members.append((place, flat(yy, c, xx, zz)))
-        key = tuple(d for _, d in sorted(members))
-        if key not in seen:
-            seen.add(key)
-            groups.append(list(key))
-    return groups
-
-
-GROUPS = cube_groups()
 
 
 def to_cube(a, m):
@@ -232,30 +211,23 @@
     )(core, *a_blocks, *b_blocks)
 
 
-def merge_kernel(place_ref, got_ref, out_ref):
-    me = place_ref[0]
-    for m in range(8):
-        parts = []
-        for k in range(8):
-            offset = (me ^ k) ^ m
-            row = jnp.int32(0)
-            for n in range(8):
-                row = jnp.where(offset == n, PLACE[n], row)
-            parts.append(got_ref[k, pl.ds(row, 1), :])
-        top = functools.reduce(jnp.maximum, parts)
-        total = functools.reduce(jnp.add, [jnp.exp2(p - top) for p in parts])
-        out_ref[PLACE[m] : PLACE[m] + 1, :] = top + jnp.log2(total)
-
-
-def merge_call(place, got):
-    return pl.pallas_call(
-        merge_kernel,
-        in_specs=[pl.BlockSpec(memory_space=pltpu.SMEM), pl.BlockSpec(memory_space=pltpu.VMEM)],
-        out_specs=pl.BlockSpec(memory_space=pltpu.VMEM),
-        out_shape=jax.ShapeDtypeStruct(got.shape[1:], jnp.float32),
+def merge_kernel(m, mine_ref, got_ref, out_ref):
+    for k in range(8):
+        j = PLACE[ORDER[k] ^ m]
+        mine, got = mine_ref[k : k + 1, :], got_ref[j : j + 1, :]
+        top = jnp.maximum(mine, got)
+        out_ref[k : k + 1, :] = top + jnp.log2(jnp.exp2(mine - top) + jnp.exp2(got - top))
+
+
+def merge_call(mine, got, m):
+    return pl.pallas_call(
+        functools.partial(merge_kernel, m),
+        in_specs=[vmem_spec()] * 2,
+        out_specs=vmem_spec(),
+        out_shape=jax.ShapeDtypeStruct(mine.shape, jnp.float32),
         compiler_params=pltpu.CompilerParams(vmem_limit_bytes=2 * 1024 * 1024),
         name="merge",
-    )(place, got)
+    )(mine, got)
 
 
 def half_copies(refs, h, out, sem):
@@ -438,32 +410,26 @@
     core = lax.axis_index("core")
     first = core == 0
     core_arr = core.astype(jnp.int32).reshape(1)
-    place = (
-        (lax.axis_index("x") & 1) | ((lax.axis_index("y") & 1) << 1) | ((lax.axis_index("z") & 1) << 2)
-    ).astype(jnp.int32).reshape(1)
-
     theirs = swap(jnp.concatenate([images, texts], axis=0))
     joined = lambda lead, follow: jnp.concatenate([lead, follow], axis=0)
     own = jnp.where(first, joined(images, theirs[:rows]), joined(texts, theirs[rows:]))
     other = jnp.where(first, joined(theirs[rows:], texts), joined(theirs[:rows], images))
     near = {m: to_cube(own, m) for m in (1, 2, 4)}
-    far = {7: to_cube(own, 7), 5: to_cube(near[1], 4), 3: to_cube(near[2], 1), 6: to_cube(near[4], 2)}
+    far = {7: to_cube(near[1], 6), 5: to_cube(near[1], 4), 3: to_cube(near[2], 1), 6: to_cube(near[4], 2)}
     blocks = {0: own, **near, **far}
-    held = lax.optimization_barrier(tuple(blocks[m] for m in (1, 2, 4, 7)))
+    held = lax.optimization_barrier(tuple(blocks[m] for m in (1, 2, 4, 5)))
     swapped = {0: other}
-    for m, a in zip((1, 2, 4, 7), held):
+    for m, a in zip((1, 2, 4, 5), held):
         swapped[m] = swap(a)
-    for m in (5, 3, 6):
+    for m in (3, 6, 7):
         swapped[m] = swap(blocks[m])
     a_blocks = [blocks[m] for m in ORDER]
     b_blocks = [swapped[m] for m in ORDER]
 
     e, a_stat, b_stat, flags = scores_call(core_arr, a_blocks, b_blocks, scale)
-    chip_stat = jnp.logaddexp2(a_stat, swap(b_stat))
-    got = lax.all_to_all(
-        jnp.broadcast_to(chip_stat[None], (8,) + chip_stat.shape), AXES, 0, 0, axis_index_groups=GROUPS
-    )
-    a_lse = merge_call(place, got)
+    a_lse = merge_call(a_stat, swap(b_stat), 0)
+    for m in (1, 2, 4):
+        a_lse = merge_call(a_lse, to_cube(a_lse, m), m)
     b_lse = swap(a_lse)
 
     w, gb_hi = weights_call(core_arr, flags, e, a_lse, b_lse, a_blocks)

time: 144 us -> 128 us (0.89)
  local copies, waits for them, and re-layouts: 14.4 us -> 0.08 us
    unnamed x44 -> x4, local copies, waits for them, and re-layouts: 13.7 us -> 0.01 us
    all_to_all x1 -> x0, waiting for transfers between devices: 8.58 us -> none  [body(): lax.all_to_all(jnp.broadcast_to(chip_stat[None], (8,) + chip_stat.shape),...]
    all_to_all x1 -> x0, starting transfers between devices: 8.07 us -> none  [body(): lax.all_to_all(jnp.broadcast_to(chip_stat[None], (8,) + chip_stat.shape),...]
    ppermute x14 -> x17, waiting for transfers between devices: 16 us -> 23.4 us  [to_cube(): return lax.ppermute(a, AXES, across(m))]
    ppermute x14 -> x17, starting transfers between devices: 32.5 us -> 39.8 us  [to_cube(): return lax.ppermute(a, AXES, across(m))]
    ppermute x14, waiting for transfers between devices: 7.37 us -> 9.12 us  [swap(): return lax.ppermute(a, AXES, SWAP)]
  transfers between devices with their start and end apart: 29 -> 31, of which waited for: 14 -> 19; matrix products, arithmetic and copies ran while one was open for 0% -> 0% of each run, Pallas kernels for 10% -> 12%
where the time goes in v5:
time: 128 us
  Pallas kernels  47.2 us (37%)
  starting transfers between devices  43.7 us (34%)
  waiting for transfers between devices  32.5 us (25%)
  other arithmetic  4 us (3%)
    ppermute x17, starting transfers between devices, to_cube(): return lax.ppermute(a, AXES, across(m))  39.8 us
    pallas_call x1, Pallas kernels, scores_call(): pl.pallas_call(functools.partial(scores_kernel, scale), in_specs=[smem_sp...  23.7 us
    ppermute x17, waiting for transfers between devices, to_cube(): return lax.ppermute(a, AXES, across(m))  23.4 us
    pallas_call x1, Pallas kernels, middle_call(): pl.pallas_call(middle_kernel, in_specs=[smem_spec(), vmem_spec()] + [any_...  10 us
    ppermute x14, waiting for transfers between devices, swap(): return lax.ppermute(a, AXES, SWAP)  9.12 us
    pallas_call x1, Pallas kernels, weights_call(): pl.pallas_call(weights_kernel, in_specs=[smem_spec()] * 2 + [vmem_spec()]...  8.53 us
    pallas_call x1, Pallas kernels, last_call(): pl.pallas_call(last_kernel, in_specs=[smem_spec(), vmem_spec()] + [any_sp...  4.03 us
    ppermute x14, starting transfers between devices, swap(): return lax.ppermute(a, AXES, SWAP)  3.94 us
  transfers between devices with their start and end apart: 31, of which 19 were waited for; matrix products, arithmetic and copies ran while one was open for 0% of the time, Pallas kernels for 12%

profile of v5, /device:TPU:1, one launch (start us, length us, event | category | flops | bytes accessed | tf_op | source)
XLA Modules:
  0.0 128.3 jit_solution(5349340069414508252)
XLA Ops:
  0.6 1.1 pad_maximum_fusion.1
  1.7 1.5 %collective-permute-start = (bf16[320,768]{1,0:T(8,128)(2,1)S(1)}, bf16[320,768]{1,0:T(8,128)(2,1)S(1)}, u32[]{:S(2)}, u32[]{:S(2)}) collective-permute-start(bf16[320,768]{1,0:T(8,128)(2,1)S(1)} %pad_maximum_fusion.1), channel_id=1, source_target_pairs={{0,16},{1,17},{2,18},{3,19},{4,20},{5,21},{6,22},{7,23},{8,24},{9,... | collective-permute-start | bytes 1474568 | tf_op jit(solution)/shard_map/ppermute | solution.py:57
  3.2 1.5 %collective-permute-done = bf16[320,768]{1,0:T(8,128)(2,1)S(1)} collective-permute-done((bf16[320,768]{1,0:T(8,128)(2,1)S(1)}, bf16[320,768]{1,0:T(8,128)(2,1)S(1)}, u32[]{:S(2)}, u32[]{:S(2)}) %collective-permute-start) | collective-permute-done | bytes 491552 | tf_op jit(solution)/shard_map/ppermute | solution.py:57
  4.8 1.5 %fusion.1 = (bf16[320,768]{1,0:T(8,128)(2,1)S(1)}, bf16[320,768]{1,0:T(8,128)(2,1)S(1)}) fusion(bf16[160,768]{1,0:T(8,128)(2,1)} %param.3, bf16[160,768]{1,0:T(8,128)(2,1)S(1)} %get-tuple-element.48, bf16[160,768]{1,0:T(8,128)(2,1)} %param.2, bf16[160,768]{1,0:T(8,128)(2,1)S(1)} %get-tuple-element.49, pred[]{:T(512)S(6)} %eq.3), kind=kLoop, calls=%fused_computation.5 | loop fusion | flops 4423680 | bytes 1966081 | tf_op jit(solution)/shard_map/jit(_where)/select_n | solution.py:416
  6.3 3.9 %collective-permute-start.3 = (bf16[320,768]{1,0:T(8,128)(2,1)S(1)}, bf16[320,768]{1,0:T(8,128)(2,1)S(1)}, u32[]{:S(2)}, u32[]{:S(2)}) collective-permute-start(bf16[320,768]{1,0:T(8,128)(2,1)S(1)} %get-tuple-element.47.refs_0_), channel_id=1, source_target_pairs={{0,1},{1,0},{2,3},{3,2},{4,5},{5,4},{6,7},{7,6},{8,9},{9,8},{10,11... | collective-permute-start | bytes 1474568 | tf_op jit(solution)/shard_map/ppermute | solution.py:53
  10.2 2.7 %collective-permute-start.2 = (bf16[320,768]{1,0:T(8,128)(2,1)S(1)}, bf16[320,768]{1,0:T(8,128)(2,1)S(1)}, u32[]{:S(2)}, u32[]{:S(2)}) collective-permute-start(bf16[320,768]{1,0:T(8,128)(2,1)S(1)} %get-tuple-element.47.refs_0_), channel_id=1, source_target_pairs={{0,32},{1,33},{2,34},{3,35},{4,36},{5,37},{6,38},{7,39},{8,40},{9,... | collective-permute-start | bytes 1474568 | tf_op jit(solution)/shard_map/ppermute | solution.py:53
  13.0 2.5 %collective-permute-start.1 = (bf16[320,768]{1,0:T(8,128)(2,1)S(1)}, bf16[320,768]{1,0:T(8,128)(2,1)S(1)}, u32[]{:S(2)}, u32[]{:S(2)}) collective-permute-start(bf16[320,768]{1,0:T(8,128)(2,1)S(1)} %get-tuple-element.47.refs_0_), channel_id=1, source_target_pairs={{0,4},{1,5},{2,6},{3,7},{4,0},{5,1},{6,2},{7,3},{8,12},{9,13},{10,... | collective-permute-start | bytes 1474568 | tf_op jit(solution)/shard_map/ppermute | solution.py:53
  15.4 1.0 collective-permute-done.3.refs_3_
  16.4 2.7 %collective-permute-start.6 = (bf16[320,768]{1,0:T(8,128)(2,1)S(1)}, bf16[320,768]{1,0:T(8,128)(2,1)S(1)}, u32[]{:S(2)}, u32[]{:S(2)}) collective-permute-start(bf16[320,768]{1,0:T(8,128)(2,1)S(1)} %collective-permute-done.3.refs_3_), channel_id=1, source_target_pairs={{0,32},{1,33},{2,34},{3,35},{4,36},{5,37},{6,38},{7,39},{8,40},{9,... | collective-permute-start | bytes 1474568 | tf_op jit(solution)/shard_map/ppermute | solution.py:53
  19.2 0.0 collective-permute-done.2.refs_2_
  19.2 2.5 %collective-permute-start.4 = (bf16[320,768]{1,0:T(8,128)(2,1)S(1)}, bf16[320,768]{1,0:T(8,128)(2,1)S(1)}, u32[]{:S(2)}, u32[]{:S(2)}) collective-permute-start(bf16[320,768]{1,0:T(8,128)(2,1)S(1)} %collective-permute-done.2.refs_2_), channel_id=1, source_target_pairs={{0,4},{1,5},{2,6},{3,7},{4,0},{5,1},{6,2},{7,3},{8,12},{9,13},{10,... | collective-permute-start | bytes 1474568 | tf_op jit(solution)/shard_map/ppermute | solution.py:53
  21.7 0.2 collective-permute-done.1.refs_1_
  21.9 2.5 %collective-permute-start.5 = (bf16[320,768]{1,0:T(8,128)(2,1)S(1)}, bf16[320,768]{1,0:T(8,128)(2,1)S(1)}, u32[]{:S(2)}, u32[]{:S(2)}) collective-permute-start(bf16[320,768]{1,0:T(8,128)(2,1)S(1)} %collective-permute-done.1.refs_1_), channel_id=1, source_target_pairs={{0,1},{1,0},{2,3},{3,2},{4,5},{5,4},{6,7},{7,6},{8,9},{9,8},{10,11... | collective-permute-start | bytes 1474568 | tf_op jit(solution)/shard_map/ppermute | solution.py:53
  24.3 2.4 %collective-permute-start.7 = (bf16[320,768]{1,0:T(8,128)(2,1)S(1)}, bf16[320,768]{1,0:T(8,128)(2,1)S(1)}, u32[]{:S(2)}, u32[]{:S(2)}) collective-permute-start(bf16[320,768]{1,0:T(8,128)(2,1)S(1)} %collective-permute-done.1.refs_1_), channel_id=1, source_target_pairs={{0,33},{1,32},{2,35},{3,34},{4,37},{5,36},{6,39},{7,38},{8,41},{9,... | collective-permute-start | bytes 1474568 | tf_op jit(solution)/shard_map/ppermute | solution.py:53
  26.7 0.0 collective-permute-done.6.refs_6_
  26.7 0.0 collective-permute-start.13
  26.7 1.5 %collective-permute-done.4.refs_4_ = bf16[320,768]{1,0:T(8,128)(2,1)S(1)} collective-permute-done((bf16[320,768]{1,0:T(8,128)(2,1)S(1)}, bf16[320,768]{1,0:T(8,128)(2,1)S(1)}, u32[]{:S(2)}, u32[]{:S(2)}) %collective-permute-start.4) | collective-permute-done | bytes 491552 | tf_op jit(solution)/shard_map/ppermute | solution.py:53
  28.2 7.8 %collective-permute-done.5.refs_5_ = bf16[320,768]{1,0:T(8,128)(2,1)S(1)} collective-permute-done((bf16[320,768]{1,0:T(8,128)(2,1)S(1)}, bf16[320,768]{1,0:T(8,128)(2,1)S(1)}, u32[]{:S(2)}, u32[]{:S(2)}) %collective-permute-start.5) | collective-permute-done | bytes 491552 | tf_op jit(solution)/shard_map/ppermute | solution.py:53
  36.0 0.5 collective-permute-start.9
  36.5 0.0 collective-permute-done.7.refs_7_
  36.5 0.0 collective-permute-start.14
  36.5 0.5 collective-permute-start.10
  37.0 0.0 collective-permute-done.11.refs_12_.refs_4_
  37.0 0.1 collective-permute-start.12
  37.1 2.2 %collective-permute-done.14.refs_15_.refs_7_ = bf16[320,768]{1,0:T(8,128)(2,1)S(1)} collective-permute-done((bf16[320,768]{1,0:T(8,128)(2,1)S(1)}, bf16[320,768]{1,0:T(8,128)(2,1)S(1)}, u32[]{:S(2)}, u32[]{:S(2)}) %collective-permute-start.14) | collective-permute-done | bytes 491552 | tf_op jit(solution)/shard_map/ppermute | solution.py:57
  39.3 0.7 collective-permute-done.10.refs_11_.refs_3_
  40.0 0.7 collective-permute-done.12.refs_13_.refs_5_
  40.7 23.7 %scores.1 = (f32[2,1280,1280]{2,1,0:T(8,128)S(1)}, f32[8,320]{1,0:T(8,128)S(1)}, f32[8,320]{1,0:T(8,128)S(1)}, s32[2]{0:T(128)S(1)}) custom-call(s32[1]{0:T(128)} %bitcast.core_ref, bf16[320,768]{1,0:T(8,128)(2,1)S(1)} %get-tuple-element.47.refs_0_, bf16[320,768]{1,0:T(8,128)(2,1)S(1)} %collective-permute-done.1.refs_1_, ...), custom_call_target="tpu_custom_call" | custom-call | flops 5033164800 | tf_op jit(solution)/shard_map/scores/pallas_call | solution.py:191
  64.4 0.2 collective-permute-start.15
  64.6 1.0 collective-permute-done.15.got_ref
  65.7 2.6 %collective-permute-start.16 = (f32[8,320]{1,0:T(8,128)S(1)}, f32[8,320]{1,0:T(8,128)S(1)}, u32[]{:S(2)}, u32[]{:S(2)}) collective-permute-start(f32[8,320]{1,0:T(8,128)S(1)} %merge.4.mine_ref), channel_id=1, source_target_pairs={{0,4},{1,5},{2,6},{3,7},{4,0},{5,1},{6,2},{7,3},{8,12},{9,13},{10,... | collective-permute-start | bytes 30728 | tf_op jit(solution)/shard_map/ppermute | solution.py:53
  68.3 1.3 collective-permute-done.16.got_ref
  69.6 2.6 %collective-permute-start.17 = (f32[8,320]{1,0:T(8,128)S(1)}, f32[8,320]{1,0:T(8,128)S(1)}, u32[]{:S(2)}, u32[]{:S(2)}) collective-permute-start(f32[8,320]{1,0:T(8,128)S(1)} %merge.5.mine_ref), channel_id=1, source_target_pairs={{0,32},{1,33},{2,34},{3,35},{4,36},{5,37},{6,38},{7,39},{8,40},{9,... | collective-permute-start | bytes 30728 | tf_op jit(solution)/shard_map/ppermute | solution.py:53
  72.1 1.3 collective-permute-done.17.got_ref
  73.4 2.6 %collective-permute-start.18 = (f32[8,320]{1,0:T(8,128)S(1)}, f32[8,320]{1,0:T(8,128)S(1)}, u32[]{:S(2)}, u32[]{:S(2)}) collective-permute-start(f32[8,320]{1,0:T(8,128)S(1)} %merge.6.mine_ref), channel_id=1, source_target_pairs={{0,1},{1,0},{2,3},{3,2},{4,5},{5,4},{6,7},{7,6},{8,9},{9,8},{10,11... | collective-permute-start | bytes 30728 | tf_op jit(solution)/shard_map/ppermute | solution.py:53
  76.0 1.3 collective-permute-done.18.got_ref
  77.3 0.1 collective-permute-start.19
  77.4 1.2 collective-permute-done.19.b_lse
  78.6 8.5 %weights.1 = (bf16[2,1280,1280]{2,1,0:T(8,128)(2,1)S(1)}, bf16[1280,768]{1,0:T(8,128)(2,1)S(1)}) custom-call(s32[1]{0:T(128)} %bitcast.core_ref, s32[2]{0:T(128)S(1)} %get-tuple-element.27.flags, f32[2,1280,1280]{2,1,0:T(8,128)S(1)} %get-tuple-element.28.e_ref, f32[8,320]{1,0:T(8,128)S(1)} %merge.7.a_lse, f32[8,320]{1,0:T(8,128)S(1)} %collective-permute-done.19.b_lse, ...), custom_call_target="tpu_custom_call" | custom-call | flops 2516582400 | bytes 19660800 | tf_op jit(solution)/shard_map/weights/pallas_call | solution.py:291
  87.1 0.2 collective-permute-start.22
  87.4 10.0 %middle.1 = (f32[1280,768]{1,0:T(8,128)S(1)}, f32[320,768]{1,0:T(8,128)S(1)}, bf16[960,768]{1,0:T(8,128)(2,1)S(1)}) custom-call(s32[1]{0:T(128)} %bitcast.core_ref, bf16[2,1280,1280]{2,1,0:T(8,128)(2,1)S(1)} %get-tuple-element.31.w_ref, bf16[320,768]{1,0:T(8,128)(2,1)S(1)} %get-tuple-element.47.refs_0_, bf16[320,768]{1,0:T(8,128)(2,1)S(1)} %collective-permute-done.1.refs_1_, ...), custom_call_target="tpu_custom_call" | custom-call | flops 5033164800 | tf_op jit(solution)/shard_map/middle/pallas_call | solution.py:324
  97.4 0.6 collective-permute-start.21
  98.0 0.1 collective-permute-start.20
  98.1 0.3 far.1
  98.4 2.6 %collective-permute-start.23 = (bf16[320,768]{1,0:T(8,128)(2,1)S(1)}, bf16[320,768]{1,0:T(8,128)(2,1)S(1)}, u32[]{:S(2)}, u32[]{:S(2)}) collective-permute-start(bf16[320,768]{1,0:T(8,128)(2,1)S(1)} %get-tuple-element.36), channel_id=1, source_target_pairs={{0,4},{1,5},{2,6},{3,7},{4,0},{5,1},{6,2},{7,3},{8,12},{9,13},{10,... | collective-permute-start | bytes 1474568 | tf_op jit(solution)/shard_map/ppermute | solution.py:53
  101.0 0.2 collective-permute-start.24
  101.2 1.3 collective-permute-start.25
  102.4 4.0 %last.1.ga_lo = f32[1280,768]{1,0:T(8,128)S(1)} custom-call(s32[1]{0:T(128)} %bitcast.core_ref, bf16[2,1280,1280]{2,1,0:T(8,128)(2,1)S(1)} %get-tuple-element.31.w_ref, bf16[320,768]{1,0:T(8,128)(2,1)S(1)} %get-tuple-element.46.refs_8_.refs_0_, bf16[320,768]{1,0:T(8,128)(2,1)S(1)} %collective-permute-done.8.refs_9_.refs_1_, ...), custom_call_target="tpu_custom_call" | custom-call | flops 2516582400 | tf_op jit(solution)/shard_map/last/pallas_call | solution.py:371
  106.5 3.6 %collective-permute-start.26 = (bf16[320,768]{1,0:T(8,128)(2,1)S(1)}, bf16[320,768]{1,0:T(8,128)(2,1)S(1)}, u32[]{:S(2)}, u32[]{:S(2)}) collective-permute-start(bf16[320,768]{1,0:T(8,128)(2,1)S(1)} %get-tuple-element.40), channel_id=1, source_target_pairs={{0,37},{1,36},{2,39},{3,38},{4,33},{5,32},{6,35},{7,34},{8,45},{9,... | collective-permute-start | bytes 1474568 | tf_op jit(solution)/shard_map/ppermute | solution.py:53
  110.1 0.1 collective-permute-done.24.r_yz
  110.1 0.2 collective-permute-done.25.r_xz
  110.3 0.5 near.1
  110.9 0.0 copy-start
  110.9 0.0 copy-start.1
  110.9 2.6 %collective-permute-start.27 = (bf16[320,768]{1,0:T(8,128)(2,1)S(1)}, bf16[320,768]{1,0:T(8,128)(2,1)S(1)}, u32[]{:S(2)}, u32[]{:S(2)}) collective-permute-start(bf16[320,768]{1,0:T(8,128)(2,1)S(1)} %get-tuple-element.41), channel_id=1, source_target_pairs={{0,4},{1,5},{2,6},{3,7},{4,0},{5,1},{6,2},{7,3},{8,12},{9,13},{10,... | collective-permute-start | bytes 1474568 | tf_op jit(solution)/shard_map/ppermute | solution.py:53
  113.5 0.2 collective-permute-start.28
  113.7 2.5 %collective-permute-start.29 = (bf16[320,768]{1,0:T(8,128)(2,1)S(1)}, bf16[320,768]{1,0:T(8,128)(2,1)S(1)}, u32[]{:S(2)}, u32[]{:S(2)}) collective-permute-start(bf16[320,768]{1,0:T(8,128)(2,1)S(1)} %get-tuple-element.43), channel_id=1, source_target_pairs={{0,1},{1,0},{2,3},{3,2},{4,5},{5,4},{6,7},{7,6},{8,9},{9,8},{10,11... | collective-permute-start | bytes 1474568 | tf_op jit(solution)/shard_map/ppermute | solution.py:53
  116.1 3.7 %collective-permute-done.26 = bf16[320,768]{1,0:T(8,128)(2,1)S(1)} collective-permute-done((bf16[320,768]{1,0:T(8,128)(2,1)S(1)}, bf16[320,768]{1,0:T(8,128)(2,1)S(1)}, u32[]{:S(2)}, u32[]{:S(2)}) %collective-permute-start.26) | collective-permute-done | bytes 491552 | tf_op jit(solution)/shard_map/ppermute | solution.py:53
  119.8 4.2 %collective-permute-done.27 = bf16[320,768]{1,0:T(8,128)(2,1)S(1)} collective-permute-done((bf16[320,768]{1,0:T(8,128)(2,1)S(1)}, bf16[320,768]{1,0:T(8,128)(2,1)S(1)}, u32[]{:S(2)}, u32[]{:S(2)}) %collective-permute-start.27) | collective-permute-done | bytes 491552 | tf_op jit(solution)/shard_map/ppermute | solution.py:53
  124.1 0.9 collective-permute-done.29
  125.0 0.3 convert_add_fusion
  125.3 0.1 collective-permute-start.30
  125.4 1.9 %collective-permute-done.30 = f32[160,768]{1,0:T(8,128)S(1)} collective-permute-done((f32[160,768]{1,0:T(8,128)S(1)}, f32[160,768]{1,0:T(8,128)S(1)}, u32[]{:S(2)}, u32[]{:S(2)}) %collective-permute-start.30) | collective-permute-done | bytes 491552 | tf_op jit(solution)/shard_map/ppermute | solution.py:57
  127.3 1.1 convert_subtract_fusion
  (18 shorter events, 0.2 us)
Async XLA Ops:
  1.7 3.0 %collective-permute-start = (bf16[320,768]{1,0:T(8,128)(2,1)S(1)}, bf16[320,768]{1,0:T(8,128)(2,1)S(1)}, u32[]{:S(2)}, u32[]{:S(2)}) collective-permute-start(bf16[320,768]{1,0:T(8,128)(2,1)S(1)} %pad_maximum_fusion.1), channel_id=1, source_target_pairs={{0,16},{1,17},{2,18},{3,19},{4,20},{5,21},{6,22},{7,23},{8,24},{9,... | collective-permute-start | bytes 1474568 | tf_op jit(solution)/shard_map/ppermute | solution.py:57
  6.3 10.1 %collective-permute-start.3 = (bf16[320,768]{1,0:T(8,128)(2,1)S(1)}, bf16[320,768]{1,0:T(8,128)(2,1)S(1)}, u32[]{:S(2)}, u32[]{:S(2)}) collective-permute-start(bf16[320,768]{1,0:T(8,128)(2,1)S(1)} %get-tuple-element.47.refs_0_), channel_id=1, source_target_pairs={{0,1},{1,0},{2,3},{3,2},{4,5},{5,4},{6,7},{7,6},{8,9},{9,8},{10,11... | collective-permute-start | bytes 1474568 | tf_op jit(solution)/shard_map/ppermute | solution.py:53
  10.2 9.0 %collective-permute-start.2 = (bf16[320,768]{1,0:T(8,128)(2,1)S(1)}, bf16[320,768]{1,0:T(8,128)(2,1)S(1)}, u32[]{:S(2)}, u32[]{:S(2)}) collective-permute-start(bf16[320,768]{1,0:T(8,128)(2,1)S(1)} %get-tuple-element.47.refs_0_), channel_id=1, source_target_pairs={{0,32},{1,33},{2,34},{3,35},{4,36},{5,37},{6,38},{7,39},{8,40},{9,... | collective-permute-start | bytes 1474568 | tf_op jit(solution)/shard_map/ppermute | solution.py:53
  13.0 8.9 %collective-permute-start.1 = (bf16[320,768]{1,0:T(8,128)(2,1)S(1)}, bf16[320,768]{1,0:T(8,128)(2,1)S(1)}, u32[]{:S(2)}, u32[]{:S(2)}) collective-permute-start(bf16[320,768]{1,0:T(8,128)(2,1)S(1)} %get-tuple-element.47.refs_0_), channel_id=1, source_target_pairs={{0,4},{1,5},{2,6},{3,7},{4,0},{5,1},{6,2},{7,3},{8,12},{9,13},{10,... | collective-permute-start | bytes 1474568 | tf_op jit(solution)/shard_map/ppermute | solution.py:53
  16.4 10.3 %collective-permute-start.6 = (bf16[320,768]{1,0:T(8,128)(2,1)S(1)}, bf16[320,768]{1,0:T(8,128)(2,1)S(1)}, u32[]{:S(2)}, u32[]{:S(2)}) collective-permute-start(bf16[320,768]{1,0:T(8,128)(2,1)S(1)} %collective-permute-done.3.refs_3_), channel_id=1, source_target_pairs={{0,32},{1,33},{2,34},{3,35},{4,36},{5,37},{6,38},{7,39},{8,40},{9,... | collective-permute-start | bytes 1474568 | tf_op jit(solution)/shard_map/ppermute | solution.py:53
  19.2 9.0 %collective-permute-start.4 = (bf16[320,768]{1,0:T(8,128)(2,1)S(1)}, bf16[320,768]{1,0:T(8,128)(2,1)S(1)}, u32[]{:S(2)}, u32[]{:S(2)}) collective-permute-start(bf16[320,768]{1,0:T(8,128)(2,1)S(1)} %collective-permute-done.2.refs_2_), channel_id=1, source_target_pairs={{0,4},{1,5},{2,6},{3,7},{4,0},{5,1},{6,2},{7,3},{8,12},{9,13},{10,... | collective-permute-start | bytes 1474568 | tf_op jit(solution)/shard_map/ppermute | solution.py:53
  21.9 14.2 %collective-permute-start.5 = (bf16[320,768]{1,0:T(8,128)(2,1)S(1)}, bf16[320,768]{1,0:T(8,128)(2,1)S(1)}, u32[]{:S(2)}, u32[]{:S(2)}) collective-permute-start(bf16[320,768]{1,0:T(8,128)(2,1)S(1)} %collective-permute-done.1.refs_1_), channel_id=1, source_target_pairs={{0,1},{1,0},{2,3},{3,2},{4,5},{5,4},{6,7},{7,6},{8,9},{9,8},{10,11... | collective-permute-start | bytes 1474568 | tf_op jit(solution)/shard_map/ppermute | solution.py:53
  24.3 12.2 %collective-permute-start.7 = (bf16[320,768]{1,0:T(8,128)(2,1)S(1)}, bf16[320,768]{1,0:T(8,128)(2,1)S(1)}, u32[]{:S(2)}, u32[]{:S(2)}) collective-permute-start(bf16[320,768]{1,0:T(8,128)(2,1)S(1)} %collective-permute-done.1.refs_1_), channel_id=1, source_target_pairs={{0,33},{1,32},{2,35},{3,34},{4,37},{5,36},{6,39},{7,38},{8,41},{9,... | collective-permute-start | bytes 1474568 | tf_op jit(solution)/shard_map/ppermute | solution.py:53
  26.7 9.8 %collective-permute-start.13 = (bf16[320,768]{1,0:T(8,128)(2,1)S(1)}, bf16[320,768]{1,0:T(8,128)(2,1)S(1)}, u32[]{:S(2)}, u32[]{:S(2)}) collective-permute-start(bf16[320,768]{1,0:T(8,128)(2,1)S(1)} %collective-permute-done.6.refs_6_), channel_id=1, source_target_pairs={{0,16},{1,17},{2,18},{3,19},{4,20},{5,21},{6,22},{7,23},{8,24},{9,... | collective-permute-start | bytes 1474568 | tf_op jit(solution)/shard_map/ppermute | solution.py:57
  28.2 8.8 %collective-permute-start.11 = (bf16[320,768]{1,0:T(8,128)(2,1)S(1)}, bf16[320,768]{1,0:T(8,128)(2,1)S(1)}, u32[]{:S(2)}, u32[]{:S(2)}) collective-permute-start(bf16[320,768]{1,0:T(8,128)(2,1)S(1)} %collective-permute-done.4.refs_4_), channel_id=1, source_target_pairs={{0,16},{1,17},{2,18},{3,19},{4,20},{5,21},{6,22},{7,23},{8,24},{9,... | collective-permute-start | bytes 1474568 | tf_op jit(solution)/shard_map/ppermute | solution.py:57
  36.0 3.3 %collective-permute-start.8 = (bf16[320,768]{1,0:T(8,128)(2,1)S(1)}, bf16[320,768]{1,0:T(8,128)(2,1)S(1)}, u32[]{:S(2)}, u32[]{:S(2)}) collective-permute-start(bf16[320,768]{1,0:T(8,128)(2,1)S(1)} %collective-permute-done.1.refs_1_), channel_id=1, source_target_pairs={{0,16},{1,17},{2,18},{3,19},{4,20},{5,21},{6,22},{7,23},{8,24},{9,... | collective-permute-start | bytes 1474568 | tf_op jit(solution)/shard_map/ppermute | solution.py:57
  36.0 3.3 %collective-permute-start.9 = (bf16[320,768]{1,0:T(8,128)(2,1)S(1)}, bf16[320,768]{1,0:T(8,128)(2,1)S(1)}, u32[]{:S(2)}, u32[]{:S(2)}) collective-permute-start(bf16[320,768]{1,0:T(8,128)(2,1)S(1)} %collective-permute-done.2.refs_2_), channel_id=1, source_target_pairs={{0,16},{1,17},{2,18},{3,19},{4,20},{5,21},{6,22},{7,23},{8,24},{9,... | collective-permute-start | bytes 1474568 | tf_op jit(solution)/shard_map/ppermute | solution.py:57
  36.5 2.8 %collective-permute-start.14 = (bf16[320,768]{1,0:T(8,128)(2,1)S(1)}, bf16[320,768]{1,0:T(8,128)(2,1)S(1)}, u32[]{:S(2)}, u32[]{:S(2)}) collective-permute-start(bf16[320,768]{1,0:T(8,128)(2,1)S(1)} %collective-permute-done.7.refs_7_), channel_id=1, source_target_pairs={{0,16},{1,17},{2,18},{3,19},{4,20},{5,21},{6,22},{7,23},{8,24},{9,... | collective-permute-start | bytes 1474568 | tf_op jit(solution)/shard_map/ppermute | solution.py:57
  36.5 3.4 %collective-permute-start.10 = (bf16[320,768]{1,0:T(8,128)(2,1)S(1)}, bf16[320,768]{1,0:T(8,128)(2,1)S(1)}, u32[]{:S(2)}, u32[]{:S(2)}) collective-permute-start(bf16[320,768]{1,0:T(8,128)(2,1)S(1)} %collective-permute-done.3.refs_3_), channel_id=1, source_target_pairs={{0,16},{1,17},{2,18},{3,19},{4,20},{5,21},{6,22},{7,23},{8,24},{9,... | collective-permute-start | bytes 1474568 | tf_op jit(solution)/shard_map/ppermute | solution.py:57
  37.0 3.6 %collective-permute-start.12 = (bf16[320,768]{1,0:T(8,128)(2,1)S(1)}, bf16[320,768]{1,0:T(8,128)(2,1)S(1)}, u32[]{:S(2)}, u32[]{:S(2)}) collective-permute-start(bf16[320,768]{1,0:T(8,128)(2,1)S(1)} %collective-permute-done.5.refs_5_), channel_id=1, source_target_pairs={{0,16},{1,17},{2,18},{3,19},{4,20},{5,21},{6,22},{7,23},{8,24},{9,... | collective-permute-start | bytes 1474568 | tf_op jit(solution)/shard_map/ppermute | solution.py:57
  64.4 1.3 collective-permute-start.15
  65.7 3.8 %collective-permute-start.16 = (f32[8,320]{1,0:T(8,128)S(1)}, f32[8,320]{1,0:T(8,128)S(1)}, u32[]{:S(2)}, u32[]{:S(2)}) collective-permute-start(f32[8,320]{1,0:T(8,128)S(1)} %merge.4.mine_ref), channel_id=1, source_target_pairs={{0,4},{1,5},{2,6},{3,7},{4,0},{5,1},{6,2},{7,3},{8,12},{9,13},{10,... | collective-permute-start | bytes 30728 | tf_op jit(solution)/shard_map/ppermute | solution.py:53
  69.6 3.8 %collective-permute-start.17 = (f32[8,320]{1,0:T(8,128)S(1)}, f32[8,320]{1,0:T(8,128)S(1)}, u32[]{:S(2)}, u32[]{:S(2)}) collective-permute-start(f32[8,320]{1,0:T(8,128)S(1)} %merge.5.mine_ref), channel_id=1, source_target_pairs={{0,32},{1,33},{2,34},{3,35},{4,36},{5,37},{6,38},{7,39},{8,40},{9,... | collective-permute-start | bytes 30728 | tf_op jit(solution)/shard_map/ppermute | solution.py:53
  73.4 3.8 %collective-permute-start.18 = (f32[8,320]{1,0:T(8,128)S(1)}, f32[8,320]{1,0:T(8,128)S(1)}, u32[]{:S(2)}, u32[]{:S(2)}) collective-permute-start(f32[8,320]{1,0:T(8,128)S(1)} %merge.6.mine_ref), channel_id=1, source_target_pairs={{0,1},{1,0},{2,3},{3,2},{4,5},{5,4},{6,7},{7,6},{8,9},{9,8},{10,11... | collective-permute-start | bytes 30728 | tf_op jit(solution)/shard_map/ppermute | solution.py:53
  77.3 1.3 collective-permute-start.19
  87.1 11.0 %collective-permute-start.22 = (bf16[1280,768]{1,0:T(8,128)(2,1)S(1)}, bf16[1280,768]{1,0:T(8,128)(2,1)S(1)}, u32[]{:S(2)}, u32[]{:S(2)}) collective-permute-start(bf16[1280,768]{1,0:T(8,128)(2,1)S(1)} %get-tuple-element.35), channel_id=1, source_target_pairs={{0,16},{1,17},{2,18},{3,19},{4,20},{5,21},{6,22},{7,23},{8,24},{9,... | collective-permute-start | bytes 5898248 | tf_op jit(solution)/shard_map/ppermute | solution.py:57
  97.4 12.7 %collective-permute-start.21 = (bf16[960,768]{1,0:T(8,128)(2,1)S(1)}, bf16[960,768]{1,0:T(8,128)(2,1)S(1)}, u32[]{:S(2)}, u32[]{:S(2)}) collective-permute-start(bf16[960,768]{1,0:T(8,128)(2,1)S(1)} %get-tuple-element.33), channel_id=1, source_target_pairs={{0,16},{1,17},{2,18},{3,19},{4,20},{5,21},{6,22},{7,23},{8,24},{9,... | collective-permute-start | bytes 4423688 | tf_op jit(solution)/shard_map/ppermute | solution.py:57
  98.0 8.5 %collective-permute-start.20 = (f32[320,768]{1,0:T(8,128)S(1)}, f32[320,768]{1,0:T(8,128)S(1)}, u32[]{:S(2)}, u32[]{:S(2)}) collective-permute-start(f32[320,768]{1,0:T(8,128)S(1)} %get-tuple-element.32), channel_id=1, source_target_pairs={{0,16},{1,17},{2,18},{3,19},{4,20},{5,21},{6,22},{7,23},{8,24},{9,... | collective-permute-start | bytes 2949128 | tf_op jit(solution)/shard_map/ppermute | solution.py:57
  98.4 11.7 %collective-permute-start.23 = (bf16[320,768]{1,0:T(8,128)(2,1)S(1)}, bf16[320,768]{1,0:T(8,128)(2,1)S(1)}, u32[]{:S(2)}, u32[]{:S(2)}) collective-permute-start(bf16[320,768]{1,0:T(8,128)(2,1)S(1)} %get-tuple-element.36), channel_id=1, source_target_pairs={{0,4},{1,5},{2,6},{3,7},{4,0},{5,1},{6,2},{7,3},{8,12},{9,13},{10,... | collective-permute-start | bytes 1474568 | tf_op jit(solution)/shard_map/ppermute | solution.py:53
  101.0 9.2 %collective-permute-start.24 = (bf16[320,768]{1,0:T(8,128)(2,1)S(1)}, bf16[320,768]{1,0:T(8,128)(2,1)S(1)}, u32[]{:S(2)}, u32[]{:S(2)}) collective-permute-start(bf16[320,768]{1,0:T(8,128)(2,1)S(1)} %get-tuple-element.37), channel_id=1, source_target_pairs={{0,32},{1,33},{2,34},{3,35},{4,36},{5,37},{6,38},{7,39},{8,40},{9,... | collective-permute-start | bytes 1474568 | tf_op jit(solution)/shard_map/ppermute | solution.py:53
  101.2 9.2 %collective-permute-start.25 = (bf16[320,768]{1,0:T(8,128)(2,1)S(1)}, bf16[320,768]{1,0:T(8,128)(2,1)S(1)}, u32[]{:S(2)}, u32[]{:S(2)}) collective-permute-start(bf16[320,768]{1,0:T(8,128)(2,1)S(1)} %get-tuple-element.38), channel_id=1, source_target_pairs={{0,1},{1,0},{2,3},{3,2},{4,5},{5,4},{6,7},{7,6},{8,9},{9,8},{10,11... | collective-permute-start | bytes 1474568 | tf_op jit(solution)/shard_map/ppermute | solution.py:53
  106.5 13.3 %collective-permute-start.26 = (bf16[320,768]{1,0:T(8,128)(2,1)S(1)}, bf16[320,768]{1,0:T(8,128)(2,1)S(1)}, u32[]{:S(2)}, u32[]{:S(2)}) collective-permute-start(bf16[320,768]{1,0:T(8,128)(2,1)S(1)} %get-tuple-element.40), channel_id=1, source_target_pairs={{0,37},{1,36},{2,39},{3,38},{4,33},{5,32},{6,35},{7,34},{8,45},{9,... | collective-permute-start | bytes 1474568 | tf_op jit(solution)/shard_map/ppermute | solution.py:53
  110.9 16.4 %copy-start = (bf16[160,768]{1,0:T(8,128)(2,1)S(1)}, bf16[160,768]{1,0:T(8,128)(2,1)}, u32[]{:S(2)}) copy-start(bf16[160,768]{1,0:T(8,128)(2,1)} %param.2) | copy-start | bytes 737284
  110.9 16.4 %copy-start.1 = (bf16[160,768]{1,0:T(8,128)(2,1)S(1)}, bf16[160,768]{1,0:T(8,128)(2,1)}, u32[]{:S(2)}) copy-start(bf16[160,768]{1,0:T(8,128)(2,1)} %param.3) | copy-start | bytes 737284
  110.9 13.2 %collective-permute-start.27 = (bf16[320,768]{1,0:T(8,128)(2,1)S(1)}, bf16[320,768]{1,0:T(8,128)(2,1)S(1)}, u32[]{:S(2)}, u32[]{:S(2)}) collective-permute-start(bf16[320,768]{1,0:T(8,128)(2,1)S(1)} %get-tuple-element.41), channel_id=1, source_target_pairs={{0,4},{1,5},{2,6},{3,7},{4,0},{5,1},{6,2},{7,3},{8,12},{9,13},{10,... | collective-permute-start | bytes 1474568 | tf_op jit(solution)/shard_map/ppermute | solution.py:53
  113.5 10.6 %collective-permute-start.28 = (bf16[320,768]{1,0:T(8,128)(2,1)S(1)}, bf16[320,768]{1,0:T(8,128)(2,1)S(1)}, u32[]{:S(2)}, u32[]{:S(2)}) collective-permute-start(bf16[320,768]{1,0:T(8,128)(2,1)S(1)} %get-tuple-element.42), channel_id=1, source_target_pairs={{0,32},{1,33},{2,34},{3,35},{4,36},{5,37},{6,38},{7,39},{8,40},{9,... | collective-permute-start | bytes 1474568 | tf_op jit(solution)/shard_map/ppermute | solution.py:53
  113.7 11.3 %collective-permute-start.29 = (bf16[320,768]{1,0:T(8,128)(2,1)S(1)}, bf16[320,768]{1,0:T(8,128)(2,1)S(1)}, u32[]{:S(2)}, u32[]{:S(2)}) collective-permute-start(bf16[320,768]{1,0:T(8,128)(2,1)S(1)} %get-tuple-element.43), channel_id=1, source_target_pairs={{0,1},{1,0},{2,3},{3,2},{4,5},{5,4},{6,7},{7,6},{8,9},{9,8},{10,11... | collective-permute-start | bytes 1474568 | tf_op jit(solution)/shard_map/ppermute | solution.py:53
  125.3 1.9 %collective-permute-start.30 = (f32[160,768]{1,0:T(8,128)S(1)}, f32[160,768]{1,0:T(8,128)S(1)}, u32[]{:S(2)}, u32[]{:S(2)}) collective-permute-start(f32[160,768]{1,0:T(8,128)S(1)} %slice.21), channel_id=1, source_target_pairs={{0,16},{1,17},{2,18},{3,19},{4,20},{5,21},{6,22},{7,23},{8,24},{9,... | collective-permute-start | bytes 1474568 | tf_op jit(solution)/shard_map/ppermute | solution.py:57

commit v6 on v5

--- a/solution.py
+++ b/solution.py
@@ -73,10 +73,6 @@
     return wide.T[:1, :rows]
 
 
-def any_spec():
-    return pl.BlockSpec(memory_space=pl.ANY)
-
-
 def vmem_spec():
     return pl.BlockSpec(memory_space=pltpu.VMEM)
 
@@ -103,45 +99,90 @@
     return lax.dot_general(a, b, (((0,), (0,)), ((), ())), preferred_element_type=jnp.float32)
 
 
+def own_kernel(core_ref, images, texts, got_images, got_texts, own, other):
+    rows = images.shape[0]
+    core = core_ref[0]
+
+    @pl.when(core == 0)
+    def _():
+        own[:rows] = images[...]
+        own[rows:] = got_images[...]
+        other[:rows] = got_texts[...]
+        other[rows:] = texts[...]
+
+    @pl.when(core != 0)
+    def _():
+        own[:rows] = texts[...]
+        own[rows:] = got_texts[...]
+        other[:rows] = got_images[...]
+        other[rows:] = images[...]
+
+
+def own_call(core, *parts):
+    rows, features = parts[0].shape
+    block = jax.ShapeDtypeStruct((2 * rows, features), parts[0].dtype)
+    return pl.pallas_call(
+        own_kernel,
+        in_specs=[smem_spec()] + [vmem_spec()] * 4,
+        out_specs=[vmem_spec()] * 2,
+        out_shape=[block, block],
+        compiler_params=params(),
+        cost_estimate=cost(0, rows, features, 1, 16),
+        name="own",
+    )(core, *parts)
+
+
+def join_kernel(b0, b1, b2, out):
+    rows = b0.shape[0]
+    for j, b in enumerate((b0, b1, b2)):
+        out[j * rows : (j + 1) * rows, :] = b[...]
+
+
+def join_call(*parts):
+    rows, features = parts[0].shape
+    return pl.pallas_call(
+        join_kernel,
+        in_specs=[vmem_spec()] * 3,
+        out_specs=vmem_spec(),
+        out_shape=jax.ShapeDtypeStruct((3 * rows, features), parts[0].dtype),
+        compiler_params=params(),
+        cost_estimate=cost(0, 3 * rows, features, 1, 4),
+        name="join",
+    )(*parts)
+
+
+def views(refs):
+    own, near = refs[:2]
+    rows = own.shape[0]
+    return [own] + [near.at[pl.ds(j * rows, rows)] for j in range(3)] + list(refs[2:])
+
+
+def take_half(core, blocks, shift, out):
+    rows = blocks[0].shape[0]
+    for c in range(2):
+
+        @pl.when(core == c)
+        def _():
+            for j in range(4):
+                out[j * rows : (j + 1) * rows, :] = blocks[4 * (c ^ shift) + j][...]
+
+
 def scores_kernel(scale, core_ref, *refs):
-    a_refs, b_refs = refs[:8], refs[8:16]
-    e_ref, a_stat, b_stat, flags, a_cat, b_cat, col_m, col_s, sem = refs[16:]
+    a_refs, b_refs = refs[:8], views(refs[8:14])
+    e_ref, a_stat, b_stat, flags, a_cat, b_cat, col_m, col_s = refs[14:]
     rows = a_refs[0].shape[0]
     half = 4 * rows
     core = core_ref[0]
-
-    def copies_a(h):
-        return [
-            pltpu.make_async_copy(a_refs[4 * h + j], a_cat.at[h, pl.ds(j * rows, rows)], sem.at[4 * h + j])
-            for j in range(4)
-        ]
-
-    def copies_b(h):
-        place = h ^ core
-        return [
-            pltpu.make_async_copy(b_refs[4 * h + j], b_cat.at[place, pl.ds(j * rows, rows)], sem.at[8 + 4 * h + j])
-            for j in range(4)
-        ]
-
-    for c in copies_b(0) + copies_a(0) + copies_b(1) + copies_a(1):
-        c.start()
+    for q in range(2):
+        take_half(core, b_refs, q, b_cat.at[q])
 
     def quadrant(q):
-        for c in copies_a(q):
-            c.wait()
-        for h in range(2):
-
-            @pl.when((h ^ core) == q)
-            def _():
-                for c in copies_b(h):
-                    c.wait()
-
         b_half = b_cat[q]
         sums = []
         col = None
         for r in range(4):
             sl = slice(r * rows, (r + 1) * rows)
-            e = jnp.exp2(dot_nt(a_cat[q, sl, :], b_half) * scale)
+            e = jnp.exp2(dot_nt(a_refs[4 * q + r][...], b_half) * scale)
             e_ref[q, sl, :] = e
             sums.append(jnp.sum(e, axis=1, keepdims=True))
             part = jnp.sum(e, axis=0, keepdims=True)
@@ -158,13 +199,15 @@
 
         @pl.when(bad)
         def _():
+            for r in range(4):
+                a_cat[r * rows : (r + 1) * rows, :] = a_refs[4 * q + r][...]
             col_m[...] = jnp.full_like(col_m, -jnp.inf)
             col_s[...] = jnp.zeros_like(col_s)
 
             @pl.loop(0, 4)
             def _(r):
                 sl = pl.ds(pl.multiple_of(r * rows, 16), rows)
-                s = dot_nt(a_cat[q, sl, :], b_cat[q]) * scale
+                s = dot_nt(a_cat[sl, :], b_cat[q]) * scale
                 e_ref[q, sl, :] = s
                 row_m = jnp.max(s, axis=1, keepdims=True)
                 row_s = jnp.sum(jnp.exp2(s - row_m), axis=1, keepdims=True)
@@ -190,7 +233,7 @@
     stat = jax.ShapeDtypeStruct((8, rows), jnp.float32)
     return pl.pallas_call(
         functools.partial(scores_kernel, scale),
-        in_specs=[smem_spec()] + [any_spec()] * 16,
+        in_specs=[smem_spec()] + [vmem_spec()] * 14,
         out_specs=[vmem_spec()] * 3 + [smem_spec()],
         out_shape=[
             pltpu.VMEM((2, half, half), jnp.float32),
@@ -199,11 +242,10 @@
             jax.ShapeDtypeStruct((2,), jnp.int32),
         ],
         scratch_shapes=[
-            pltpu.VMEM((2, half, features), jnp.bfloat16),
+            pltpu.VMEM((half, features), jnp.bfloat16),
             pltpu.VMEM((2, half, features), jnp.bfloat16),
             pltpu.VMEM((1, half), jnp.float32),
             pltpu.VMEM((1, half), jnp.float32),
-            pltpu.SemaphoreType.DMA((16,)),
         ],
         compiler_params=params(),
         cost_estimate=cost(2, half, half, features),
@@ -230,37 +272,12 @@
     )(mine, got)
 
 
-def half_copies(refs, h, out, sem):
-    rows = refs[0].shape[0]
-    return [
-        pltpu.make_async_copy(refs[4 * h + j], out.at[pl.ds(j * rows, rows)], sem.at[j]) for j in range(4)
-    ]
-
-
-def start_half(core, refs, shift, out, sem):
-    for c in range(2):
-
-        @pl.when(core == c)
-        def _():
-            for copy in half_copies(refs, c ^ shift, out, sem):
-                copy.start()
-
-
-def wait_half(refs, out, sem):
-    for copy in half_copies(refs, 0, out, sem):
-        copy.wait()
-
-
-def half_scratch(block):
-    return [pltpu.VMEM((4 * block.shape[0], block.shape[1]), block.dtype), pltpu.SemaphoreType.DMA((4,))]
-
-
 def weights_kernel(core_ref, flags, e_ref, a_lse, b_lse, *refs):
-    a_refs, (w_ref, gb_hi, a_half, a_sem) = refs[:8], refs[8:]
+    a_refs, (w_ref, gb_hi, a_half) = refs[:8], refs[8:]
     rows = a_lse.shape[1]
     half = 4 * rows
     core = core_ref[0]
-    start_half(core, a_refs, 1, a_half, a_sem)
+    take_half(core, a_refs, 1, a_half)
     for q in range(2):
         a_row = jnp.concatenate([a_lse[4 * q + j : 4 * q + j + 1, :] for j in range(4)], axis=1)
         b_row = jnp.concatenate([b_lse[pl.ds((q ^ core) * 4 + j, 1), :] for j in range(4)], axis=1)
@@ -281,7 +298,6 @@
                 s = e_ref[q, sl, :]
                 w_ref[q, sl, :] = (jnp.exp2(s - a_col[sl, :]) + jnp.exp2(s - b_row)).astype(jnp.bfloat16)
 
-    wait_half(a_refs, a_half, a_sem)
     gb_hi[...] = (0.5 * dot_tn(w_ref[1 - core], a_half[...])).astype(jnp.bfloat16)
 
 
@@ -290,13 +306,13 @@
     half = 4 * rows
     return pl.pallas_call(
         weights_kernel,
-        in_specs=[smem_spec()] * 2 + [vmem_spec()] * 3 + [any_spec()] * 8,
+        in_specs=[smem_spec()] * 2 + [vmem_spec()] * 11,
         out_specs=[vmem_spec()] * 2,
         out_shape=[
             pltpu.VMEM((2, half, half), jnp.bfloat16),
             jax.ShapeDtypeStruct((half, features), jnp.bfloat16),
         ],
-        scratch_shapes=half_scratch(a_blocks[0]),
+        scratch_shapes=[pltpu.VMEM((half, features), jnp.bfloat16)],
         compiler_params=params(),
         cost_estimate=cost(1, half, half, features, 12),
         name="weights",
@@ -304,17 +320,15 @@
 
 
 def middle_kernel(core_ref, w_ref, *refs):
-    a_refs, b_refs = refs[:8], refs[8:16]
-    ga_hi, gb0, gb_lo, a_half, a_sem, b_half, b_sem = refs[16:]
+    a_refs, b_refs = refs[:8], views(refs[8:14])
+    ga_hi, gb0, gb_lo, a_half, b_half = refs[14:]
     rows = gb0.shape[0]
     core = core_ref[0]
-    start_half(core, a_refs, 0, a_half, a_sem)
-    start_half(core, b_refs, 1, b_half, b_sem)
-    wait_half(a_refs, a_half, a_sem)
+    take_half(core, a_refs, 0, a_half)
+    take_half(core, b_refs, 1, b_half)
     g = 0.5 * dot_tn(w_ref[core], a_half[...])
     gb0[...] = g[:rows]
     gb_lo[...] = g[rows:].astype(jnp.bfloat16)
-    wait_half(b_refs, b_half, b_sem)
     ga_hi[...] = 0.5 * jnp.dot(w_ref[1], b_half[...], preferred_element_type=jnp.float32)
 
 
@@ -323,14 +337,14 @@
     half = 4 * rows
     return pl.pallas_call(
         middle_kernel,
-        in_specs=[smem_spec(), vmem_spec()] + [any_spec()] * 16,
+        in_specs=[smem_spec()] + [vmem_spec()] * 15,
         out_specs=[vmem_spec()] * 3,
         out_shape=[
             pltpu.VMEM((half, features), jnp.float32),
             jax.ShapeDtypeStruct((rows, features), jnp.float32),
             jax.ShapeDtypeStruct((half - rows, features), jnp.bfloat16),
         ],
-        scratch_shapes=half_scratch(a_blocks[0]) + half_scratch(b_blocks[0]),
+        scratch_shapes=[pltpu.VMEM((half, features), jnp.bfloat16)] * 2,
         compiler_params=params(),
         cost_estimate=cost(2, half, half, features),
         name="middle",
@@ -359,9 +373,8 @@
 
 
 def last_kernel(core_ref, w_ref, *refs):
-    b_refs, (ga_lo, b_half, b_sem) = refs[:8], refs[8:]
-    start_half(core_ref[0], b_refs, 0, b_half, b_sem)
-    wait_half(b_refs, b_half, b_sem)
+    b_refs, (ga_lo, b_half) = views(refs[:6]), refs[6:]
+    take_half(core_ref[0], b_refs, 0, b_half)
     ga_lo[...] = 0.5 * jnp.dot(w_ref[0], b_half[...], preferred_element_type=jnp.float32)
 
 
@@ -370,10 +383,10 @@
     half = 4 * rows
     return pl.pallas_call(
         last_kernel,
-        in_specs=[smem_spec(), vmem_spec()] + [any_spec()] * 8,
+        in_specs=[smem_spec()] + [vmem_spec()] * 7,
         out_specs=vmem_spec(),
         out_shape=pltpu.VMEM((half, features), jnp.float32),
-        scratch_shapes=half_scratch(b_blocks[0]),
+        scratch_shapes=[pltpu.VMEM((half, features), jnp.bfloat16)],
         compiler_params=params(),
         cost_estimate=cost(1, half, half, features),
         name="last",
@@ -410,21 +423,14 @@
     core = lax.axis_index("core")
     first = core == 0
     core_arr = core.astype(jnp.int32).reshape(1)
-    theirs = swap(jnp.concatenate([images, texts], axis=0))
-    joined = lambda lead, follow: jnp.concatenate([lead, follow], axis=0)
-    own = jnp.where(first, joined(images, theirs[:rows]), joined(texts, theirs[rows:]))
-    other = jnp.where(first, joined(theirs[rows:], texts), joined(theirs[:rows], images))
-    near = {m: to_cube(own, m) for m in (1, 2, 4)}
+    own, other = own_call(core_arr, images, texts, swap(images), swap(texts))
+    near = {m: to_cube(own, m) for m in (4, 2, 1)}
     far = {7: to_cube(near[1], 6), 5: to_cube(near[1], 4), 3: to_cube(near[2], 1), 6: to_cube(near[4], 2)}
     blocks = {0: own, **near, **far}
-    held = lax.optimization_barrier(tuple(blocks[m] for m in (1, 2, 4, 5)))
-    swapped = {0: other}
-    for m, a in zip((1, 2, 4, 5), held):
-        swapped[m] = swap(a)
-    for m in (3, 6, 7):
-        swapped[m] = swap(blocks[m])
-    a_blocks = [blocks[m] for m in ORDER]
-    b_blocks = [swapped[m] for m in ORDER]
+    in_vmem = lambda a: pltpu.with_memory_space_constraint(a, pltpu.VMEM)
+    a_blocks = [in_vmem(blocks[m]) for m in ORDER]
+    b_blocks = [other, swap(join_call(near[1], near[2], near[4]))] + [swap(far[m]) for m in ORDER[4:]]
+    b_blocks = [in_vmem(b) for b in b_blocks]
 
     e, a_stat, b_stat, flags = scores_call(core_arr, a_blocks, b_blocks, scale)
     a_lse = merge_call(a_stat, swap(b_stat), 0)

time: 128 us -> 118 us (0.922)
  Pallas kernels: 47.2 us -> 35.9 us
  waiting for transfers between devices: 32.5 us -> 40.6 us
  starting transfers between devices: 43.7 us -> 37.7 us
  other arithmetic: 4 us -> 1.34 us
  local copies, waits for them, and re-layouts: 0.08 us -> 1.93 us
    ppermute x17, waiting for transfers between devices: 23.4 us -> 33.4 us  [to_cube(): return lax.ppermute(a, AXES, across(m))]
    ppermute x17, starting transfers between devices: 39.8 us -> 31.7 us  [to_cube(): return lax.ppermute(a, AXES, across(m))]
    pallas_call x2 -> x4, Pallas kernels: 14 us -> 8.76 us  [the longest x1 5.76 us: middle_call(): pl.pallas_call(middle_kernel, in_specs=[smem_spec()] + [vmem_spec()] * 15...]
    pallas_call x1, Pallas kernels: 23.7 us -> 18.8 us  [scores_call(): pl.pallas_call(functools.partial(scores_kernel, scale), in_specs=[smem_sp...]
    ppermute x14 -> x13, starting transfers between devices: 3.94 us -> 6.02 us  [swap(): return lax.ppermute(a, AXES, SWAP)]
    ppermute x14 -> x13, waiting for transfers between devices: 9.12 us -> 7.19 us  [swap(): return lax.ppermute(a, AXES, SWAP)]
    unnamed x4 -> x8, local copies, waits for them, and re-layouts: 0.01 us -> 1.9 us
    select_n x1 -> x0, other arithmetic: 1.55 us -> none  [body(): jnp.where(first, joined(theirs[rows:], texts), joined(theirs[:rows], imag...]
  transfers between devices with their start and end apart: 31 -> 30, of which waited for: 19 -> 19; matrix products, arithmetic and copies ran while one was open for 0% -> 0% of each run, Pallas kernels for 12% -> 8%
where the time goes in v6:
time: 118 us
  waiting for transfers between devices  40.6 us (34%)
  starting transfers between devices  37.7 us (32%)
  Pallas kernels  35.9 us (30%)
  local copies, waits for them, and re-layouts  1.93 us (2%)
  other arithmetic  1.34 us (1%)
    ppermute x17, waiting for transfers between devices, to_cube(): return lax.ppermute(a, AXES, across(m))  33.4 us
    ppermute x17, starting transfers between devices, to_cube(): return lax.ppermute(a, AXES, across(m))  31.7 us
    pallas_call x1, Pallas kernels, scores_call(): pl.pallas_call(functools.partial(scores_kernel, scale), in_specs=[smem_sp...  18.8 us
    pallas_call x1, Pallas kernels, weights_call(): pl.pallas_call(weights_kernel, in_specs=[smem_spec()] * 2 + [vmem_spec()]...  7.36 us
    ppermute x13, waiting for transfers between devices, swap(): return lax.ppermute(a, AXES, SWAP)  7.19 us
    ppermute x13, starting transfers between devices, swap(): return lax.ppermute(a, AXES, SWAP)  6.02 us
    pallas_call x1, Pallas kernels, middle_call(): pl.pallas_call(middle_kernel, in_specs=[smem_spec()] + [vmem_spec()] * 15...  5.76 us
    pallas_call x1, Pallas kernels, last_call(): pl.pallas_call(last_kernel, in_specs=[smem_spec()] + [vmem_spec()] * 7, o...  2.84 us
  transfers between devices with their start and end apart: 30, of which 19 were waited for; matrix products, arithmetic and copies ran while one was open for 0% of the time, Pallas kernels for 8%

profile of v6, /device:TPU:1, one launch (start us, length us, event | category | flops | bytes accessed | tf_op | source)
XLA Modules:
  0.0 118.3 jit_solution(15721570667666736808)
XLA Ops:
  0.6 1.5 %collective-permute-start = (bf16[160,768]{1,0:T(8,128)(2,1)}, bf16[160,768]{1,0:T(8,128)(2,1)S(1)}, u32[]{:S(2)}, u32[]{:S(2)}) collective-permute-start(bf16[160,768]{1,0:T(8,128)(2,1)} %images.1), channel_id=1, source_target_pairs={{0,16},{1,17},{2,18},{3,19},{4,20},{5,21},{6,22},{7,23},{8,24},{9,... | collective-permute-start | bytes 737288 | tf_op jit(solution)/shard_map/ppermute | solution.py:57
  2.1 0.1 collective-permute-start.1
  2.2 1.3 %collective-permute-done.got_images = bf16[160,768]{1,0:T(8,128)(2,1)S(1)} collective-permute-done((bf16[160,768]{1,0:T(8,128)(2,1)}, bf16[160,768]{1,0:T(8,128)(2,1)S(1)}, u32[]{:S(2)}, u32[]{:S(2)}) %collective-permute-start) | collective-permute-done | bytes 245792 | tf_op jit(solution)/shard_map/ppermute | solution.py:57
  3.5 0.4 collective-permute-done.1.got_texts
  3.9 0.9 copy-done
  4.8 0.9 copy-done.2
  5.7 0.1 own.1
  5.8 2.6 %collective-permute-start.2 = (bf16[320,768]{1,0:T(8,128)(2,1)S(1)}, bf16[320,768]{1,0:T(8,128)(2,1)S(1)}, u32[]{:S(2)}, u32[]{:S(2)}) collective-permute-start(bf16[320,768]{1,0:T(8,128)(2,1)S(1)} %get-tuple-element.21.refs_0_), channel_id=1, source_target_pairs={{0,4},{1,5},{2,6},{3,7},{4,0},{5,1},{6,2},{7,3},{8,12},{9,13},{10,... | collective-permute-start | bytes 1474568 | tf_op jit(solution)/shard_map/ppermute | solution.py:53
  8.5 2.7 %collective-permute-start.3 = (bf16[320,768]{1,0:T(8,128)(2,1)S(1)}, bf16[320,768]{1,0:T(8,128)(2,1)S(1)}, u32[]{:S(2)}, u32[]{:S(2)}) collective-permute-start(bf16[320,768]{1,0:T(8,128)(2,1)S(1)} %get-tuple-element.21.refs_0_), channel_id=1, source_target_pairs={{0,32},{1,33},{2,34},{3,35},{4,36},{5,37},{6,38},{7,39},{8,40},{9,... | collective-permute-start | bytes 1474568 | tf_op jit(solution)/shard_map/ppermute | solution.py:53
  11.2 3.8 %collective-permute-start.4 = (bf16[320,768]{1,0:T(8,128)(2,1)S(1)}, bf16[320,768]{1,0:T(8,128)(2,1)S(1)}, u32[]{:S(2)}, u32[]{:S(2)}) collective-permute-start(bf16[320,768]{1,0:T(8,128)(2,1)S(1)} %get-tuple-element.21.refs_0_), channel_id=1, source_target_pairs={{0,1},{1,0},{2,3},{3,2},{4,5},{5,4},{6,7},{7,6},{8,9},{9,8},{10,11... | collective-permute-start | bytes 1474568 | tf_op jit(solution)/shard_map/ppermute | solution.py:53
  14.9 0.0 collective-permute-done.2.b0.refs_1_
  14.9 2.5 %collective-permute-done.3.b1.refs_2_ = bf16[320,768]{1,0:T(8,128)(2,1)S(1)} collective-permute-done((bf16[320,768]{1,0:T(8,128)(2,1)S(1)}, bf16[320,768]{1,0:T(8,128)(2,1)S(1)}, u32[]{:S(2)}, u32[]{:S(2)}) %collective-permute-start.3) | collective-permute-done | bytes 491552 | tf_op jit(solution)/shard_map/ppermute | solution.py:53
  17.4 3.8 %collective-permute-done.4.b2.refs_3_ = bf16[320,768]{1,0:T(8,128)(2,1)S(1)} collective-permute-done((bf16[320,768]{1,0:T(8,128)(2,1)S(1)}, bf16[320,768]{1,0:T(8,128)(2,1)S(1)}, u32[]{:S(2)}, u32[]{:S(2)}) %collective-permute-start.4) | collective-permute-done | bytes 491552 | tf_op jit(solution)/shard_map/ppermute | solution.py:53
  21.2 0.1 join.1
  21.3 0.1 collective-permute-start.9
  21.4 2.8 %collective-permute-start.6 = (bf16[320,768]{1,0:T(8,128)(2,1)S(1)}, bf16[320,768]{1,0:T(8,128)(2,1)S(1)}, u32[]{:S(2)}, u32[]{:S(2)}) collective-permute-start(bf16[320,768]{1,0:T(8,128)(2,1)S(1)} %collective-permute-done.2.b0.refs_1_), channel_id=1, source_target_pairs={{0,1},{1,0},{2,3},{3,2},{4,5},{5,4},{6,7},{7,6},{8,9},{9,8},{10,11... | collective-permute-start | bytes 1474568 | tf_op jit(solution)/shard_map/ppermute | solution.py:53
  24.1 0.0 collective-permute-start.8
  24.1 1.5 %collective-permute-start.5 = (bf16[320,768]{1,0:T(8,128)(2,1)S(1)}, bf16[320,768]{1,0:T(8,128)(2,1)S(1)}, u32[]{:S(2)}, u32[]{:S(2)}) collective-permute-start(bf16[320,768]{1,0:T(8,128)(2,1)S(1)} %collective-permute-done.3.b1.refs_2_), channel_id=1, source_target_pairs={{0,4},{1,5},{2,6},{3,7},{4,0},{5,1},{6,2},{7,3},{8,12},{9,13},{10,... | collective-permute-start | bytes 1474568 | tf_op jit(solution)/shard_map/ppermute | solution.py:53
  25.6 1.2 %collective-permute-start.7 = (bf16[320,768]{1,0:T(8,128)(2,1)S(1)}, bf16[320,768]{1,0:T(8,128)(2,1)S(1)}, u32[]{:S(2)}, u32[]{:S(2)}) collective-permute-start(bf16[320,768]{1,0:T(8,128)(2,1)S(1)} %collective-permute-done.4.b2.refs_3_), channel_id=1, source_target_pairs={{0,32},{1,33},{2,34},{3,35},{4,36},{5,37},{6,38},{7,39},{8,40},{9,... | collective-permute-start | bytes 1474568 | tf_op jit(solution)/shard_map/ppermute | solution.py:53
  26.8 8.8 %collective-permute-done.6.refs_5_ = bf16[320,768]{1,0:T(8,128)(2,1)S(1)} collective-permute-done((bf16[320,768]{1,0:T(8,128)(2,1)S(1)}, bf16[320,768]{1,0:T(8,128)(2,1)S(1)}, u32[]{:S(2)}, u32[]{:S(2)}) %collective-permute-start.6) | collective-permute-done | bytes 491552 | tf_op jit(solution)/shard_map/ppermute | solution.py:53
  35.6 0.4 collective-permute-start.11
  36.0 0.0 collective-permute-done.8.refs_7_
  36.0 0.2 collective-permute-start.13
  36.1 0.4 collective-permute-start.10
  36.5 1.7 %collective-permute-done.7.refs_6_ = bf16[320,768]{1,0:T(8,128)(2,1)S(1)} collective-permute-done((bf16[320,768]{1,0:T(8,128)(2,1)S(1)}, bf16[320,768]{1,0:T(8,128)(2,1)S(1)}, u32[]{:S(2)}, u32[]{:S(2)}) %collective-permute-start.7) | collective-permute-done | bytes 491552 | tf_op jit(solution)/shard_map/ppermute | solution.py:53
  38.1 0.0 collective-permute-start.12
  38.1 0.0 collective-permute-done.13.refs_13_.refs_5_
  38.2 0.7 collective-permute-done.10.refs_10_.refs_2_
  38.9 1.1 collective-permute-done.12.refs_12_.refs_4_
  40.0 18.8 %scores.1 = (f32[2,1280,1280]{2,1,0:T(8,128)S(1)}, f32[8,320]{1,0:T(8,128)S(1)}, f32[8,320]{1,0:T(8,128)S(1)}, s32[2]{0:T(128)S(1)}) custom-call(s32[1]{0:T(128)} %bitcast.core_ref, bf16[320,768]{1,0:T(8,128)(2,1)S(1)} %get-tuple-element.21.refs_0_, bf16[320,768]{1,0:T(8,128)(2,1)S(1)} %collective-permute-done.2.b0.refs_1_, ...), custom_call_target="tpu_custom_call" | custom-call | flops 5033164800 | tf_op jit(solution)/shard_map/scores/pallas_call | solution.py:234
  58.8 0.2 collective-permute-start.14
  59.1 1.0 collective-permute-done.14.got_ref
  60.1 0.3 collective-permute-start.15
  60.4 3.6 %collective-permute-done.15.got_ref = f32[8,320]{1,0:T(8,128)S(1)} collective-permute-done((f32[8,320]{1,0:T(8,128)S(1)}, f32[8,320]{1,0:T(8,128)S(1)}, u32[]{:S(2)}, u32[]{:S(2)}) %collective-permute-start.15) | collective-permute-done | bytes 10272 | tf_op jit(solution)/shard_map/ppermute | solution.py:53
  64.0 0.3 collective-permute-start.16
  64.3 3.6 %collective-permute-done.16.got_ref = f32[8,320]{1,0:T(8,128)S(1)} collective-permute-done((f32[8,320]{1,0:T(8,128)S(1)}, f32[8,320]{1,0:T(8,128)S(1)}, u32[]{:S(2)}, u32[]{:S(2)}) %collective-permute-start.16) | collective-permute-done | bytes 10272 | tf_op jit(solution)/shard_map/ppermute | solution.py:53
  67.9 2.6 %collective-permute-start.17 = (f32[8,320]{1,0:T(8,128)S(1)}, f32[8,320]{1,0:T(8,128)S(1)}, u32[]{:S(2)}, u32[]{:S(2)}) collective-permute-start(f32[8,320]{1,0:T(8,128)S(1)} %merge.6.mine_ref), channel_id=1, source_target_pairs={{0,1},{1,0},{2,3},{3,2},{4,5},{5,4},{6,7},{7,6},{8,9},{9,8},{10,11... | collective-permute-start | bytes 30728 | tf_op jit(solution)/shard_map/ppermute | solution.py:53
  70.5 1.2 %collective-permute-done.17.got_ref = f32[8,320]{1,0:T(8,128)S(1)} collective-permute-done((f32[8,320]{1,0:T(8,128)S(1)}, f32[8,320]{1,0:T(8,128)S(1)}, u32[]{:S(2)}, u32[]{:S(2)}) %collective-permute-start.17) | collective-permute-done | bytes 10272 | tf_op jit(solution)/shard_map/ppermute | solution.py:53
  71.7 0.1 collective-permute-start.18
  71.8 1.2 collective-permute-done.18.b_lse
  73.0 7.4 %weights.1 = (bf16[2,1280,1280]{2,1,0:T(8,128)(2,1)S(1)}, bf16[1280,768]{1,0:T(8,128)(2,1)S(1)}) custom-call(s32[1]{0:T(128)} %bitcast.core_ref, s32[2]{0:T(128)S(1)} %get-tuple-element.23.flags, f32[2,1280,1280]{2,1,0:T(8,128)S(1)} %get-tuple-element.24.e_ref, f32[8,320]{1,0:T(8,128)S(1)} %merge.7.a_lse, f32[8,320]{1,0:T(8,128)S(1)} %collective-permute-done.18.b_lse, ...), custom_call_target="tpu_custom_call" | custom-call | flops 2516582400 | bytes 19660800 | tf_op jit(solution)/shard_map/weights/pallas_call | solution.py:307
  80.4 0.2 collective-permute-start.21
  80.6 5.8 %middle.1 = (f32[1280,768]{1,0:T(8,128)S(1)}, f32[320,768]{1,0:T(8,128)S(1)}, bf16[960,768]{1,0:T(8,128)(2,1)S(1)}) custom-call(s32[1]{0:T(128)} %bitcast.core_ref, bf16[2,1280,1280]{2,1,0:T(8,128)(2,1)S(1)} %get-tuple-element.27.w_ref, bf16[320,768]{1,0:T(8,128)(2,1)S(1)} %get-tuple-element.21.refs_0_, ...), custom_call_target="tpu_custom_call" | custom-call | flops 5033164800 | tf_op jit(solution)/shard_map/middle/pallas_call | solution.py:338
  86.4 0.4 collective-permute-start.20
  86.8 0.2 collective-permute-start.19
  87.0 0.3 far.1
  87.3 0.3 collective-permute-start.22
  87.6 1.5 %collective-permute-start.23 = (bf16[320,768]{1,0:T(8,128)(2,1)S(1)}, bf16[320,768]{1,0:T(8,128)(2,1)S(1)}, u32[]{:S(2)}, u32[]{:S(2)}) collective-permute-start(bf16[320,768]{1,0:T(8,128)(2,1)S(1)} %get-tuple-element.33), channel_id=1, source_target_pairs={{0,32},{1,33},{2,34},{3,35},{4,36},{5,37},{6,38},{7,39},{8,40},{9,... | collective-permute-start | bytes 1474568 | tf_op jit(solution)/shard_map/ppermute | solution.py:53
  89.0 2.7 %collective-permute-start.24 = (bf16[320,768]{1,0:T(8,128)(2,1)S(1)}, bf16[320,768]{1,0:T(8,128)(2,1)S(1)}, u32[]{:S(2)}, u32[]{:S(2)}) collective-permute-start(bf16[320,768]{1,0:T(8,128)(2,1)S(1)} %get-tuple-element.34), channel_id=1, source_target_pairs={{0,1},{1,0},{2,3},{3,2},{4,5},{5,4},{6,7},{7,6},{8,9},{9,8},{10,11... | collective-permute-start | bytes 1474568 | tf_op jit(solution)/shard_map/ppermute | solution.py:53
  91.7 2.8 %last.1.ga_lo = f32[1280,768]{1,0:T(8,128)S(1)} custom-call(s32[1]{0:T(128)} %bitcast.core_ref, bf16[2,1280,1280]{2,1,0:T(8,128)(2,1)S(1)} %get-tuple-element.27.w_ref, bf16[320,768]{1,0:T(8,128)(2,1)S(1)} %get-tuple-element.22.refs_8_.refs_0_, bf16[960,768]{1,0:T(8,128)(2,1)S(1)} %collective-permute-done.9.refs_9_.refs_1_, ...), custom_call_target="tpu_custom_call" | custom-call | flops 2516582400 | tf_op jit(solution)/shard_map/last/pallas_call | solution.py:384
  94.6 3.2 %collective-permute-start.25 = (bf16[320,768]{1,0:T(8,128)(2,1)S(1)}, bf16[320,768]{1,0:T(8,128)(2,1)S(1)}, u32[]{:S(2)}, u32[]{:S(2)}) collective-permute-start(bf16[320,768]{1,0:T(8,128)(2,1)S(1)} %get-tuple-element.36), channel_id=1, source_target_pairs={{0,37},{1,36},{2,39},{3,38},{4,33},{5,32},{6,35},{7,34},{8,45},{9,... | collective-permute-start | bytes 1474568 | tf_op jit(solution)/shard_map/ppermute | solution.py:53
  97.8 0.4 collective-permute-done.24.r_xz
  98.2 0.5 near.1
  98.8 1.3 %collective-permute-start.26 = (bf16[320,768]{1,0:T(8,128)(2,1)S(1)}, bf16[320,768]{1,0:T(8,128)(2,1)S(1)}, u32[]{:S(2)}, u32[]{:S(2)}) collective-permute-start(bf16[320,768]{1,0:T(8,128)(2,1)S(1)} %get-tuple-element.37), channel_id=1, source_target_pairs={{0,4},{1,5},{2,6},{3,7},{4,0},{5,1},{6,2},{7,3},{8,12},{9,13},{10,... | collective-permute-start | bytes 1474568 | tf_op jit(solution)/shard_map/ppermute | solution.py:53
  100.0 2.5 %collective-permute-start.27 = (bf16[320,768]{1,0:T(8,128)(2,1)S(1)}, bf16[320,768]{1,0:T(8,128)(2,1)S(1)}, u32[]{:S(2)}, u32[]{:S(2)}) collective-permute-start(bf16[320,768]{1,0:T(8,128)(2,1)S(1)} %get-tuple-element.38), channel_id=1, source_target_pairs={{0,32},{1,33},{2,34},{3,35},{4,36},{5,37},{6,38},{7,39},{8,40},{9,... | collective-permute-start | bytes 1474568 | tf_op jit(solution)/shard_map/ppermute | solution.py:53
  102.5 2.6 %collective-permute-start.28 = (bf16[320,768]{1,0:T(8,128)(2,1)S(1)}, bf16[320,768]{1,0:T(8,128)(2,1)S(1)}, u32[]{:S(2)}, u32[]{:S(2)}) collective-permute-start(bf16[320,768]{1,0:T(8,128)(2,1)S(1)} %get-tuple-element.39), channel_id=1, source_target_pairs={{0,1},{1,0},{2,3},{3,2},{4,5},{5,4},{6,7},{7,6},{8,9},{9,8},{10,11... | collective-permute-start | bytes 1474568 | tf_op jit(solution)/shard_map/ppermute | solution.py:53
  105.1 2.8 %collective-permute-done.25 = bf16[320,768]{1,0:T(8,128)(2,1)S(1)} collective-permute-done((bf16[320,768]{1,0:T(8,128)(2,1)S(1)}, bf16[320,768]{1,0:T(8,128)(2,1)S(1)}, u32[]{:S(2)}, u32[]{:S(2)}) %collective-permute-start.25) | collective-permute-done | bytes 491552 | tf_op jit(solution)/shard_map/ppermute | solution.py:53
  107.9 1.5 %collective-permute-done.26 = bf16[320,768]{1,0:T(8,128)(2,1)S(1)} collective-permute-done((bf16[320,768]{1,0:T(8,128)(2,1)S(1)}, bf16[320,768]{1,0:T(8,128)(2,1)S(1)}, u32[]{:S(2)}, u32[]{:S(2)}) %collective-permute-start.26) | collective-permute-done | bytes 491552 | tf_op jit(solution)/shard_map/ppermute | solution.py:53
  109.4 1.2 %collective-permute-done.27 = bf16[320,768]{1,0:T(8,128)(2,1)S(1)} collective-permute-done((bf16[320,768]{1,0:T(8,128)(2,1)S(1)}, bf16[320,768]{1,0:T(8,128)(2,1)S(1)}, u32[]{:S(2)}, u32[]{:S(2)}) %collective-permute-start.27) | collective-permute-done | bytes 491552 | tf_op jit(solution)/shard_map/ppermute | solution.py:53
  110.6 2.4 %collective-permute-done.28 = bf16[320,768]{1,0:T(8,128)(2,1)S(1)} collective-permute-done((bf16[320,768]{1,0:T(8,128)(2,1)S(1)}, bf16[320,768]{1,0:T(8,128)(2,1)S(1)}, u32[]{:S(2)}, u32[]{:S(2)}) %collective-permute-start.28) | collective-permute-done | bytes 491552 | tf_op jit(solution)/shard_map/ppermute | solution.py:53
  113.1 0.3 convert_add_fusion
  113.4 2.3 %collective-permute-start.29 = (f32[160,768]{1,0:T(8,128)S(1)}, f32[160,768]{1,0:T(8,128)S(1)}, u32[]{:S(2)}, u32[]{:S(2)}) collective-permute-start(f32[160,768]{1,0:T(8,128)S(1)} %slice.9), channel_id=1, source_target_pairs={{0,16},{1,17},{2,18},{3,19},{4,20},{5,21},{6,22},{7,23},{8,24},{9,... | collective-permute-start | bytes 1474568 | tf_op jit(solution)/shard_map/ppermute | solution.py:57
  115.7 1.5 %collective-permute-done.29 = f32[160,768]{1,0:T(8,128)S(1)} collective-permute-done((f32[160,768]{1,0:T(8,128)S(1)}, f32[160,768]{1,0:T(8,128)S(1)}, u32[]{:S(2)}, u32[]{:S(2)}) %collective-permute-start.29) | collective-permute-done | bytes 491552 | tf_op jit(solution)/shard_map/ppermute | solution.py:57
  117.2 1.0 convert_subtract_fusion
  (19 shorter events, 0.2 us)
Async XLA Ops:
  0.6 2.9 %collective-permute-start = (bf16[160,768]{1,0:T(8,128)(2,1)}, bf16[160,768]{1,0:T(8,128)(2,1)S(1)}, u32[]{:S(2)}, u32[]{:S(2)}) collective-permute-start(bf16[160,768]{1,0:T(8,128)(2,1)} %images.1), channel_id=1, source_target_pairs={{0,16},{1,17},{2,18},{3,19},{4,20},{5,21},{6,22},{7,23},{8,24},{9,... | collective-permute-start | bytes 737288 | tf_op jit(solution)/shard_map/ppermute | solution.py:57
  2.1 1.7 %collective-permute-start.1 = (bf16[160,768]{1,0:T(8,128)(2,1)}, bf16[160,768]{1,0:T(8,128)(2,1)S(1)}, u32[]{:S(2)}, u32[]{:S(2)}) collective-permute-start(bf16[160,768]{1,0:T(8,128)(2,1)} %texts.1), channel_id=1, source_target_pairs={{0,16},{1,17},{2,18},{3,19},{4,20},{5,21},{6,22},{7,23},{8,24},{9,... | collective-permute-start | bytes 737288 | tf_op jit(solution)/shard_map/ppermute | solution.py:57
  3.9 0.9 copy-start
  4.8 0.9 copy-start.2
  5.8 9.1 %collective-permute-start.2 = (bf16[320,768]{1,0:T(8,128)(2,1)S(1)}, bf16[320,768]{1,0:T(8,128)(2,1)S(1)}, u32[]{:S(2)}, u32[]{:S(2)}) collective-permute-start(bf16[320,768]{1,0:T(8,128)(2,1)S(1)} %get-tuple-element.21.refs_0_), channel_id=1, source_target_pairs={{0,4},{1,5},{2,6},{3,7},{4,0},{5,1},{6,2},{7,3},{8,12},{9,13},{10,... | collective-permute-start | bytes 1474568 | tf_op jit(solution)/shard_map/ppermute | solution.py:53
  8.5 9.0 %collective-permute-start.3 = (bf16[320,768]{1,0:T(8,128)(2,1)S(1)}, bf16[320,768]{1,0:T(8,128)(2,1)S(1)}, u32[]{:S(2)}, u32[]{:S(2)}) collective-permute-start(bf16[320,768]{1,0:T(8,128)(2,1)S(1)} %get-tuple-element.21.refs_0_), channel_id=1, source_target_pairs={{0,32},{1,33},{2,34},{3,35},{4,36},{5,37},{6,38},{7,39},{8,40},{9,... | collective-permute-start | bytes 1474568 | tf_op jit(solution)/shard_map/ppermute | solution.py:53
  11.2 10.0 %collective-permute-start.4 = (bf16[320,768]{1,0:T(8,128)(2,1)S(1)}, bf16[320,768]{1,0:T(8,128)(2,1)S(1)}, u32[]{:S(2)}, u32[]{:S(2)}) collective-permute-start(bf16[320,768]{1,0:T(8,128)(2,1)S(1)} %get-tuple-element.21.refs_0_), channel_id=1, source_target_pairs={{0,1},{1,0},{2,3},{3,2},{4,5},{5,4},{6,7},{7,6},{8,9},{9,8},{10,11... | collective-permute-start | bytes 1474568 | tf_op jit(solution)/shard_map/ppermute | solution.py:53
  21.3 18.7 %collective-permute-start.9 = (bf16[960,768]{1,0:T(8,128)(2,1)S(1)}, bf16[960,768]{1,0:T(8,128)(2,1)S(1)}, u32[]{:S(2)}, u32[]{:S(2)}) collective-permute-start(bf16[960,768]{1,0:T(8,128)(2,1)S(1)} %join.1), channel_id=1, source_target_pairs={{0,16},{1,17},{2,18},{3,19},{4,20},{5,21},{6,22},{7,23},{8,24},{9,... | collective-permute-start | bytes 4423688 | tf_op jit(solution)/shard_map/ppermute | solution.py:57
  21.4 14.2 %collective-permute-start.6 = (bf16[320,768]{1,0:T(8,128)(2,1)S(1)}, bf16[320,768]{1,0:T(8,128)(2,1)S(1)}, u32[]{:S(2)}, u32[]{:S(2)}) collective-permute-start(bf16[320,768]{1,0:T(8,128)(2,1)S(1)} %collective-permute-done.2.b0.refs_1_), channel_id=1, source_target_pairs={{0,1},{1,0},{2,3},{3,2},{4,5},{5,4},{6,7},{7,6},{8,9},{9,8},{10,11... | collective-permute-start | bytes 1474568 | tf_op jit(solution)/shard_map/ppermute | solution.py:53
  24.1 11.8 %collective-permute-start.8 = (bf16[320,768]{1,0:T(8,128)(2,1)S(1)}, bf16[320,768]{1,0:T(8,128)(2,1)S(1)}, u32[]{:S(2)}, u32[]{:S(2)}) collective-permute-start(bf16[320,768]{1,0:T(8,128)(2,1)S(1)} %collective-permute-done.2.b0.refs_1_), channel_id=1, source_target_pairs={{0,33},{1,32},{2,35},{3,34},{4,37},{5,36},{6,39},{7,38},{8,41},{9,... | collective-permute-start | bytes 1474568 | tf_op jit(solution)/shard_map/ppermute | solution.py:53
  24.1 12.0 %collective-permute-start.5 = (bf16[320,768]{1,0:T(8,128)(2,1)S(1)}, bf16[320,768]{1,0:T(8,128)(2,1)S(1)}, u32[]{:S(2)}, u32[]{:S(2)}) collective-permute-start(bf16[320,768]{1,0:T(8,128)(2,1)S(1)} %collective-permute-done.3.b1.refs_2_), channel_id=1, source_target_pairs={{0,4},{1,5},{2,6},{3,7},{4,0},{5,1},{6,2},{7,3},{8,12},{9,13},{10,... | collective-permute-start | bytes 1474568 | tf_op jit(solution)/shard_map/ppermute | solution.py:53
  25.6 12.5 %collective-permute-start.7 = (bf16[320,768]{1,0:T(8,128)(2,1)S(1)}, bf16[320,768]{1,0:T(8,128)(2,1)S(1)}, u32[]{:S(2)}, u32[]{:S(2)}) collective-permute-start(bf16[320,768]{1,0:T(8,128)(2,1)S(1)} %collective-permute-done.4.b2.refs_3_), channel_id=1, source_target_pairs={{0,32},{1,33},{2,34},{3,35},{4,36},{5,37},{6,38},{7,39},{8,40},{9,... | collective-permute-start | bytes 1474568 | tf_op jit(solution)/shard_map/ppermute | solution.py:53
  35.6 2.5 %collective-permute-start.11 = (bf16[320,768]{1,0:T(8,128)(2,1)S(1)}, bf16[320,768]{1,0:T(8,128)(2,1)S(1)}, u32[]{:S(2)}, u32[]{:S(2)}) collective-permute-start(bf16[320,768]{1,0:T(8,128)(2,1)S(1)} %collective-permute-done.6.refs_5_), channel_id=1, source_target_pairs={{0,16},{1,17},{2,18},{3,19},{4,20},{5,21},{6,22},{7,23},{8,24},{9,... | collective-permute-start | bytes 1474568 | tf_op jit(solution)/shard_map/ppermute | solution.py:57
  36.0 2.2 %collective-permute-start.13 = (bf16[320,768]{1,0:T(8,128)(2,1)S(1)}, bf16[320,768]{1,0:T(8,128)(2,1)S(1)}, u32[]{:S(2)}, u32[]{:S(2)}) collective-permute-start(bf16[320,768]{1,0:T(8,128)(2,1)S(1)} %collective-permute-done.8.refs_7_), channel_id=1, source_target_pairs={{0,16},{1,17},{2,18},{3,19},{4,20},{5,21},{6,22},{7,23},{8,24},{9,... | collective-permute-start | bytes 1474568 | tf_op jit(solution)/shard_map/ppermute | solution.py:57
  36.1 2.8 %collective-permute-start.10 = (bf16[320,768]{1,0:T(8,128)(2,1)S(1)}, bf16[320,768]{1,0:T(8,128)(2,1)S(1)}, u32[]{:S(2)}, u32[]{:S(2)}) collective-permute-start(bf16[320,768]{1,0:T(8,128)(2,1)S(1)} %collective-permute-done.5.refs_4_), channel_id=1, source_target_pairs={{0,16},{1,17},{2,18},{3,19},{4,20},{5,21},{6,22},{7,23},{8,24},{9,... | collective-permute-start | bytes 1474568 | tf_op jit(solution)/shard_map/ppermute | solution.py:57
  38.1 1.9 %collective-permute-start.12 = (bf16[320,768]{1,0:T(8,128)(2,1)S(1)}, bf16[320,768]{1,0:T(8,128)(2,1)S(1)}, u32[]{:S(2)}, u32[]{:S(2)}) collective-permute-start(bf16[320,768]{1,0:T(8,128)(2,1)S(1)} %collective-permute-done.7.refs_6_), channel_id=1, source_target_pairs={{0,16},{1,17},{2,18},{3,19},{4,20},{5,21},{6,22},{7,23},{8,24},{9,... | collective-permute-start | bytes 1474568 | tf_op jit(solution)/shard_map/ppermute | solution.py:57
  58.8 1.3 %collective-permute-start.14 = (f32[8,320]{1,0:T(8,128)S(1)}, f32[8,320]{1,0:T(8,128)S(1)}, u32[]{:S(2)}, u32[]{:S(2)}) collective-permute-start(f32[8,320]{1,0:T(8,128)S(1)} %get-tuple-element.26), channel_id=1, source_target_pairs={{0,16},{1,17},{2,18},{3,19},{4,20},{5,21},{6,22},{7,23},{8,24},{9,... | collective-permute-start | bytes 30728 | tf_op jit(solution)/shard_map/ppermute | solution.py:57
  60.1 3.8 %collective-permute-start.15 = (f32[8,320]{1,0:T(8,128)S(1)}, f32[8,320]{1,0:T(8,128)S(1)}, u32[]{:S(2)}, u32[]{:S(2)}) collective-permute-start(f32[8,320]{1,0:T(8,128)S(1)} %merge.4.mine_ref), channel_id=1, source_target_pairs={{0,4},{1,5},{2,6},{3,7},{4,0},{5,1},{6,2},{7,3},{8,12},{9,13},{10,... | collective-permute-start | bytes 30728 | tf_op jit(solution)/shard_map/ppermute | solution.py:53
  64.0 3.8 %collective-permute-start.16 = (f32[8,320]{1,0:T(8,128)S(1)}, f32[8,320]{1,0:T(8,128)S(1)}, u32[]{:S(2)}, u32[]{:S(2)}) collective-permute-start(f32[8,320]{1,0:T(8,128)S(1)} %merge.5.mine_ref), channel_id=1, source_target_pairs={{0,32},{1,33},{2,34},{3,35},{4,36},{5,37},{6,38},{7,39},{8,40},{9,... | collective-permute-start | bytes 30728 | tf_op jit(solution)/shard_map/ppermute | solution.py:53
  67.9 3.8 %collective-permute-start.17 = (f32[8,320]{1,0:T(8,128)S(1)}, f32[8,320]{1,0:T(8,128)S(1)}, u32[]{:S(2)}, u32[]{:S(2)}) collective-permute-start(f32[8,320]{1,0:T(8,128)S(1)} %merge.6.mine_ref), channel_id=1, source_target_pairs={{0,1},{1,0},{2,3},{3,2},{4,5},{5,4},{6,7},{7,6},{8,9},{9,8},{10,11... | collective-permute-start | bytes 30728 | tf_op jit(solution)/shard_map/ppermute | solution.py:53
  71.7 1.3 %collective-permute-start.18 = (f32[8,320]{1,0:T(8,128)S(1)}, f32[8,320]{1,0:T(8,128)S(1)}, u32[]{:S(2)}, u32[]{:S(2)}) collective-permute-start(f32[8,320]{1,0:T(8,128)S(1)} %merge.7.a_lse), channel_id=1, source_target_pairs={{0,16},{1,17},{2,18},{3,19},{4,20},{5,21},{6,22},{7,23},{8,24},{9,... | collective-permute-start | bytes 30728 | tf_op jit(solution)/shard_map/ppermute | solution.py:57
  80.4 6.6 %collective-permute-start.21 = (bf16[1280,768]{1,0:T(8,128)(2,1)S(1)}, bf16[1280,768]{1,0:T(8,128)(2,1)S(1)}, u32[]{:S(2)}, u32[]{:S(2)}) collective-permute-start(bf16[1280,768]{1,0:T(8,128)(2,1)S(1)} %get-tuple-element.31), channel_id=1, source_target_pairs={{0,16},{1,17},{2,18},{3,19},{4,20},{5,21},{6,22},{7,23},{8,24},{9,... | collective-permute-start | bytes 5898248 | tf_op jit(solution)/shard_map/ppermute | solution.py:57
  86.4 11.4 %collective-permute-start.20 = (bf16[960,768]{1,0:T(8,128)(2,1)S(1)}, bf16[960,768]{1,0:T(8,128)(2,1)S(1)}, u32[]{:S(2)}, u32[]{:S(2)}) collective-permute-start(bf16[960,768]{1,0:T(8,128)(2,1)S(1)} %get-tuple-element.29), channel_id=1, source_target_pairs={{0,16},{1,17},{2,18},{3,19},{4,20},{5,21},{6,22},{7,23},{8,24},{9,... | collective-permute-start | bytes 4423688 | tf_op jit(solution)/shard_map/ppermute | solution.py:57
  86.8 7.8 %collective-permute-start.19 = (f32[320,768]{1,0:T(8,128)S(1)}, f32[320,768]{1,0:T(8,128)S(1)}, u32[]{:S(2)}, u32[]{:S(2)}) collective-permute-start(f32[320,768]{1,0:T(8,128)S(1)} %get-tuple-element.28), channel_id=1, source_target_pairs={{0,16},{1,17},{2,18},{3,19},{4,20},{5,21},{6,22},{7,23},{8,24},{9,... | collective-permute-start | bytes 2949128 | tf_op jit(solution)/shard_map/ppermute | solution.py:57
  87.3 10.5 %collective-permute-start.22 = (bf16[320,768]{1,0:T(8,128)(2,1)S(1)}, bf16[320,768]{1,0:T(8,128)(2,1)S(1)}, u32[]{:S(2)}, u32[]{:S(2)}) collective-permute-start(bf16[320,768]{1,0:T(8,128)(2,1)S(1)} %get-tuple-element.32), channel_id=1, source_target_pairs={{0,4},{1,5},{2,6},{3,7},{4,0},{5,1},{6,2},{7,3},{8,12},{9,13},{10,... | collective-permute-start | bytes 1474568 | tf_op jit(solution)/shard_map/ppermute | solution.py:53
  87.6 10.2 %collective-permute-start.23 = (bf16[320,768]{1,0:T(8,128)(2,1)S(1)}, bf16[320,768]{1,0:T(8,128)(2,1)S(1)}, u32[]{:S(2)}, u32[]{:S(2)}) collective-permute-start(bf16[320,768]{1,0:T(8,128)(2,1)S(1)} %get-tuple-element.33), channel_id=1, source_target_pairs={{0,32},{1,33},{2,34},{3,35},{4,36},{5,37},{6,38},{7,39},{8,40},{9,... | collective-permute-start | bytes 1474568 | tf_op jit(solution)/shard_map/ppermute | solution.py:53
  89.0 9.2 %collective-permute-start.24 = (bf16[320,768]{1,0:T(8,128)(2,1)S(1)}, bf16[320,768]{1,0:T(8,128)(2,1)S(1)}, u32[]{:S(2)}, u32[]{:S(2)}) collective-permute-start(bf16[320,768]{1,0:T(8,128)(2,1)S(1)} %get-tuple-element.34), channel_id=1, source_target_pairs={{0,1},{1,0},{2,3},{3,2},{4,5},{5,4},{6,7},{7,6},{8,9},{9,8},{10,11... | collective-permute-start | bytes 1474568 | tf_op jit(solution)/shard_map/ppermute | solution.py:53
  94.6 13.3 %collective-permute-start.25 = (bf16[320,768]{1,0:T(8,128)(2,1)S(1)}, bf16[320,768]{1,0:T(8,128)(2,1)S(1)}, u32[]{:S(2)}, u32[]{:S(2)}) collective-permute-start(bf16[320,768]{1,0:T(8,128)(2,1)S(1)} %get-tuple-element.36), channel_id=1, source_target_pairs={{0,37},{1,36},{2,39},{3,38},{4,33},{5,32},{6,35},{7,34},{8,45},{9,... | collective-permute-start | bytes 1474568 | tf_op jit(solution)/shard_map/ppermute | solution.py:53
  98.8 10.7 %collective-permute-start.26 = (bf16[320,768]{1,0:T(8,128)(2,1)S(1)}, bf16[320,768]{1,0:T(8,128)(2,1)S(1)}, u32[]{:S(2)}, u32[]{:S(2)}) collective-permute-start(bf16[320,768]{1,0:T(8,128)(2,1)S(1)} %get-tuple-element.37), channel_id=1, source_target_pairs={{0,4},{1,5},{2,6},{3,7},{4,0},{5,1},{6,2},{7,3},{8,12},{9,13},{10,... | collective-permute-start | bytes 1474568 | tf_op jit(solution)/shard_map/ppermute | solution.py:53
  100.0 10.6 %collective-permute-start.27 = (bf16[320,768]{1,0:T(8,128)(2,1)S(1)}, bf16[320,768]{1,0:T(8,128)(2,1)S(1)}, u32[]{:S(2)}, u32[]{:S(2)}) collective-permute-start(bf16[320,768]{1,0:T(8,128)(2,1)S(1)} %get-tuple-element.38), channel_id=1, source_target_pairs={{0,32},{1,33},{2,34},{3,35},{4,36},{5,37},{6,38},{7,39},{8,40},{9,... | collective-permute-start | bytes 1474568 | tf_op jit(solution)/shard_map/ppermute | solution.py:53
  102.5 10.5 %collective-permute-start.28 = (bf16[320,768]{1,0:T(8,128)(2,1)S(1)}, bf16[320,768]{1,0:T(8,128)(2,1)S(1)}, u32[]{:S(2)}, u32[]{:S(2)}) collective-permute-start(bf16[320,768]{1,0:T(8,128)(2,1)S(1)} %get-tuple-element.39), channel_id=1, source_target_pairs={{0,1},{1,0},{2,3},{3,2},{4,5},{5,4},{6,7},{7,6},{8,9},{9,8},{10,11... | collective-permute-start | bytes 1474568 | tf_op jit(solution)/shard_map/ppermute | solution.py:53
  113.1 4.2 %copy-start.1 = (bf16[160,768]{1,0:T(8,128)(2,1)S(1)}, bf16[160,768]{1,0:T(8,128)(2,1)}, u32[]{:S(2)}) copy-start(bf16[160,768]{1,0:T(8,128)(2,1)} %images.1) | copy-start | bytes 737284
  113.1 4.2 %copy-start.3 = (bf16[160,768]{1,0:T(8,128)(2,1)S(1)}, bf16[160,768]{1,0:T(8,128)(2,1)}, u32[]{:S(2)}) copy-start(bf16[160,768]{1,0:T(8,128)(2,1)} %texts.1) | copy-start | bytes 737284
  113.4 3.8 %collective-permute-start.29 = (f32[160,768]{1,0:T(8,128)S(1)}, f32[160,768]{1,0:T(8,128)S(1)}, u32[]{:S(2)}, u32[]{:S(2)}) collective-permute-start(f32[160,768]{1,0:T(8,128)S(1)} %slice.9), channel_id=1, source_target_pairs={{0,16},{1,17},{2,18},{3,19},{4,20},{5,21},{6,22},{7,23},{8,24},{9,... | collective-permute-start | bytes 1474568 | tf_op jit(solution)/shard_map/ppermute | solution.py:57

commit v7 on v6

--- a/solution.py
+++ b/solution.py
@@ -29,18 +29,18 @@
                     yield y, c, x, z
 
 
-def partner(v, c):
-    return v ^ 1 if c == 0 else 3 - v
+def partner(v, wrapped):
+    return 3 - v if wrapped else v ^ 1
 
 
 def across(m):
     pairs = []
     for y, c, x, z in coords():
         target = (
-            partner(y, c) if m & 2 else y,
+            partner(y, c == 0) if m & 2 else y,
             c,
-            partner(x, c) if m & 1 else x,
-            partner(z, c) if m & 4 else z,
+            partner(x, c == 1) if m & 1 else x,
+            partner(z, c == 1) if m & 4 else z,
         )
         pairs.append((flat(y, c, x, z), flat(*target)))
     return pairs
@@ -99,33 +99,35 @@
     return lax.dot_general(a, b, (((0,), (0,)), ((), ())), preferred_element_type=jnp.float32)
 
 
-def own_kernel(core_ref, images, texts, got_images, got_texts, own, other):
+def own_kernel(core_ref, images, texts, got_images, got_texts, own, other, sem):
     rows = images.shape[0]
     core = core_ref[0]
-
-    @pl.when(core == 0)
-    def _():
-        own[:rows] = images[...]
-        own[rows:] = got_images[...]
-        other[:rows] = got_texts[...]
-        other[rows:] = texts[...]
-
-    @pl.when(core != 0)
-    def _():
-        own[:rows] = texts[...]
-        own[rows:] = got_texts[...]
-        other[:rows] = got_images[...]
-        other[rows:] = images[...]
+    top, low = pl.ds(0, rows), pl.ds(rows, rows)
+    orders = ((images, got_images, got_texts, texts), (texts, got_texts, got_images, images))
+
+    def copies(order):
+        places = (own.at[top], own.at[low], other.at[top], other.at[low])
+        return [pltpu.make_async_copy(a, p, sem.at[j]) for j, (a, p) in enumerate(zip(order, places))]
+
+    for c in range(2):
+
+        @pl.when(core == c)
+        def _():
+            for copy in copies(orders[c]):
+                copy.start()
+            for copy in copies(orders[c]):
+                copy.wait()
 
 
 def own_call(core, *parts):
     rows, features = parts[0].shape
-    block = jax.ShapeDtypeStruct((2 * rows, features), parts[0].dtype)
+    block = pltpu.VMEM((2 * rows, features), parts[0].dtype)
     return pl.pallas_call(
         own_kernel,
-        in_specs=[smem_spec()] + [vmem_spec()] * 4,
+        in_specs=[smem_spec()] + [pl.BlockSpec(memory_space=pl.ANY)] * 4,
         out_specs=[vmem_spec()] * 2,
         out_shape=[block, block],
+        scratch_shapes=[pltpu.SemaphoreType.DMA((4,))],
         compiler_params=params(),
         cost_estimate=cost(0, rows, features, 1, 16),
         name="own",
@@ -298,7 +300,8 @@
                 s = e_ref[q, sl, :]
                 w_ref[q, sl, :] = (jnp.exp2(s - a_col[sl, :]) + jnp.exp2(s - b_row)).astype(jnp.bfloat16)
 
-    gb_hi[...] = (0.5 * dot_tn(w_ref[1 - core], a_half[...])).astype(jnp.bfloat16)
+    half_rows = gb_hi.shape[0]
+    gb_hi[...] = (0.5 * dot_tn(w_ref[1 - core, :, :half_rows], a_half[...])).astype(jnp.bfloat16)
 
 
 def weights_call(core, flags, e, a_lse, b_lse, a_blocks):
@@ -310,7 +313,7 @@
         out_specs=[vmem_spec()] * 2,
         out_shape=[
             pltpu.VMEM((2, half, half), jnp.bfloat16),
-            jax.ShapeDtypeStruct((half, features), jnp.bfloat16),
+            jax.ShapeDtypeStruct((2 * rows, features), jnp.bfloat16),
         ],
         scratch_shapes=[pltpu.VMEM((half, features), jnp.bfloat16)],
         compiler_params=params(),
@@ -319,77 +322,95 @@
     )(core, flags, e, a_lse, b_lse, *a_blocks)
 
 
-def middle_kernel(core_ref, w_ref, *refs):
-    a_refs, b_refs = refs[:8], views(refs[8:14])
-    ga_hi, gb0, gb_lo, a_half, b_half = refs[14:]
+def second_kernel(core_ref, w_ref, *refs):
+    a_refs, (gb, a_half) = refs[:8], refs[8:]
+    core = core_ref[0]
+    take_half(core, a_refs, 1, a_half)
+    gb[...] = (0.5 * dot_tn(w_ref[1 - core, :, gb.shape[0] :], a_half[...])).astype(jnp.bfloat16)
+
+
+def second_call(core, w, a_blocks):
+    rows, features = a_blocks[0].shape
+    half = 4 * rows
+    return pl.pallas_call(
+        second_kernel,
+        in_specs=[smem_spec()] + [vmem_spec()] * 9,
+        out_specs=vmem_spec(),
+        out_shape=jax.ShapeDtypeStruct((2 * rows, features), jnp.bfloat16),
+        scratch_shapes=[pltpu.VMEM((half, features), jnp.bfloat16)],
+        compiler_params=params(),
+        cost_estimate=cost(1, half, 2 * rows, features),
+        name="second",
+    )(core, w, *a_blocks)
+
+
+def low_kernel(core_ref, w_ref, *refs):
+    a_refs, (gb0, gb_lo, a_half) = refs[:8], refs[8:]
     rows = gb0.shape[0]
     core = core_ref[0]
     take_half(core, a_refs, 0, a_half)
-    take_half(core, b_refs, 1, b_half)
     g = 0.5 * dot_tn(w_ref[core], a_half[...])
     gb0[...] = g[:rows]
     gb_lo[...] = g[rows:].astype(jnp.bfloat16)
-    ga_hi[...] = 0.5 * jnp.dot(w_ref[1], b_half[...], preferred_element_type=jnp.float32)
-
-
-def middle_call(core, w, a_blocks, b_blocks):
+
+
+def low_call(core, w, a_blocks):
     rows, features = a_blocks[0].shape
     half = 4 * rows
     return pl.pallas_call(
-        middle_kernel,
-        in_specs=[smem_spec()] + [vmem_spec()] * 15,
-        out_specs=[vmem_spec()] * 3,
+        low_kernel,
+        in_specs=[smem_spec()] + [vmem_spec()] * 9,
+        out_specs=[vmem_spec()] * 2,
         out_shape=[
-            pltpu.VMEM((half, features), jnp.float32),
             jax.ShapeDtypeStruct((rows, features), jnp.float32),
             jax.ShapeDtypeStruct((half - rows, features), jnp.bfloat16),
         ],
-        scratch_shapes=[pltpu.VMEM((half, features), jnp.bfloat16)] * 2,
-        compiler_params=params(),
-        cost_estimate=cost(2, half, half, features),
-        name="middle",
-    )(core, w, *a_blocks, *b_blocks)
-
-
-def far_kernel(ga_hi, got, *outs):
+        scratch_shapes=[pltpu.VMEM((half, features), jnp.bfloat16)],
+        compiler_params=params(),
+        cost_estimate=cost(1, half, half, features),
+        name="low",
+    )(core, w, *a_blocks)
+
+
+def far_kernel(ga_hi, got, more, *outs):
     rows = outs[0].shape[0]
     for j in range(4):
-        sl = slice(j * rows, (j + 1) * rows)
-        outs[j][...] = (ga_hi[sl, :] + got[sl, :].astype(jnp.float32)).astype(jnp.bfloat16)
-
-
-def far_call(ga_hi, got):
+        part = (got if j < 2 else more)[(j % 2) * rows : (j % 2 + 1) * rows, :]
+        outs[j][...] = (ga_hi[j * rows : (j + 1) * rows, :] + part.astype(jnp.float32)).astype(jnp.bfloat16)
+
+
+def far_call(ga_hi, got, more):
     half, features = ga_hi.shape
     rows = half // 4
     return pl.pallas_call(
         far_kernel,
-        in_specs=[vmem_spec()] * 2,
+        in_specs=[vmem_spec()] * 3,
         out_specs=[vmem_spec()] * 4,
         out_shape=[jax.ShapeDtypeStruct((rows, features), jnp.bfloat16)] * 4,
         compiler_params=params(),
         cost_estimate=cost(0, half, features, 1, 8),
         name="far",
-    )(ga_hi, got)
-
-
-def last_kernel(core_ref, w_ref, *refs):
-    b_refs, (ga_lo, b_half) = views(refs[:6]), refs[6:]
-    take_half(core_ref[0], b_refs, 0, b_half)
-    ga_lo[...] = 0.5 * jnp.dot(w_ref[0], b_half[...], preferred_element_type=jnp.float32)
-
-
-def last_call(core, w, b_blocks):
+    )(ga_hi, got, more)
+
+
+def side_kernel(q, core_ref, w_ref, *refs):
+    b_refs, (ga, b_half) = views(refs[:6]), refs[6:]
+    take_half(core_ref[0], b_refs, q, b_half)
+    ga[...] = 0.5 * jnp.dot(w_ref[q], b_half[...], preferred_element_type=jnp.float32)
+
+
+def side_call(q, core, w, b_blocks):
     rows, features = b_blocks[0].shape
     half = 4 * rows
     return pl.pallas_call(
-        last_kernel,
+        functools.partial(side_kernel, q),
         in_specs=[smem_spec()] + [vmem_spec()] * 7,
         out_specs=vmem_spec(),
         out_shape=pltpu.VMEM((half, features), jnp.float32),
         scratch_shapes=[pltpu.VMEM((half, features), jnp.bfloat16)],
         compiler_params=params(),
-        cost_estimate=cost(1, half, half, features),
-        name="last",
+        cost_estimate=cost(1, half, half if q == 0 else rows // 4, features),
+        name="side",
     )(core, w, *b_blocks)
 
 
@@ -429,7 +450,10 @@
     blocks = {0: own, **near, **far}
     in_vmem = lambda a: pltpu.with_memory_space_constraint(a, pltpu.VMEM)
     a_blocks = [in_vmem(blocks[m]) for m in ORDER]
-    b_blocks = [other, swap(join_call(near[1], near[2], near[4]))] + [swap(far[m]) for m in ORDER[4:]]
+    swapped = {m: swap(far[m]) for m in (3, 5, 6)}
+    last, swapped[3], swapped[5], swapped[6] = lax.optimization_barrier((far[7], swapped[3], swapped[5], swapped[6]))
+    swapped[7] = swap(last)
+    b_blocks = [other, swap(join_call(near[1], near[2], near[4]))] + [swapped[m] for m in ORDER[4:]]
     b_blocks = [in_vmem(b) for b in b_blocks]
 
     e, a_stat, b_stat, flags = scores_call(core_arr, a_blocks, b_blocks, scale)
@@ -440,14 +464,17 @@
 
     w, gb_hi = weights_call(core_arr, flags, e, a_lse, b_lse, a_blocks)
     got_hi = swap(gb_hi)
-    ga_hi, gb0, gb_lo = middle_call(core_arr, w, a_blocks, b_blocks)
-    got0, got_lo = swap(gb0), swap(gb_lo)
-    p = dict(zip(ORDER[4:], far_call(ga_hi, got_hi)))
+    got_more = swap(second_call(core_arr, w, a_blocks))
+    ga_hi = side_call(1, core_arr, w, b_blocks)
+    p = dict(zip(ORDER[4:], far_call(ga_hi, got_hi, got_more)))
+    p[7], w = lax.optimization_barrier((p[7], w))
     from_xy = to_cube(p[3], 1)
     from_yz = to_cube(p[6], 2)
     from_xz = to_cube(p[5], 4)
     from_xyz = to_cube(p[7], 7)
-    ga_lo = last_call(core_arr, w, b_blocks)
+    gb0, gb_lo = low_call(core_arr, w, a_blocks)
+    got0, got_lo = swap(gb0), swap(gb_lo)
+    ga_lo = side_call(0, core_arr, w, b_blocks)
     p0, p1, p2, p4 = near_call(ga_lo, got0, got_lo, from_xy, from_yz, from_xz)
     wide = lambda a: a.astype(jnp.float32)
     total = p0 + wide(from_xyz) + wide(to_cube(p1, 1)) + wide(to_cube(p2, 2)) + wide(to_cube(p4, 4))

time: 118 us -> 119 us (level)
  Pallas kernels: 35.9 us -> 37.8 us
  waiting for transfers between devices: 40.6 us -> 38.8 us
    pallas_call x4 -> x6, Pallas kernels: 8.99 us -> 12 us  [the longest x2 5.9 us: side_call(): pl.pallas_call(functools.partial(side_kernel, q), in_specs=[smem_spec()]...]
    ppermute x17, waiting for transfers between devices: 33.4 us -> 31.7 us  [to_cube(): return lax.ppermute(a, AXES, across(m))]
    ppermute x13 -> x14, starting transfers between devices: 6.02 us -> 7.51 us  [swap(): return lax.ppermute(a, AXES, SWAP)]
    pallas_call x1, Pallas kernels: 7.36 us -> 6.07 us  [weights_call(): pl.pallas_call(weights_kernel, in_specs=[smem_spec()] * 2 + [vmem_spec()]...]
    ppermute x17, starting transfers between devices: 31.7 us -> 30.4 us  [to_cube(): return lax.ppermute(a, AXES, across(m))]
    ppermute x13 -> x14, waiting for transfers between devices: 7.19 us -> 7.03 us  [swap(): return lax.ppermute(a, AXES, SWAP)]
  transfers between devices with their start and end apart: 30 -> 31, of which waited for: 19 -> 21; matrix products, arithmetic and copies ran while one was open for 0% -> 0% of each run, Pallas kernels for 8% -> 6%
where the time goes in v7:
time: 119 us
  waiting for transfers between devices  38.8 us (33%)
  starting transfers between devices  37.9 us (32%)
  Pallas kernels  37.8 us (32%)
  local copies, waits for them, and re-layouts  1.93 us (2%)
  other arithmetic  1.34 us (1%)
    ppermute x17, waiting for transfers between devices, to_cube(): return lax.ppermute(a, AXES, across(m))  31.7 us
    ppermute x17, starting transfers between devices, to_cube(): return lax.ppermute(a, AXES, across(m))  30.4 us
    pallas_call x1, Pallas kernels, scores_call(): pl.pallas_call(functools.partial(scores_kernel, scale), in_specs=[smem_sp...  18.8 us
    ppermute x14, starting transfers between devices, swap(): return lax.ppermute(a, AXES, SWAP)  7.51 us
    ppermute x14, waiting for transfers between devices, swap(): return lax.ppermute(a, AXES, SWAP)  7.03 us
    pallas_call x1, Pallas kernels, weights_call(): pl.pallas_call(weights_kernel, in_specs=[smem_spec()] * 2 + [vmem_spec()]...  6.07 us
    pallas_call x2, Pallas kernels, side_call(): pl.pallas_call(functools.partial(side_kernel, q), in_specs=[smem_spec()]...  5.9 us
    pallas_call x1, Pallas kernels, low_call(): pl.pallas_call(low_kernel, in_specs=[smem_spec()] + [vmem_spec()] * 9, ou...  2.9 us
  transfers between devices with their start and end apart: 31, of which 21 were waited for; matrix products, arithmetic and copies ran while one was open for 0% of the time, Pallas kernels for 6%

profile of v7, /device:TPU:1, one launch (start us, length us, event | category | flops | bytes accessed | tf_op | source)
XLA Modules:
  0.0 118.6 jit_solution(1329337479000803770)
XLA Ops:
  0.6 1.5 %collective-permute-start = (bf16[160,768]{1,0:T(8,128)(2,1)}, bf16[160,768]{1,0:T(8,128)(2,1)S(1)}, u32[]{:S(2)}, u32[]{:S(2)}) collective-permute-start(bf16[160,768]{1,0:T(8,128)(2,1)} %images.1), channel_id=1, source_target_pairs={{0,16},{1,17},{2,18},{3,19},{4,20},{5,21},{6,22},{7,23},{8,24},{9,... | collective-permute-start | bytes 737288 | tf_op jit(solution)/shard_map/ppermute | solution.py:57
  2.1 0.1 collective-permute-start.1
  2.2 1.3 %collective-permute-done.got_images = bf16[160,768]{1,0:T(8,128)(2,1)S(1)} collective-permute-done((bf16[160,768]{1,0:T(8,128)(2,1)}, bf16[160,768]{1,0:T(8,128)(2,1)S(1)}, u32[]{:S(2)}, u32[]{:S(2)}) %collective-permute-start) | collective-permute-done | bytes 245792 | tf_op jit(solution)/shard_map/ppermute | solution.py:57
  3.5 0.4 collective-permute-done.1.got_texts
  3.9 0.9 copy-done
  4.8 0.9 copy-done.2
  5.7 1.3 %own.1 = (bf16[320,768]{1,0:T(8,128)(2,1)S(1)}, bf16[320,768]{1,0:T(8,128)(2,1)S(1)}) custom-call(s32[1]{0:T(128)} %bitcast.core_ref, bf16[160,768]{1,0:T(8,128)(2,1)S(1)} %copy-done, bf16[160,768]{1,0:T(8,128)(2,1)S(1)} %copy-done.2, bf16[160,768]{1,0:T(8,128)(2,1)S(1)} %collective-permute-done.got_images, bf16[160,768]{1,0:T(8,128)(2,1)S(1)} %collective-permute-done.1.got_texts), custom_call_target="tpu_custom_call" | custom-call | bytes 1966080 | tf_op jit(solution)/shard_map/own/pallas_call | solution.py:125
  7.0 2.6 %collective-permute-start.2 = (bf16[320,768]{1,0:T(8,128)(2,1)S(1)}, bf16[320,768]{1,0:T(8,128)(2,1)S(1)}, u32[]{:S(2)}, u32[]{:S(2)}) collective-permute-start(bf16[320,768]{1,0:T(8,128)(2,1)S(1)} %get-tuple-element.26.refs_0_), channel_id=1, source_target_pairs={{0,4},{1,5},{2,6},{3,7},{4,0},{5,1},{6,2},{7,3},{8,12},{9,13},{10,... | collective-permute-start | bytes 1474568 | tf_op jit(solution)/shard_map/ppermute | solution.py:53
  9.7 1.3 %collective-permute-start.3 = (bf16[320,768]{1,0:T(8,128)(2,1)S(1)}, bf16[320,768]{1,0:T(8,128)(2,1)S(1)}, u32[]{:S(2)}, u32[]{:S(2)}) collective-permute-start(bf16[320,768]{1,0:T(8,128)(2,1)S(1)} %get-tuple-element.26.refs_0_), channel_id=1, source_target_pairs={{0,96},{1,97},{2,98},{3,99},{4,100},{5,101},{6,102},{7,103},{8,104... | collective-permute-start | bytes 1474568 | tf_op jit(solution)/shard_map/ppermute | solution.py:53
  11.0 3.8 %collective-permute-start.4 = (bf16[320,768]{1,0:T(8,128)(2,1)S(1)}, bf16[320,768]{1,0:T(8,128)(2,1)S(1)}, u32[]{:S(2)}, u32[]{:S(2)}) collective-permute-start(bf16[320,768]{1,0:T(8,128)(2,1)S(1)} %get-tuple-element.26.refs_0_), channel_id=1, source_target_pairs={{0,1},{1,0},{2,3},{3,2},{4,5},{5,4},{6,7},{7,6},{8,9},{9,8},{10,11... | collective-permute-start | bytes 1474568 | tf_op jit(solution)/shard_map/ppermute | solution.py:53
  14.7 1.6 %collective-permute-done.2.b0.refs_1_ = bf16[320,768]{1,0:T(8,128)(2,1)S(1)} collective-permute-done((bf16[320,768]{1,0:T(8,128)(2,1)S(1)}, bf16[320,768]{1,0:T(8,128)(2,1)S(1)}, u32[]{:S(2)}, u32[]{:S(2)}) %collective-permute-start.2) | collective-permute-done | bytes 491552 | tf_op jit(solution)/shard_map/ppermute | solution.py:53
  16.3 3.8 %collective-permute-start.6 = (bf16[320,768]{1,0:T(8,128)(2,1)S(1)}, bf16[320,768]{1,0:T(8,128)(2,1)S(1)}, u32[]{:S(2)}, u32[]{:S(2)}) collective-permute-start(bf16[320,768]{1,0:T(8,128)(2,1)S(1)} %collective-permute-done.2.b0.refs_1_), channel_id=1, source_target_pairs={{0,1},{1,0},{2,3},{3,2},{4,5},{5,4},{6,7},{7,6},{8,9},{9,8},{10,11... | collective-permute-start | bytes 1474568 | tf_op jit(solution)/shard_map/ppermute | solution.py:53
  20.1 2.5 %collective-permute-start.5 = (bf16[320,768]{1,0:T(8,128)(2,1)S(1)}, bf16[320,768]{1,0:T(8,128)(2,1)S(1)}, u32[]{:S(2)}, u32[]{:S(2)}) collective-permute-start(bf16[320,768]{1,0:T(8,128)(2,1)S(1)} %collective-permute-done.3.b1.refs_2_), channel_id=1, source_target_pairs={{0,4},{1,5},{2,6},{3,7},{4,0},{5,1},{6,2},{7,3},{8,12},{9,13},{10,... | collective-permute-start | bytes 1474568 | tf_op jit(solution)/shard_map/ppermute | solution.py:53
  22.6 1.0 collective-permute-start.7
  23.6 0.1 join.1
  23.7 0.1 collective-permute-start.9
  23.8 1.3 %collective-permute-start.8 = (bf16[320,768]{1,0:T(8,128)(2,1)S(1)}, bf16[320,768]{1,0:T(8,128)(2,1)S(1)}, u32[]{:S(2)}, u32[]{:S(2)}) collective-permute-start(bf16[320,768]{1,0:T(8,128)(2,1)S(1)} %collective-permute-done.2.b0.refs_1_), channel_id=1, source_target_pairs={{0,97},{1,96},{2,99},{3,98},{4,101},{5,100},{6,103},{7,102},{8,105... | collective-permute-start | bytes 1474568 | tf_op jit(solution)/shard_map/ppermute | solution.py:53
  25.1 1.6 %collective-permute-done.6.refs_5_ = bf16[320,768]{1,0:T(8,128)(2,1)S(1)} collective-permute-done((bf16[320,768]{1,0:T(8,128)(2,1)S(1)}, bf16[320,768]{1,0:T(8,128)(2,1)S(1)}, u32[]{:S(2)}, u32[]{:S(2)}) %collective-permute-start.6) | collective-permute-done | bytes 491552 | tf_op jit(solution)/shard_map/ppermute | solution.py:53
  26.6 2.7 %collective-permute-done.5.refs_4_ = bf16[320,768]{1,0:T(8,128)(2,1)S(1)} collective-permute-done((bf16[320,768]{1,0:T(8,128)(2,1)S(1)}, bf16[320,768]{1,0:T(8,128)(2,1)S(1)}, u32[]{:S(2)}, u32[]{:S(2)}) %collective-permute-start.5) | collective-permute-done | bytes 491552 | tf_op jit(solution)/shard_map/ppermute | solution.py:53
  29.3 1.2 %collective-permute-done.7.refs_6_ = bf16[320,768]{1,0:T(8,128)(2,1)S(1)} collective-permute-done((bf16[320,768]{1,0:T(8,128)(2,1)S(1)}, bf16[320,768]{1,0:T(8,128)(2,1)S(1)}, u32[]{:S(2)}, u32[]{:S(2)}) %collective-permute-start.7) | collective-permute-done | bytes 491552 | tf_op jit(solution)/shard_map/ppermute | solution.py:53
  30.5 0.4 collective-permute-start.12
  30.9 5.7 %collective-permute-done.8.refs_7_ = bf16[320,768]{1,0:T(8,128)(2,1)S(1)} collective-permute-done((bf16[320,768]{1,0:T(8,128)(2,1)S(1)}, bf16[320,768]{1,0:T(8,128)(2,1)S(1)}, u32[]{:S(2)}, u32[]{:S(2)}) %collective-permute-start.8) | collective-permute-done | bytes 491552 | tf_op jit(solution)/shard_map/ppermute | solution.py:53
  36.6 1.0 collective-permute-start.13
  37.6 1.5 %collective-permute-done.13.refs_13_.refs_5_ = bf16[320,768]{1,0:T(8,128)(2,1)S(1)} collective-permute-done((bf16[320,768]{1,0:T(8,128)(2,1)S(1)}, bf16[320,768]{1,0:T(8,128)(2,1)S(1)}, u32[]{:S(2)}, u32[]{:S(2)}) %collective-permute-start.13) | collective-permute-done | bytes 491552 | tf_op jit(solution)/shard_map/ppermute | solution.py:57
  39.1 18.8 %scores.1 = (f32[2,1280,1280]{2,1,0:T(8,128)S(1)}, f32[8,320]{1,0:T(8,128)S(1)}, f32[8,320]{1,0:T(8,128)S(1)}, s32[2]{0:T(128)S(1)}) custom-call(s32[1]{0:T(128)} %bitcast.core_ref, bf16[320,768]{1,0:T(8,128)(2,1)S(1)} %get-tuple-element.26.refs_0_, bf16[320,768]{1,0:T(8,128)(2,1)S(1)} %collective-permute-done.2.b0.refs_1_, ...), custom_call_target="tpu_custom_call" | custom-call | flops 5033164800 | tf_op jit(solution)/shard_map/scores/pallas_call | solution.py:236
  58.0 0.5 collective-permute-start.14
  58.4 0.8 collective-permute-done.14.got_ref
  59.3 1.9 %collective-permute-start.15 = (f32[8,320]{1,0:T(8,128)S(1)}, f32[8,320]{1,0:T(8,128)S(1)}, u32[]{:S(2)}, u32[]{:S(2)}) collective-permute-start(f32[8,320]{1,0:T(8,128)S(1)} %merge.4.mine_ref), channel_id=1, source_target_pairs={{0,4},{1,5},{2,6},{3,7},{4,0},{5,1},{6,2},{7,3},{8,12},{9,13},{10,... | collective-permute-start | bytes 30728 | tf_op jit(solution)/shard_map/ppermute | solution.py:53
  61.2 1.9 %collective-permute-done.15.got_ref = f32[8,320]{1,0:T(8,128)S(1)} collective-permute-done((f32[8,320]{1,0:T(8,128)S(1)}, f32[8,320]{1,0:T(8,128)S(1)}, u32[]{:S(2)}, u32[]{:S(2)}) %collective-permute-start.15) | collective-permute-done | bytes 10272 | tf_op jit(solution)/shard_map/ppermute | solution.py:53
  63.1 0.1 collective-permute-start.16
  63.2 2.5 %collective-permute-done.16.got_ref = f32[8,320]{1,0:T(8,128)S(1)} collective-permute-done((f32[8,320]{1,0:T(8,128)S(1)}, f32[8,320]{1,0:T(8,128)S(1)}, u32[]{:S(2)}, u32[]{:S(2)}) %collective-permute-start.16) | collective-permute-done | bytes 10272 | tf_op jit(solution)/shard_map/ppermute | solution.py:53
  65.8 2.3 %collective-permute-start.17 = (f32[8,320]{1,0:T(8,128)S(1)}, f32[8,320]{1,0:T(8,128)S(1)}, u32[]{:S(2)}, u32[]{:S(2)}) collective-permute-start(f32[8,320]{1,0:T(8,128)S(1)} %merge.6.mine_ref), channel_id=1, source_target_pairs={{0,1},{1,0},{2,3},{3,2},{4,5},{5,4},{6,7},{7,6},{8,9},{9,8},{10,11... | collective-permute-start | bytes 30728 | tf_op jit(solution)/shard_map/ppermute | solution.py:53
  68.1 1.5 %collective-permute-done.17.got_ref = f32[8,320]{1,0:T(8,128)S(1)} collective-permute-done((f32[8,320]{1,0:T(8,128)S(1)}, f32[8,320]{1,0:T(8,128)S(1)}, u32[]{:S(2)}, u32[]{:S(2)}) %collective-permute-start.17) | collective-permute-done | bytes 10272 | tf_op jit(solution)/shard_map/ppermute | solution.py:53
  69.7 2.7 %collective-permute-start.18 = (f32[8,320]{1,0:T(8,128)S(1)}, f32[8,320]{1,0:T(8,128)S(1)}, u32[]{:S(2)}, u32[]{:S(2)}) collective-permute-start(f32[8,320]{1,0:T(8,128)S(1)} %merge.7.a_lse), channel_id=1, source_target_pairs={{0,16},{1,17},{2,18},{3,19},{4,20},{5,21},{6,22},{7,23},{8,24},{9,... | collective-permute-start | bytes 30728 | tf_op jit(solution)/shard_map/ppermute | solution.py:57
  72.3 0.8 collective-permute-done.18.b_lse
  73.2 6.1 %weights.1 = (bf16[2,1280,1280]{2,1,0:T(8,128)(2,1)S(1)}, bf16[640,768]{1,0:T(8,128)(2,1)S(1)}) custom-call(s32[1]{0:T(128)} %bitcast.core_ref, s32[2]{0:T(128)S(1)} %get-tuple-element.32.flags, f32[2,1280,1280]{2,1,0:T(8,128)S(1)} %get-tuple-element.33.e_ref, f32[8,320]{1,0:T(8,128)S(1)} %merge.7.a_lse, f32[8,320]{1,0:T(8,128)S(1)} %collective-permute-done.18.b_lse, ...), custom_call_target="tpu_custom_call" | custom-call | flops 2516582400 | bytes 19660800 | tf_op jit(solution)/shard_map/weights/pallas_call | solution.py:310
  79.2 1.6 %second.1 = bf16[640,768]{1,0:T(8,128)(2,1)S(1)} custom-call(s32[1]{0:T(128)} %bitcast.core_ref, bf16[2,1280,1280]{2,1,0:T(8,128)(2,1)S(1)} %get-tuple-element.39.w_ref, bf16[320,768]{1,0:T(8,128)(2,1)S(1)} %get-tuple-element.26.refs_0_, bf16[320,768]{1,0:T(8,128)(2,1)S(1)} %collective-permute-done.2.b0.refs_1_, ...), custom_call_target="tpu_custom_call" | custom-call | flops 1258291200 | tf_op jit(solution)/shard_map/second/pallas_call | solution.py:335
  80.9 0.4 collective-permute-start.20
  81.3 0.2 collective-permute-start.19
  81.5 3.1 %side.2.ga_hi = f32[1280,768]{1,0:T(8,128)S(1)} custom-call(s32[1]{0:T(128)} %bitcast.core_ref, bf16[2,1280,1280]{2,1,0:T(8,128)(2,1)S(1)} %get-tuple-element.39.w_ref, bf16[320,768]{1,0:T(8,128)(2,1)S(1)} %get-tuple-element.27.refs_8_.refs_0_, bf16[960,768]{1,0:T(8,128)(2,1)S(1)} %collective-permute-done.9.refs_9_.refs_1_, ...), custom_call_target="tpu_custom_call" | custom-call | flops 157286400 | tf_op jit(solution)/shard_map/side/pallas_call | solution.py:405
  84.5 0.4 collective-permute-done.19.got
  84.9 0.4 far.1
  85.3 2.9 %low.1 = (f32[320,768]{1,0:T(8,128)S(1)}, bf16[960,768]{1,0:T(8,128)(2,1)S(1)}) custom-call(s32[1]{0:T(128)} %bitcast.core_ref, bf16[2,1280,1280]{2,1,0:T(8,128)(2,1)S(1)} %get-tuple-element.39.w_ref, bf16[320,768]{1,0:T(8,128)(2,1)S(1)} %get-tuple-element.26.refs_0_, bf16[320,768]{1,0:T(8,128)(2,1)S(1)} %collective-permute-done.2.b0.refs_1_, ...), custom_call_target="tpu_custom_call" | custom-call | flops 2516582400 | tf_op jit(solution)/shard_map/low/pallas_call | solution.py:360
  88.2 0.4 collective-permute-start.22
  88.6 0.2 collective-permute-start.21
  88.8 1.8 %collective-permute-start.23 = (bf16[320,768]{1,0:T(8,128)(2,1)S(1)}, bf16[320,768]{1,0:T(8,128)(2,1)S(1)}, u32[]{:S(2)}, u32[]{:S(2)}) collective-permute-start(bf16[320,768]{1,0:T(8,128)(2,1)S(1)} %get-tuple-element.42), channel_id=1, source_target_pairs={{0,4},{1,5},{2,6},{3,7},{4,0},{5,1},{6,2},{7,3},{8,12},{9,13},{10,... | collective-permute-start | bytes 1474568 | tf_op jit(solution)/shard_map/ppermute | solution.py:53
  90.6 2.2 %collective-permute-start.25 = (bf16[320,768]{1,0:T(8,128)(2,1)S(1)}, bf16[320,768]{1,0:T(8,128)(2,1)S(1)}, u32[]{:S(2)}, u32[]{:S(2)}) collective-permute-start(bf16[320,768]{1,0:T(8,128)(2,1)S(1)} %get-tuple-element.44), channel_id=1, source_target_pairs={{0,1},{1,0},{2,3},{3,2},{4,5},{5,4},{6,7},{7,6},{8,9},{9,8},{10,11... | collective-permute-start | bytes 1474568 | tf_op jit(solution)/shard_map/ppermute | solution.py:53
  92.8 2.8 %side.3.ga_lo = f32[1280,768]{1,0:T(8,128)S(1)} custom-call(s32[1]{0:T(128)} %bitcast.core_ref, bf16[2,1280,1280]{2,1,0:T(8,128)(2,1)S(1)} %get-tuple-element.39.w_ref, bf16[320,768]{1,0:T(8,128)(2,1)S(1)} %get-tuple-element.27.refs_8_.refs_0_, bf16[960,768]{1,0:T(8,128)(2,1)S(1)} %collective-permute-done.9.refs_9_.refs_1_, ...), custom_call_target="tpu_custom_call" | custom-call | flops 2516582400 | tf_op jit(solution)/shard_map/side/pallas_call | solution.py:405
  95.7 2.3 %collective-permute-done.23.r_xy = bf16[320,768]{1,0:T(8,128)(2,1)S(1)} collective-permute-done((bf16[320,768]{1,0:T(8,128)(2,1)S(1)}, bf16[320,768]{1,0:T(8,128)(2,1)S(1)}, u32[]{:S(2)}, u32[]{:S(2)}) %collective-permute-start.23) | collective-permute-done | bytes 491552 | tf_op jit(solution)/shard_map/ppermute | solution.py:53
  98.0 1.0 collective-permute-start.26
  98.9 0.6 collective-permute-done.25.r_xz
  99.5 0.6 near.1
  100.1 0.0 copy-start.1
  100.1 1.2 %collective-permute-start.27 = (bf16[320,768]{1,0:T(8,128)(2,1)S(1)}, bf16[320,768]{1,0:T(8,128)(2,1)S(1)}, u32[]{:S(2)}, u32[]{:S(2)}) collective-permute-start(bf16[320,768]{1,0:T(8,128)(2,1)S(1)} %get-tuple-element.47), channel_id=1, source_target_pairs={{0,4},{1,5},{2,6},{3,7},{4,0},{5,1},{6,2},{7,3},{8,12},{9,13},{10,... | collective-permute-start | bytes 1474568 | tf_op jit(solution)/shard_map/ppermute | solution.py:53
  101.4 3.2 %collective-permute-start.28 = (bf16[320,768]{1,0:T(8,128)(2,1)S(1)}, bf16[320,768]{1,0:T(8,128)(2,1)S(1)}, u32[]{:S(2)}, u32[]{:S(2)}) collective-permute-start(bf16[320,768]{1,0:T(8,128)(2,1)S(1)} %get-tuple-element.48), channel_id=1, source_target_pairs={{0,96},{1,97},{2,98},{3,99},{4,100},{5,101},{6,102},{7,103},{8,104... | collective-permute-start | bytes 1474568 | tf_op jit(solution)/shard_map/ppermute | solution.py:53
  104.5 0.4 collective-permute-start.29
  105.0 5.1 %collective-permute-done.26 = bf16[320,768]{1,0:T(8,128)(2,1)S(1)} collective-permute-done((bf16[320,768]{1,0:T(8,128)(2,1)S(1)}, bf16[320,768]{1,0:T(8,128)(2,1)S(1)}, u32[]{:S(2)}, u32[]{:S(2)}) %collective-permute-start.26) | collective-permute-done | bytes 491552 | tf_op jit(solution)/shard_map/ppermute | solution.py:53
  110.1 1.9 %collective-permute-done.27 = bf16[320,768]{1,0:T(8,128)(2,1)S(1)} collective-permute-done((bf16[320,768]{1,0:T(8,128)(2,1)S(1)}, bf16[320,768]{1,0:T(8,128)(2,1)S(1)}, u32[]{:S(2)}, u32[]{:S(2)}) %collective-permute-start.27) | collective-permute-done | bytes 491552 | tf_op jit(solution)/shard_map/ppermute | solution.py:53
  111.9 3.1 %collective-permute-done.28 = bf16[320,768]{1,0:T(8,128)(2,1)S(1)} collective-permute-done((bf16[320,768]{1,0:T(8,128)(2,1)S(1)}, bf16[320,768]{1,0:T(8,128)(2,1)S(1)}, u32[]{:S(2)}, u32[]{:S(2)}) %collective-permute-start.28) | collective-permute-done | bytes 491552 | tf_op jit(solution)/shard_map/ppermute | solution.py:53
  115.0 0.2 collective-permute-done.29
  115.2 0.3 convert_add_fusion
  115.6 0.1 collective-permute-start.30
  115.7 1.8 %collective-permute-done.30 = f32[160,768]{1,0:T(8,128)S(1)} collective-permute-done((f32[160,768]{1,0:T(8,128)S(1)}, f32[160,768]{1,0:T(8,128)S(1)}, u32[]{:S(2)}, u32[]{:S(2)}) %collective-permute-start.30) | collective-permute-done | bytes 491552 | tf_op jit(solution)/shard_map/ppermute | solution.py:57
  117.5 1.0 convert_subtract_fusion
  (23 shorter events, 0.2 us)
Async XLA Ops:
  0.6 2.9 %collective-permute-start = (bf16[160,768]{1,0:T(8,128)(2,1)}, bf16[160,768]{1,0:T(8,128)(2,1)S(1)}, u32[]{:S(2)}, u32[]{:S(2)}) collective-permute-start(bf16[160,768]{1,0:T(8,128)(2,1)} %images.1), channel_id=1, source_target_pairs={{0,16},{1,17},{2,18},{3,19},{4,20},{5,21},{6,22},{7,23},{8,24},{9,... | collective-permute-start | bytes 737288 | tf_op jit(solution)/shard_map/ppermute | solution.py:57
  2.1 1.7 %collective-permute-start.1 = (bf16[160,768]{1,0:T(8,128)(2,1)}, bf16[160,768]{1,0:T(8,128)(2,1)S(1)}, u32[]{:S(2)}, u32[]{:S(2)}) collective-permute-start(bf16[160,768]{1,0:T(8,128)(2,1)} %texts.1), channel_id=1, source_target_pairs={{0,16},{1,17},{2,18},{3,19},{4,20},{5,21},{6,22},{7,23},{8,24},{9,... | collective-permute-start | bytes 737288 | tf_op jit(solution)/shard_map/ppermute | solution.py:57
  3.9 0.9 copy-start
  4.8 0.9 copy-start.2
  7.0 9.3 %collective-permute-start.2 = (bf16[320,768]{1,0:T(8,128)(2,1)S(1)}, bf16[320,768]{1,0:T(8,128)(2,1)S(1)}, u32[]{:S(2)}, u32[]{:S(2)}) collective-permute-start(bf16[320,768]{1,0:T(8,128)(2,1)S(1)} %get-tuple-element.26.refs_0_), channel_id=1, source_target_pairs={{0,4},{1,5},{2,6},{3,7},{4,0},{5,1},{6,2},{7,3},{8,12},{9,13},{10,... | collective-permute-start | bytes 1474568 | tf_op jit(solution)/shard_map/ppermute | solution.py:53
  9.7 10.5 %collective-permute-start.3 = (bf16[320,768]{1,0:T(8,128)(2,1)S(1)}, bf16[320,768]{1,0:T(8,128)(2,1)S(1)}, u32[]{:S(2)}, u32[]{:S(2)}) collective-permute-start(bf16[320,768]{1,0:T(8,128)(2,1)S(1)} %get-tuple-element.26.refs_0_), channel_id=1, source_target_pairs={{0,96},{1,97},{2,98},{3,99},{4,100},{5,101},{6,102},{7,103},{8,104... | collective-permute-start | bytes 1474568 | tf_op jit(solution)/shard_map/ppermute | solution.py:53
  11.0 11.7 %collective-permute-start.4 = (bf16[320,768]{1,0:T(8,128)(2,1)S(1)}, bf16[320,768]{1,0:T(8,128)(2,1)S(1)}, u32[]{:S(2)}, u32[]{:S(2)}) collective-permute-start(bf16[320,768]{1,0:T(8,128)(2,1)S(1)} %get-tuple-element.26.refs_0_), channel_id=1, source_target_pairs={{0,1},{1,0},{2,3},{3,2},{4,5},{5,4},{6,7},{7,6},{8,9},{9,8},{10,11... | collective-permute-start | bytes 1474568 | tf_op jit(solution)/shard_map/ppermute | solution.py:53
  16.3 10.4 %collective-permute-start.6 = (bf16[320,768]{1,0:T(8,128)(2,1)S(1)}, bf16[320,768]{1,0:T(8,128)(2,1)S(1)}, u32[]{:S(2)}, u32[]{:S(2)}) collective-permute-start(bf16[320,768]{1,0:T(8,128)(2,1)S(1)} %collective-permute-done.2.b0.refs_1_), channel_id=1, source_target_pairs={{0,1},{1,0},{2,3},{3,2},{4,5},{5,4},{6,7},{7,6},{8,9},{9,8},{10,11... | collective-permute-start | bytes 1474568 | tf_op jit(solution)/shard_map/ppermute | solution.py:53
  20.1 9.2 %collective-permute-start.5 = (bf16[320,768]{1,0:T(8,128)(2,1)S(1)}, bf16[320,768]{1,0:T(8,128)(2,1)S(1)}, u32[]{:S(2)}, u32[]{:S(2)}) collective-permute-start(bf16[320,768]{1,0:T(8,128)(2,1)S(1)} %collective-permute-done.3.b1.refs_2_), channel_id=1, source_target_pairs={{0,4},{1,5},{2,6},{3,7},{4,0},{5,1},{6,2},{7,3},{8,12},{9,13},{10,... | collective-permute-start | bytes 1474568 | tf_op jit(solution)/shard_map/ppermute | solution.py:53
  22.6 7.9 %collective-permute-start.7 = (bf16[320,768]{1,0:T(8,128)(2,1)S(1)}, bf16[320,768]{1,0:T(8,128)(2,1)S(1)}, u32[]{:S(2)}, u32[]{:S(2)}) collective-permute-start(bf16[320,768]{1,0:T(8,128)(2,1)S(1)} %collective-permute-done.4.b2.refs_3_), channel_id=1, source_target_pairs={{0,96},{1,97},{2,98},{3,99},{4,100},{5,101},{6,102},{7,103},{8,104... | collective-permute-start | bytes 1474568 | tf_op jit(solution)/shard_map/ppermute | solution.py:53
  23.7 13.9 %collective-permute-start.9 = (bf16[960,768]{1,0:T(8,128)(2,1)S(1)}, bf16[960,768]{1,0:T(8,128)(2,1)S(1)}, u32[]{:S(2)}, u32[]{:S(2)}) collective-permute-start(bf16[960,768]{1,0:T(8,128)(2,1)S(1)} %join.1), channel_id=1, source_target_pairs={{0,16},{1,17},{2,18},{3,19},{4,20},{5,21},{6,22},{7,23},{8,24},{9,... | collective-permute-start | bytes 4423688 | tf_op jit(solution)/shard_map/ppermute | solution.py:57
  23.8 12.8 %collective-permute-start.8 = (bf16[320,768]{1,0:T(8,128)(2,1)S(1)}, bf16[320,768]{1,0:T(8,128)(2,1)S(1)}, u32[]{:S(2)}, u32[]{:S(2)}) collective-permute-start(bf16[320,768]{1,0:T(8,128)(2,1)S(1)} %collective-permute-done.2.b0.refs_1_), channel_id=1, source_target_pairs={{0,97},{1,96},{2,99},{3,98},{4,101},{5,100},{6,103},{7,102},{8,105... | collective-permute-start | bytes 1474568 | tf_op jit(solution)/shard_map/ppermute | solution.py:53
  26.6 9.9 %collective-permute-start.11 = (bf16[320,768]{1,0:T(8,128)(2,1)S(1)}, bf16[320,768]{1,0:T(8,128)(2,1)S(1)}, u32[]{:S(2)}, u32[]{:S(2)}) collective-permute-start(bf16[320,768]{1,0:T(8,128)(2,1)S(1)} %collective-permute-done.6.refs_5_), channel_id=1, source_target_pairs={{0,16},{1,17},{2,18},{3,19},{4,20},{5,21},{6,22},{7,23},{8,24},{9,... | collective-permute-start | bytes 1474568 | tf_op jit(solution)/shard_map/ppermute | solution.py:57
  29.3 7.3 %collective-permute-start.10 = (bf16[320,768]{1,0:T(8,128)(2,1)S(1)}, bf16[320,768]{1,0:T(8,128)(2,1)S(1)}, u32[]{:S(2)}, u32[]{:S(2)}) collective-permute-start(bf16[320,768]{1,0:T(8,128)(2,1)S(1)} %collective-permute-done.5.refs_4_), channel_id=1, source_target_pairs={{0,16},{1,17},{2,18},{3,19},{4,20},{5,21},{6,22},{7,23},{8,24},{9,... | collective-permute-start | bytes 1474568 | tf_op jit(solution)/shard_map/ppermute | solution.py:57
  30.5 6.1 %collective-permute-start.12 = (bf16[320,768]{1,0:T(8,128)(2,1)S(1)}, bf16[320,768]{1,0:T(8,128)(2,1)S(1)}, u32[]{:S(2)}, u32[]{:S(2)}) collective-permute-start(bf16[320,768]{1,0:T(8,128)(2,1)S(1)} %collective-permute-done.7.refs_6_), channel_id=1, source_target_pairs={{0,16},{1,17},{2,18},{3,19},{4,20},{5,21},{6,22},{7,23},{8,24},{9,... | collective-permute-start | bytes 1474568 | tf_op jit(solution)/shard_map/ppermute | solution.py:57
  36.6 2.5 %collective-permute-start.13 = (bf16[320,768]{1,0:T(8,128)(2,1)S(1)}, bf16[320,768]{1,0:T(8,128)(2,1)S(1)}, u32[]{:S(2)}, u32[]{:S(2)}) collective-permute-start(bf16[320,768]{1,0:T(8,128)(2,1)S(1)} %collective-permute-done.8.refs_7_), channel_id=1, source_target_pairs={{0,16},{1,17},{2,18},{3,19},{4,20},{5,21},{6,22},{7,23},{8,24},{9,... | collective-permute-start | bytes 1474568 | tf_op jit(solution)/shard_map/ppermute | solution.py:57
  58.0 1.3 %collective-permute-start.14 = (f32[8,320]{1,0:T(8,128)S(1)}, f32[8,320]{1,0:T(8,128)S(1)}, u32[]{:S(2)}, u32[]{:S(2)}) collective-permute-start(f32[8,320]{1,0:T(8,128)S(1)} %get-tuple-element.35), channel_id=1, source_target_pairs={{0,16},{1,17},{2,18},{3,19},{4,20},{5,21},{6,22},{7,23},{8,24},{9,... | collective-permute-start | bytes 30728 | tf_op jit(solution)/shard_map/ppermute | solution.py:57
  59.3 3.8 %collective-permute-start.15 = (f32[8,320]{1,0:T(8,128)S(1)}, f32[8,320]{1,0:T(8,128)S(1)}, u32[]{:S(2)}, u32[]{:S(2)}) collective-permute-start(f32[8,320]{1,0:T(8,128)S(1)} %merge.4.mine_ref), channel_id=1, source_target_pairs={{0,4},{1,5},{2,6},{3,7},{4,0},{5,1},{6,2},{7,3},{8,12},{9,13},{10,... | collective-permute-start | bytes 30728 | tf_op jit(solution)/shard_map/ppermute | solution.py:53
  63.1 2.6 %collective-permute-start.16 = (f32[8,320]{1,0:T(8,128)S(1)}, f32[8,320]{1,0:T(8,128)S(1)}, u32[]{:S(2)}, u32[]{:S(2)}) collective-permute-start(f32[8,320]{1,0:T(8,128)S(1)} %merge.5.mine_ref), channel_id=1, source_target_pairs={{0,96},{1,97},{2,98},{3,99},{4,100},{5,101},{6,102},{7,103},{8,104... | collective-permute-start | bytes 30728 | tf_op jit(solution)/shard_map/ppermute | solution.py:53
  65.8 3.8 %collective-permute-start.17 = (f32[8,320]{1,0:T(8,128)S(1)}, f32[8,320]{1,0:T(8,128)S(1)}, u32[]{:S(2)}, u32[]{:S(2)}) collective-permute-start(f32[8,320]{1,0:T(8,128)S(1)} %merge.6.mine_ref), channel_id=1, source_target_pairs={{0,1},{1,0},{2,3},{3,2},{4,5},{5,4},{6,7},{7,6},{8,9},{9,8},{10,11... | collective-permute-start | bytes 30728 | tf_op jit(solution)/shard_map/ppermute | solution.py:53
  69.7 3.5 %collective-permute-start.18 = (f32[8,320]{1,0:T(8,128)S(1)}, f32[8,320]{1,0:T(8,128)S(1)}, u32[]{:S(2)}, u32[]{:S(2)}) collective-permute-start(f32[8,320]{1,0:T(8,128)S(1)} %merge.7.a_lse), channel_id=1, source_target_pairs={{0,16},{1,17},{2,18},{3,19},{4,20},{5,21},{6,22},{7,23},{8,24},{9,... | collective-permute-start | bytes 30728 | tf_op jit(solution)/shard_map/ppermute | solution.py:57
  80.9 3.7 %collective-permute-start.20 = (bf16[640,768]{1,0:T(8,128)(2,1)S(1)}, bf16[640,768]{1,0:T(8,128)(2,1)S(1)}, u32[]{:S(2)}, u32[]{:S(2)}) collective-permute-start(bf16[640,768]{1,0:T(8,128)(2,1)S(1)} %second.1), channel_id=1, source_target_pairs={{0,16},{1,17},{2,18},{3,19},{4,20},{5,21},{6,22},{7,23},{8,24},{9,... | collective-permute-start | bytes 2949128 | tf_op jit(solution)/shard_map/ppermute | solution.py:57
  81.3 3.6 %collective-permute-start.19 = (bf16[640,768]{1,0:T(8,128)(2,1)S(1)}, bf16[640,768]{1,0:T(8,128)(2,1)S(1)}, u32[]{:S(2)}, u32[]{:S(2)}) collective-permute-start(bf16[640,768]{1,0:T(8,128)(2,1)S(1)} %get-tuple-element.37), channel_id=1, source_target_pairs={{0,16},{1,17},{2,18},{3,19},{4,20},{5,21},{6,22},{7,23},{8,24},{9,... | collective-permute-start | bytes 2949128 | tf_op jit(solution)/shard_map/ppermute | solution.py:57
  88.2 11.3 %collective-permute-start.22 = (bf16[960,768]{1,0:T(8,128)(2,1)S(1)}, bf16[960,768]{1,0:T(8,128)(2,1)S(1)}, u32[]{:S(2)}, u32[]{:S(2)}) collective-permute-start(bf16[960,768]{1,0:T(8,128)(2,1)S(1)} %get-tuple-element.41), channel_id=1, source_target_pairs={{0,16},{1,17},{2,18},{3,19},{4,20},{5,21},{6,22},{7,23},{8,24},{9,... | collective-permute-start | bytes 4423688 | tf_op jit(solution)/shard_map/ppermute | solution.py:57
  88.6 10.9 %collective-permute-start.21 = (f32[320,768]{1,0:T(8,128)S(1)}, f32[320,768]{1,0:T(8,128)S(1)}, u32[]{:S(2)}, u32[]{:S(2)}) collective-permute-start(f32[320,768]{1,0:T(8,128)S(1)} %get-tuple-element.40), channel_id=1, source_target_pairs={{0,16},{1,17},{2,18},{3,19},{4,20},{5,21},{6,22},{7,23},{8,24},{9,... | collective-permute-start | bytes 2949128 | tf_op jit(solution)/shard_map/ppermute | solution.py:57
  88.8 9.2 %collective-permute-start.23 = (bf16[320,768]{1,0:T(8,128)(2,1)S(1)}, bf16[320,768]{1,0:T(8,128)(2,1)S(1)}, u32[]{:S(2)}, u32[]{:S(2)}) collective-permute-start(bf16[320,768]{1,0:T(8,128)(2,1)S(1)} %get-tuple-element.42), channel_id=1, source_target_pairs={{0,4},{1,5},{2,6},{3,7},{4,0},{5,1},{6,2},{7,3},{8,12},{9,13},{10,... | collective-permute-start | bytes 1474568 | tf_op jit(solution)/shard_map/ppermute | solution.py:53
  90.6 8.3 %collective-permute-start.24 = (bf16[320,768]{1,0:T(8,128)(2,1)S(1)}, bf16[320,768]{1,0:T(8,128)(2,1)S(1)}, u32[]{:S(2)}, u32[]{:S(2)}) collective-permute-start(bf16[320,768]{1,0:T(8,128)(2,1)S(1)} %get-tuple-element.43), channel_id=1, source_target_pairs={{0,96},{1,97},{2,98},{3,99},{4,100},{5,101},{6,102},{7,103},{8,104... | collective-permute-start | bytes 1474568 | tf_op jit(solution)/shard_map/ppermute | solution.py:53
  90.6 8.9 %collective-permute-start.25 = (bf16[320,768]{1,0:T(8,128)(2,1)S(1)}, bf16[320,768]{1,0:T(8,128)(2,1)S(1)}, u32[]{:S(2)}, u32[]{:S(2)}) collective-permute-start(bf16[320,768]{1,0:T(8,128)(2,1)S(1)} %get-tuple-element.44), channel_id=1, source_target_pairs={{0,1},{1,0},{2,3},{3,2},{4,5},{5,4},{6,7},{7,6},{8,9},{9,8},{10,11... | collective-permute-start | bytes 1474568 | tf_op jit(solution)/shard_map/ppermute | solution.py:53
  98.0 12.1 %collective-permute-start.26 = (bf16[320,768]{1,0:T(8,128)(2,1)S(1)}, bf16[320,768]{1,0:T(8,128)(2,1)S(1)}, u32[]{:S(2)}, u32[]{:S(2)}) collective-permute-start(bf16[320,768]{1,0:T(8,128)(2,1)S(1)} %get-tuple-element.46), channel_id=1, source_target_pairs={{0,101},{1,100},{2,103},{3,102},{4,97},{5,96},{6,99},{7,98},{8,109... | collective-permute-start | bytes 1474568 | tf_op jit(solution)/shard_map/ppermute | solution.py:53
  100.1 17.4 %copy-start.1 = (bf16[160,768]{1,0:T(8,128)(2,1)S(1)}, bf16[160,768]{1,0:T(8,128)(2,1)}, u32[]{:S(2)}) copy-start(bf16[160,768]{1,0:T(8,128)(2,1)} %images.1) | copy-start | bytes 737284
  100.1 17.4 %copy-start.3 = (bf16[160,768]{1,0:T(8,128)(2,1)S(1)}, bf16[160,768]{1,0:T(8,128)(2,1)}, u32[]{:S(2)}) copy-start(bf16[160,768]{1,0:T(8,128)(2,1)} %texts.1) | copy-start | bytes 737284
  100.1 11.8 %collective-permute-start.27 = (bf16[320,768]{1,0:T(8,128)(2,1)S(1)}, bf16[320,768]{1,0:T(8,128)(2,1)S(1)}, u32[]{:S(2)}, u32[]{:S(2)}) collective-permute-start(bf16[320,768]{1,0:T(8,128)(2,1)S(1)} %get-tuple-element.47), channel_id=1, source_target_pairs={{0,4},{1,5},{2,6},{3,7},{4,0},{5,1},{6,2},{7,3},{8,12},{9,13},{10,... | collective-permute-start | bytes 1474568 | tf_op jit(solution)/shard_map/ppermute | solution.py:53
  101.4 13.6 %collective-permute-start.28 = (bf16[320,768]{1,0:T(8,128)(2,1)S(1)}, bf16[320,768]{1,0:T(8,128)(2,1)S(1)}, u32[]{:S(2)}, u32[]{:S(2)}) collective-permute-start(bf16[320,768]{1,0:T(8,128)(2,1)S(1)} %get-tuple-element.48), channel_id=1, source_target_pairs={{0,96},{1,97},{2,98},{3,99},{4,100},{5,101},{6,102},{7,103},{8,104... | collective-permute-start | bytes 1474568 | tf_op jit(solution)/shard_map/ppermute | solution.py:53
  104.5 10.7 %collective-permute-start.29 = (bf16[320,768]{1,0:T(8,128)(2,1)S(1)}, bf16[320,768]{1,0:T(8,128)(2,1)S(1)}, u32[]{:S(2)}, u32[]{:S(2)}) collective-permute-start(bf16[320,768]{1,0:T(8,128)(2,1)S(1)} %get-tuple-element.49), channel_id=1, source_target_pairs={{0,1},{1,0},{2,3},{3,2},{4,5},{5,4},{6,7},{7,6},{8,9},{9,8},{10,11... | collective-permute-start | bytes 1474568 | tf_op jit(solution)/shard_map/ppermute | solution.py:53
  115.6 1.9 %collective-permute-start.30 = (f32[160,768]{1,0:T(8,128)S(1)}, f32[160,768]{1,0:T(8,128)S(1)}, u32[]{:S(2)}, u32[]{:S(2)}) collective-permute-start(f32[160,768]{1,0:T(8,128)S(1)} %slice.9), channel_id=1, source_target_pairs={{0,16},{1,17},{2,18},{3,19},{4,20},{5,21},{6,22},{7,23},{8,24},{9,... | collective-permute-start | bytes 1474568 | tf_op jit(solution)/shard_map/ppermute | solution.py:57

commit v8 on v6

--- a/solution.py
+++ b/solution.py
@@ -14,7 +14,7 @@
 PLACE = tuple(ORDER.index(m) for m in range(8))
 LOG2E = 1.4426950408889634
 VMEM_LIMIT = 12 * 1024 * 1024
-RANGE = 60.0
+RANGE = 80.0
 
 
 def flat(y, c, x, z):
@@ -29,18 +29,18 @@
                     yield y, c, x, z
 
 
-def partner(v, c):
-    return v ^ 1 if c == 0 else 3 - v
+def partner(v, wrapped):
+    return 3 - v if wrapped else v ^ 1
 
 
 def across(m):
     pairs = []
     for y, c, x, z in coords():
         target = (
-            partner(y, c) if m & 2 else y,
+            partner(y, c == 0) if m & 2 else y,
             c,
-            partner(x, c) if m & 1 else x,
-            partner(z, c) if m & 4 else z,
+            partner(x, c == 1) if m & 1 else x,
+            partner(z, c == 1) if m & 4 else z,
         )
         pairs.append((flat(y, c, x, z), flat(*target)))
     return pairs
@@ -99,33 +99,35 @@
     return lax.dot_general(a, b, (((0,), (0,)), ((), ())), preferred_element_type=jnp.float32)
 
 
-def own_kernel(core_ref, images, texts, got_images, got_texts, own, other):
+def own_kernel(core_ref, images, texts, got_images, got_texts, own, other, sem):
     rows = images.shape[0]
     core = core_ref[0]
-
-    @pl.when(core == 0)
-    def _():
-        own[:rows] = images[...]
-        own[rows:] = got_images[...]
-        other[:rows] = got_texts[...]
-        other[rows:] = texts[...]
-
-    @pl.when(core != 0)
-    def _():
-        own[:rows] = texts[...]
-        own[rows:] = got_texts[...]
-        other[:rows] = got_images[...]
-        other[rows:] = images[...]
+    top, low = pl.ds(0, rows), pl.ds(rows, rows)
+    orders = ((images, got_images, got_texts, texts), (texts, got_texts, got_images, images))
+
+    def copies(order):
+        places = (own.at[top], own.at[low], other.at[top], other.at[low])
+        return [pltpu.make_async_copy(a, p, sem.at[j]) for j, (a, p) in enumerate(zip(order, places))]
+
+    for c in range(2):
+
+        @pl.when(core == c)
+        def _():
+            for copy in copies(orders[c]):
+                copy.start()
+            for copy in copies(orders[c]):
+                copy.wait()
 
 
 def own_call(core, *parts):
     rows, features = parts[0].shape
-    block = jax.ShapeDtypeStruct((2 * rows, features), parts[0].dtype)
+    block = pltpu.VMEM((2 * rows, features), parts[0].dtype)
     return pl.pallas_call(
         own_kernel,
-        in_specs=[smem_spec()] + [vmem_spec()] * 4,
+        in_specs=[smem_spec()] + [pl.BlockSpec(memory_space=pl.ANY)] * 4,
         out_specs=[vmem_spec()] * 2,
         out_shape=[block, block],
+        scratch_shapes=[pltpu.SemaphoreType.DMA((4,))],
         compiler_params=params(),
         cost_estimate=cost(0, rows, features, 1, 16),
         name="own",
@@ -393,10 +395,10 @@
     )(core, w, *b_blocks)
 
 
-def near_kernel(ga_lo, got0, got_lo, r_xy, r_yz, r_xz, p0, p1, p2, p4):
+def near_kernel(ga_lo, got0, got_lo, r_xy, r_yz, r_xz, r_xyz, p0, p1, p2, p4):
     rows = p0.shape[0]
     wide = lambda ref: ref[...].astype(jnp.float32)
-    p0[...] = ga_lo[:rows] + got0[...]
+    p0[...] = ga_lo[:rows] + got0[...] + wide(r_xyz)
     part = lambda j: ga_lo[j * rows : (j + 1) * rows, :] + got_lo[(j - 1) * rows : j * rows, :].astype(jnp.float32)
     p1[...] = (part(1) + wide(r_xz)).astype(jnp.bfloat16)
     p2[...] = (part(2) + wide(r_xy)).astype(jnp.bfloat16)
@@ -408,7 +410,7 @@
     narrow = jax.ShapeDtypeStruct((rows, features), jnp.bfloat16)
     return pl.pallas_call(
         near_kernel,
-        in_specs=[vmem_spec()] * 6,
+        in_specs=[vmem_spec()] * 7,
         out_specs=[vmem_spec()] * 4,
         out_shape=[pltpu.VMEM((rows, features), jnp.float32)] + [narrow] * 3,
         compiler_params=params(),
@@ -423,13 +425,17 @@
     core = lax.axis_index("core")
     first = core == 0
     core_arr = core.astype(jnp.int32).reshape(1)
-    own, other = own_call(core_arr, images, texts, swap(images), swap(texts))
+    in_hbm = lambda a: pltpu.with_memory_space_constraint(a, pltpu.HBM)
+    own, other = own_call(core_arr, in_hbm(images), in_hbm(texts), swap(images), swap(texts))
     near = {m: to_cube(own, m) for m in (4, 2, 1)}
     far = {7: to_cube(near[1], 6), 5: to_cube(near[1], 4), 3: to_cube(near[2], 1), 6: to_cube(near[4], 2)}
     blocks = {0: own, **near, **far}
     in_vmem = lambda a: pltpu.with_memory_space_constraint(a, pltpu.VMEM)
     a_blocks = [in_vmem(blocks[m]) for m in ORDER]
-    b_blocks = [other, swap(join_call(near[1], near[2], near[4]))] + [swap(far[m]) for m in ORDER[4:]]
+    swapped = {m: swap(far[m]) for m in (3, 5, 6)}
+    last, swapped[3], swapped[5], swapped[6] = lax.optimization_barrier((far[7], swapped[3], swapped[5], swapped[6]))
+    swapped[7] = swap(last)
+    b_blocks = [other, swap(join_call(near[1], near[2], near[4]))] + [swapped[m] for m in ORDER[4:]]
     b_blocks = [in_vmem(b) for b in b_blocks]
 
     e, a_stat, b_stat, flags = scores_call(core_arr, a_blocks, b_blocks, scale)
@@ -448,9 +454,9 @@
     from_xz = to_cube(p[5], 4)
     from_xyz = to_cube(p[7], 7)
     ga_lo = last_call(core_arr, w, b_blocks)
-    p0, p1, p2, p4 = near_call(ga_lo, got0, got_lo, from_xy, from_yz, from_xz)
+    p0, p1, p2, p4 = near_call(ga_lo, got0, got_lo, from_xy, from_yz, from_xz, from_xyz)
     wide = lambda a: a.astype(jnp.float32)
-    total = p0 + wide(from_xyz) + wide(to_cube(p1, 1)) + wide(to_cube(p2, 2)) + wide(to_cube(p4, 4))
+    total = p0 + wide(to_cube(p1, 1)) + wide(to_cube(p2, 2)) + wide(to_cube(p4, 4))
     kept, sent = total[:rows], total[rows:]
     got_sum = swap(sent)
     image_sum = jnp.where(first, kept, got_sum)

time: 118 us -> 118 us (level)
  local copies, waits for them, and re-layouts: 1.93 us -> 0.04 us
  Pallas kernels: 35.9 us -> 37.5 us
  starting transfers between devices: 37.7 us -> 39.1 us
  waiting for transfers between devices: 40.6 us -> 39.4 us
    unnamed x8 -> x4, local copies, waits for them, and re-layouts: 1.9 us -> 0.01 us
    ppermute x13, starting transfers between devices: 6.02 us -> 7.69 us  [swap(): return lax.ppermute(a, AXES, SWAP)]
    pallas_call x2, Pallas kernels: 0.6 us -> 2.2 us  [the longest x1 1.61 us: own_call(): pl.pallas_call(own_kernel, in_specs=[smem_spec()] + [pl.BlockSpec(memory_...]
  transfers between devices with their start and end apart: 30 -> 30, of which waited for: 19 -> 21; matrix products, arithmetic and copies ran while one was open for 0% -> 0% of each run, Pallas kernels for 8% -> 8%
where the time goes in v8:
time: 118 us
  waiting for transfers between devices  39.4 us (33%)
  starting transfers between devices  39.1 us (33%)
  Pallas kernels  37.5 us (32%)
  other arithmetic  1.25 us (1%)
    ppermute x17, waiting for transfers between devices, to_cube(): return lax.ppermute(a, AXES, across(m))  33.1 us
    ppermute x17, starting transfers between devices, to_cube(): return lax.ppermute(a, AXES, across(m))  31.4 us
    pallas_call x1, Pallas kernels, scores_call(): pl.pallas_call(functools.partial(scores_kernel, scale), in_specs=[smem_sp...  18.8 us
    ppermute x13, starting transfers between devices, swap(): return lax.ppermute(a, AXES, SWAP)  7.69 us
    pallas_call x1, Pallas kernels, weights_call(): pl.pallas_call(weights_kernel, in_specs=[smem_spec()] * 2 + [vmem_spec()]...  7.35 us
    ppermute x13, waiting for transfers between devices, swap(): return lax.ppermute(a, AXES, SWAP)  6.31 us
    pallas_call x1, Pallas kernels, middle_call(): pl.pallas_call(middle_kernel, in_specs=[smem_spec()] + [vmem_spec()] * 15...  5.76 us
    pallas_call x1, Pallas kernels, last_call(): pl.pallas_call(last_kernel, in_specs=[smem_spec()] + [vmem_spec()] * 7, o...  2.84 us
  transfers between devices with their start and end apart: 30, of which 21 were waited for; matrix products, arithmetic and copies ran while one was open for 0% of the time, Pallas kernels for 8%

profile of v8, /device:TPU:1, one launch (start us, length us, event | category | flops | bytes accessed | tf_op | source)
XLA Modules:
  0.0 118.1 jit_solution(15807175786399144908)
XLA Ops:
  0.6 1.5 %collective-permute-start = (bf16[160,768]{1,0:T(8,128)(2,1)}, bf16[160,768]{1,0:T(8,128)(2,1)S(1)}, u32[]{:S(2)}, u32[]{:S(2)}) collective-permute-start(bf16[160,768]{1,0:T(8,128)(2,1)} %images.1), channel_id=1, source_target_pairs={{0,16},{1,17},{2,18},{3,19},{4,20},{5,21},{6,22},{7,23},{8,24},{9,... | collective-permute-start | bytes 737288 | tf_op jit(solution)/shard_map/ppermute | solution.py:57
  2.1 0.1 collective-permute-start.1
  2.2 1.3 %collective-permute-done.got_images = bf16[160,768]{1,0:T(8,128)(2,1)S(1)} collective-permute-done((bf16[160,768]{1,0:T(8,128)(2,1)}, bf16[160,768]{1,0:T(8,128)(2,1)S(1)}, u32[]{:S(2)}, u32[]{:S(2)}) %collective-permute-start) | collective-permute-done | bytes 245792 | tf_op jit(solution)/shard_map/ppermute | solution.py:57
  3.5 0.4 collective-permute-done.1.got_texts
  3.9 1.6 %own.1 = (bf16[320,768]{1,0:T(8,128)(2,1)S(1)}, bf16[320,768]{1,0:T(8,128)(2,1)S(1)}) custom-call(s32[1]{0:T(128)} %bitcast.core_ref, bf16[160,768]{1,0:T(8,128)(2,1)} %images.1, bf16[160,768]{1,0:T(8,128)(2,1)} %texts.1, bf16[160,768]{1,0:T(8,128)(2,1)S(1)} %collective-permute-done.got_images, bf16[160,768]{1,0:T(8,128)(2,1)S(1)} %collective-permute-done.1.got_texts), custom_call_target="tpu_custom_call" | custom-call | bytes 1966080 | tf_op jit(solution)/shard_map/own/pallas_call | solution.py:125
  5.5 2.6 %collective-permute-start.2 = (bf16[320,768]{1,0:T(8,128)(2,1)S(1)}, bf16[320,768]{1,0:T(8,128)(2,1)S(1)}, u32[]{:S(2)}, u32[]{:S(2)}) collective-permute-start(bf16[320,768]{1,0:T(8,128)(2,1)S(1)} %get-tuple-element.25.refs_0_), channel_id=1, source_target_pairs={{0,4},{1,5},{2,6},{3,7},{4,0},{5,1},{6,2},{7,3},{8,12},{9,13},{10,... | collective-permute-start | bytes 1474568 | tf_op jit(solution)/shard_map/ppermute | solution.py:53
  8.1 1.3 %collective-permute-start.3 = (bf16[320,768]{1,0:T(8,128)(2,1)S(1)}, bf16[320,768]{1,0:T(8,128)(2,1)S(1)}, u32[]{:S(2)}, u32[]{:S(2)}) collective-permute-start(bf16[320,768]{1,0:T(8,128)(2,1)S(1)} %get-tuple-element.25.refs_0_), channel_id=1, source_target_pairs={{0,96},{1,97},{2,98},{3,99},{4,100},{5,101},{6,102},{7,103},{8,104... | collective-permute-start | bytes 1474568 | tf_op jit(solution)/shard_map/ppermute | solution.py:53
  9.4 3.8 %collective-permute-start.4 = (bf16[320,768]{1,0:T(8,128)(2,1)S(1)}, bf16[320,768]{1,0:T(8,128)(2,1)S(1)}, u32[]{:S(2)}, u32[]{:S(2)}) collective-permute-start(bf16[320,768]{1,0:T(8,128)(2,1)S(1)} %get-tuple-element.25.refs_0_), channel_id=1, source_target_pairs={{0,1},{1,0},{2,3},{3,2},{4,5},{5,4},{6,7},{7,6},{8,9},{9,8},{10,11... | collective-permute-start | bytes 1474568 | tf_op jit(solution)/shard_map/ppermute | solution.py:53
  13.2 1.6 %collective-permute-done.2.b0.refs_1_ = bf16[320,768]{1,0:T(8,128)(2,1)S(1)} collective-permute-done((bf16[320,768]{1,0:T(8,128)(2,1)S(1)}, bf16[320,768]{1,0:T(8,128)(2,1)S(1)}, u32[]{:S(2)}, u32[]{:S(2)}) %collective-permute-start.2) | collective-permute-done | bytes 491552 | tf_op jit(solution)/shard_map/ppermute | solution.py:53
  14.7 3.8 %collective-permute-start.6 = (bf16[320,768]{1,0:T(8,128)(2,1)S(1)}, bf16[320,768]{1,0:T(8,128)(2,1)S(1)}, u32[]{:S(2)}, u32[]{:S(2)}) collective-permute-start(bf16[320,768]{1,0:T(8,128)(2,1)S(1)} %collective-permute-done.2.b0.refs_1_), channel_id=1, source_target_pairs={{0,1},{1,0},{2,3},{3,2},{4,5},{5,4},{6,7},{7,6},{8,9},{9,8},{10,11... | collective-permute-start | bytes 1474568 | tf_op jit(solution)/shard_map/ppermute | solution.py:53
  18.6 2.5 %collective-permute-start.5 = (bf16[320,768]{1,0:T(8,128)(2,1)S(1)}, bf16[320,768]{1,0:T(8,128)(2,1)S(1)}, u32[]{:S(2)}, u32[]{:S(2)}) collective-permute-start(bf16[320,768]{1,0:T(8,128)(2,1)S(1)} %collective-permute-done.3.b1.refs_2_), channel_id=1, source_target_pairs={{0,4},{1,5},{2,6},{3,7},{4,0},{5,1},{6,2},{7,3},{8,12},{9,13},{10,... | collective-permute-start | bytes 1474568 | tf_op jit(solution)/shard_map/ppermute | solution.py:53
  21.1 0.0 collective-permute-done.4.b2.refs_3_
  21.1 1.0 collective-permute-start.7
  22.1 0.1 join.1
  22.2 0.1 collective-permute-start.9
  22.3 1.3 %collective-permute-start.8 = (bf16[320,768]{1,0:T(8,128)(2,1)S(1)}, bf16[320,768]{1,0:T(8,128)(2,1)S(1)}, u32[]{:S(2)}, u32[]{:S(2)}) collective-permute-start(bf16[320,768]{1,0:T(8,128)(2,1)S(1)} %collective-permute-done.2.b0.refs_1_), channel_id=1, source_target_pairs={{0,97},{1,96},{2,99},{3,98},{4,101},{5,100},{6,103},{7,102},{8,105... | collective-permute-start | bytes 1474568 | tf_op jit(solution)/shard_map/ppermute | solution.py:53
  23.5 1.6 %collective-permute-done.6.refs_5_ = bf16[320,768]{1,0:T(8,128)(2,1)S(1)} collective-permute-done((bf16[320,768]{1,0:T(8,128)(2,1)S(1)}, bf16[320,768]{1,0:T(8,128)(2,1)S(1)}, u32[]{:S(2)}, u32[]{:S(2)}) %collective-permute-start.6) | collective-permute-done | bytes 491552 | tf_op jit(solution)/shard_map/ppermute | solution.py:53
  25.1 0.0 collective-permute-start.11
  25.1 2.7 %collective-permute-done.5.refs_4_ = bf16[320,768]{1,0:T(8,128)(2,1)S(1)} collective-permute-done((bf16[320,768]{1,0:T(8,128)(2,1)S(1)}, bf16[320,768]{1,0:T(8,128)(2,1)S(1)}, u32[]{:S(2)}, u32[]{:S(2)}) %collective-permute-start.5) | collective-permute-done | bytes 491552 | tf_op jit(solution)/shard_map/ppermute | solution.py:53
  27.8 1.2 %collective-permute-done.7.refs_6_ = bf16[320,768]{1,0:T(8,128)(2,1)S(1)} collective-permute-done((bf16[320,768]{1,0:T(8,128)(2,1)S(1)}, bf16[320,768]{1,0:T(8,128)(2,1)S(1)}, u32[]{:S(2)}, u32[]{:S(2)}) %collective-permute-start.7) | collective-permute-done | bytes 491552 | tf_op jit(solution)/shard_map/ppermute | solution.py:53
  29.0 0.4 collective-permute-start.12
  29.4 5.7 %collective-permute-done.8.refs_7_ = bf16[320,768]{1,0:T(8,128)(2,1)S(1)} collective-permute-done((bf16[320,768]{1,0:T(8,128)(2,1)S(1)}, bf16[320,768]{1,0:T(8,128)(2,1)S(1)}, u32[]{:S(2)}, u32[]{:S(2)}) %collective-permute-start.8) | collective-permute-done | bytes 491552 | tf_op jit(solution)/shard_map/ppermute | solution.py:53
  35.0 0.0 collective-permute-done.11.refs_11_.refs_3_
  35.0 0.0 collective-permute-done.10.refs_10_.refs_2_
  35.0 0.0 collective-permute-done.12.refs_12_.refs_4_
  35.0 1.0 collective-permute-start.13
  36.1 0.0 collective-permute-done.9.refs_9_.refs_1_
  36.1 1.5 %collective-permute-done.13.refs_13_.refs_5_ = bf16[320,768]{1,0:T(8,128)(2,1)S(1)} collective-permute-done((bf16[320,768]{1,0:T(8,128)(2,1)S(1)}, bf16[320,768]{1,0:T(8,128)(2,1)S(1)}, u32[]{:S(2)}, u32[]{:S(2)}) %collective-permute-start.13) | collective-permute-done | bytes 491552 | tf_op jit(solution)/shard_map/ppermute | solution.py:57
  37.6 18.8 %scores.1 = (f32[2,1280,1280]{2,1,0:T(8,128)S(1)}, f32[8,320]{1,0:T(8,128)S(1)}, f32[8,320]{1,0:T(8,128)S(1)}, s32[2]{0:T(128)S(1)}) custom-call(s32[1]{0:T(128)} %bitcast.core_ref, bf16[320,768]{1,0:T(8,128)(2,1)S(1)} %get-tuple-element.25.refs_0_, bf16[320,768]{1,0:T(8,128)(2,1)S(1)} %collective-permute-done.2.b0.refs_1_, ...), custom_call_target="tpu_custom_call" | custom-call | flops 5033164800 | tf_op jit(solution)/shard_map/scores/pallas_call | solution.py:236
  56.4 0.5 collective-permute-start.14
  56.9 0.8 collective-permute-done.14.got_ref
  57.7 1.9 %collective-permute-start.15 = (f32[8,320]{1,0:T(8,128)S(1)}, f32[8,320]{1,0:T(8,128)S(1)}, u32[]{:S(2)}, u32[]{:S(2)}) collective-permute-start(f32[8,320]{1,0:T(8,128)S(1)} %merge.4.mine_ref), channel_id=1, source_target_pairs={{0,4},{1,5},{2,6},{3,7},{4,0},{5,1},{6,2},{7,3},{8,12},{9,13},{10,... | collective-permute-start | bytes 30728 | tf_op jit(solution)/shard_map/ppermute | solution.py:53
  59.6 1.9 %collective-permute-done.15.got_ref = f32[8,320]{1,0:T(8,128)S(1)} collective-permute-done((f32[8,320]{1,0:T(8,128)S(1)}, f32[8,320]{1,0:T(8,128)S(1)}, u32[]{:S(2)}, u32[]{:S(2)}) %collective-permute-start.15) | collective-permute-done | bytes 10272 | tf_op jit(solution)/shard_map/ppermute | solution.py:53
  61.6 0.1 collective-permute-start.16
  61.7 2.5 %collective-permute-done.16.got_ref = f32[8,320]{1,0:T(8,128)S(1)} collective-permute-done((f32[8,320]{1,0:T(8,128)S(1)}, f32[8,320]{1,0:T(8,128)S(1)}, u32[]{:S(2)}, u32[]{:S(2)}) %collective-permute-start.16) | collective-permute-done | bytes 10272 | tf_op jit(solution)/shard_map/ppermute | solution.py:53
  64.3 2.3 %collective-permute-start.17 = (f32[8,320]{1,0:T(8,128)S(1)}, f32[8,320]{1,0:T(8,128)S(1)}, u32[]{:S(2)}, u32[]{:S(2)}) collective-permute-start(f32[8,320]{1,0:T(8,128)S(1)} %merge.6.mine_ref), channel_id=1, source_target_pairs={{0,1},{1,0},{2,3},{3,2},{4,5},{5,4},{6,7},{7,6},{8,9},{9,8},{10,11... | collective-permute-start | bytes 30728 | tf_op jit(solution)/shard_map/ppermute | solution.py:53
  66.6 1.5 %collective-permute-done.17.got_ref = f32[8,320]{1,0:T(8,128)S(1)} collective-permute-done((f32[8,320]{1,0:T(8,128)S(1)}, f32[8,320]{1,0:T(8,128)S(1)}, u32[]{:S(2)}, u32[]{:S(2)}) %collective-permute-start.17) | collective-permute-done | bytes 10272 | tf_op jit(solution)/shard_map/ppermute | solution.py:53
  68.1 2.7 %collective-permute-start.18 = (f32[8,320]{1,0:T(8,128)S(1)}, f32[8,320]{1,0:T(8,128)S(1)}, u32[]{:S(2)}, u32[]{:S(2)}) collective-permute-start(f32[8,320]{1,0:T(8,128)S(1)} %merge.7.a_lse), channel_id=1, source_target_pairs={{0,16},{1,17},{2,18},{3,19},{4,20},{5,21},{6,22},{7,23},{8,24},{9,... | collective-permute-start | bytes 30728 | tf_op jit(solution)/shard_map/ppermute | solution.py:57
  70.8 0.8 collective-permute-done.18.b_lse
  71.6 7.4 %weights.1 = (bf16[2,1280,1280]{2,1,0:T(8,128)(2,1)S(1)}, bf16[1280,768]{1,0:T(8,128)(2,1)S(1)}) custom-call(s32[1]{0:T(128)} %bitcast.core_ref, s32[2]{0:T(128)S(1)} %get-tuple-element.31.flags, f32[2,1280,1280]{2,1,0:T(8,128)S(1)} %get-tuple-element.32.e_ref, f32[8,320]{1,0:T(8,128)S(1)} %merge.7.a_lse, f32[8,320]{1,0:T(8,128)S(1)} %collective-permute-done.18.b_lse, ...), custom_call_target="tpu_custom_call" | custom-call | flops 2516582400 | bytes 19660800 | tf_op jit(solution)/shard_map/weights/pallas_call | solution.py:309
  79.0 0.4 collective-permute-start.21
  79.4 5.8 %middle.1 = (f32[1280,768]{1,0:T(8,128)S(1)}, f32[320,768]{1,0:T(8,128)S(1)}, bf16[960,768]{1,0:T(8,128)(2,1)S(1)}) custom-call(s32[1]{0:T(128)} %bitcast.core_ref, bf16[2,1280,1280]{2,1,0:T(8,128)(2,1)S(1)} %get-tuple-element.35.w_ref, bf16[320,768]{1,0:T(8,128)(2,1)S(1)} %get-tuple-element.25.refs_0_, ...), custom_call_target="tpu_custom_call" | custom-call | flops 5033164800 | tf_op jit(solution)/shard_map/middle/pallas_call | solution.py:340
  85.2 0.3 collective-permute-start.20
  85.4 0.3 collective-permute-start.19
  85.8 0.3 far.1
  86.1 1.9 %collective-permute-start.22 = (bf16[320,768]{1,0:T(8,128)(2,1)S(1)}, bf16[320,768]{1,0:T(8,128)(2,1)S(1)}, u32[]{:S(2)}, u32[]{:S(2)}) collective-permute-start(bf16[320,768]{1,0:T(8,128)(2,1)S(1)} %get-tuple-element.40), channel_id=1, source_target_pairs={{0,4},{1,5},{2,6},{3,7},{4,0},{5,1},{6,2},{7,3},{8,12},{9,13},{10,... | collective-permute-start | bytes 1474568 | tf_op jit(solution)/shard_map/ppermute | solution.py:53
  88.0 2.3 %collective-permute-start.24 = (bf16[320,768]{1,0:T(8,128)(2,1)S(1)}, bf16[320,768]{1,0:T(8,128)(2,1)S(1)}, u32[]{:S(2)}, u32[]{:S(2)}) collective-permute-start(bf16[320,768]{1,0:T(8,128)(2,1)S(1)} %get-tuple-element.42), channel_id=1, source_target_pairs={{0,1},{1,0},{2,3},{3,2},{4,5},{5,4},{6,7},{7,6},{8,9},{9,8},{10,11... | collective-permute-start | bytes 1474568 | tf_op jit(solution)/shard_map/ppermute | solution.py:53
  90.3 2.2 %collective-permute-start.25 = (bf16[320,768]{1,0:T(8,128)(2,1)S(1)}, bf16[320,768]{1,0:T(8,128)(2,1)S(1)}, u32[]{:S(2)}, u32[]{:S(2)}) collective-permute-start(bf16[320,768]{1,0:T(8,128)(2,1)S(1)} %get-tuple-element.43), channel_id=1, source_target_pairs={{0,101},{1,100},{2,103},{3,102},{4,97},{5,96},{6,99},{7,98},{8,109... | collective-permute-start | bytes 1474568 | tf_op jit(solution)/shard_map/ppermute | solution.py:53
  92.4 2.8 %last.1.ga_lo = f32[1280,768]{1,0:T(8,128)S(1)} custom-call(s32[1]{0:T(128)} %bitcast.core_ref, bf16[2,1280,1280]{2,1,0:T(8,128)(2,1)S(1)} %get-tuple-element.35.w_ref, bf16[320,768]{1,0:T(8,128)(2,1)S(1)} %get-tuple-element.26.refs_8_.refs_0_, bf16[960,768]{1,0:T(8,128)(2,1)S(1)} %collective-permute-done.9.refs_9_.refs_1_, ...), custom_call_target="tpu_custom_call" | custom-call | flops 2516582400 | tf_op jit(solution)/shard_map/last/pallas_call | solution.py:386
  95.3 0.1 collective-permute-done.22.r_xy
  95.4 0.6 collective-permute-done.23.r_yz
  96.0 5.3 %collective-permute-done.24.r_xz = bf16[320,768]{1,0:T(8,128)(2,1)S(1)} collective-permute-done((bf16[320,768]{1,0:T(8,128)(2,1)S(1)}, bf16[320,768]{1,0:T(8,128)(2,1)S(1)}, u32[]{:S(2)}, u32[]{:S(2)}) %collective-permute-start.24) | collective-permute-done | bytes 491552 | tf_op jit(solution)/shard_map/ppermute | solution.py:53
  101.3 1.0 collective-permute-done.25.r_xyz
  102.3 0.6 near.1
  102.9 1.6 %collective-permute-start.26 = (bf16[320,768]{1,0:T(8,128)(2,1)S(1)}, bf16[320,768]{1,0:T(8,128)(2,1)S(1)}, u32[]{:S(2)}, u32[]{:S(2)}) collective-permute-start(bf16[320,768]{1,0:T(8,128)(2,1)S(1)} %get-tuple-element.45), channel_id=1, source_target_pairs={{0,4},{1,5},{2,6},{3,7},{4,0},{5,1},{6,2},{7,3},{8,12},{9,13},{10,... | collective-permute-start | bytes 1474568 | tf_op jit(solution)/shard_map/ppermute | solution.py:53
  104.4 1.5 %collective-permute-start.27 = (bf16[320,768]{1,0:T(8,128)(2,1)S(1)}, bf16[320,768]{1,0:T(8,128)(2,1)S(1)}, u32[]{:S(2)}, u32[]{:S(2)}) collective-permute-start(bf16[320,768]{1,0:T(8,128)(2,1)S(1)} %get-tuple-element.46), channel_id=1, source_target_pairs={{0,96},{1,97},{2,98},{3,99},{4,100},{5,101},{6,102},{7,103},{8,104... | collective-permute-start | bytes 1474568 | tf_op jit(solution)/shard_map/ppermute | solution.py:53
  106.0 1.4 %collective-permute-start.28 = (bf16[320,768]{1,0:T(8,128)(2,1)S(1)}, bf16[320,768]{1,0:T(8,128)(2,1)S(1)}, u32[]{:S(2)}, u32[]{:S(2)}) collective-permute-start(bf16[320,768]{1,0:T(8,128)(2,1)S(1)} %get-tuple-element.47), channel_id=1, source_target_pairs={{0,1},{1,0},{2,3},{3,2},{4,5},{5,4},{6,7},{7,6},{8,9},{9,8},{10,11... | collective-permute-start | bytes 1474568 | tf_op jit(solution)/shard_map/ppermute | solution.py:53
  107.4 4.7 %collective-permute-done.26 = bf16[320,768]{1,0:T(8,128)(2,1)S(1)} collective-permute-done((bf16[320,768]{1,0:T(8,128)(2,1)S(1)}, bf16[320,768]{1,0:T(8,128)(2,1)S(1)}, u32[]{:S(2)}, u32[]{:S(2)}) %collective-permute-start.26) | collective-permute-done | bytes 491552 | tf_op jit(solution)/shard_map/ppermute | solution.py:53
  112.1 0.4 collective-permute-done.27
  112.5 2.4 %collective-permute-done.28 = bf16[320,768]{1,0:T(8,128)(2,1)S(1)} collective-permute-done((bf16[320,768]{1,0:T(8,128)(2,1)S(1)}, bf16[320,768]{1,0:T(8,128)(2,1)S(1)}, u32[]{:S(2)}, u32[]{:S(2)}) %collective-permute-start.28) | collective-permute-done | bytes 491552 | tf_op jit(solution)/shard_map/ppermute | solution.py:53
  114.9 0.2 convert_add_fusion
  115.1 0.4 collective-permute-start.29
  115.6 1.5 %collective-permute-done.29 = f32[160,768]{1,0:T(8,128)S(1)} collective-permute-done((f32[160,768]{1,0:T(8,128)S(1)}, f32[160,768]{1,0:T(8,128)S(1)}, u32[]{:S(2)}, u32[]{:S(2)}) %collective-permute-start.29) | collective-permute-done | bytes 491552 | tf_op jit(solution)/shard_map/ppermute | solution.py:57
  117.1 1.0 convert_subtract_fusion
  (15 shorter events, 0.2 us)
Async XLA Ops:
  0.6 2.9 %collective-permute-start = (bf16[160,768]{1,0:T(8,128)(2,1)}, bf16[160,768]{1,0:T(8,128)(2,1)S(1)}, u32[]{:S(2)}, u32[]{:S(2)}) collective-permute-start(bf16[160,768]{1,0:T(8,128)(2,1)} %images.1), channel_id=1, source_target_pairs={{0,16},{1,17},{2,18},{3,19},{4,20},{5,21},{6,22},{7,23},{8,24},{9,... | collective-permute-start | bytes 737288 | tf_op jit(solution)/shard_map/ppermute | solution.py:57
  2.1 1.7 %collective-permute-start.1 = (bf16[160,768]{1,0:T(8,128)(2,1)}, bf16[160,768]{1,0:T(8,128)(2,1)S(1)}, u32[]{:S(2)}, u32[]{:S(2)}) collective-permute-start(bf16[160,768]{1,0:T(8,128)(2,1)} %texts.1), channel_id=1, source_target_pairs={{0,16},{1,17},{2,18},{3,19},{4,20},{5,21},{6,22},{7,23},{8,24},{9,... | collective-permute-start | bytes 737288 | tf_op jit(solution)/shard_map/ppermute | solution.py:57
  5.5 9.3 %collective-permute-start.2 = (bf16[320,768]{1,0:T(8,128)(2,1)S(1)}, bf16[320,768]{1,0:T(8,128)(2,1)S(1)}, u32[]{:S(2)}, u32[]{:S(2)}) collective-permute-start(bf16[320,768]{1,0:T(8,128)(2,1)S(1)} %get-tuple-element.25.refs_0_), channel_id=1, source_target_pairs={{0,4},{1,5},{2,6},{3,7},{4,0},{5,1},{6,2},{7,3},{8,12},{9,13},{10,... | collective-permute-start | bytes 1474568 | tf_op jit(solution)/shard_map/ppermute | solution.py:53
  8.1 10.5 %collective-permute-start.3 = (bf16[320,768]{1,0:T(8,128)(2,1)S(1)}, bf16[320,768]{1,0:T(8,128)(2,1)S(1)}, u32[]{:S(2)}, u32[]{:S(2)}) collective-permute-start(bf16[320,768]{1,0:T(8,128)(2,1)S(1)} %get-tuple-element.25.refs_0_), channel_id=1, source_target_pairs={{0,96},{1,97},{2,98},{3,99},{4,100},{5,101},{6,102},{7,103},{8,104... | collective-permute-start | bytes 1474568 | tf_op jit(solution)/shard_map/ppermute | solution.py:53
  9.4 11.7 %collective-permute-start.4 = (bf16[320,768]{1,0:T(8,128)(2,1)S(1)}, bf16[320,768]{1,0:T(8,128)(2,1)S(1)}, u32[]{:S(2)}, u32[]{:S(2)}) collective-permute-start(bf16[320,768]{1,0:T(8,128)(2,1)S(1)} %get-tuple-element.25.refs_0_), channel_id=1, source_target_pairs={{0,1},{1,0},{2,3},{3,2},{4,5},{5,4},{6,7},{7,6},{8,9},{9,8},{10,11... | collective-permute-start | bytes 1474568 | tf_op jit(solution)/shard_map/ppermute | solution.py:53
  14.7 10.4 %collective-permute-start.6 = (bf16[320,768]{1,0:T(8,128)(2,1)S(1)}, bf16[320,768]{1,0:T(8,128)(2,1)S(1)}, u32[]{:S(2)}, u32[]{:S(2)}) collective-permute-start(bf16[320,768]{1,0:T(8,128)(2,1)S(1)} %collective-permute-done.2.b0.refs_1_), channel_id=1, source_target_pairs={{0,1},{1,0},{2,3},{3,2},{4,5},{5,4},{6,7},{7,6},{8,9},{9,8},{10,11... | collective-permute-start | bytes 1474568 | tf_op jit(solution)/shard_map/ppermute | solution.py:53
  18.6 9.2 %collective-permute-start.5 = (bf16[320,768]{1,0:T(8,128)(2,1)S(1)}, bf16[320,768]{1,0:T(8,128)(2,1)S(1)}, u32[]{:S(2)}, u32[]{:S(2)}) collective-permute-start(bf16[320,768]{1,0:T(8,128)(2,1)S(1)} %collective-permute-done.3.b1.refs_2_), channel_id=1, source_target_pairs={{0,4},{1,5},{2,6},{3,7},{4,0},{5,1},{6,2},{7,3},{8,12},{9,13},{10,... | collective-permute-start | bytes 1474568 | tf_op jit(solution)/shard_map/ppermute | solution.py:53
  21.1 7.9 %collective-permute-start.7 = (bf16[320,768]{1,0:T(8,128)(2,1)S(1)}, bf16[320,768]{1,0:T(8,128)(2,1)S(1)}, u32[]{:S(2)}, u32[]{:S(2)}) collective-permute-start(bf16[320,768]{1,0:T(8,128)(2,1)S(1)} %collective-permute-done.4.b2.refs_3_), channel_id=1, source_target_pairs={{0,96},{1,97},{2,98},{3,99},{4,100},{5,101},{6,102},{7,103},{8,104... | collective-permute-start | bytes 1474568 | tf_op jit(solution)/shard_map/ppermute | solution.py:53
  22.2 13.9 %collective-permute-start.9 = (bf16[960,768]{1,0:T(8,128)(2,1)S(1)}, bf16[960,768]{1,0:T(8,128)(2,1)S(1)}, u32[]{:S(2)}, u32[]{:S(2)}) collective-permute-start(bf16[960,768]{1,0:T(8,128)(2,1)S(1)} %join.1), channel_id=1, source_target_pairs={{0,16},{1,17},{2,18},{3,19},{4,20},{5,21},{6,22},{7,23},{8,24},{9,... | collective-permute-start | bytes 4423688 | tf_op jit(solution)/shard_map/ppermute | solution.py:57
  22.3 12.8 %collective-permute-start.8 = (bf16[320,768]{1,0:T(8,128)(2,1)S(1)}, bf16[320,768]{1,0:T(8,128)(2,1)S(1)}, u32[]{:S(2)}, u32[]{:S(2)}) collective-permute-start(bf16[320,768]{1,0:T(8,128)(2,1)S(1)} %collective-permute-done.2.b0.refs_1_), channel_id=1, source_target_pairs={{0,97},{1,96},{2,99},{3,98},{4,101},{5,100},{6,103},{7,102},{8,105... | collective-permute-start | bytes 1474568 | tf_op jit(solution)/shard_map/ppermute | solution.py:53
  25.1 9.9 %collective-permute-start.11 = (bf16[320,768]{1,0:T(8,128)(2,1)S(1)}, bf16[320,768]{1,0:T(8,128)(2,1)S(1)}, u32[]{:S(2)}, u32[]{:S(2)}) collective-permute-start(bf16[320,768]{1,0:T(8,128)(2,1)S(1)} %collective-permute-done.6.refs_5_), channel_id=1, source_target_pairs={{0,16},{1,17},{2,18},{3,19},{4,20},{5,21},{6,22},{7,23},{8,24},{9,... | collective-permute-start | bytes 1474568 | tf_op jit(solution)/shard_map/ppermute | solution.py:57
  27.8 7.3 %collective-permute-start.10 = (bf16[320,768]{1,0:T(8,128)(2,1)S(1)}, bf16[320,768]{1,0:T(8,128)(2,1)S(1)}, u32[]{:S(2)}, u32[]{:S(2)}) collective-permute-start(bf16[320,768]{1,0:T(8,128)(2,1)S(1)} %collective-permute-done.5.refs_4_), channel_id=1, source_target_pairs={{0,16},{1,17},{2,18},{3,19},{4,20},{5,21},{6,22},{7,23},{8,24},{9,... | collective-permute-start | bytes 1474568 | tf_op jit(solution)/shard_map/ppermute | solution.py:57
  29.0 6.1 %collective-permute-start.12 = (bf16[320,768]{1,0:T(8,128)(2,1)S(1)}, bf16[320,768]{1,0:T(8,128)(2,1)S(1)}, u32[]{:S(2)}, u32[]{:S(2)}) collective-permute-start(bf16[320,768]{1,0:T(8,128)(2,1)S(1)} %collective-permute-done.7.refs_6_), channel_id=1, source_target_pairs={{0,16},{1,17},{2,18},{3,19},{4,20},{5,21},{6,22},{7,23},{8,24},{9,... | collective-permute-start | bytes 1474568 | tf_op jit(solution)/shard_map/ppermute | solution.py:57
  35.0 2.5 %collective-permute-start.13 = (bf16[320,768]{1,0:T(8,128)(2,1)S(1)}, bf16[320,768]{1,0:T(8,128)(2,1)S(1)}, u32[]{:S(2)}, u32[]{:S(2)}) collective-permute-start(bf16[320,768]{1,0:T(8,128)(2,1)S(1)} %collective-permute-done.8.refs_7_), channel_id=1, source_target_pairs={{0,16},{1,17},{2,18},{3,19},{4,20},{5,21},{6,22},{7,23},{8,24},{9,... | collective-permute-start | bytes 1474568 | tf_op jit(solution)/shard_map/ppermute | solution.py:57
  56.4 1.3 %collective-permute-start.14 = (f32[8,320]{1,0:T(8,128)S(1)}, f32[8,320]{1,0:T(8,128)S(1)}, u32[]{:S(2)}, u32[]{:S(2)}) collective-permute-start(f32[8,320]{1,0:T(8,128)S(1)} %get-tuple-element.34), channel_id=1, source_target_pairs={{0,16},{1,17},{2,18},{3,19},{4,20},{5,21},{6,22},{7,23},{8,24},{9,... | collective-permute-start | bytes 30728 | tf_op jit(solution)/shard_map/ppermute | solution.py:57
  57.7 3.8 %collective-permute-start.15 = (f32[8,320]{1,0:T(8,128)S(1)}, f32[8,320]{1,0:T(8,128)S(1)}, u32[]{:S(2)}, u32[]{:S(2)}) collective-permute-start(f32[8,320]{1,0:T(8,128)S(1)} %merge.4.mine_ref), channel_id=1, source_target_pairs={{0,4},{1,5},{2,6},{3,7},{4,0},{5,1},{6,2},{7,3},{8,12},{9,13},{10,... | collective-permute-start | bytes 30728 | tf_op jit(solution)/shard_map/ppermute | solution.py:53
  61.6 2.6 %collective-permute-start.16 = (f32[8,320]{1,0:T(8,128)S(1)}, f32[8,320]{1,0:T(8,128)S(1)}, u32[]{:S(2)}, u32[]{:S(2)}) collective-permute-start(f32[8,320]{1,0:T(8,128)S(1)} %merge.5.mine_ref), channel_id=1, source_target_pairs={{0,96},{1,97},{2,98},{3,99},{4,100},{5,101},{6,102},{7,103},{8,104... | collective-permute-start | bytes 30728 | tf_op jit(solution)/shard_map/ppermute | solution.py:53
  64.3 3.8 %collective-permute-start.17 = (f32[8,320]{1,0:T(8,128)S(1)}, f32[8,320]{1,0:T(8,128)S(1)}, u32[]{:S(2)}, u32[]{:S(2)}) collective-permute-start(f32[8,320]{1,0:T(8,128)S(1)} %merge.6.mine_ref), channel_id=1, source_target_pairs={{0,1},{1,0},{2,3},{3,2},{4,5},{5,4},{6,7},{7,6},{8,9},{9,8},{10,11... | collective-permute-start | bytes 30728 | tf_op jit(solution)/shard_map/ppermute | solution.py:53
  68.1 3.5 %collective-permute-start.18 = (f32[8,320]{1,0:T(8,128)S(1)}, f32[8,320]{1,0:T(8,128)S(1)}, u32[]{:S(2)}, u32[]{:S(2)}) collective-permute-start(f32[8,320]{1,0:T(8,128)S(1)} %merge.7.a_lse), channel_id=1, source_target_pairs={{0,16},{1,17},{2,18},{3,19},{4,20},{5,21},{6,22},{7,23},{8,24},{9,... | collective-permute-start | bytes 30728 | tf_op jit(solution)/shard_map/ppermute | solution.py:57
  79.0 6.8 %collective-permute-start.21 = (bf16[1280,768]{1,0:T(8,128)(2,1)S(1)}, bf16[1280,768]{1,0:T(8,128)(2,1)S(1)}, u32[]{:S(2)}, u32[]{:S(2)}) collective-permute-start(bf16[1280,768]{1,0:T(8,128)(2,1)S(1)} %get-tuple-element.39), channel_id=1, source_target_pairs={{0,16},{1,17},{2,18},{3,19},{4,20},{5,21},{6,22},{7,23},{8,24},{9,... | collective-permute-start | bytes 5898248 | tf_op jit(solution)/shard_map/ppermute | solution.py:57
  85.2 10.1 %collective-permute-start.20 = (bf16[960,768]{1,0:T(8,128)(2,1)S(1)}, bf16[960,768]{1,0:T(8,128)(2,1)S(1)}, u32[]{:S(2)}, u32[]{:S(2)}) collective-permute-start(bf16[960,768]{1,0:T(8,128)(2,1)S(1)} %get-tuple-element.37), channel_id=1, source_target_pairs={{0,16},{1,17},{2,18},{3,19},{4,20},{5,21},{6,22},{7,23},{8,24},{9,... | collective-permute-start | bytes 4423688 | tf_op jit(solution)/shard_map/ppermute | solution.py:57
  85.4 4.8 %collective-permute-start.19 = (f32[320,768]{1,0:T(8,128)S(1)}, f32[320,768]{1,0:T(8,128)S(1)}, u32[]{:S(2)}, u32[]{:S(2)}) collective-permute-start(f32[320,768]{1,0:T(8,128)S(1)} %get-tuple-element.36), channel_id=1, source_target_pairs={{0,16},{1,17},{2,18},{3,19},{4,20},{5,21},{6,22},{7,23},{8,24},{9,... | collective-permute-start | bytes 2949128 | tf_op jit(solution)/shard_map/ppermute | solution.py:57
  86.1 9.3 %collective-permute-start.22 = (bf16[320,768]{1,0:T(8,128)(2,1)S(1)}, bf16[320,768]{1,0:T(8,128)(2,1)S(1)}, u32[]{:S(2)}, u32[]{:S(2)}) collective-permute-start(bf16[320,768]{1,0:T(8,128)(2,1)S(1)} %get-tuple-element.40), channel_id=1, source_target_pairs={{0,4},{1,5},{2,6},{3,7},{4,0},{5,1},{6,2},{7,3},{8,12},{9,13},{10,... | collective-permute-start | bytes 1474568 | tf_op jit(solution)/shard_map/ppermute | solution.py:53
  88.0 8.0 %collective-permute-start.23 = (bf16[320,768]{1,0:T(8,128)(2,1)S(1)}, bf16[320,768]{1,0:T(8,128)(2,1)S(1)}, u32[]{:S(2)}, u32[]{:S(2)}) collective-permute-start(bf16[320,768]{1,0:T(8,128)(2,1)S(1)} %get-tuple-element.41), channel_id=1, source_target_pairs={{0,96},{1,97},{2,98},{3,99},{4,100},{5,101},{6,102},{7,103},{8,104... | collective-permute-start | bytes 1474568 | tf_op jit(solution)/shard_map/ppermute | solution.py:53
  88.0 13.3 %collective-permute-start.24 = (bf16[320,768]{1,0:T(8,128)(2,1)S(1)}, bf16[320,768]{1,0:T(8,128)(2,1)S(1)}, u32[]{:S(2)}, u32[]{:S(2)}) collective-permute-start(bf16[320,768]{1,0:T(8,128)(2,1)S(1)} %get-tuple-element.42), channel_id=1, source_target_pairs={{0,1},{1,0},{2,3},{3,2},{4,5},{5,4},{6,7},{7,6},{8,9},{9,8},{10,11... | collective-permute-start | bytes 1474568 | tf_op jit(solution)/shard_map/ppermute | solution.py:53
  90.3 12.0 %collective-permute-start.25 = (bf16[320,768]{1,0:T(8,128)(2,1)S(1)}, bf16[320,768]{1,0:T(8,128)(2,1)S(1)}, u32[]{:S(2)}, u32[]{:S(2)}) collective-permute-start(bf16[320,768]{1,0:T(8,128)(2,1)S(1)} %get-tuple-element.43), channel_id=1, source_target_pairs={{0,101},{1,100},{2,103},{3,102},{4,97},{5,96},{6,99},{7,98},{8,109... | collective-permute-start | bytes 1474568 | tf_op jit(solution)/shard_map/ppermute | solution.py:53
  102.9 9.3 %collective-permute-start.26 = (bf16[320,768]{1,0:T(8,128)(2,1)S(1)}, bf16[320,768]{1,0:T(8,128)(2,1)S(1)}, u32[]{:S(2)}, u32[]{:S(2)}) collective-permute-start(bf16[320,768]{1,0:T(8,128)(2,1)S(1)} %get-tuple-element.45), channel_id=1, source_target_pairs={{0,4},{1,5},{2,6},{3,7},{4,0},{5,1},{6,2},{7,3},{8,12},{9,13},{10,... | collective-permute-start | bytes 1474568 | tf_op jit(solution)/shard_map/ppermute | solution.py:53
  104.4 8.1 %collective-permute-start.27 = (bf16[320,768]{1,0:T(8,128)(2,1)S(1)}, bf16[320,768]{1,0:T(8,128)(2,1)S(1)}, u32[]{:S(2)}, u32[]{:S(2)}) collective-permute-start(bf16[320,768]{1,0:T(8,128)(2,1)S(1)} %get-tuple-element.46), channel_id=1, source_target_pairs={{0,96},{1,97},{2,98},{3,99},{4,100},{5,101},{6,102},{7,103},{8,104... | collective-permute-start | bytes 1474568 | tf_op jit(solution)/shard_map/ppermute | solution.py:53
  106.0 8.9 %collective-permute-start.28 = (bf16[320,768]{1,0:T(8,128)(2,1)S(1)}, bf16[320,768]{1,0:T(8,128)(2,1)S(1)}, u32[]{:S(2)}, u32[]{:S(2)}) collective-permute-start(bf16[320,768]{1,0:T(8,128)(2,1)S(1)} %get-tuple-element.47), channel_id=1, source_target_pairs={{0,1},{1,0},{2,3},{3,2},{4,5},{5,4},{6,7},{7,6},{8,9},{9,8},{10,11... | collective-permute-start | bytes 1474568 | tf_op jit(solution)/shard_map/ppermute | solution.py:53
  114.9 2.2 %copy-start = (bf16[160,768]{1,0:T(8,128)(2,1)S(1)}, bf16[160,768]{1,0:T(8,128)(2,1)}, u32[]{:S(2)}) copy-start(bf16[160,768]{1,0:T(8,128)(2,1)} %images.1) | copy-start | bytes 737284
  114.9 2.2 %copy-start.1 = (bf16[160,768]{1,0:T(8,128)(2,1)S(1)}, bf16[160,768]{1,0:T(8,128)(2,1)}, u32[]{:S(2)}) copy-start(bf16[160,768]{1,0:T(8,128)(2,1)} %texts.1) | copy-start | bytes 737284
  115.1 1.9 %collective-permute-start.29 = (f32[160,768]{1,0:T(8,128)S(1)}, f32[160,768]{1,0:T(8,128)S(1)}, u32[]{:S(2)}, u32[]{:S(2)}) collective-permute-start(f32[160,768]{1,0:T(8,128)S(1)} %slice.9), channel_id=1, source_target_pairs={{0,16},{1,17},{2,18},{3,19},{4,20},{5,21},{6,22},{7,23},{8,24},{9,... | collective-permute-start | bytes 1474568 | tf_op jit(solution)/shard_map/ppermute | solution.py:57

commit v9 on v8

--- a/solution.py
+++ b/solution.py
@@ -395,10 +395,10 @@
     )(core, w, *b_blocks)
 
 
-def near_kernel(ga_lo, got0, got_lo, r_xy, r_yz, r_xz, r_xyz, p0, p1, p2, p4):
+def near_kernel(ga_lo, got0, got_lo, r_xy, r_yz, r_xz, p0, p1, p2, p4):
     rows = p0.shape[0]
     wide = lambda ref: ref[...].astype(jnp.float32)
-    p0[...] = ga_lo[:rows] + got0[...] + wide(r_xyz)
+    p0[...] = ga_lo[:rows] + got0[...]
     part = lambda j: ga_lo[j * rows : (j + 1) * rows, :] + got_lo[(j - 1) * rows : j * rows, :].astype(jnp.float32)
     p1[...] = (part(1) + wide(r_xz)).astype(jnp.bfloat16)
     p2[...] = (part(2) + wide(r_xy)).astype(jnp.bfloat16)
@@ -410,7 +410,7 @@
     narrow = jax.ShapeDtypeStruct((rows, features), jnp.bfloat16)
     return pl.pallas_call(
         near_kernel,
-        in_specs=[vmem_spec()] * 7,
+        in_specs=[vmem_spec()] * 6,
         out_specs=[vmem_spec()] * 4,
         out_shape=[pltpu.VMEM((rows, features), jnp.float32)] + [narrow] * 3,
         compiler_params=params(),
@@ -428,13 +428,14 @@
     in_hbm = lambda a: pltpu.with_memory_space_constraint(a, pltpu.HBM)
     own, other = own_call(core_arr, in_hbm(images), in_hbm(texts), swap(images), swap(texts))
     near = {m: to_cube(own, m) for m in (4, 2, 1)}
-    far = {7: to_cube(near[1], 6), 5: to_cube(near[1], 4), 3: to_cube(near[2], 1), 6: to_cube(near[4], 2)}
+    far = {7: to_cube(own, 7), 5: to_cube(near[1], 4), 3: to_cube(near[2], 1), 6: to_cube(near[4], 2)}
     blocks = {0: own, **near, **far}
     in_vmem = lambda a: pltpu.with_memory_space_constraint(a, pltpu.VMEM)
     a_blocks = [in_vmem(blocks[m]) for m in ORDER]
-    swapped = {m: swap(far[m]) for m in (3, 5, 6)}
-    last, swapped[3], swapped[5], swapped[6] = lax.optimization_barrier((far[7], swapped[3], swapped[5], swapped[6]))
-    swapped[7] = swap(last)
+    swapped = {m: swap(far[m]) for m in (7, 5, 3)}
+    last, *held = lax.optimization_barrier((far[6], swapped[7], swapped[5], swapped[3]))
+    swapped.update(zip((7, 5, 3), held))
+    swapped[6] = swap(last)
     b_blocks = [other, swap(join_call(near[1], near[2], near[4]))] + [swapped[m] for m in ORDER[4:]]
     b_blocks = [in_vmem(b) for b in b_blocks]
 
@@ -454,9 +455,9 @@
     from_xz = to_cube(p[5], 4)
     from_xyz = to_cube(p[7], 7)
     ga_lo = last_call(core_arr, w, b_blocks)
-    p0, p1, p2, p4 = near_call(ga_lo, got0, got_lo, from_xy, from_yz, from_xz, from_xyz)
+    p0, p1, p2, p4 = near_call(ga_lo, got0, got_lo, from_xy, from_yz, from_xz)
     wide = lambda a: a.astype(jnp.float32)
-    total = p0 + wide(to_cube(p1, 1)) + wide(to_cube(p2, 2)) + wide(to_cube(p4, 4))
+    total = p0 + wide(from_xyz) + wide(to_cube(p1, 1)) + wide(to_cube(p2, 2)) + wide(to_cube(p4, 4))
     kept, sent = total[:rows], total[rows:]
     got_sum = swap(sent)
     image_sum = jnp.where(first, kept, got_sum)

time: 118 us -> 115 us (0.975)
  waiting for transfers between devices: 39.4 us -> 32.7 us
  starting transfers between devices: 39.1 us -> 41.8 us
    ppermute x17, waiting for transfers between devices: 33.1 us -> 25.9 us  [to_cube(): return lax.ppermute(a, AXES, across(m))]
    ppermute x13, starting transfers between devices: 7.69 us -> 9.82 us  [swap(): return lax.ppermute(a, AXES, SWAP)]
  transfers between devices with their start and end apart: 30 -> 30, of which waited for: 21 -> 19; matrix products, arithmetic and copies ran while one was open for 0% -> 0% of each run, Pallas kernels for 8% -> 8%
where the time goes in v9:
time: 115 us; the launch traced here: 114 us
  starting transfers between devices  41.8 us (36%)
  Pallas kernels  37.5 us (33%)
  waiting for transfers between devices  32.7 us (28%)
  other arithmetic  1.35 us (1%)
    ppermute x17, starting transfers between devices, to_cube(): return lax.ppermute(a, AXES, across(m))  32 us
    ppermute x17, waiting for transfers between devices, to_cube(): return lax.ppermute(a, AXES, across(m))  25.9 us
    pallas_call x1, Pallas kernels, scores_call(): pl.pallas_call(functools.partial(scores_kernel, scale), in_specs=[smem_sp...  18.8 us
    ppermute x13, starting transfers between devices, swap(): return lax.ppermute(a, AXES, SWAP)  9.82 us
    pallas_call x1, Pallas kernels, weights_call(): pl.pallas_call(weights_kernel, in_specs=[smem_spec()] * 2 + [vmem_spec()]...  7.35 us
    ppermute x13, waiting for transfers between devices, swap(): return lax.ppermute(a, AXES, SWAP)  6.82 us
    pallas_call x1, Pallas kernels, middle_call(): pl.pallas_call(middle_kernel, in_specs=[smem_spec()] + [vmem_spec()] * 15...  5.76 us
    pallas_call x1, Pallas kernels, last_call(): pl.pallas_call(last_kernel, in_specs=[smem_spec()] + [vmem_spec()] * 7, o...  2.84 us
  transfers between devices with their start and end apart: 30, of which 19 were waited for; matrix products, arithmetic and copies ran while one was open for 0% of the time, Pallas kernels for 8%

profile of v9, /device:TPU:1, one launch (start us, length us, event | category | flops | bytes accessed | tf_op | source)
XLA Modules:
  0.0 114.2 jit_solution(12762852658672967148)
XLA Ops:
  0.6 1.5 %collective-permute-start = (bf16[160,768]{1,0:T(8,128)(2,1)}, bf16[160,768]{1,0:T(8,128)(2,1)S(1)}, u32[]{:S(2)}, u32[]{:S(2)}) collective-permute-start(bf16[160,768]{1,0:T(8,128)(2,1)} %images.1), channel_id=1, source_target_pairs={{0,16},{1,17},{2,18},{3,19},{4,20},{5,21},{6,22},{7,23},{8,24},{9,... | collective-permute-start | bytes 737288 | tf_op jit(solution)/shard_map/ppermute | solution.py:57
  2.1 0.1 collective-permute-start.1
  2.2 1.3 %collective-permute-done.got_images = bf16[160,768]{1,0:T(8,128)(2,1)S(1)} collective-permute-done((bf16[160,768]{1,0:T(8,128)(2,1)}, bf16[160,768]{1,0:T(8,128)(2,1)S(1)}, u32[]{:S(2)}, u32[]{:S(2)}) %collective-permute-start) | collective-permute-done | bytes 245792 | tf_op jit(solution)/shard_map/ppermute | solution.py:57
  3.5 0.4 collective-permute-done.1.got_texts
  3.9 1.6 %own.1 = (bf16[320,768]{1,0:T(8,128)(2,1)S(1)}, bf16[320,768]{1,0:T(8,128)(2,1)S(1)}) custom-call(s32[1]{0:T(128)} %bitcast.core_ref, bf16[160,768]{1,0:T(8,128)(2,1)} %images.1, bf16[160,768]{1,0:T(8,128)(2,1)} %texts.1, bf16[160,768]{1,0:T(8,128)(2,1)S(1)} %collective-permute-done.got_images, bf16[160,768]{1,0:T(8,128)(2,1)S(1)} %collective-permute-done.1.got_texts), custom_call_target="tpu_custom_call" | custom-call | bytes 1966080 | tf_op jit(solution)/shard_map/own/pallas_call | solution.py:125
  5.5 2.6 %collective-permute-start.2 = (bf16[320,768]{1,0:T(8,128)(2,1)S(1)}, bf16[320,768]{1,0:T(8,128)(2,1)S(1)}, u32[]{:S(2)}, u32[]{:S(2)}) collective-permute-start(bf16[320,768]{1,0:T(8,128)(2,1)S(1)} %get-tuple-element.25.refs_0_), channel_id=1, source_target_pairs={{0,4},{1,5},{2,6},{3,7},{4,0},{5,1},{6,2},{7,3},{8,12},{9,13},{10,... | collective-permute-start | bytes 1474568 | tf_op jit(solution)/shard_map/ppermute | solution.py:53
  8.1 1.3 %collective-permute-start.3 = (bf16[320,768]{1,0:T(8,128)(2,1)S(1)}, bf16[320,768]{1,0:T(8,128)(2,1)S(1)}, u32[]{:S(2)}, u32[]{:S(2)}) collective-permute-start(bf16[320,768]{1,0:T(8,128)(2,1)S(1)} %get-tuple-element.25.refs_0_), channel_id=1, source_target_pairs={{0,96},{1,97},{2,98},{3,99},{4,100},{5,101},{6,102},{7,103},{8,104... | collective-permute-start | bytes 1474568 | tf_op jit(solution)/shard_map/ppermute | solution.py:53
  9.4 3.8 %collective-permute-start.4 = (bf16[320,768]{1,0:T(8,128)(2,1)S(1)}, bf16[320,768]{1,0:T(8,128)(2,1)S(1)}, u32[]{:S(2)}, u32[]{:S(2)}) collective-permute-start(bf16[320,768]{1,0:T(8,128)(2,1)S(1)} %get-tuple-element.25.refs_0_), channel_id=1, source_target_pairs={{0,1},{1,0},{2,3},{3,2},{4,5},{5,4},{6,7},{7,6},{8,9},{9,8},{10,11... | collective-permute-start | bytes 1474568 | tf_op jit(solution)/shard_map/ppermute | solution.py:53
  13.2 1.6 %collective-permute-done.2.b0.refs_1_ = bf16[320,768]{1,0:T(8,128)(2,1)S(1)} collective-permute-done((bf16[320,768]{1,0:T(8,128)(2,1)S(1)}, bf16[320,768]{1,0:T(8,128)(2,1)S(1)}, u32[]{:S(2)}, u32[]{:S(2)}) %collective-permute-start.2) | collective-permute-done | bytes 491552 | tf_op jit(solution)/shard_map/ppermute | solution.py:53
  14.7 3.8 %collective-permute-start.6 = (bf16[320,768]{1,0:T(8,128)(2,1)S(1)}, bf16[320,768]{1,0:T(8,128)(2,1)S(1)}, u32[]{:S(2)}, u32[]{:S(2)}) collective-permute-start(bf16[320,768]{1,0:T(8,128)(2,1)S(1)} %collective-permute-done.2.b0.refs_1_), channel_id=1, source_target_pairs={{0,1},{1,0},{2,3},{3,2},{4,5},{5,4},{6,7},{7,6},{8,9},{9,8},{10,11... | collective-permute-start | bytes 1474568 | tf_op jit(solution)/shard_map/ppermute | solution.py:53
  18.6 0.0 collective-permute-done.3.b1.refs_2_
  18.6 2.5 %collective-permute-start.5 = (bf16[320,768]{1,0:T(8,128)(2,1)S(1)}, bf16[320,768]{1,0:T(8,128)(2,1)S(1)}, u32[]{:S(2)}, u32[]{:S(2)}) collective-permute-start(bf16[320,768]{1,0:T(8,128)(2,1)S(1)} %collective-permute-done.3.b1.refs_2_), channel_id=1, source_target_pairs={{0,4},{1,5},{2,6},{3,7},{4,0},{5,1},{6,2},{7,3},{8,12},{9,13},{10,... | collective-permute-start | bytes 1474568 | tf_op jit(solution)/shard_map/ppermute | solution.py:53
  21.1 3.1 %collective-permute-done.4.b2.refs_3_ = bf16[320,768]{1,0:T(8,128)(2,1)S(1)} collective-permute-done((bf16[320,768]{1,0:T(8,128)(2,1)S(1)}, bf16[320,768]{1,0:T(8,128)(2,1)S(1)}, u32[]{:S(2)}, u32[]{:S(2)}) %collective-permute-start.4) | collective-permute-done | bytes 491552 | tf_op jit(solution)/shard_map/ppermute | solution.py:53
  24.2 0.1 join.1
  24.3 0.5 collective-permute-start.9
  24.8 0.0 collective-permute-start.7
  24.8 0.4 collective-permute-done.8.refs_7_
  25.2 1.9 %collective-permute-start.10 = (bf16[320,768]{1,0:T(8,128)(2,1)S(1)}, bf16[320,768]{1,0:T(8,128)(2,1)S(1)}, u32[]{:S(2)}, u32[]{:S(2)}) collective-permute-start(bf16[320,768]{1,0:T(8,128)(2,1)S(1)} %collective-permute-done.8.refs_7_), channel_id=1, source_target_pairs={{0,16},{1,17},{2,18},{3,19},{4,20},{5,21},{6,22},{7,23},{8,24},{9,... | collective-permute-start | bytes 1474568 | tf_op jit(solution)/shard_map/ppermute | solution.py:57
  27.1 3.3 %collective-permute-done.6.refs_5_ = bf16[320,768]{1,0:T(8,128)(2,1)S(1)} collective-permute-done((bf16[320,768]{1,0:T(8,128)(2,1)S(1)}, bf16[320,768]{1,0:T(8,128)(2,1)S(1)}, u32[]{:S(2)}, u32[]{:S(2)}) %collective-permute-start.6) | collective-permute-done | bytes 491552 | tf_op jit(solution)/shard_map/ppermute | solution.py:53
  30.4 0.6 collective-permute-start.12
  30.9 1.8 %collective-permute-done.7.refs_6_ = bf16[320,768]{1,0:T(8,128)(2,1)S(1)} collective-permute-done((bf16[320,768]{1,0:T(8,128)(2,1)S(1)}, bf16[320,768]{1,0:T(8,128)(2,1)S(1)}, u32[]{:S(2)}, u32[]{:S(2)}) %collective-permute-start.7) | collective-permute-done | bytes 491552 | tf_op jit(solution)/shard_map/ppermute | solution.py:53
  32.7 0.0 collective-permute-done.10.refs_13_.refs_5_
  32.7 0.0 collective-permute-done.11.refs_11_.refs_3_
  32.7 0.2 collective-permute-done.12.refs_10_.refs_2_
  32.9 2.1 %collective-permute-start.13 = (bf16[320,768]{1,0:T(8,128)(2,1)S(1)}, bf16[320,768]{1,0:T(8,128)(2,1)S(1)}, u32[]{:S(2)}, u32[]{:S(2)}) collective-permute-start(bf16[320,768]{1,0:T(8,128)(2,1)S(1)} %collective-permute-done.7.refs_6_), channel_id=1, source_target_pairs={{0,16},{1,17},{2,18},{3,19},{4,20},{5,21},{6,22},{7,23},{8,24},{9,... | collective-permute-start | bytes 1474568 | tf_op jit(solution)/shard_map/ppermute | solution.py:57
  35.0 0.0 collective-permute-done.9.refs_9_.refs_1_
  35.0 1.5 %collective-permute-done.13.refs_12_.refs_4_ = bf16[320,768]{1,0:T(8,128)(2,1)S(1)} collective-permute-done((bf16[320,768]{1,0:T(8,128)(2,1)S(1)}, bf16[320,768]{1,0:T(8,128)(2,1)S(1)}, u32[]{:S(2)}, u32[]{:S(2)}) %collective-permute-start.13) | collective-permute-done | bytes 491552 | tf_op jit(solution)/shard_map/ppermute | solution.py:57
  36.5 18.8 %scores.1 = (f32[2,1280,1280]{2,1,0:T(8,128)S(1)}, f32[8,320]{1,0:T(8,128)S(1)}, f32[8,320]{1,0:T(8,128)S(1)}, s32[2]{0:T(128)S(1)}) custom-call(s32[1]{0:T(128)} %bitcast.core_ref, bf16[320,768]{1,0:T(8,128)(2,1)S(1)} %get-tuple-element.25.refs_0_, bf16[320,768]{1,0:T(8,128)(2,1)S(1)} %collective-permute-done.2.b0.refs_1_, ...), custom_call_target="tpu_custom_call" | custom-call | flops 5033164800 | tf_op jit(solution)/shard_map/scores/pallas_call | solution.py:236
  55.4 0.5 collective-permute-start.14
  55.8 0.8 collective-permute-done.14.got_ref
  56.7 1.3 %collective-permute-start.15 = (f32[8,320]{1,0:T(8,128)S(1)}, f32[8,320]{1,0:T(8,128)S(1)}, u32[]{:S(2)}, u32[]{:S(2)}) collective-permute-start(f32[8,320]{1,0:T(8,128)S(1)} %merge.4.mine_ref), channel_id=1, source_target_pairs={{0,4},{1,5},{2,6},{3,7},{4,0},{5,1},{6,2},{7,3},{8,12},{9,13},{10,... | collective-permute-start | bytes 30728 | tf_op jit(solution)/shard_map/ppermute | solution.py:53
  58.0 2.5 %collective-permute-done.15.got_ref = f32[8,320]{1,0:T(8,128)S(1)} collective-permute-done((f32[8,320]{1,0:T(8,128)S(1)}, f32[8,320]{1,0:T(8,128)S(1)}, u32[]{:S(2)}, u32[]{:S(2)}) %collective-permute-start.15) | collective-permute-done | bytes 10272 | tf_op jit(solution)/shard_map/ppermute | solution.py:53
  60.6 0.1 collective-permute-start.16
  60.6 2.5 %collective-permute-done.16.got_ref = f32[8,320]{1,0:T(8,128)S(1)} collective-permute-done((f32[8,320]{1,0:T(8,128)S(1)}, f32[8,320]{1,0:T(8,128)S(1)}, u32[]{:S(2)}, u32[]{:S(2)}) %collective-permute-start.16) | collective-permute-done | bytes 10272 | tf_op jit(solution)/shard_map/ppermute | solution.py:53
  63.2 3.8 %collective-permute-start.17 = (f32[8,320]{1,0:T(8,128)S(1)}, f32[8,320]{1,0:T(8,128)S(1)}, u32[]{:S(2)}, u32[]{:S(2)}) collective-permute-start(f32[8,320]{1,0:T(8,128)S(1)} %merge.6.mine_ref), channel_id=1, source_target_pairs={{0,1},{1,0},{2,3},{3,2},{4,5},{5,4},{6,7},{7,6},{8,9},{9,8},{10,11... | collective-permute-start | bytes 30728 | tf_op jit(solution)/shard_map/ppermute | solution.py:53
  67.0 1.1 collective-permute-done.17.got_ref
  68.1 1.6 %collective-permute-start.18 = (f32[8,320]{1,0:T(8,128)S(1)}, f32[8,320]{1,0:T(8,128)S(1)}, u32[]{:S(2)}, u32[]{:S(2)}) collective-permute-start(f32[8,320]{1,0:T(8,128)S(1)} %merge.7.a_lse), channel_id=1, source_target_pairs={{0,16},{1,17},{2,18},{3,19},{4,20},{5,21},{6,22},{7,23},{8,24},{9,... | collective-permute-start | bytes 30728 | tf_op jit(solution)/shard_map/ppermute | solution.py:57
  69.7 0.8 collective-permute-done.18.b_lse
  70.6 7.4 %weights.1 = (bf16[2,1280,1280]{2,1,0:T(8,128)(2,1)S(1)}, bf16[1280,768]{1,0:T(8,128)(2,1)S(1)}) custom-call(s32[1]{0:T(128)} %bitcast.core_ref, s32[2]{0:T(128)S(1)} %get-tuple-element.31.flags, f32[2,1280,1280]{2,1,0:T(8,128)S(1)} %get-tuple-element.32.e_ref, f32[8,320]{1,0:T(8,128)S(1)} %merge.7.a_lse, f32[8,320]{1,0:T(8,128)S(1)} %collective-permute-done.18.b_lse, ...), custom_call_target="tpu_custom_call" | custom-call | flops 2516582400 | bytes 19660800 | tf_op jit(solution)/shard_map/weights/pallas_call | solution.py:309
  77.9 0.4 collective-permute-start.21
  78.4 5.8 %middle.1 = (f32[1280,768]{1,0:T(8,128)S(1)}, f32[320,768]{1,0:T(8,128)S(1)}, bf16[960,768]{1,0:T(8,128)(2,1)S(1)}) custom-call(s32[1]{0:T(128)} %bitcast.core_ref, bf16[2,1280,1280]{2,1,0:T(8,128)(2,1)S(1)} %get-tuple-element.35.w_ref, bf16[320,768]{1,0:T(8,128)(2,1)S(1)} %get-tuple-element.25.refs_0_, ...), custom_call_target="tpu_custom_call" | custom-call | flops 5033164800 | tf_op jit(solution)/shard_map/middle/pallas_call | solution.py:340
  84.1 0.3 collective-permute-start.20
  84.4 0.3 collective-permute-start.19
  84.7 0.0 collective-permute-done.21.got
  84.7 0.3 far.1
  85.0 1.8 %collective-permute-start.22 = (bf16[320,768]{1,0:T(8,128)(2,1)S(1)}, bf16[320,768]{1,0:T(8,128)(2,1)S(1)}, u32[]{:S(2)}, u32[]{:S(2)}) collective-permute-start(bf16[320,768]{1,0:T(8,128)(2,1)S(1)} %get-tuple-element.40), channel_id=1, source_target_pairs={{0,4},{1,5},{2,6},{3,7},{4,0},{5,1},{6,2},{7,3},{8,12},{9,13},{10,... | collective-permute-start | bytes 1474568 | tf_op jit(solution)/shard_map/ppermute | solution.py:53
  86.8 0.0 collective-permute-start.23
  86.8 3.9 %collective-permute-start.24 = (bf16[320,768]{1,0:T(8,128)(2,1)S(1)}, bf16[320,768]{1,0:T(8,128)(2,1)S(1)}, u32[]{:S(2)}, u32[]{:S(2)}) collective-permute-start(bf16[320,768]{1,0:T(8,128)(2,1)S(1)} %get-tuple-element.42), channel_id=1, source_target_pairs={{0,1},{1,0},{2,3},{3,2},{4,5},{5,4},{6,7},{7,6},{8,9},{9,8},{10,11... | collective-permute-start | bytes 1474568 | tf_op jit(solution)/shard_map/ppermute | solution.py:53
  90.7 2.8 %last.1.ga_lo = f32[1280,768]{1,0:T(8,128)S(1)} custom-call(s32[1]{0:T(128)} %bitcast.core_ref, bf16[2,1280,1280]{2,1,0:T(8,128)(2,1)S(1)} %get-tuple-element.35.w_ref, bf16[320,768]{1,0:T(8,128)(2,1)S(1)} %get-tuple-element.26.refs_8_.refs_0_, bf16[960,768]{1,0:T(8,128)(2,1)S(1)} %collective-permute-done.9.refs_9_.refs_1_, ...), custom_call_target="tpu_custom_call" | custom-call | flops 2516582400 | tf_op jit(solution)/shard_map/last/pallas_call | solution.py:386
  93.5 0.0 collective-permute-done.19.got0
  93.5 1.8 %collective-permute-start.25 = (bf16[320,768]{1,0:T(8,128)(2,1)S(1)}, bf16[320,768]{1,0:T(8,128)(2,1)S(1)}, u32[]{:S(2)}, u32[]{:S(2)}) collective-permute-start(bf16[320,768]{1,0:T(8,128)(2,1)S(1)} %get-tuple-element.44), channel_id=1, source_target_pairs={{0,101},{1,100},{2,103},{3,102},{4,97},{5,96},{6,99},{7,98},{8,109... | collective-permute-start | bytes 1474568 | tf_op jit(solution)/shard_map/ppermute | solution.py:53
  95.4 0.0 collective-permute-done.20.got_lo
  95.4 1.5 %collective-permute-done.24.r_xz = bf16[320,768]{1,0:T(8,128)(2,1)S(1)} collective-permute-done((bf16[320,768]{1,0:T(8,128)(2,1)S(1)}, bf16[320,768]{1,0:T(8,128)(2,1)S(1)}, u32[]{:S(2)}, u32[]{:S(2)}) %collective-permute-start.24) | collective-permute-done | bytes 491552 | tf_op jit(solution)/shard_map/ppermute | solution.py:53
  96.9 0.5 near.1
  97.4 1.1 collective-permute-start.26
  98.5 1.6 %collective-permute-start.27 = (bf16[320,768]{1,0:T(8,128)(2,1)S(1)}, bf16[320,768]{1,0:T(8,128)(2,1)S(1)}, u32[]{:S(2)}, u32[]{:S(2)}) collective-permute-start(bf16[320,768]{1,0:T(8,128)(2,1)S(1)} %get-tuple-element.46), channel_id=1, source_target_pairs={{0,96},{1,97},{2,98},{3,99},{4,100},{5,101},{6,102},{7,103},{8,104... | collective-permute-start | bytes 1474568 | tf_op jit(solution)/shard_map/ppermute | solution.py:53
  100.1 2.7 %collective-permute-start.28 = (bf16[320,768]{1,0:T(8,128)(2,1)S(1)}, bf16[320,768]{1,0:T(8,128)(2,1)S(1)}, u32[]{:S(2)}, u32[]{:S(2)}) collective-permute-start(bf16[320,768]{1,0:T(8,128)(2,1)S(1)} %get-tuple-element.47), channel_id=1, source_target_pairs={{0,1},{1,0},{2,3},{3,2},{4,5},{5,4},{6,7},{7,6},{8,9},{9,8},{10,11... | collective-permute-start | bytes 1474568 | tf_op jit(solution)/shard_map/ppermute | solution.py:53
  102.8 2.9 %collective-permute-done.25 = bf16[320,768]{1,0:T(8,128)(2,1)S(1)} collective-permute-done((bf16[320,768]{1,0:T(8,128)(2,1)S(1)}, bf16[320,768]{1,0:T(8,128)(2,1)S(1)}, u32[]{:S(2)}, u32[]{:S(2)}) %collective-permute-start.25) | collective-permute-done | bytes 491552 | tf_op jit(solution)/shard_map/ppermute | solution.py:53
  105.7 3.1 %collective-permute-done.26 = bf16[320,768]{1,0:T(8,128)(2,1)S(1)} collective-permute-done((bf16[320,768]{1,0:T(8,128)(2,1)S(1)}, bf16[320,768]{1,0:T(8,128)(2,1)S(1)}, u32[]{:S(2)}, u32[]{:S(2)}) %collective-permute-start.26) | collective-permute-done | bytes 491552 | tf_op jit(solution)/shard_map/ppermute | solution.py:53
  108.7 2.1 %collective-permute-done.28 = bf16[320,768]{1,0:T(8,128)(2,1)S(1)} collective-permute-done((bf16[320,768]{1,0:T(8,128)(2,1)S(1)}, bf16[320,768]{1,0:T(8,128)(2,1)S(1)}, u32[]{:S(2)}, u32[]{:S(2)}) %collective-permute-start.28) | collective-permute-done | bytes 491552 | tf_op jit(solution)/shard_map/ppermute | solution.py:53
  110.8 0.3 convert_add_fusion
  111.2 0.1 collective-permute-start.29
  111.3 1.8 %collective-permute-done.29 = f32[160,768]{1,0:T(8,128)S(1)} collective-permute-done((f32[160,768]{1,0:T(8,128)S(1)}, f32[160,768]{1,0:T(8,128)S(1)}, u32[]{:S(2)}, u32[]{:S(2)}) %collective-permute-start.29) | collective-permute-done | bytes 491552 | tf_op jit(solution)/shard_map/ppermute | solution.py:57
  113.1 1.0 convert_subtract_fusion
  (15 shorter events, 0.2 us)
Async XLA Ops:
  0.6 2.9 %collective-permute-start = (bf16[160,768]{1,0:T(8,128)(2,1)}, bf16[160,768]{1,0:T(8,128)(2,1)S(1)}, u32[]{:S(2)}, u32[]{:S(2)}) collective-permute-start(bf16[160,768]{1,0:T(8,128)(2,1)} %images.1), channel_id=1, source_target_pairs={{0,16},{1,17},{2,18},{3,19},{4,20},{5,21},{6,22},{7,23},{8,24},{9,... | collective-permute-start | bytes 737288 | tf_op jit(solution)/shard_map/ppermute | solution.py:57
  2.1 1.7 %collective-permute-start.1 = (bf16[160,768]{1,0:T(8,128)(2,1)}, bf16[160,768]{1,0:T(8,128)(2,1)S(1)}, u32[]{:S(2)}, u32[]{:S(2)}) collective-permute-start(bf16[160,768]{1,0:T(8,128)(2,1)} %texts.1), channel_id=1, source_target_pairs={{0,16},{1,17},{2,18},{3,19},{4,20},{5,21},{6,22},{7,23},{8,24},{9,... | collective-permute-start | bytes 737288 | tf_op jit(solution)/shard_map/ppermute | solution.py:57
  5.5 9.3 %collective-permute-start.2 = (bf16[320,768]{1,0:T(8,128)(2,1)S(1)}, bf16[320,768]{1,0:T(8,128)(2,1)S(1)}, u32[]{:S(2)}, u32[]{:S(2)}) collective-permute-start(bf16[320,768]{1,0:T(8,128)(2,1)S(1)} %get-tuple-element.25.refs_0_), channel_id=1, source_target_pairs={{0,4},{1,5},{2,6},{3,7},{4,0},{5,1},{6,2},{7,3},{8,12},{9,13},{10,... | collective-permute-start | bytes 1474568 | tf_op jit(solution)/shard_map/ppermute | solution.py:53
  8.1 10.5 %collective-permute-start.3 = (bf16[320,768]{1,0:T(8,128)(2,1)S(1)}, bf16[320,768]{1,0:T(8,128)(2,1)S(1)}, u32[]{:S(2)}, u32[]{:S(2)}) collective-permute-start(bf16[320,768]{1,0:T(8,128)(2,1)S(1)} %get-tuple-element.25.refs_0_), channel_id=1, source_target_pairs={{0,96},{1,97},{2,98},{3,99},{4,100},{5,101},{6,102},{7,103},{8,104... | collective-permute-start | bytes 1474568 | tf_op jit(solution)/shard_map/ppermute | solution.py:53
  9.4 14.8 %collective-permute-start.4 = (bf16[320,768]{1,0:T(8,128)(2,1)S(1)}, bf16[320,768]{1,0:T(8,128)(2,1)S(1)}, u32[]{:S(2)}, u32[]{:S(2)}) collective-permute-start(bf16[320,768]{1,0:T(8,128)(2,1)S(1)} %get-tuple-element.25.refs_0_), channel_id=1, source_target_pairs={{0,1},{1,0},{2,3},{3,2},{4,5},{5,4},{6,7},{7,6},{8,9},{9,8},{10,11... | collective-permute-start | bytes 1474568 | tf_op jit(solution)/shard_map/ppermute | solution.py:53
  13.2 12.0 %collective-permute-start.8 = (bf16[320,768]{1,0:T(8,128)(2,1)S(1)}, bf16[320,768]{1,0:T(8,128)(2,1)S(1)}, u32[]{:S(2)}, u32[]{:S(2)}) collective-permute-start(bf16[320,768]{1,0:T(8,128)(2,1)S(1)} %get-tuple-element.25.refs_0_), channel_id=1, source_target_pairs={{0,101},{1,100},{2,103},{3,102},{4,97},{5,96},{6,99},{7,98},{8,109... | collective-permute-start | bytes 1474568 | tf_op jit(solution)/shard_map/ppermute | solution.py:53
  14.7 15.6 %collective-permute-start.6 = (bf16[320,768]{1,0:T(8,128)(2,1)S(1)}, bf16[320,768]{1,0:T(8,128)(2,1)S(1)}, u32[]{:S(2)}, u32[]{:S(2)}) collective-permute-start(bf16[320,768]{1,0:T(8,128)(2,1)S(1)} %collective-permute-done.2.b0.refs_1_), channel_id=1, source_target_pairs={{0,1},{1,0},{2,3},{3,2},{4,5},{5,4},{6,7},{7,6},{8,9},{9,8},{10,11... | collective-permute-start | bytes 1474568 | tf_op jit(solution)/shard_map/ppermute | solution.py:53
  18.6 11.8 %collective-permute-start.5 = (bf16[320,768]{1,0:T(8,128)(2,1)S(1)}, bf16[320,768]{1,0:T(8,128)(2,1)S(1)}, u32[]{:S(2)}, u32[]{:S(2)}) collective-permute-start(bf16[320,768]{1,0:T(8,128)(2,1)S(1)} %collective-permute-done.3.b1.refs_2_), channel_id=1, source_target_pairs={{0,4},{1,5},{2,6},{3,7},{4,0},{5,1},{6,2},{7,3},{8,12},{9,13},{10,... | collective-permute-start | bytes 1474568 | tf_op jit(solution)/shard_map/ppermute | solution.py:53
  24.3 10.7 %collective-permute-start.9 = (bf16[960,768]{1,0:T(8,128)(2,1)S(1)}, bf16[960,768]{1,0:T(8,128)(2,1)S(1)}, u32[]{:S(2)}, u32[]{:S(2)}) collective-permute-start(bf16[960,768]{1,0:T(8,128)(2,1)S(1)} %join.1), channel_id=1, source_target_pairs={{0,16},{1,17},{2,18},{3,19},{4,20},{5,21},{6,22},{7,23},{8,24},{9,... | collective-permute-start | bytes 4423688 | tf_op jit(solution)/shard_map/ppermute | solution.py:57
  24.8 8.0 %collective-permute-start.7 = (bf16[320,768]{1,0:T(8,128)(2,1)S(1)}, bf16[320,768]{1,0:T(8,128)(2,1)S(1)}, u32[]{:S(2)}, u32[]{:S(2)}) collective-permute-start(bf16[320,768]{1,0:T(8,128)(2,1)S(1)} %collective-permute-done.4.b2.refs_3_), channel_id=1, source_target_pairs={{0,96},{1,97},{2,98},{3,99},{4,100},{5,101},{6,102},{7,103},{8,104... | collective-permute-start | bytes 1474568 | tf_op jit(solution)/shard_map/ppermute | solution.py:53
  25.2 7.6 %collective-permute-start.10 = (bf16[320,768]{1,0:T(8,128)(2,1)S(1)}, bf16[320,768]{1,0:T(8,128)(2,1)S(1)}, u32[]{:S(2)}, u32[]{:S(2)}) collective-permute-start(bf16[320,768]{1,0:T(8,128)(2,1)S(1)} %collective-permute-done.8.refs_7_), channel_id=1, source_target_pairs={{0,16},{1,17},{2,18},{3,19},{4,20},{5,21},{6,22},{7,23},{8,24},{9,... | collective-permute-start | bytes 1474568 | tf_op jit(solution)/shard_map/ppermute | solution.py:57
  30.4 2.4 %collective-permute-start.11 = (bf16[320,768]{1,0:T(8,128)(2,1)S(1)}, bf16[320,768]{1,0:T(8,128)(2,1)S(1)}, u32[]{:S(2)}, u32[]{:S(2)}) collective-permute-start(bf16[320,768]{1,0:T(8,128)(2,1)S(1)} %collective-permute-done.6.refs_5_), channel_id=1, source_target_pairs={{0,16},{1,17},{2,18},{3,19},{4,20},{5,21},{6,22},{7,23},{8,24},{9,... | collective-permute-start | bytes 1474568 | tf_op jit(solution)/shard_map/ppermute | solution.py:57
  30.4 2.6 %collective-permute-start.12 = (bf16[320,768]{1,0:T(8,128)(2,1)S(1)}, bf16[320,768]{1,0:T(8,128)(2,1)S(1)}, u32[]{:S(2)}, u32[]{:S(2)}) collective-permute-start(bf16[320,768]{1,0:T(8,128)(2,1)S(1)} %collective-permute-done.5.refs_4_), channel_id=1, source_target_pairs={{0,16},{1,17},{2,18},{3,19},{4,20},{5,21},{6,22},{7,23},{8,24},{9,... | collective-permute-start | bytes 1474568 | tf_op jit(solution)/shard_map/ppermute | solution.py:57
  32.9 3.6 %collective-permute-start.13 = (bf16[320,768]{1,0:T(8,128)(2,1)S(1)}, bf16[320,768]{1,0:T(8,128)(2,1)S(1)}, u32[]{:S(2)}, u32[]{:S(2)}) collective-permute-start(bf16[320,768]{1,0:T(8,128)(2,1)S(1)} %collective-permute-done.7.refs_6_), channel_id=1, source_target_pairs={{0,16},{1,17},{2,18},{3,19},{4,20},{5,21},{6,22},{7,23},{8,24},{9,... | collective-permute-start | bytes 1474568 | tf_op jit(solution)/shard_map/ppermute | solution.py:57
  55.4 1.3 %collective-permute-start.14 = (f32[8,320]{1,0:T(8,128)S(1)}, f32[8,320]{1,0:T(8,128)S(1)}, u32[]{:S(2)}, u32[]{:S(2)}) collective-permute-start(f32[8,320]{1,0:T(8,128)S(1)} %get-tuple-element.34), channel_id=1, source_target_pairs={{0,16},{1,17},{2,18},{3,19},{4,20},{5,21},{6,22},{7,23},{8,24},{9,... | collective-permute-start | bytes 30728 | tf_op jit(solution)/shard_map/ppermute | solution.py:57
  56.7 3.8 %collective-permute-start.15 = (f32[8,320]{1,0:T(8,128)S(1)}, f32[8,320]{1,0:T(8,128)S(1)}, u32[]{:S(2)}, u32[]{:S(2)}) collective-permute-start(f32[8,320]{1,0:T(8,128)S(1)} %merge.4.mine_ref), channel_id=1, source_target_pairs={{0,4},{1,5},{2,6},{3,7},{4,0},{5,1},{6,2},{7,3},{8,12},{9,13},{10,... | collective-permute-start | bytes 30728 | tf_op jit(solution)/shard_map/ppermute | solution.py:53
  60.6 2.6 %collective-permute-start.16 = (f32[8,320]{1,0:T(8,128)S(1)}, f32[8,320]{1,0:T(8,128)S(1)}, u32[]{:S(2)}, u32[]{:S(2)}) collective-permute-start(f32[8,320]{1,0:T(8,128)S(1)} %merge.5.mine_ref), channel_id=1, source_target_pairs={{0,96},{1,97},{2,98},{3,99},{4,100},{5,101},{6,102},{7,103},{8,104... | collective-permute-start | bytes 30728 | tf_op jit(solution)/shard_map/ppermute | solution.py:53
  63.2 4.9 %collective-permute-start.17 = (f32[8,320]{1,0:T(8,128)S(1)}, f32[8,320]{1,0:T(8,128)S(1)}, u32[]{:S(2)}, u32[]{:S(2)}) collective-permute-start(f32[8,320]{1,0:T(8,128)S(1)} %merge.6.mine_ref), channel_id=1, source_target_pairs={{0,1},{1,0},{2,3},{3,2},{4,5},{5,4},{6,7},{7,6},{8,9},{9,8},{10,11... | collective-permute-start | bytes 30728 | tf_op jit(solution)/shard_map/ppermute | solution.py:53
  68.1 2.4 %collective-permute-start.18 = (f32[8,320]{1,0:T(8,128)S(1)}, f32[8,320]{1,0:T(8,128)S(1)}, u32[]{:S(2)}, u32[]{:S(2)}) collective-permute-start(f32[8,320]{1,0:T(8,128)S(1)} %merge.7.a_lse), channel_id=1, source_target_pairs={{0,16},{1,17},{2,18},{3,19},{4,20},{5,21},{6,22},{7,23},{8,24},{9,... | collective-permute-start | bytes 30728 | tf_op jit(solution)/shard_map/ppermute | solution.py:57
  77.9 6.8 %collective-permute-start.21 = (bf16[1280,768]{1,0:T(8,128)(2,1)S(1)}, bf16[1280,768]{1,0:T(8,128)(2,1)S(1)}, u32[]{:S(2)}, u32[]{:S(2)}) collective-permute-start(bf16[1280,768]{1,0:T(8,128)(2,1)S(1)} %get-tuple-element.39), channel_id=1, source_target_pairs={{0,16},{1,17},{2,18},{3,19},{4,20},{5,21},{6,22},{7,23},{8,24},{9,... | collective-permute-start | bytes 5898248 | tf_op jit(solution)/shard_map/ppermute | solution.py:57
  84.1 11.2 %collective-permute-start.20 = (bf16[960,768]{1,0:T(8,128)(2,1)S(1)}, bf16[960,768]{1,0:T(8,128)(2,1)S(1)}, u32[]{:S(2)}, u32[]{:S(2)}) collective-permute-start(bf16[960,768]{1,0:T(8,128)(2,1)S(1)} %get-tuple-element.37), channel_id=1, source_target_pairs={{0,16},{1,17},{2,18},{3,19},{4,20},{5,21},{6,22},{7,23},{8,24},{9,... | collective-permute-start | bytes 4423688 | tf_op jit(solution)/shard_map/ppermute | solution.py:57
  84.4 9.1 %collective-permute-start.19 = (f32[320,768]{1,0:T(8,128)S(1)}, f32[320,768]{1,0:T(8,128)S(1)}, u32[]{:S(2)}, u32[]{:S(2)}) collective-permute-start(f32[320,768]{1,0:T(8,128)S(1)} %get-tuple-element.36), channel_id=1, source_target_pairs={{0,16},{1,17},{2,18},{3,19},{4,20},{5,21},{6,22},{7,23},{8,24},{9,... | collective-permute-start | bytes 2949128 | tf_op jit(solution)/shard_map/ppermute | solution.py:57
  85.0 10.3 %collective-permute-start.22 = (bf16[320,768]{1,0:T(8,128)(2,1)S(1)}, bf16[320,768]{1,0:T(8,128)(2,1)S(1)}, u32[]{:S(2)}, u32[]{:S(2)}) collective-permute-start(bf16[320,768]{1,0:T(8,128)(2,1)S(1)} %get-tuple-element.40), channel_id=1, source_target_pairs={{0,4},{1,5},{2,6},{3,7},{4,0},{5,1},{6,2},{7,3},{8,12},{9,13},{10,... | collective-permute-start | bytes 1474568 | tf_op jit(solution)/shard_map/ppermute | solution.py:53
  86.8 8.6 %collective-permute-start.23 = (bf16[320,768]{1,0:T(8,128)(2,1)S(1)}, bf16[320,768]{1,0:T(8,128)(2,1)S(1)}, u32[]{:S(2)}, u32[]{:S(2)}) collective-permute-start(bf16[320,768]{1,0:T(8,128)(2,1)S(1)} %get-tuple-element.41), channel_id=1, source_target_pairs={{0,96},{1,97},{2,98},{3,99},{4,100},{5,101},{6,102},{7,103},{8,104... | collective-permute-start | bytes 1474568 | tf_op jit(solution)/shard_map/ppermute | solution.py:53
  86.8 10.1 %collective-permute-start.24 = (bf16[320,768]{1,0:T(8,128)(2,1)S(1)}, bf16[320,768]{1,0:T(8,128)(2,1)S(1)}, u32[]{:S(2)}, u32[]{:S(2)}) collective-permute-start(bf16[320,768]{1,0:T(8,128)(2,1)S(1)} %get-tuple-element.42), channel_id=1, source_target_pairs={{0,1},{1,0},{2,3},{3,2},{4,5},{5,4},{6,7},{7,6},{8,9},{9,8},{10,11... | collective-permute-start | bytes 1474568 | tf_op jit(solution)/shard_map/ppermute | solution.py:53
  93.5 12.1 %collective-permute-start.25 = (bf16[320,768]{1,0:T(8,128)(2,1)S(1)}, bf16[320,768]{1,0:T(8,128)(2,1)S(1)}, u32[]{:S(2)}, u32[]{:S(2)}) collective-permute-start(bf16[320,768]{1,0:T(8,128)(2,1)S(1)} %get-tuple-element.44), channel_id=1, source_target_pairs={{0,101},{1,100},{2,103},{3,102},{4,97},{5,96},{6,99},{7,98},{8,109... | collective-permute-start | bytes 1474568 | tf_op jit(solution)/shard_map/ppermute | solution.py:53
  97.4 11.3 %collective-permute-start.26 = (bf16[320,768]{1,0:T(8,128)(2,1)S(1)}, bf16[320,768]{1,0:T(8,128)(2,1)S(1)}, u32[]{:S(2)}, u32[]{:S(2)}) collective-permute-start(bf16[320,768]{1,0:T(8,128)(2,1)S(1)} %get-tuple-element.45), channel_id=1, source_target_pairs={{0,4},{1,5},{2,6},{3,7},{4,0},{5,1},{6,2},{7,3},{8,12},{9,13},{10,... | collective-permute-start | bytes 1474568 | tf_op jit(solution)/shard_map/ppermute | solution.py:53
  98.5 10.2 %collective-permute-start.27 = (bf16[320,768]{1,0:T(8,128)(2,1)S(1)}, bf16[320,768]{1,0:T(8,128)(2,1)S(1)}, u32[]{:S(2)}, u32[]{:S(2)}) collective-permute-start(bf16[320,768]{1,0:T(8,128)(2,1)S(1)} %get-tuple-element.46), channel_id=1, source_target_pairs={{0,96},{1,97},{2,98},{3,99},{4,100},{5,101},{6,102},{7,103},{8,104... | collective-permute-start | bytes 1474568 | tf_op jit(solution)/shard_map/ppermute | solution.py:53
  100.1 10.7 %collective-permute-start.28 = (bf16[320,768]{1,0:T(8,128)(2,1)S(1)}, bf16[320,768]{1,0:T(8,128)(2,1)S(1)}, u32[]{:S(2)}, u32[]{:S(2)}) collective-permute-start(bf16[320,768]{1,0:T(8,128)(2,1)S(1)} %get-tuple-element.47), channel_id=1, source_target_pairs={{0,1},{1,0},{2,3},{3,2},{4,5},{5,4},{6,7},{7,6},{8,9},{9,8},{10,11... | collective-permute-start | bytes 1474568 | tf_op jit(solution)/shard_map/ppermute | solution.py:53
  110.8 2.3 %copy-start = (bf16[160,768]{1,0:T(8,128)(2,1)S(1)}, bf16[160,768]{1,0:T(8,128)(2,1)}, u32[]{:S(2)}) copy-start(bf16[160,768]{1,0:T(8,128)(2,1)} %images.1) | copy-start | bytes 737284
  110.8 2.3 %copy-start.1 = (bf16[160,768]{1,0:T(8,128)(2,1)S(1)}, bf16[160,768]{1,0:T(8,128)(2,1)}, u32[]{:S(2)}) copy-start(bf16[160,768]{1,0:T(8,128)(2,1)} %texts.1) | copy-start | bytes 737284
  111.2 1.9 %collective-permute-start.29 = (f32[160,768]{1,0:T(8,128)S(1)}, f32[160,768]{1,0:T(8,128)S(1)}, u32[]{:S(2)}, u32[]{:S(2)}) collective-permute-start(f32[160,768]{1,0:T(8,128)S(1)} %slice.9), channel_id=1, source_target_pairs={{0,16},{1,17},{2,18},{3,19},{4,20},{5,21},{6,22},{7,23},{8,24},{9,... | collective-permute-start | bytes 1474568 | tf_op jit(solution)/shard_map/ppermute | solution.py:57

commit v10 on v9

--- a/solution.py
+++ b/solution.py
@@ -99,24 +99,43 @@
     return lax.dot_general(a, b, (((0,), (0,)), ((), ())), preferred_element_type=jnp.float32)
 
 
-def own_kernel(core_ref, images, texts, got_images, got_texts, own, other, sem):
-    rows = images.shape[0]
+def load_kernel(core_ref, images, texts, mine, yours, sem):
     core = core_ref[0]
-    top, low = pl.ds(0, rows), pl.ds(rows, rows)
-    orders = ((images, got_images, got_texts, texts), (texts, got_texts, got_images, images))
-
-    def copies(order):
-        places = (own.at[top], own.at[low], other.at[top], other.at[low])
-        return [pltpu.make_async_copy(a, p, sem.at[j]) for j, (a, p) in enumerate(zip(order, places))]
-
-    for c in range(2):
+    for c, order in enumerate(((mine, yours), (yours, mine))):
 
         @pl.when(core == c)
         def _():
-            for copy in copies(orders[c]):
+            copies = [pltpu.make_async_copy(a, o, sem.at[j]) for j, (a, o) in enumerate(zip((images, texts), order))]
+            for copy in copies:
                 copy.start()
-            for copy in copies(orders[c]):
+            for copy in copies:
                 copy.wait()
+
+
+def load_call(core, images, texts):
+    block = pltpu.VMEM(images.shape, images.dtype)
+    return pl.pallas_call(
+        load_kernel,
+        in_specs=[smem_spec()] + [pl.BlockSpec(memory_space=pl.ANY)] * 2,
+        out_specs=[vmem_spec()] * 2,
+        out_shape=[block, block],
+        scratch_shapes=[pltpu.SemaphoreType.DMA((2,))],
+        compiler_params=params(),
+        cost_estimate=cost(0, images.shape[0], images.shape[1], 1, 32),
+        name="load",
+    )(core, images, texts)
+
+
+def own_kernel(core_ref, mine, yours, got_images, got_texts, own, other):
+    rows = mine.shape[0]
+    own[:rows] = mine[...]
+    other[rows:] = yours[...]
+    for c, (low, top) in enumerate(((got_images, got_texts), (got_texts, got_images))):
+
+        @pl.when(core_ref[0] == c)
+        def _():
+            own[rows:] = low[...]
+            other[:rows] = top[...]
 
 
 def own_call(core, *parts):
@@ -124,54 +143,60 @@
     block = pltpu.VMEM((2 * rows, features), parts[0].dtype)
     return pl.pallas_call(
         own_kernel,
-        in_specs=[smem_spec()] + [pl.BlockSpec(memory_space=pl.ANY)] * 4,
+        in_specs=[smem_spec()] + [vmem_spec()] * 4,
         out_specs=[vmem_spec()] * 2,
         out_shape=[block, block],
-        scratch_shapes=[pltpu.SemaphoreType.DMA((4,))],
         compiler_params=params(),
         cost_estimate=cost(0, rows, features, 1, 16),
         name="own",
     )(core, *parts)
 
 
-def join_kernel(b0, b1, b2, out):
+def join_kernel(b0, b1, b2, out0, out1):
     rows = b0.shape[0]
-    for j, b in enumerate((b0, b1, b2)):
-        out[j * rows : (j + 1) * rows, :] = b[...]
+    cut = rows // 2
+    out0[:rows] = b0[...]
+    out0[rows:] = b1[:cut]
+    out1[:cut] = b1[cut:]
+    out1[cut:] = b2[...]
 
 
 def join_call(*parts):
     rows, features = parts[0].shape
+    out = jax.ShapeDtypeStruct((3 * rows // 2, features), parts[0].dtype)
     return pl.pallas_call(
         join_kernel,
         in_specs=[vmem_spec()] * 3,
-        out_specs=vmem_spec(),
-        out_shape=jax.ShapeDtypeStruct((3 * rows, features), parts[0].dtype),
+        out_specs=[vmem_spec()] * 2,
+        out_shape=[out, out],
         compiler_params=params(),
         cost_estimate=cost(0, 3 * rows, features, 1, 4),
         name="join",
     )(*parts)
 
 
-def views(refs):
-    own, near = refs[:2]
-    rows = own.shape[0]
-    return [own] + [near.at[pl.ds(j * rows, rows)] for j in range(3)] + list(refs[2:])
-
-
-def take_half(core, blocks, shift, out):
-    rows = blocks[0].shape[0]
+def take_half(core, halves, shift, out):
     for c in range(2):
 
         @pl.when(core == c)
         def _():
-            for j in range(4):
-                out[j * rows : (j + 1) * rows, :] = blocks[4 * (c ^ shift) + j][...]
+            at = 0
+            for part in halves[c ^ shift]:
+                out[at : at + part.shape[0], :] = part[...]
+                at += part.shape[0]
+
+
+def a_halves(refs):
+    return refs[:4], refs[4:8]
+
+
+def b_halves(refs):
+    return refs[:3], refs[3:7]
 
 
 def scores_kernel(scale, core_ref, *refs):
-    a_refs, b_refs = refs[:8], views(refs[8:14])
-    e_ref, a_stat, b_stat, flags, a_cat, b_cat, col_m, col_s = refs[14:]
+    a_refs, b_refs = refs[:8], b_halves(refs[8:15])
+    e_ref, a_stat, b_stat, flags, a_cat, b_cat, col_m, col_s = refs[15:]
     rows = a_refs[0].shape[0]
     half = 4 * rows
     core = core_ref[0]
@@ -195,38 +220,40 @@
             sl = slice(j * rows, (j + 1) * rows)
             a_stat[4 * q + j : 4 * q + j + 1, :] = row_lse[:, sl]
             b_stat[pl.ds((q ^ core) * 4 + j, 1), :] = col_lse[:, sl]
-        reach = jnp.max(jnp.maximum(jnp.abs(row_lse), jnp.abs(col_lse)))
-        bad = jnp.logical_not(reach <= RANGE)
-        flags[q] = bad.astype(jnp.int32)
-
-        @pl.when(bad)
-        def _():
-            for r in range(4):
-                a_cat[r * rows : (r + 1) * rows, :] = a_refs[4 * q + r][...]
-            col_m[...] = jnp.full_like(col_m, -jnp.inf)
-            col_s[...] = jnp.zeros_like(col_s)
-
-            @pl.loop(0, 4)
-            def _(r):
-                sl = pl.ds(pl.multiple_of(r * rows, 16), rows)
-                s = dot_nt(a_cat[sl, :], b_cat[q]) * scale
-                e_ref[q, sl, :] = s
-                row_m = jnp.max(s, axis=1, keepdims=True)
-                row_s = jnp.sum(jnp.exp2(s - row_m), axis=1, keepdims=True)
-                a_stat[pl.ds(4 * q + r, 1), :] = row_of(row_m + jnp.log2(row_s), rows)
-                blk_m = jnp.max(s, axis=0, keepdims=True)
-                blk_s = jnp.sum(jnp.exp2(s - blk_m), axis=0, keepdims=True)
-                before = col_m[...]
-                top = jnp.maximum(before, blk_m)
-                col_s[...] = col_s[...] * jnp.exp2(before - top) + blk_s * jnp.exp2(blk_m - top)
-                col_m[...] = top
-
-            lse = col_m[...] + jnp.log2(col_s[...])
-            for j in range(4):
-                b_stat[pl.ds((q ^ core) * 4 + j, 1), :] = lse[:, j * rows : (j + 1) * rows]
-
-    quadrant(0)
-    quadrant(1)
+        return jnp.maximum(jnp.abs(row_lse), jnp.abs(col_lse))
+
+    def by_maxima(q):
+        for r in range(4):
+            a_cat[r * rows : (r + 1) * rows, :] = a_refs[4 * q + r][...]
+        col_m[...] = jnp.full_like(col_m, -jnp.inf)
+        col_s[...] = jnp.zeros_like(col_s)
+
+        @pl.loop(0, 4)
+        def _(r):
+            sl = pl.ds(pl.multiple_of(r * rows, 16), rows)
+            s = dot_nt(a_cat[sl, :], b_cat[q]) * scale
+            e_ref[q, sl, :] = s
+            row_m = jnp.max(s, axis=1, keepdims=True)
+            row_s = jnp.sum(jnp.exp2(s - row_m), axis=1, keepdims=True)
+            a_stat[pl.ds(4 * q + r, 1), :] = row_of(row_m + jnp.log2(row_s), rows)
+            blk_m = jnp.max(s, axis=0, keepdims=True)
+            blk_s = jnp.sum(jnp.exp2(s - blk_m), axis=0, keepdims=True)
+            before = col_m[...]
+            top = jnp.maximum(before, blk_m)
+            col_s[...] = col_s[...] * jnp.exp2(before - top) + blk_s * jnp.exp2(blk_m - top)
+            col_m[...] = top
+
+        lse = col_m[...] + jnp.log2(col_s[...])
+        for j in range(4):
+            b_stat[pl.ds((q ^ core) * 4 + j, 1), :] = lse[:, j * rows : (j + 1) * rows]
+
+    bad = jnp.logical_not(jnp.max(jnp.maximum(quadrant(0), quadrant(1))) <= RANGE)
+    flags[0] = bad.astype(jnp.int32)
+
+    @pl.when(bad)
+    def _():
+        by_maxima(0)
+        by_maxima(1)
 
 
 def scores_call(core, a_blocks, b_blocks, scale):
@@ -235,13 +262,13 @@
     stat = jax.ShapeDtypeStruct((8, rows), jnp.float32)
     return pl.pallas_call(
         functools.partial(scores_kernel, scale),
-        in_specs=[smem_spec()] + [vmem_spec()] * 14,
+        in_specs=[smem_spec()] + [vmem_spec()] * 15,
         out_specs=[vmem_spec()] * 3 + [smem_spec()],
         out_shape=[
             pltpu.VMEM((2, half, half), jnp.float32),
             stat,
             stat,
-            jax.ShapeDtypeStruct((2,), jnp.int32),
+            jax.ShapeDtypeStruct((1,), jnp.int32),
         ],
         scratch_shapes=[
             pltpu.VMEM((half, features), jnp.bfloat16),
@@ -279,12 +306,12 @@
     rows = a_lse.shape[1]
     half = 4 * rows
     core = core_ref[0]
-    take_half(core, a_refs, 1, a_half)
+    take_half(core, a_halves(a_refs), 1, a_half)
     for q in range(2):
         a_row = jnp.concatenate([a_lse[4 * q + j : 4 * q + j + 1, :] for j in range(4)], axis=1)
         b_row = jnp.concatenate([b_lse[pl.ds((q ^ core) * 4 + j, 1), :] for j in range(4)], axis=1)
 
-        @pl.when(flags[q] == 0)
+        @pl.when(flags[0] == 0)
         def _():
             a_col = column_of(jnp.exp2(-a_row), half)
             b_exp = jnp.exp2(-b_row)
@@ -292,7 +319,7 @@
                 sl = slice(r * rows, (r + 1) * rows)
                 w_ref[q, sl, :] = (e_ref[q, sl, :] * (a_col[sl, :] + b_exp)).astype(jnp.bfloat16)
 
-        @pl.when(flags[q] != 0)
+        @pl.when(flags[0] != 0)
         def _():
             a_col = column_of(a_row, half)
             for r in range(4):
@@ -322,15 +349,17 @@
 
 
 def middle_kernel(core_ref, w_ref, *refs):
-    a_refs, b_refs = refs[:8], views(refs[8:14])
-    ga_hi, gb0, gb_lo, a_half, b_half = refs[14:]
-    rows = gb0.shape[0]
+    a_refs, b_refs = refs[:8], b_halves(refs[8:15])
+    ga_hi, gb_lo, a_half, b_half = refs[15:]
+    rows = a_refs[0].shape[0]
     core = core_ref[0]
-    take_half(core, a_refs, 0, a_half)
+    take_half(core, a_halves(a_refs), 0, a_half)
     take_half(core, b_refs, 1, b_half)
     g = 0.5 * dot_tn(w_ref[core], a_half[...])
-    gb0[...] = g[:rows]
-    gb_lo[...] = g[rows:].astype(jnp.bfloat16)
+    high = g[:rows].astype(jnp.bfloat16)
+    gb_lo[:rows] = high
+    gb_lo[rows : 2 * rows] = (g[:rows] - high.astype(jnp.float32)).astype(jnp.bfloat16)
+    gb_lo[2 * rows :] = g[rows:].astype(jnp.bfloat16)
     ga_hi[...] = 0.5 * jnp.dot(w_ref[1], b_half[...], preferred_element_type=jnp.float32)
 
 
@@ -339,12 +368,11 @@
     half = 4 * rows
     return pl.pallas_call(
         middle_kernel,
-        in_specs=[smem_spec()] + [vmem_spec()] * 15,
-        out_specs=[vmem_spec()] * 3,
+        in_specs=[smem_spec()] + [vmem_spec()] * 16,
+        out_specs=[vmem_spec()] * 2,
         out_shape=[
             pltpu.VMEM((half, features), jnp.float32),
-            jax.ShapeDtypeStruct((rows, features), jnp.float32),
-            jax.ShapeDtypeStruct((half - rows, features), jnp.bfloat16),
+            jax.ShapeDtypeStruct((half + rows, features), jnp.bfloat16),
         ],
         scratch_shapes=[pltpu.VMEM((half, features), jnp.bfloat16)] * 2,
         compiler_params=params(),
@@ -375,7 +403,7 @@
 
 
 def last_kernel(core_ref, w_ref, *refs):
-    b_refs, (ga_lo, b_half) = views(refs[:6]), refs[6:]
+    b_refs, (ga_lo, b_half) = b_halves(refs[:7]), refs[7:]
     take_half(core_ref[0], b_refs, 0, b_half)
     ga_lo[...] = 0.5 * jnp.dot(w_ref[0], b_half[...], preferred_element_type=jnp.float32)
 
@@ -385,7 +413,7 @@
     half = 4 * rows
     return pl.pallas_call(
         last_kernel,
-        in_specs=[smem_spec()] + [vmem_spec()] * 7,
+        in_specs=[smem_spec()] + [vmem_spec()] * 8,
         out_specs=vmem_spec(),
         out_shape=pltpu.VMEM((half, features), jnp.float32),
         scratch_shapes=[pltpu.VMEM((half, features), jnp.bfloat16)],
@@ -395,28 +423,28 @@
     )(core, w, *b_blocks)
 
 
-def near_kernel(ga_lo, got0, got_lo, r_xy, r_yz, r_xz, p0, p1, p2, p4):
+def near_kernel(ga_lo, got_lo, r_xy, r_yz, r_xz, p0, p1, p2, p4):
     rows = p0.shape[0]
-    wide = lambda ref: ref[...].astype(jnp.float32)
-    p0[...] = ga_lo[:rows] + got0[...]
-    part = lambda j: ga_lo[j * rows : (j + 1) * rows, :] + got_lo[(j - 1) * rows : j * rows, :].astype(jnp.float32)
-    p1[...] = (part(1) + wide(r_xz)).astype(jnp.bfloat16)
-    p2[...] = (part(2) + wide(r_xy)).astype(jnp.bfloat16)
-    p4[...] = (part(3) + wide(r_yz)).astype(jnp.bfloat16)
-
-
-def near_call(ga_lo, got0, got_lo, *received):
-    rows, features = got0.shape
+    wide = lambda a: a.astype(jnp.float32)
+    p0[...] = ga_lo[:rows] + (wide(got_lo[:rows]) + wide(got_lo[rows : 2 * rows]))
+    part = lambda j: ga_lo[j * rows : (j + 1) * rows, :] + wide(got_lo[(j + 1) * rows : (j + 2) * rows, :])
+    p1[...] = (part(1) + wide(r_xz[...])).astype(jnp.bfloat16)
+    p2[...] = (part(2) + wide(r_xy[...])).astype(jnp.bfloat16)
+    p4[...] = (part(3) + wide(r_yz[...])).astype(jnp.bfloat16)
+
+
+def near_call(ga_lo, got_lo, *received):
+    rows, features = received[0].shape
     narrow = jax.ShapeDtypeStruct((rows, features), jnp.bfloat16)
     return pl.pallas_call(
         near_kernel,
-        in_specs=[vmem_spec()] * 6,
+        in_specs=[vmem_spec()] * 5,
         out_specs=[vmem_spec()] * 4,
         out_shape=[pltpu.VMEM((rows, features), jnp.float32)] + [narrow] * 3,
         compiler_params=params(),
         cost_estimate=cost(0, 4 * rows, features, 1, 12),
         name="near",
-    )(ga_lo, got0, got_lo, *received)
+    )(ga_lo, got_lo, *received)
 
 
 def body(images, texts):
@@ -426,17 +454,19 @@
     first = core == 0
     core_arr = core.astype(jnp.int32).reshape(1)
     in_hbm = lambda a: pltpu.with_memory_space_constraint(a, pltpu.HBM)
-    own, other = own_call(core_arr, in_hbm(images), in_hbm(texts), swap(images), swap(texts))
+    got = swap(images), swap(texts)
+    own, other = own_call(core_arr, *load_call(core_arr, in_hbm(images), in_hbm(texts)), *got)
     near = {m: to_cube(own, m) for m in (4, 2, 1)}
     far = {7: to_cube(own, 7), 5: to_cube(near[1], 4), 3: to_cube(near[2], 1), 6: to_cube(near[4], 2)}
     blocks = {0: own, **near, **far}
     in_vmem = lambda a: pltpu.with_memory_space_constraint(a, pltpu.VMEM)
     a_blocks = [in_vmem(blocks[m]) for m in ORDER]
     swapped = {m: swap(far[m]) for m in (7, 5, 3)}
-    last, *held = lax.optimization_barrier((far[6], swapped[7], swapped[5], swapped[3]))
+    joined = [swap(a) for a in join_call(near[1], near[2], near[4])]
+    last, *held = lax.optimization_barrier((far[6], swapped[7], swapped[5], swapped[3], *joined))
     swapped.update(zip((7, 5, 3), held))
     swapped[6] = swap(last)
-    b_blocks = [other, swap(join_call(near[1], near[2], near[4]))] + [swapped[m] for m in ORDER[4:]]
+    b_blocks = [other] + held[3:] + [swapped[m] for m in ORDER[4:]]
     b_blocks = [in_vmem(b) for b in b_blocks]
 
     e, a_stat, b_stat, flags = scores_call(core_arr, a_blocks, b_blocks, scale)
@@ -447,15 +477,15 @@
 
     w, gb_hi = weights_call(core_arr, flags, e, a_lse, b_lse, a_blocks)
     got_hi = swap(gb_hi)
-    ga_hi, gb0, gb_lo = middle_call(core_arr, w, a_blocks, b_blocks)
-    got0, got_lo = swap(gb0), swap(gb_lo)
+    ga_hi, gb_lo = middle_call(core_arr, w, a_blocks, b_blocks)
+    got_lo = swap(gb_lo)
     p = dict(zip(ORDER[4:], far_call(ga_hi, got_hi)))
     from_xy = to_cube(p[3], 1)
     from_yz = to_cube(p[6], 2)
     from_xz = to_cube(p[5], 4)
     from_xyz = to_cube(p[7], 7)
     ga_lo = last_call(core_arr, w, b_blocks)
-    p0, p1, p2, p4 = near_call(ga_lo, got0, got_lo, from_xy, from_yz, from_xz)
+    p0, p1, p2, p4 = near_call(ga_lo, got_lo, from_xy, from_yz, from_xz)
     wide = lambda a: a.astype(jnp.float32)
     total = p0 + wide(from_xyz) + wide(to_cube(p1, 1)) + wide(to_cube(p2, 2)) + wide(to_cube(p4, 4))
     kept, sent = total[:rows], total[rows:]

time: 115 us -> 114 us (level)
    pallas_call x5 -> x6, Pallas kernels: 10.8 us -> 10.2 us  [the longest x1 5.56 us: middle_call(): pl.pallas_call(middle_kernel, in_specs=[smem_spec()] + [vmem_spec()] * 16...]
  transfers between devices with their start and end apart: 30 -> 30, of which waited for: 19 -> 18; matrix products, arithmetic and copies ran while one was open for 0% -> 0% of each run, Pallas kernels for 8% -> 9%
where the time goes in v10:
time: 114 us; the launch traced here: 113 us
  starting transfers between devices  42.3 us (37%)
  Pallas kernels  36.4 us (32%)
  waiting for transfers between devices  32.3 us (28%)
  other arithmetic  1.34 us (1%)
    ppermute x17, starting transfers between devices, to_cube(): return lax.ppermute(a, AXES, across(m))  32.3 us
    ppermute x17, waiting for transfers between devices, to_cube(): return lax.ppermute(a, AXES, across(m))  25.3 us
    pallas_call x1, Pallas kernels, scores_call(): pl.pallas_call(functools.partial(scores_kernel, scale), in_specs=[smem_sp...  18.1 us
    ppermute x13, starting transfers between devices, swap(): return lax.ppermute(a, AXES, SWAP)  9.93 us
    pallas_call x1, Pallas kernels, weights_call(): pl.pallas_call(weights_kernel, in_specs=[smem_spec()] * 2 + [vmem_spec()]...  7.68 us
    ppermute x13, waiting for transfers between devices, swap(): return lax.ppermute(a, AXES, SWAP)  7.03 us
    pallas_call x1, Pallas kernels, middle_call(): pl.pallas_call(middle_kernel, in_specs=[smem_spec()] + [vmem_spec()] * 16...  5.56 us
    pallas_call x1, Pallas kernels, last_call(): pl.pallas_call(last_kernel, in_specs=[smem_spec()] + [vmem_spec()] * 8, o...  2.84 us
  transfers between devices with their start and end apart: 30, of which 18 were waited for; matrix products, arithmetic and copies ran while one was open for 0% of the time, Pallas kernels for 9%

profile of v10, /device:TPU:1, one launch (start us, length us, event | category | flops | bytes accessed | tf_op | source)
XLA Modules:
  0.0 113.1 jit_solution(3886181144839083014)
XLA Ops:
  0.6 1.5 %collective-permute-start = (bf16[160,768]{1,0:T(8,128)(2,1)}, bf16[160,768]{1,0:T(8,128)(2,1)S(1)}, u32[]{:S(2)}, u32[]{:S(2)}) collective-permute-start(bf16[160,768]{1,0:T(8,128)(2,1)} %images.1), channel_id=1, source_target_pairs={{0,16},{1,17},{2,18},{3,19},{4,20},{5,21},{6,22},{7,23},{8,24},{9,... | collective-permute-start | bytes 737288 | tf_op jit(solution)/shard_map/ppermute | solution.py:57
  2.1 0.1 collective-permute-start.1
  2.2 1.1 load.1
  3.3 0.2 collective-permute-done.got_images
  3.5 0.4 collective-permute-done.1.got_texts
  3.9 0.1 own.1
  3.9 2.6 %collective-permute-start.2 = (bf16[320,768]{1,0:T(8,128)(2,1)S(1)}, bf16[320,768]{1,0:T(8,128)(2,1)S(1)}, u32[]{:S(2)}, u32[]{:S(2)}) collective-permute-start(bf16[320,768]{1,0:T(8,128)(2,1)S(1)} %get-tuple-element.32.refs_0_), channel_id=1, source_target_pairs={{0,4},{1,5},{2,6},{3,7},{4,0},{5,1},{6,2},{7,3},{8,12},{9,13},{10,... | collective-permute-start | bytes 1474568 | tf_op jit(solution)/shard_map/ppermute | solution.py:53
  6.6 1.3 %collective-permute-start.3 = (bf16[320,768]{1,0:T(8,128)(2,1)S(1)}, bf16[320,768]{1,0:T(8,128)(2,1)S(1)}, u32[]{:S(2)}, u32[]{:S(2)}) collective-permute-start(bf16[320,768]{1,0:T(8,128)(2,1)S(1)} %get-tuple-element.32.refs_0_), channel_id=1, source_target_pairs={{0,96},{1,97},{2,98},{3,99},{4,100},{5,101},{6,102},{7,103},{8,104... | collective-permute-start | bytes 1474568 | tf_op jit(solution)/shard_map/ppermute | solution.py:53
  7.9 3.8 %collective-permute-start.4 = (bf16[320,768]{1,0:T(8,128)(2,1)S(1)}, bf16[320,768]{1,0:T(8,128)(2,1)S(1)}, u32[]{:S(2)}, u32[]{:S(2)}) collective-permute-start(bf16[320,768]{1,0:T(8,128)(2,1)S(1)} %get-tuple-element.32.refs_0_), channel_id=1, source_target_pairs={{0,1},{1,0},{2,3},{3,2},{4,5},{5,4},{6,7},{7,6},{8,9},{9,8},{10,11... | collective-permute-start | bytes 1474568 | tf_op jit(solution)/shard_map/ppermute | solution.py:53
  11.6 0.0 collective-permute-start.8
  11.6 1.6 %collective-permute-done.2.b0.refs_1_ = bf16[320,768]{1,0:T(8,128)(2,1)S(1)} collective-permute-done((bf16[320,768]{1,0:T(8,128)(2,1)S(1)}, bf16[320,768]{1,0:T(8,128)(2,1)S(1)}, u32[]{:S(2)}, u32[]{:S(2)}) %collective-permute-start.2) | collective-permute-done | bytes 491552 | tf_op jit(solution)/shard_map/ppermute | solution.py:53
  13.2 3.8 %collective-permute-start.6 = (bf16[320,768]{1,0:T(8,128)(2,1)S(1)}, bf16[320,768]{1,0:T(8,128)(2,1)S(1)}, u32[]{:S(2)}, u32[]{:S(2)}) collective-permute-start(bf16[320,768]{1,0:T(8,128)(2,1)S(1)} %collective-permute-done.2.b0.refs_1_), channel_id=1, source_target_pairs={{0,1},{1,0},{2,3},{3,2},{4,5},{5,4},{6,7},{7,6},{8,9},{9,8},{10,11... | collective-permute-start | bytes 1474568 | tf_op jit(solution)/shard_map/ppermute | solution.py:53
  17.0 2.5 %collective-permute-start.5 = (bf16[320,768]{1,0:T(8,128)(2,1)S(1)}, bf16[320,768]{1,0:T(8,128)(2,1)S(1)}, u32[]{:S(2)}, u32[]{:S(2)}) collective-permute-start(bf16[320,768]{1,0:T(8,128)(2,1)S(1)} %collective-permute-done.3.b1.refs_2_), channel_id=1, source_target_pairs={{0,4},{1,5},{2,6},{3,7},{4,0},{5,1},{6,2},{7,3},{8,12},{9,13},{10,... | collective-permute-start | bytes 1474568 | tf_op jit(solution)/shard_map/ppermute | solution.py:53
  19.5 3.1 %collective-permute-done.4.b2.refs_3_ = bf16[320,768]{1,0:T(8,128)(2,1)S(1)} collective-permute-done((bf16[320,768]{1,0:T(8,128)(2,1)S(1)}, bf16[320,768]{1,0:T(8,128)(2,1)S(1)}, u32[]{:S(2)}, u32[]{:S(2)}) %collective-permute-start.4) | collective-permute-done | bytes 491552 | tf_op jit(solution)/shard_map/ppermute | solution.py:53
  22.7 0.2 collective-permute-start.7
  22.8 0.1 join.1
  22.9 2.0 %collective-permute-start.12 = (bf16[480,768]{1,0:T(8,128)(2,1)S(1)}, bf16[480,768]{1,0:T(8,128)(2,1)S(1)}, u32[]{:S(2)}, u32[]{:S(2)}) collective-permute-start(bf16[480,768]{1,0:T(8,128)(2,1)S(1)} %get-tuple-element.34), channel_id=1, source_target_pairs={{0,16},{1,17},{2,18},{3,19},{4,20},{5,21},{6,22},{7,23},{8,24},{9,... | collective-permute-start | bytes 2211848 | tf_op jit(solution)/shard_map/ppermute | solution.py:57
  25.0 0.0 collective-permute-done.8.refs_7_
  25.0 0.1 collective-permute-start.13
  25.1 3.7 %collective-permute-done.6.refs_5_ = bf16[320,768]{1,0:T(8,128)(2,1)S(1)} collective-permute-done((bf16[320,768]{1,0:T(8,128)(2,1)S(1)}, bf16[320,768]{1,0:T(8,128)(2,1)S(1)}, u32[]{:S(2)}, u32[]{:S(2)}) %collective-permute-start.6) | collective-permute-done | bytes 491552 | tf_op jit(solution)/shard_map/ppermute | solution.py:53
  28.8 0.0 collective-permute-start.9
  28.8 0.0 collective-permute-done.5.refs_4_
  28.8 0.6 collective-permute-start.10
  29.4 1.2 %collective-permute-done.7.refs_6_ = bf16[320,768]{1,0:T(8,128)(2,1)S(1)} collective-permute-done((bf16[320,768]{1,0:T(8,128)(2,1)S(1)}, bf16[320,768]{1,0:T(8,128)(2,1)S(1)}, u32[]{:S(2)}, u32[]{:S(2)}) %collective-permute-start.7) | collective-permute-done | bytes 491552 | tf_op jit(solution)/shard_map/ppermute | solution.py:53
  30.6 2.4 %collective-permute-start.11 = (bf16[320,768]{1,0:T(8,128)(2,1)S(1)}, bf16[320,768]{1,0:T(8,128)(2,1)S(1)}, u32[]{:S(2)}, u32[]{:S(2)}) collective-permute-start(bf16[320,768]{1,0:T(8,128)(2,1)S(1)} %collective-permute-done.5.refs_4_), channel_id=1, source_target_pairs={{0,16},{1,17},{2,18},{3,19},{4,20},{5,21},{6,22},{7,23},{8,24},{9,... | collective-permute-start | bytes 1474568 | tf_op jit(solution)/shard_map/ppermute | solution.py:57
  33.1 0.0 collective-permute-done.9.refs_14_.refs_6_
  33.1 0.0 collective-permute-done.12.refs_9_.refs_1_
  33.1 1.5 %collective-permute-done.11.refs_11_.refs_3_ = bf16[320,768]{1,0:T(8,128)(2,1)S(1)} collective-permute-done((bf16[320,768]{1,0:T(8,128)(2,1)S(1)}, bf16[320,768]{1,0:T(8,128)(2,1)S(1)}, u32[]{:S(2)}, u32[]{:S(2)}) %collective-permute-start.11) | collective-permute-done | bytes 491552 | tf_op jit(solution)/shard_map/ppermute | solution.py:57
  34.6 0.4 collective-permute-start.14
  35.0 1.5 %collective-permute-done.14.refs_13_.refs_5_ = bf16[320,768]{1,0:T(8,128)(2,1)S(1)} collective-permute-done((bf16[320,768]{1,0:T(8,128)(2,1)S(1)}, bf16[320,768]{1,0:T(8,128)(2,1)S(1)}, u32[]{:S(2)}, u32[]{:S(2)}) %collective-permute-start.14) | collective-permute-done | bytes 491552 | tf_op jit(solution)/shard_map/ppermute | solution.py:57
  36.4 18.1 %scores.1 = (f32[2,1280,1280]{2,1,0:T(8,128)S(1)}, f32[8,320]{1,0:T(8,128)S(1)}, f32[8,320]{1,0:T(8,128)S(1)}, s32[1]{0:T(128)}) custom-call(s32[1]{0:T(128)} %bitcast.core_ref, bf16[320,768]{1,0:T(8,128)(2,1)S(1)} %get-tuple-element.32.refs_0_, bf16[320,768]{1,0:T(8,128)(2,1)S(1)} %collective-permute-done.2.b0.refs_1_, ...), custom_call_target="tpu_custom_call" | custom-call | flops 5033164800 | tf_op jit(solution)/shard_map/scores/pallas_call | solution.py:263
  54.6 0.5 collective-permute-start.15
  55.0 0.8 collective-permute-done.15.got_ref
  55.9 1.3 %collective-permute-start.16 = (f32[8,320]{1,0:T(8,128)S(1)}, f32[8,320]{1,0:T(8,128)S(1)}, u32[]{:S(2)}, u32[]{:S(2)}) collective-permute-start(f32[8,320]{1,0:T(8,128)S(1)} %merge.4.mine_ref), channel_id=1, source_target_pairs={{0,4},{1,5},{2,6},{3,7},{4,0},{5,1},{6,2},{7,3},{8,12},{9,13},{10,... | collective-permute-start | bytes 30728 | tf_op jit(solution)/shard_map/ppermute | solution.py:53
  57.2 2.5 %collective-permute-done.16.got_ref = f32[8,320]{1,0:T(8,128)S(1)} collective-permute-done((f32[8,320]{1,0:T(8,128)S(1)}, f32[8,320]{1,0:T(8,128)S(1)}, u32[]{:S(2)}, u32[]{:S(2)}) %collective-permute-start.16) | collective-permute-done | bytes 10272 | tf_op jit(solution)/shard_map/ppermute | solution.py:53
  59.7 0.1 collective-permute-start.17
  59.8 2.5 %collective-permute-done.17.got_ref = f32[8,320]{1,0:T(8,128)S(1)} collective-permute-done((f32[8,320]{1,0:T(8,128)S(1)}, f32[8,320]{1,0:T(8,128)S(1)}, u32[]{:S(2)}, u32[]{:S(2)}) %collective-permute-start.17) | collective-permute-done | bytes 10272 | tf_op jit(solution)/shard_map/ppermute | solution.py:53
  62.4 3.8 %collective-permute-start.18 = (f32[8,320]{1,0:T(8,128)S(1)}, f32[8,320]{1,0:T(8,128)S(1)}, u32[]{:S(2)}, u32[]{:S(2)}) collective-permute-start(f32[8,320]{1,0:T(8,128)S(1)} %merge.6.mine_ref), channel_id=1, source_target_pairs={{0,1},{1,0},{2,3},{3,2},{4,5},{5,4},{6,7},{7,6},{8,9},{9,8},{10,11... | collective-permute-start | bytes 30728 | tf_op jit(solution)/shard_map/ppermute | solution.py:53
  66.2 1.1 collective-permute-done.18.got_ref
  67.4 1.6 %collective-permute-start.19 = (f32[8,320]{1,0:T(8,128)S(1)}, f32[8,320]{1,0:T(8,128)S(1)}, u32[]{:S(2)}, u32[]{:S(2)}) collective-permute-start(f32[8,320]{1,0:T(8,128)S(1)} %merge.7.a_lse), channel_id=1, source_target_pairs={{0,16},{1,17},{2,18},{3,19},{4,20},{5,21},{6,22},{7,23},{8,24},{9,... | collective-permute-start | bytes 30728 | tf_op jit(solution)/shard_map/ppermute | solution.py:57
  68.9 0.8 collective-permute-done.19.b_lse
  69.8 7.7 %weights.1 = (bf16[2,1280,1280]{2,1,0:T(8,128)(2,1)S(1)}, bf16[1280,768]{1,0:T(8,128)(2,1)S(1)}) custom-call(s32[1]{0:T(128)} %bitcast.core_ref, s32[1]{0:T(128)} %get-tuple-element.42.flags, f32[2,1280,1280]{2,1,0:T(8,128)S(1)} %get-tuple-element.43.e_ref, f32[8,320]{1,0:T(8,128)S(1)} %merge.7.a_lse, f32[8,320]{1,0:T(8,128)S(1)} %collective-permute-done.19.b_lse, ...), custom_call_target="tpu_custom_call" | custom-call | flops 2516582400 | bytes 19660800 | tf_op jit(solution)/shard_map/weights/pallas_call | solution.py:336
  77.5 0.4 collective-permute-start.21
  77.9 5.6 %middle.1 = (f32[1280,768]{1,0:T(8,128)S(1)}, bf16[1600,768]{1,0:T(8,128)(2,1)S(1)}) custom-call(s32[1]{0:T(128)} %bitcast.core_ref, bf16[2,1280,1280]{2,1,0:T(8,128)(2,1)S(1)} %get-tuple-element.46.w_ref, bf16[320,768]{1,0:T(8,128)(2,1)S(1)} %get-tuple-element.32.refs_0_, bf16[320,768]{1,0:T(8,128)(2,1)S(1)} %collective-permute-done.2.b0.refs_1_, ...), custom_call_target="tpu_custom_call" | custom-call | flops 5033164800 | tf_op jit(solution)/shard_map/middle/pallas_call | solution.py:369
  83.4 0.3 collective-permute-start.20
  83.7 0.3 far.1
  84.0 1.8 %collective-permute-start.22 = (bf16[320,768]{1,0:T(8,128)(2,1)S(1)}, bf16[320,768]{1,0:T(8,128)(2,1)S(1)}, u32[]{:S(2)}, u32[]{:S(2)}) collective-permute-start(bf16[320,768]{1,0:T(8,128)(2,1)S(1)} %get-tuple-element.50), channel_id=1, source_target_pairs={{0,4},{1,5},{2,6},{3,7},{4,0},{5,1},{6,2},{7,3},{8,12},{9,13},{10,... | collective-permute-start | bytes 1474568 | tf_op jit(solution)/shard_map/ppermute | solution.py:53
  85.8 3.9 %collective-permute-start.24 = (bf16[320,768]{1,0:T(8,128)(2,1)S(1)}, bf16[320,768]{1,0:T(8,128)(2,1)S(1)}, u32[]{:S(2)}, u32[]{:S(2)}) collective-permute-start(bf16[320,768]{1,0:T(8,128)(2,1)S(1)} %get-tuple-element.52), channel_id=1, source_target_pairs={{0,1},{1,0},{2,3},{3,2},{4,5},{5,4},{6,7},{7,6},{8,9},{9,8},{10,11... | collective-permute-start | bytes 1474568 | tf_op jit(solution)/shard_map/ppermute | solution.py:53
  89.7 2.8 %last.1.ga_lo = f32[1280,768]{1,0:T(8,128)S(1)} custom-call(s32[1]{0:T(128)} %bitcast.core_ref, bf16[2,1280,1280]{2,1,0:T(8,128)(2,1)S(1)} %get-tuple-element.46.w_ref, bf16[320,768]{1,0:T(8,128)(2,1)S(1)} %get-tuple-element.33.refs_8_.refs_0_, bf16[480,768]{1,0:T(8,128)(2,1)S(1)} %collective-permute-done.12.refs_9_.refs_1_, ...), custom_call_target="tpu_custom_call" | custom-call | flops 2516582400 | tf_op jit(solution)/shard_map/last/pallas_call | solution.py:414
  92.5 1.8 %collective-permute-start.25 = (bf16[320,768]{1,0:T(8,128)(2,1)S(1)}, bf16[320,768]{1,0:T(8,128)(2,1)S(1)}, u32[]{:S(2)}, u32[]{:S(2)}) collective-permute-start(bf16[320,768]{1,0:T(8,128)(2,1)S(1)} %get-tuple-element.54), channel_id=1, source_target_pairs={{0,101},{1,100},{2,103},{3,102},{4,97},{5,96},{6,99},{7,98},{8,109... | collective-permute-start | bytes 1474568 | tf_op jit(solution)/shard_map/ppermute | solution.py:53
  94.4 1.5 %collective-permute-done.24.r_xz = bf16[320,768]{1,0:T(8,128)(2,1)S(1)} collective-permute-done((bf16[320,768]{1,0:T(8,128)(2,1)S(1)}, bf16[320,768]{1,0:T(8,128)(2,1)S(1)}, u32[]{:S(2)}, u32[]{:S(2)}) %collective-permute-start.24) | collective-permute-done | bytes 491552 | tf_op jit(solution)/shard_map/ppermute | solution.py:53
  95.9 0.6 near.1
  96.5 0.0 copy-start
  96.5 0.0 copy-start.1
  96.5 1.2 %collective-permute-start.26 = (bf16[320,768]{1,0:T(8,128)(2,1)S(1)}, bf16[320,768]{1,0:T(8,128)(2,1)S(1)}, u32[]{:S(2)}, u32[]{:S(2)}) collective-permute-start(bf16[320,768]{1,0:T(8,128)(2,1)S(1)} %get-tuple-element.55), channel_id=1, source_target_pairs={{0,4},{1,5},{2,6},{3,7},{4,0},{5,1},{6,2},{7,3},{8,12},{9,13},{10,... | collective-permute-start | bytes 1474568 | tf_op jit(solution)/shard_map/ppermute | solution.py:53
  97.7 1.5 %collective-permute-start.27 = (bf16[320,768]{1,0:T(8,128)(2,1)S(1)}, bf16[320,768]{1,0:T(8,128)(2,1)S(1)}, u32[]{:S(2)}, u32[]{:S(2)}) collective-permute-start(bf16[320,768]{1,0:T(8,128)(2,1)S(1)} %get-tuple-element.56), channel_id=1, source_target_pairs={{0,96},{1,97},{2,98},{3,99},{4,100},{5,101},{6,102},{7,103},{8,104... | collective-permute-start | bytes 1474568 | tf_op jit(solution)/shard_map/ppermute | solution.py:53
  99.2 2.7 %collective-permute-start.28 = (bf16[320,768]{1,0:T(8,128)(2,1)S(1)}, bf16[320,768]{1,0:T(8,128)(2,1)S(1)}, u32[]{:S(2)}, u32[]{:S(2)}) collective-permute-start(bf16[320,768]{1,0:T(8,128)(2,1)S(1)} %get-tuple-element.57), channel_id=1, source_target_pairs={{0,1},{1,0},{2,3},{3,2},{4,5},{5,4},{6,7},{7,6},{8,9},{9,8},{10,11... | collective-permute-start | bytes 1474568 | tf_op jit(solution)/shard_map/ppermute | solution.py:53
  101.9 2.8 %collective-permute-done.25 = bf16[320,768]{1,0:T(8,128)(2,1)S(1)} collective-permute-done((bf16[320,768]{1,0:T(8,128)(2,1)S(1)}, bf16[320,768]{1,0:T(8,128)(2,1)S(1)}, u32[]{:S(2)}, u32[]{:S(2)}) %collective-permute-start.25) | collective-permute-done | bytes 491552 | tf_op jit(solution)/shard_map/ppermute | solution.py:53
  104.7 3.2 %collective-permute-done.26 = bf16[320,768]{1,0:T(8,128)(2,1)S(1)} collective-permute-done((bf16[320,768]{1,0:T(8,128)(2,1)S(1)}, bf16[320,768]{1,0:T(8,128)(2,1)S(1)}, u32[]{:S(2)}, u32[]{:S(2)}) %collective-permute-start.26) | collective-permute-done | bytes 491552 | tf_op jit(solution)/shard_map/ppermute | solution.py:53
  107.9 1.9 %collective-permute-done.28 = bf16[320,768]{1,0:T(8,128)(2,1)S(1)} collective-permute-done((bf16[320,768]{1,0:T(8,128)(2,1)S(1)}, bf16[320,768]{1,0:T(8,128)(2,1)S(1)}, u32[]{:S(2)}, u32[]{:S(2)}) %collective-permute-start.28) | collective-permute-done | bytes 491552 | tf_op jit(solution)/shard_map/ppermute | solution.py:53
  109.8 0.3 convert_add_fusion
  110.1 0.1 collective-permute-start.29
  110.2 1.8 %collective-permute-done.29 = f32[160,768]{1,0:T(8,128)S(1)} collective-permute-done((f32[160,768]{1,0:T(8,128)S(1)}, f32[160,768]{1,0:T(8,128)S(1)}, u32[]{:S(2)}, u32[]{:S(2)}) %collective-permute-start.29) | collective-permute-done | bytes 491552 | tf_op jit(solution)/shard_map/ppermute | solution.py:57
  112.1 1.0 convert_subtract_fusion
  (16 shorter events, 0.2 us)
Async XLA Ops:
  0.6 2.9 %collective-permute-start = (bf16[160,768]{1,0:T(8,128)(2,1)}, bf16[160,768]{1,0:T(8,128)(2,1)S(1)}, u32[]{:S(2)}, u32[]{:S(2)}) collective-permute-start(bf16[160,768]{1,0:T(8,128)(2,1)} %images.1), channel_id=1, source_target_pairs={{0,16},{1,17},{2,18},{3,19},{4,20},{5,21},{6,22},{7,23},{8,24},{9,... | collective-permute-start | bytes 737288 | tf_op jit(solution)/shard_map/ppermute | solution.py:57
  2.1 1.7 %collective-permute-start.1 = (bf16[160,768]{1,0:T(8,128)(2,1)}, bf16[160,768]{1,0:T(8,128)(2,1)S(1)}, u32[]{:S(2)}, u32[]{:S(2)}) collective-permute-start(bf16[160,768]{1,0:T(8,128)(2,1)} %texts.1), channel_id=1, source_target_pairs={{0,16},{1,17},{2,18},{3,19},{4,20},{5,21},{6,22},{7,23},{8,24},{9,... | collective-permute-start | bytes 737288 | tf_op jit(solution)/shard_map/ppermute | solution.py:57
  3.9 9.3 %collective-permute-start.2 = (bf16[320,768]{1,0:T(8,128)(2,1)S(1)}, bf16[320,768]{1,0:T(8,128)(2,1)S(1)}, u32[]{:S(2)}, u32[]{:S(2)}) collective-permute-start(bf16[320,768]{1,0:T(8,128)(2,1)S(1)} %get-tuple-element.32.refs_0_), channel_id=1, source_target_pairs={{0,4},{1,5},{2,6},{3,7},{4,0},{5,1},{6,2},{7,3},{8,12},{9,13},{10,... | collective-permute-start | bytes 1474568 | tf_op jit(solution)/shard_map/ppermute | solution.py:53
  6.6 10.5 %collective-permute-start.3 = (bf16[320,768]{1,0:T(8,128)(2,1)S(1)}, bf16[320,768]{1,0:T(8,128)(2,1)S(1)}, u32[]{:S(2)}, u32[]{:S(2)}) collective-permute-start(bf16[320,768]{1,0:T(8,128)(2,1)S(1)} %get-tuple-element.32.refs_0_), channel_id=1, source_target_pairs={{0,96},{1,97},{2,98},{3,99},{4,100},{5,101},{6,102},{7,103},{8,104... | collective-permute-start | bytes 1474568 | tf_op jit(solution)/shard_map/ppermute | solution.py:53
  7.9 14.8 %collective-permute-start.4 = (bf16[320,768]{1,0:T(8,128)(2,1)S(1)}, bf16[320,768]{1,0:T(8,128)(2,1)S(1)}, u32[]{:S(2)}, u32[]{:S(2)}) collective-permute-start(bf16[320,768]{1,0:T(8,128)(2,1)S(1)} %get-tuple-element.32.refs_0_), channel_id=1, source_target_pairs={{0,1},{1,0},{2,3},{3,2},{4,5},{5,4},{6,7},{7,6},{8,9},{9,8},{10,11... | collective-permute-start | bytes 1474568 | tf_op jit(solution)/shard_map/ppermute | solution.py:53
  11.6 13.4 %collective-permute-start.8 = (bf16[320,768]{1,0:T(8,128)(2,1)S(1)}, bf16[320,768]{1,0:T(8,128)(2,1)S(1)}, u32[]{:S(2)}, u32[]{:S(2)}) collective-permute-start(bf16[320,768]{1,0:T(8,128)(2,1)S(1)} %get-tuple-element.32.refs_0_), channel_id=1, source_target_pairs={{0,101},{1,100},{2,103},{3,102},{4,97},{5,96},{6,99},{7,98},{8,109... | collective-permute-start | bytes 1474568 | tf_op jit(solution)/shard_map/ppermute | solution.py:53
  13.2 15.6 %collective-permute-start.6 = (bf16[320,768]{1,0:T(8,128)(2,1)S(1)}, bf16[320,768]{1,0:T(8,128)(2,1)S(1)}, u32[]{:S(2)}, u32[]{:S(2)}) collective-permute-start(bf16[320,768]{1,0:T(8,128)(2,1)S(1)} %collective-permute-done.2.b0.refs_1_), channel_id=1, source_target_pairs={{0,1},{1,0},{2,3},{3,2},{4,5},{5,4},{6,7},{7,6},{8,9},{9,8},{10,11... | collective-permute-start | bytes 1474568 | tf_op jit(solution)/shard_map/ppermute | solution.py:53
  17.0 11.8 %collective-permute-start.5 = (bf16[320,768]{1,0:T(8,128)(2,1)S(1)}, bf16[320,768]{1,0:T(8,128)(2,1)S(1)}, u32[]{:S(2)}, u32[]{:S(2)}) collective-permute-start(bf16[320,768]{1,0:T(8,128)(2,1)S(1)} %collective-permute-done.3.b1.refs_2_), channel_id=1, source_target_pairs={{0,4},{1,5},{2,6},{3,7},{4,0},{5,1},{6,2},{7,3},{8,12},{9,13},{10,... | collective-permute-start | bytes 1474568 | tf_op jit(solution)/shard_map/ppermute | solution.py:53
  22.7 8.0 %collective-permute-start.7 = (bf16[320,768]{1,0:T(8,128)(2,1)S(1)}, bf16[320,768]{1,0:T(8,128)(2,1)S(1)}, u32[]{:S(2)}, u32[]{:S(2)}) collective-permute-start(bf16[320,768]{1,0:T(8,128)(2,1)S(1)} %collective-permute-done.4.b2.refs_3_), channel_id=1, source_target_pairs={{0,96},{1,97},{2,98},{3,99},{4,100},{5,101},{6,102},{7,103},{8,104... | collective-permute-start | bytes 1474568 | tf_op jit(solution)/shard_map/ppermute | solution.py:53
  22.9 10.2 %collective-permute-start.12 = (bf16[480,768]{1,0:T(8,128)(2,1)S(1)}, bf16[480,768]{1,0:T(8,128)(2,1)S(1)}, u32[]{:S(2)}, u32[]{:S(2)}) collective-permute-start(bf16[480,768]{1,0:T(8,128)(2,1)S(1)} %get-tuple-element.34), channel_id=1, source_target_pairs={{0,16},{1,17},{2,18},{3,19},{4,20},{5,21},{6,22},{7,23},{8,24},{9,... | collective-permute-start | bytes 2211848 | tf_op jit(solution)/shard_map/ppermute | solution.py:57
  25.0 8.1 %collective-permute-start.13 = (bf16[480,768]{1,0:T(8,128)(2,1)S(1)}, bf16[480,768]{1,0:T(8,128)(2,1)S(1)}, u32[]{:S(2)}, u32[]{:S(2)}) collective-permute-start(bf16[480,768]{1,0:T(8,128)(2,1)S(1)} %get-tuple-element.35), channel_id=1, source_target_pairs={{0,16},{1,17},{2,18},{3,19},{4,20},{5,21},{6,22},{7,23},{8,24},{9,... | collective-permute-start | bytes 2211848 | tf_op jit(solution)/shard_map/ppermute | solution.py:57
  28.8 4.3 %collective-permute-start.9 = (bf16[320,768]{1,0:T(8,128)(2,1)S(1)}, bf16[320,768]{1,0:T(8,128)(2,1)S(1)}, u32[]{:S(2)}, u32[]{:S(2)}) collective-permute-start(bf16[320,768]{1,0:T(8,128)(2,1)S(1)} %collective-permute-done.8.refs_7_), channel_id=1, source_target_pairs={{0,16},{1,17},{2,18},{3,19},{4,20},{5,21},{6,22},{7,23},{8,24},{9,... | collective-permute-start | bytes 1474568 | tf_op jit(solution)/shard_map/ppermute | solution.py:57
  28.8 4.3 %collective-permute-start.10 = (bf16[320,768]{1,0:T(8,128)(2,1)S(1)}, bf16[320,768]{1,0:T(8,128)(2,1)S(1)}, u32[]{:S(2)}, u32[]{:S(2)}) collective-permute-start(bf16[320,768]{1,0:T(8,128)(2,1)S(1)} %collective-permute-done.6.refs_5_), channel_id=1, source_target_pairs={{0,16},{1,17},{2,18},{3,19},{4,20},{5,21},{6,22},{7,23},{8,24},{9,... | collective-permute-start | bytes 1474568 | tf_op jit(solution)/shard_map/ppermute | solution.py:57
  30.6 3.9 %collective-permute-start.11 = (bf16[320,768]{1,0:T(8,128)(2,1)S(1)}, bf16[320,768]{1,0:T(8,128)(2,1)S(1)}, u32[]{:S(2)}, u32[]{:S(2)}) collective-permute-start(bf16[320,768]{1,0:T(8,128)(2,1)S(1)} %collective-permute-done.5.refs_4_), channel_id=1, source_target_pairs={{0,16},{1,17},{2,18},{3,19},{4,20},{5,21},{6,22},{7,23},{8,24},{9,... | collective-permute-start | bytes 1474568 | tf_op jit(solution)/shard_map/ppermute | solution.py:57
  34.6 1.9 %collective-permute-start.14 = (bf16[320,768]{1,0:T(8,128)(2,1)S(1)}, bf16[320,768]{1,0:T(8,128)(2,1)S(1)}, u32[]{:S(2)}, u32[]{:S(2)}) collective-permute-start(bf16[320,768]{1,0:T(8,128)(2,1)S(1)} %collective-permute-done.7.refs_6_), channel_id=1, source_target_pairs={{0,16},{1,17},{2,18},{3,19},{4,20},{5,21},{6,22},{7,23},{8,24},{9,... | collective-permute-start | bytes 1474568 | tf_op jit(solution)/shard_map/ppermute | solution.py:57
  54.6 1.3 %collective-permute-start.15 = (f32[8,320]{1,0:T(8,128)S(1)}, f32[8,320]{1,0:T(8,128)S(1)}, u32[]{:S(2)}, u32[]{:S(2)}) collective-permute-start(f32[8,320]{1,0:T(8,128)S(1)} %get-tuple-element.45), channel_id=1, source_target_pairs={{0,16},{1,17},{2,18},{3,19},{4,20},{5,21},{6,22},{7,23},{8,24},{9,... | collective-permute-start | bytes 30728 | tf_op jit(solution)/shard_map/ppermute | solution.py:57
  55.9 3.8 %collective-permute-start.16 = (f32[8,320]{1,0:T(8,128)S(1)}, f32[8,320]{1,0:T(8,128)S(1)}, u32[]{:S(2)}, u32[]{:S(2)}) collective-permute-start(f32[8,320]{1,0:T(8,128)S(1)} %merge.4.mine_ref), channel_id=1, source_target_pairs={{0,4},{1,5},{2,6},{3,7},{4,0},{5,1},{6,2},{7,3},{8,12},{9,13},{10,... | collective-permute-start | bytes 30728 | tf_op jit(solution)/shard_map/ppermute | solution.py:53
  59.7 2.6 %collective-permute-start.17 = (f32[8,320]{1,0:T(8,128)S(1)}, f32[8,320]{1,0:T(8,128)S(1)}, u32[]{:S(2)}, u32[]{:S(2)}) collective-permute-start(f32[8,320]{1,0:T(8,128)S(1)} %merge.5.mine_ref), channel_id=1, source_target_pairs={{0,96},{1,97},{2,98},{3,99},{4,100},{5,101},{6,102},{7,103},{8,104... | collective-permute-start | bytes 30728 | tf_op jit(solution)/shard_map/ppermute | solution.py:53
  62.4 4.9 %collective-permute-start.18 = (f32[8,320]{1,0:T(8,128)S(1)}, f32[8,320]{1,0:T(8,128)S(1)}, u32[]{:S(2)}, u32[]{:S(2)}) collective-permute-start(f32[8,320]{1,0:T(8,128)S(1)} %merge.6.mine_ref), channel_id=1, source_target_pairs={{0,1},{1,0},{2,3},{3,2},{4,5},{5,4},{6,7},{7,6},{8,9},{9,8},{10,11... | collective-permute-start | bytes 30728 | tf_op jit(solution)/shard_map/ppermute | solution.py:53
  67.4 2.4 %collective-permute-start.19 = (f32[8,320]{1,0:T(8,128)S(1)}, f32[8,320]{1,0:T(8,128)S(1)}, u32[]{:S(2)}, u32[]{:S(2)}) collective-permute-start(f32[8,320]{1,0:T(8,128)S(1)} %merge.7.a_lse), channel_id=1, source_target_pairs={{0,16},{1,17},{2,18},{3,19},{4,20},{5,21},{6,22},{7,23},{8,24},{9,... | collective-permute-start | bytes 30728 | tf_op jit(solution)/shard_map/ppermute | solution.py:57
  77.5 6.2 %collective-permute-start.21 = (bf16[1280,768]{1,0:T(8,128)(2,1)S(1)}, bf16[1280,768]{1,0:T(8,128)(2,1)S(1)}, u32[]{:S(2)}, u32[]{:S(2)}) collective-permute-start(bf16[1280,768]{1,0:T(8,128)(2,1)S(1)} %get-tuple-element.49), channel_id=1, source_target_pairs={{0,16},{1,17},{2,18},{3,19},{4,20},{5,21},{6,22},{7,23},{8,24},{9,... | collective-permute-start | bytes 5898248 | tf_op jit(solution)/shard_map/ppermute | solution.py:57
  83.4 12.5 %collective-permute-start.20 = (bf16[1600,768]{1,0:T(8,128)(2,1)S(1)}, bf16[1600,768]{1,0:T(8,128)(2,1)S(1)}, u32[]{:S(2)}, u32[]{:S(2)}) collective-permute-start(bf16[1600,768]{1,0:T(8,128)(2,1)S(1)} %get-tuple-element.47), channel_id=1, source_target_pairs={{0,16},{1,17},{2,18},{3,19},{4,20},{5,21},{6,22},{7,23},{8,24},{9,... | collective-permute-start | bytes 7372808 | tf_op jit(solution)/shard_map/ppermute | solution.py:57
  84.0 10.4 %collective-permute-start.22 = (bf16[320,768]{1,0:T(8,128)(2,1)S(1)}, bf16[320,768]{1,0:T(8,128)(2,1)S(1)}, u32[]{:S(2)}, u32[]{:S(2)}) collective-permute-start(bf16[320,768]{1,0:T(8,128)(2,1)S(1)} %get-tuple-element.50), channel_id=1, source_target_pairs={{0,4},{1,5},{2,6},{3,7},{4,0},{5,1},{6,2},{7,3},{8,12},{9,13},{10,... | collective-permute-start | bytes 1474568 | tf_op jit(solution)/shard_map/ppermute | solution.py:53
  85.8 8.6 %collective-permute-start.23 = (bf16[320,768]{1,0:T(8,128)(2,1)S(1)}, bf16[320,768]{1,0:T(8,128)(2,1)S(1)}, u32[]{:S(2)}, u32[]{:S(2)}) collective-permute-start(bf16[320,768]{1,0:T(8,128)(2,1)S(1)} %get-tuple-element.51), channel_id=1, source_target_pairs={{0,96},{1,97},{2,98},{3,99},{4,100},{5,101},{6,102},{7,103},{8,104... | collective-permute-start | bytes 1474568 | tf_op jit(solution)/shard_map/ppermute | solution.py:53
  85.8 10.1 %collective-permute-start.24 = (bf16[320,768]{1,0:T(8,128)(2,1)S(1)}, bf16[320,768]{1,0:T(8,128)(2,1)S(1)}, u32[]{:S(2)}, u32[]{:S(2)}) collective-permute-start(bf16[320,768]{1,0:T(8,128)(2,1)S(1)} %get-tuple-element.52), channel_id=1, source_target_pairs={{0,1},{1,0},{2,3},{3,2},{4,5},{5,4},{6,7},{7,6},{8,9},{9,8},{10,11... | collective-permute-start | bytes 1474568 | tf_op jit(solution)/shard_map/ppermute | solution.py:53
  92.5 12.1 %collective-permute-start.25 = (bf16[320,768]{1,0:T(8,128)(2,1)S(1)}, bf16[320,768]{1,0:T(8,128)(2,1)S(1)}, u32[]{:S(2)}, u32[]{:S(2)}) collective-permute-start(bf16[320,768]{1,0:T(8,128)(2,1)S(1)} %get-tuple-element.54), channel_id=1, source_target_pairs={{0,101},{1,100},{2,103},{3,102},{4,97},{5,96},{6,99},{7,98},{8,109... | collective-permute-start | bytes 1474568 | tf_op jit(solution)/shard_map/ppermute | solution.py:53
  96.5 15.6 %copy-start = (bf16[160,768]{1,0:T(8,128)(2,1)S(1)}, bf16[160,768]{1,0:T(8,128)(2,1)}, u32[]{:S(2)}) copy-start(bf16[160,768]{1,0:T(8,128)(2,1)} %images.1) | copy-start | bytes 737284
  96.5 15.6 %copy-start.1 = (bf16[160,768]{1,0:T(8,128)(2,1)S(1)}, bf16[160,768]{1,0:T(8,128)(2,1)}, u32[]{:S(2)}) copy-start(bf16[160,768]{1,0:T(8,128)(2,1)} %texts.1) | copy-start | bytes 737284
  96.5 11.4 %collective-permute-start.26 = (bf16[320,768]{1,0:T(8,128)(2,1)S(1)}, bf16[320,768]{1,0:T(8,128)(2,1)S(1)}, u32[]{:S(2)}, u32[]{:S(2)}) collective-permute-start(bf16[320,768]{1,0:T(8,128)(2,1)S(1)} %get-tuple-element.55), channel_id=1, source_target_pairs={{0,4},{1,5},{2,6},{3,7},{4,0},{5,1},{6,2},{7,3},{8,12},{9,13},{10,... | collective-permute-start | bytes 1474568 | tf_op jit(solution)/shard_map/ppermute | solution.py:53
  97.7 10.2 %collective-permute-start.27 = (bf16[320,768]{1,0:T(8,128)(2,1)S(1)}, bf16[320,768]{1,0:T(8,128)(2,1)S(1)}, u32[]{:S(2)}, u32[]{:S(2)}) collective-permute-start(bf16[320,768]{1,0:T(8,128)(2,1)S(1)} %get-tuple-element.56), channel_id=1, source_target_pairs={{0,96},{1,97},{2,98},{3,99},{4,100},{5,101},{6,102},{7,103},{8,104... | collective-permute-start | bytes 1474568 | tf_op jit(solution)/shard_map/ppermute | solution.py:53
  99.2 10.6 %collective-permute-start.28 = (bf16[320,768]{1,0:T(8,128)(2,1)S(1)}, bf16[320,768]{1,0:T(8,128)(2,1)S(1)}, u32[]{:S(2)}, u32[]{:S(2)}) collective-permute-start(bf16[320,768]{1,0:T(8,128)(2,1)S(1)} %get-tuple-element.57), channel_id=1, source_target_pairs={{0,1},{1,0},{2,3},{3,2},{4,5},{5,4},{6,7},{7,6},{8,9},{9,8},{10,11... | collective-permute-start | bytes 1474568 | tf_op jit(solution)/shard_map/ppermute | solution.py:53
  110.1 1.9 %collective-permute-start.29 = (f32[160,768]{1,0:T(8,128)S(1)}, f32[160,768]{1,0:T(8,128)S(1)}, u32[]{:S(2)}, u32[]{:S(2)}) collective-permute-start(f32[160,768]{1,0:T(8,128)S(1)} %slice.9), channel_id=1, source_target_pairs={{0,16},{1,17},{2,18},{3,19},{4,20},{5,21},{6,22},{7,23},{8,24},{9,... | collective-permute-start | bytes 1474568 | tf_op jit(solution)/shard_map/ppermute | solution.py:57

commit v11 on v10

--- a/solution.py
+++ b/solution.py
@@ -457,7 +457,8 @@
     got = swap(images), swap(texts)
     own, other = own_call(core_arr, *load_call(core_arr, in_hbm(images), in_hbm(texts)), *got)
     near = {m: to_cube(own, m) for m in (4, 2, 1)}
-    far = {7: to_cube(own, 7), 5: to_cube(near[1], 4), 3: to_cube(near[2], 1), 6: to_cube(near[4], 2)}
+    late = lax.optimization_barrier((own, near[1]))[0]
+    far = {7: to_cube(late, 7), 5: to_cube(near[1], 4), 3: to_cube(near[2], 1), 6: to_cube(near[4], 2)}
     blocks = {0: own, **near, **far}
     in_vmem = lambda a: pltpu.with_memory_space_constraint(a, pltpu.VMEM)
     a_blocks = [in_vmem(blocks[m]) for m in ORDER]

time: 114 us -> 113 us (level)
  starting transfers between devices: 42.3 us -> 37.5 us
  waiting for transfers between devices: 32.3 us -> 36.4 us
    ppermute x13, starting transfers between devices: 9.93 us -> 5.8 us  [swap(): return lax.ppermute(a, AXES, SWAP)]
    ppermute x17, waiting for transfers between devices: 25.3 us -> 27.9 us  [to_cube(): return lax.ppermute(a, AXES, across(m))]
    ppermute x13, waiting for transfers between devices: 7.03 us -> 8.5 us  [swap(): return lax.ppermute(a, AXES, SWAP)]
  transfers between devices with their start and end apart: 30 -> 30, of which waited for: 18 -> 21; matrix products, arithmetic and copies ran while one was open for 0% -> 0% of each run, Pallas kernels for 9% -> 9%
where the time goes in v11:
time: 113 us; the launch traced here: 112 us
  starting transfers between devices  37.5 us (33%)
  Pallas kernels  36.4 us (32%)
  waiting for transfers between devices  36.4 us (32%)
  other arithmetic  1.34 us (1%)
    ppermute x17, starting transfers between devices, to_cube(): return lax.ppermute(a, AXES, across(m))  31.7 us
    ppermute x17, waiting for transfers between devices, to_cube(): return lax.ppermute(a, AXES, across(m))  27.9 us
    pallas_call x1, Pallas kernels, scores_call(): pl.pallas_call(functools.partial(scores_kernel, scale), in_specs=[smem_sp...  18.1 us
    ppermute x13, waiting for transfers between devices, swap(): return lax.ppermute(a, AXES, SWAP)  8.5 us
    pallas_call x1, Pallas kernels, weights_call(): pl.pallas_call(weights_kernel, in_specs=[smem_spec()] * 2 + [vmem_spec()]...  7.68 us
    ppermute x13, starting transfers between devices, swap(): return lax.ppermute(a, AXES, SWAP)  5.8 us
    pallas_call x1, Pallas kernels, middle_call(): pl.pallas_call(middle_kernel, in_specs=[smem_spec()] + [vmem_spec()] * 16...  5.56 us
    pallas_call x1, Pallas kernels, last_call(): pl.pallas_call(last_kernel, in_specs=[smem_spec()] + [vmem_spec()] * 8, o...  2.84 us
  transfers between devices with their start and end apart: 30, of which 21 were waited for; matrix products, arithmetic and copies ran while one was open for 0% of the time, Pallas kernels for 9%

profile of v11, /device:TPU:1, one launch (start us, length us, event | category | flops | bytes accessed | tf_op | source)
XLA Modules:
  0.0 112.5 jit_solution(7591208085323243555)
XLA Ops:
  0.6 1.5 %collective-permute-start = (bf16[160,768]{1,0:T(8,128)(2,1)}, bf16[160,768]{1,0:T(8,128)(2,1)S(1)}, u32[]{:S(2)}, u32[]{:S(2)}) collective-permute-start(bf16[160,768]{1,0:T(8,128)(2,1)} %images.1), channel_id=1, source_target_pairs={{0,16},{1,17},{2,18},{3,19},{4,20},{5,21},{6,22},{7,23},{8,24},{9,... | collective-permute-start | bytes 737288 | tf_op jit(solution)/shard_map/ppermute | solution.py:57
  2.1 0.1 collective-permute-start.1
  2.2 1.1 load.1
  3.3 0.2 collective-permute-done.got_images
  3.5 0.4 collective-permute-done.1.got_texts
  3.9 0.1 own.1
  3.9 2.6 %collective-permute-start.2 = (bf16[320,768]{1,0:T(8,128)(2,1)S(1)}, bf16[320,768]{1,0:T(8,128)(2,1)S(1)}, u32[]{:S(2)}, u32[]{:S(2)}) collective-permute-start(bf16[320,768]{1,0:T(8,128)(2,1)S(1)} %get-tuple-element.34.refs_0_), channel_id=1, source_target_pairs={{0,4},{1,5},{2,6},{3,7},{4,0},{5,1},{6,2},{7,3},{8,12},{9,13},{10,... | collective-permute-start | bytes 1474568 | tf_op jit(solution)/shard_map/ppermute | solution.py:53
  6.6 1.3 %collective-permute-start.3 = (bf16[320,768]{1,0:T(8,128)(2,1)S(1)}, bf16[320,768]{1,0:T(8,128)(2,1)S(1)}, u32[]{:S(2)}, u32[]{:S(2)}) collective-permute-start(bf16[320,768]{1,0:T(8,128)(2,1)S(1)} %get-tuple-element.34.refs_0_), channel_id=1, source_target_pairs={{0,96},{1,97},{2,98},{3,99},{4,100},{5,101},{6,102},{7,103},{8,104... | collective-permute-start | bytes 1474568 | tf_op jit(solution)/shard_map/ppermute | solution.py:53
  7.9 3.8 %collective-permute-start.4 = (bf16[320,768]{1,0:T(8,128)(2,1)S(1)}, bf16[320,768]{1,0:T(8,128)(2,1)S(1)}, u32[]{:S(2)}, u32[]{:S(2)}) collective-permute-start(bf16[320,768]{1,0:T(8,128)(2,1)S(1)} %get-tuple-element.34.refs_0_), channel_id=1, source_target_pairs={{0,1},{1,0},{2,3},{3,2},{4,5},{5,4},{6,7},{7,6},{8,9},{9,8},{10,11... | collective-permute-start | bytes 1474568 | tf_op jit(solution)/shard_map/ppermute | solution.py:53
  11.6 1.6 %collective-permute-done.2.b0.refs_1_ = bf16[320,768]{1,0:T(8,128)(2,1)S(1)} collective-permute-done((bf16[320,768]{1,0:T(8,128)(2,1)S(1)}, bf16[320,768]{1,0:T(8,128)(2,1)S(1)}, u32[]{:S(2)}, u32[]{:S(2)}) %collective-permute-start.2) | collective-permute-done | bytes 491552 | tf_op jit(solution)/shard_map/ppermute | solution.py:53
  13.2 6.8 %collective-permute-start.8 = (bf16[320,768]{1,0:T(8,128)(2,1)S(1)}, bf16[320,768]{1,0:T(8,128)(2,1)S(1)}, u32[]{:S(2)}, u32[]{:S(2)}) collective-permute-start(bf16[320,768]{1,0:T(8,128)(2,1)S(1)} %get-tuple-element.34.refs_0_), channel_id=1, source_target_pairs={{0,101},{1,100},{2,103},{3,102},{4,97},{5,96},{6,99},{7,98},{8,109... | collective-permute-start | bytes 1474568 | tf_op jit(solution)/shard_map/ppermute | solution.py:53
  19.9 0.0 collective-permute-start.6
  20.0 0.2 collective-permute-start.5
  20.2 0.5 collective-permute-start.7
  20.6 0.1 join.1
  20.7 0.1 collective-permute-start.12
  20.8 5.5 %collective-permute-done.8.refs_7_ = bf16[320,768]{1,0:T(8,128)(2,1)S(1)} collective-permute-done((bf16[320,768]{1,0:T(8,128)(2,1)S(1)}, bf16[320,768]{1,0:T(8,128)(2,1)S(1)}, u32[]{:S(2)}, u32[]{:S(2)}) %collective-permute-start.8) | collective-permute-done | bytes 491552 | tf_op jit(solution)/shard_map/ppermute | solution.py:53
  26.3 0.0 collective-permute-start.13
  26.3 5.1 %collective-permute-done.6.refs_5_ = bf16[320,768]{1,0:T(8,128)(2,1)S(1)} collective-permute-done((bf16[320,768]{1,0:T(8,128)(2,1)S(1)}, bf16[320,768]{1,0:T(8,128)(2,1)S(1)}, u32[]{:S(2)}, u32[]{:S(2)}) %collective-permute-start.6) | collective-permute-done | bytes 491552 | tf_op jit(solution)/shard_map/ppermute | solution.py:53
  31.4 0.2 collective-permute-done.5.refs_4_
  31.7 0.3 collective-permute-start.10
  31.9 0.2 collective-permute-start.11
  32.2 0.0 collective-permute-done.12.refs_9_.refs_1_
  32.2 1.1 collective-permute-done.9.refs_14_.refs_6_
  33.3 0.7 collective-permute-done.10.refs_12_.refs_4_
  34.0 0.7 collective-permute-done.11.refs_11_.refs_3_
  34.7 0.1 collective-permute-start.14
  34.8 1.7 %collective-permute-done.14.refs_13_.refs_5_ = bf16[320,768]{1,0:T(8,128)(2,1)S(1)} collective-permute-done((bf16[320,768]{1,0:T(8,128)(2,1)S(1)}, bf16[320,768]{1,0:T(8,128)(2,1)S(1)}, u32[]{:S(2)}, u32[]{:S(2)}) %collective-permute-start.14) | collective-permute-done | bytes 491552 | tf_op jit(solution)/shard_map/ppermute | solution.py:57
  36.6 18.1 %scores.1 = (f32[2,1280,1280]{2,1,0:T(8,128)S(1)}, f32[8,320]{1,0:T(8,128)S(1)}, f32[8,320]{1,0:T(8,128)S(1)}, s32[1]{0:T(128)}) custom-call(s32[1]{0:T(128)} %bitcast.core_ref, bf16[320,768]{1,0:T(8,128)(2,1)S(1)} %get-tuple-element.34.refs_0_, bf16[320,768]{1,0:T(8,128)(2,1)S(1)} %collective-permute-done.2.b0.refs_1_, ...), custom_call_target="tpu_custom_call" | custom-call | flops 5033164800 | tf_op jit(solution)/shard_map/scores/pallas_call | solution.py:263
  54.7 0.2 collective-permute-start.15
  54.9 1.0 collective-permute-done.15.got_ref
  56.0 2.1 %collective-permute-start.16 = (f32[8,320]{1,0:T(8,128)S(1)}, f32[8,320]{1,0:T(8,128)S(1)}, u32[]{:S(2)}, u32[]{:S(2)}) collective-permute-start(f32[8,320]{1,0:T(8,128)S(1)} %merge.4.mine_ref), channel_id=1, source_target_pairs={{0,4},{1,5},{2,6},{3,7},{4,0},{5,1},{6,2},{7,3},{8,12},{9,13},{10,... | collective-permute-start | bytes 30728 | tf_op jit(solution)/shard_map/ppermute | solution.py:53
  58.1 1.7 %collective-permute-done.16.got_ref = f32[8,320]{1,0:T(8,128)S(1)} collective-permute-done((f32[8,320]{1,0:T(8,128)S(1)}, f32[8,320]{1,0:T(8,128)S(1)}, u32[]{:S(2)}, u32[]{:S(2)}) %collective-permute-start.16) | collective-permute-done | bytes 10272 | tf_op jit(solution)/shard_map/ppermute | solution.py:53
  59.8 0.5 collective-permute-start.17
  60.4 2.1 %collective-permute-done.17.got_ref = f32[8,320]{1,0:T(8,128)S(1)} collective-permute-done((f32[8,320]{1,0:T(8,128)S(1)}, f32[8,320]{1,0:T(8,128)S(1)}, u32[]{:S(2)}, u32[]{:S(2)}) %collective-permute-start.17) | collective-permute-done | bytes 10272 | tf_op jit(solution)/shard_map/ppermute | solution.py:53
  62.5 2.7 %collective-permute-start.18 = (f32[8,320]{1,0:T(8,128)S(1)}, f32[8,320]{1,0:T(8,128)S(1)}, u32[]{:S(2)}, u32[]{:S(2)}) collective-permute-start(f32[8,320]{1,0:T(8,128)S(1)} %merge.6.mine_ref), channel_id=1, source_target_pairs={{0,1},{1,0},{2,3},{3,2},{4,5},{5,4},{6,7},{7,6},{8,9},{9,8},{10,11... | collective-permute-start | bytes 30728 | tf_op jit(solution)/shard_map/ppermute | solution.py:53
  65.2 1.1 collective-permute-done.18.got_ref
  66.4 2.5 %collective-permute-start.19 = (f32[8,320]{1,0:T(8,128)S(1)}, f32[8,320]{1,0:T(8,128)S(1)}, u32[]{:S(2)}, u32[]{:S(2)}) collective-permute-start(f32[8,320]{1,0:T(8,128)S(1)} %merge.7.a_lse), channel_id=1, source_target_pairs={{0,16},{1,17},{2,18},{3,19},{4,20},{5,21},{6,22},{7,23},{8,24},{9,... | collective-permute-start | bytes 30728 | tf_op jit(solution)/shard_map/ppermute | solution.py:57
  68.8 0.8 collective-permute-done.19.b_lse
  69.7 7.7 %weights.1 = (bf16[2,1280,1280]{2,1,0:T(8,128)(2,1)S(1)}, bf16[1280,768]{1,0:T(8,128)(2,1)S(1)}) custom-call(s32[1]{0:T(128)} %bitcast.core_ref, s32[1]{0:T(128)} %get-tuple-element.44.flags, f32[2,1280,1280]{2,1,0:T(8,128)S(1)} %get-tuple-element.45.e_ref, f32[8,320]{1,0:T(8,128)S(1)} %merge.7.a_lse, f32[8,320]{1,0:T(8,128)S(1)} %collective-permute-done.19.b_lse, ...), custom_call_target="tpu_custom_call" | custom-call | flops 2516582400 | bytes 19660800 | tf_op jit(solution)/shard_map/weights/pallas_call | solution.py:336
  77.4 0.4 collective-permute-start.21
  77.8 5.6 %middle.1 = (f32[1280,768]{1,0:T(8,128)S(1)}, bf16[1600,768]{1,0:T(8,128)(2,1)S(1)}) custom-call(s32[1]{0:T(128)} %bitcast.core_ref, bf16[2,1280,1280]{2,1,0:T(8,128)(2,1)S(1)} %get-tuple-element.48.w_ref, bf16[320,768]{1,0:T(8,128)(2,1)S(1)} %get-tuple-element.34.refs_0_, bf16[320,768]{1,0:T(8,128)(2,1)S(1)} %collective-permute-done.2.b0.refs_1_, ...), custom_call_target="tpu_custom_call" | custom-call | flops 5033164800 | tf_op jit(solution)/shard_map/middle/pallas_call | solution.py:369
  83.4 0.3 collective-permute-start.20
  83.6 0.3 far.1
  83.9 2.1 %collective-permute-start.22 = (bf16[320,768]{1,0:T(8,128)(2,1)S(1)}, bf16[320,768]{1,0:T(8,128)(2,1)S(1)}, u32[]{:S(2)}, u32[]{:S(2)}) collective-permute-start(bf16[320,768]{1,0:T(8,128)(2,1)S(1)} %get-tuple-element.52), channel_id=1, source_target_pairs={{0,4},{1,5},{2,6},{3,7},{4,0},{5,1},{6,2},{7,3},{8,12},{9,13},{10,... | collective-permute-start | bytes 1474568 | tf_op jit(solution)/shard_map/ppermute | solution.py:53
  86.0 3.0 %collective-permute-start.24 = (bf16[320,768]{1,0:T(8,128)(2,1)S(1)}, bf16[320,768]{1,0:T(8,128)(2,1)S(1)}, u32[]{:S(2)}, u32[]{:S(2)}) collective-permute-start(bf16[320,768]{1,0:T(8,128)(2,1)S(1)} %get-tuple-element.54), channel_id=1, source_target_pairs={{0,1},{1,0},{2,3},{3,2},{4,5},{5,4},{6,7},{7,6},{8,9},{9,8},{10,11... | collective-permute-start | bytes 1474568 | tf_op jit(solution)/shard_map/ppermute | solution.py:53
  89.0 2.8 %last.1.ga_lo = f32[1280,768]{1,0:T(8,128)S(1)} custom-call(s32[1]{0:T(128)} %bitcast.core_ref, bf16[2,1280,1280]{2,1,0:T(8,128)(2,1)S(1)} %get-tuple-element.48.w_ref, bf16[320,768]{1,0:T(8,128)(2,1)S(1)} %get-tuple-element.35.refs_8_.refs_0_, bf16[480,768]{1,0:T(8,128)(2,1)S(1)} %collective-permute-done.12.refs_9_.refs_1_, ...), custom_call_target="tpu_custom_call" | custom-call | flops 2516582400 | tf_op jit(solution)/shard_map/last/pallas_call | solution.py:414
  91.9 1.3 %collective-permute-start.25 = (bf16[320,768]{1,0:T(8,128)(2,1)S(1)}, bf16[320,768]{1,0:T(8,128)(2,1)S(1)}, u32[]{:S(2)}, u32[]{:S(2)}) collective-permute-start(bf16[320,768]{1,0:T(8,128)(2,1)S(1)} %get-tuple-element.56), channel_id=1, source_target_pairs={{0,101},{1,100},{2,103},{3,102},{4,97},{5,96},{6,99},{7,98},{8,109... | collective-permute-start | bytes 1474568 | tf_op jit(solution)/shard_map/ppermute | solution.py:53
  93.2 0.0 collective-permute-done.22.r_xy
  93.2 0.8 collective-permute-done.23.r_yz
  94.0 1.3 %collective-permute-done.24.r_xz = bf16[320,768]{1,0:T(8,128)(2,1)S(1)} collective-permute-done((bf16[320,768]{1,0:T(8,128)(2,1)S(1)}, bf16[320,768]{1,0:T(8,128)(2,1)S(1)}, u32[]{:S(2)}, u32[]{:S(2)}) %collective-permute-start.24) | collective-permute-done | bytes 491552 | tf_op jit(solution)/shard_map/ppermute | solution.py:53
  95.3 0.6 near.1
  95.8 0.0 copy-start
  95.8 0.0 copy-start.1
  95.8 0.7 collective-permute-start.26
  96.5 1.5 %collective-permute-start.27 = (bf16[320,768]{1,0:T(8,128)(2,1)S(1)}, bf16[320,768]{1,0:T(8,128)(2,1)S(1)}, u32[]{:S(2)}, u32[]{:S(2)}) collective-permute-start(bf16[320,768]{1,0:T(8,128)(2,1)S(1)} %get-tuple-element.58), channel_id=1, source_target_pairs={{0,96},{1,97},{2,98},{3,99},{4,100},{5,101},{6,102},{7,103},{8,104... | collective-permute-start | bytes 1474568 | tf_op jit(solution)/shard_map/ppermute | solution.py:53
  98.0 2.7 %collective-permute-start.28 = (bf16[320,768]{1,0:T(8,128)(2,1)S(1)}, bf16[320,768]{1,0:T(8,128)(2,1)S(1)}, u32[]{:S(2)}, u32[]{:S(2)}) collective-permute-start(bf16[320,768]{1,0:T(8,128)(2,1)S(1)} %get-tuple-element.59), channel_id=1, source_target_pairs={{0,1},{1,0},{2,3},{3,2},{4,5},{5,4},{6,7},{7,6},{8,9},{9,8},{10,11... | collective-permute-start | bytes 1474568 | tf_op jit(solution)/shard_map/ppermute | solution.py:53
  100.7 3.3 %collective-permute-done.25 = bf16[320,768]{1,0:T(8,128)(2,1)S(1)} collective-permute-done((bf16[320,768]{1,0:T(8,128)(2,1)S(1)}, bf16[320,768]{1,0:T(8,128)(2,1)S(1)}, u32[]{:S(2)}, u32[]{:S(2)}) %collective-permute-start.25) | collective-permute-done | bytes 491552 | tf_op jit(solution)/shard_map/ppermute | solution.py:53
  104.0 3.3 %collective-permute-done.26 = bf16[320,768]{1,0:T(8,128)(2,1)S(1)} collective-permute-done((bf16[320,768]{1,0:T(8,128)(2,1)S(1)}, bf16[320,768]{1,0:T(8,128)(2,1)S(1)}, u32[]{:S(2)}, u32[]{:S(2)}) %collective-permute-start.26) | collective-permute-done | bytes 491552 | tf_op jit(solution)/shard_map/ppermute | solution.py:53
  107.3 1.8 %collective-permute-done.28 = bf16[320,768]{1,0:T(8,128)(2,1)S(1)} collective-permute-done((bf16[320,768]{1,0:T(8,128)(2,1)S(1)}, bf16[320,768]{1,0:T(8,128)(2,1)S(1)}, u32[]{:S(2)}, u32[]{:S(2)}) %collective-permute-start.28) | collective-permute-done | bytes 491552 | tf_op jit(solution)/shard_map/ppermute | solution.py:53
  109.2 0.3 convert_add_fusion
  109.5 0.1 collective-permute-start.29
  109.6 1.8 %collective-permute-done.29 = f32[160,768]{1,0:T(8,128)S(1)} collective-permute-done((f32[160,768]{1,0:T(8,128)S(1)}, f32[160,768]{1,0:T(8,128)S(1)}, u32[]{:S(2)}, u32[]{:S(2)}) %collective-permute-start.29) | collective-permute-done | bytes 491552 | tf_op jit(solution)/shard_map/ppermute | solution.py:57
  111.5 1.0 convert_subtract_fusion
  (16 shorter events, 0.2 us)
Async XLA Ops:
  0.6 2.9 %collective-permute-start = (bf16[160,768]{1,0:T(8,128)(2,1)}, bf16[160,768]{1,0:T(8,128)(2,1)S(1)}, u32[]{:S(2)}, u32[]{:S(2)}) collective-permute-start(bf16[160,768]{1,0:T(8,128)(2,1)} %images.1), channel_id=1, source_target_pairs={{0,16},{1,17},{2,18},{3,19},{4,20},{5,21},{6,22},{7,23},{8,24},{9,... | collective-permute-start | bytes 737288 | tf_op jit(solution)/shard_map/ppermute | solution.py:57
  2.1 1.7 %collective-permute-start.1 = (bf16[160,768]{1,0:T(8,128)(2,1)}, bf16[160,768]{1,0:T(8,128)(2,1)S(1)}, u32[]{:S(2)}, u32[]{:S(2)}) collective-permute-start(bf16[160,768]{1,0:T(8,128)(2,1)} %texts.1), channel_id=1, source_target_pairs={{0,16},{1,17},{2,18},{3,19},{4,20},{5,21},{6,22},{7,23},{8,24},{9,... | collective-permute-start | bytes 737288 | tf_op jit(solution)/shard_map/ppermute | solution.py:57
  3.9 9.3 %collective-permute-start.2 = (bf16[320,768]{1,0:T(8,128)(2,1)S(1)}, bf16[320,768]{1,0:T(8,128)(2,1)S(1)}, u32[]{:S(2)}, u32[]{:S(2)}) collective-permute-start(bf16[320,768]{1,0:T(8,128)(2,1)S(1)} %get-tuple-element.34.refs_0_), channel_id=1, source_target_pairs={{0,4},{1,5},{2,6},{3,7},{4,0},{5,1},{6,2},{7,3},{8,12},{9,13},{10,... | collective-permute-start | bytes 1474568 | tf_op jit(solution)/shard_map/ppermute | solution.py:53
  6.6 13.4 %collective-permute-start.3 = (bf16[320,768]{1,0:T(8,128)(2,1)S(1)}, bf16[320,768]{1,0:T(8,128)(2,1)S(1)}, u32[]{:S(2)}, u32[]{:S(2)}) collective-permute-start(bf16[320,768]{1,0:T(8,128)(2,1)S(1)} %get-tuple-element.34.refs_0_), channel_id=1, source_target_pairs={{0,96},{1,97},{2,98},{3,99},{4,100},{5,101},{6,102},{7,103},{8,104... | collective-permute-start | bytes 1474568 | tf_op jit(solution)/shard_map/ppermute | solution.py:53
  7.9 12.3 %collective-permute-start.4 = (bf16[320,768]{1,0:T(8,128)(2,1)S(1)}, bf16[320,768]{1,0:T(8,128)(2,1)S(1)}, u32[]{:S(2)}, u32[]{:S(2)}) collective-permute-start(bf16[320,768]{1,0:T(8,128)(2,1)S(1)} %get-tuple-element.34.refs_0_), channel_id=1, source_target_pairs={{0,1},{1,0},{2,3},{3,2},{4,5},{5,4},{6,7},{7,6},{8,9},{9,8},{10,11... | collective-permute-start | bytes 1474568 | tf_op jit(solution)/shard_map/ppermute | solution.py:53
  13.2 13.1 %collective-permute-start.8 = (bf16[320,768]{1,0:T(8,128)(2,1)S(1)}, bf16[320,768]{1,0:T(8,128)(2,1)S(1)}, u32[]{:S(2)}, u32[]{:S(2)}) collective-permute-start(bf16[320,768]{1,0:T(8,128)(2,1)S(1)} %get-tuple-element.34.refs_0_), channel_id=1, source_target_pairs={{0,101},{1,100},{2,103},{3,102},{4,97},{5,96},{6,99},{7,98},{8,109... | collective-permute-start | bytes 1474568 | tf_op jit(solution)/shard_map/ppermute | solution.py:53
  19.9 11.5 %collective-permute-start.6 = (bf16[320,768]{1,0:T(8,128)(2,1)S(1)}, bf16[320,768]{1,0:T(8,128)(2,1)S(1)}, u32[]{:S(2)}, u32[]{:S(2)}) collective-permute-start(bf16[320,768]{1,0:T(8,128)(2,1)S(1)} %collective-permute-done.2.b0.refs_1_), channel_id=1, source_target_pairs={{0,1},{1,0},{2,3},{3,2},{4,5},{5,4},{6,7},{7,6},{8,9},{9,8},{10,11... | collective-permute-start | bytes 1474568 | tf_op jit(solution)/shard_map/ppermute | solution.py:53
  20.0 11.7 %collective-permute-start.5 = (bf16[320,768]{1,0:T(8,128)(2,1)S(1)}, bf16[320,768]{1,0:T(8,128)(2,1)S(1)}, u32[]{:S(2)}, u32[]{:S(2)}) collective-permute-start(bf16[320,768]{1,0:T(8,128)(2,1)S(1)} %collective-permute-done.3.b1.refs_2_), channel_id=1, source_target_pairs={{0,4},{1,5},{2,6},{3,7},{4,0},{5,1},{6,2},{7,3},{8,12},{9,13},{10,... | collective-permute-start | bytes 1474568 | tf_op jit(solution)/shard_map/ppermute | solution.py:53
  20.2 11.8 %collective-permute-start.7 = (bf16[320,768]{1,0:T(8,128)(2,1)S(1)}, bf16[320,768]{1,0:T(8,128)(2,1)S(1)}, u32[]{:S(2)}, u32[]{:S(2)}) collective-permute-start(bf16[320,768]{1,0:T(8,128)(2,1)S(1)} %collective-permute-done.4.b2.refs_3_), channel_id=1, source_target_pairs={{0,96},{1,97},{2,98},{3,99},{4,100},{5,101},{6,102},{7,103},{8,104... | collective-permute-start | bytes 1474568 | tf_op jit(solution)/shard_map/ppermute | solution.py:53
  20.7 11.5 %collective-permute-start.12 = (bf16[480,768]{1,0:T(8,128)(2,1)S(1)}, bf16[480,768]{1,0:T(8,128)(2,1)S(1)}, u32[]{:S(2)}, u32[]{:S(2)}) collective-permute-start(bf16[480,768]{1,0:T(8,128)(2,1)S(1)} %get-tuple-element.36), channel_id=1, source_target_pairs={{0,16},{1,17},{2,18},{3,19},{4,20},{5,21},{6,22},{7,23},{8,24},{9,... | collective-permute-start | bytes 2211848 | tf_op jit(solution)/shard_map/ppermute | solution.py:57
  26.3 5.9 %collective-permute-start.13 = (bf16[480,768]{1,0:T(8,128)(2,1)S(1)}, bf16[480,768]{1,0:T(8,128)(2,1)S(1)}, u32[]{:S(2)}, u32[]{:S(2)}) collective-permute-start(bf16[480,768]{1,0:T(8,128)(2,1)S(1)} %get-tuple-element.37), channel_id=1, source_target_pairs={{0,16},{1,17},{2,18},{3,19},{4,20},{5,21},{6,22},{7,23},{8,24},{9,... | collective-permute-start | bytes 2211848 | tf_op jit(solution)/shard_map/ppermute | solution.py:57
  31.4 1.9 %collective-permute-start.9 = (bf16[320,768]{1,0:T(8,128)(2,1)S(1)}, bf16[320,768]{1,0:T(8,128)(2,1)S(1)}, u32[]{:S(2)}, u32[]{:S(2)}) collective-permute-start(bf16[320,768]{1,0:T(8,128)(2,1)S(1)} %collective-permute-done.8.refs_7_), channel_id=1, source_target_pairs={{0,16},{1,17},{2,18},{3,19},{4,20},{5,21},{6,22},{7,23},{8,24},{9,... | collective-permute-start | bytes 1474568 | tf_op jit(solution)/shard_map/ppermute | solution.py:57
  31.7 2.3 %collective-permute-start.10 = (bf16[320,768]{1,0:T(8,128)(2,1)S(1)}, bf16[320,768]{1,0:T(8,128)(2,1)S(1)}, u32[]{:S(2)}, u32[]{:S(2)}) collective-permute-start(bf16[320,768]{1,0:T(8,128)(2,1)S(1)} %collective-permute-done.6.refs_5_), channel_id=1, source_target_pairs={{0,16},{1,17},{2,18},{3,19},{4,20},{5,21},{6,22},{7,23},{8,24},{9,... | collective-permute-start | bytes 1474568 | tf_op jit(solution)/shard_map/ppermute | solution.py:57
  31.9 2.8 %collective-permute-start.11 = (bf16[320,768]{1,0:T(8,128)(2,1)S(1)}, bf16[320,768]{1,0:T(8,128)(2,1)S(1)}, u32[]{:S(2)}, u32[]{:S(2)}) collective-permute-start(bf16[320,768]{1,0:T(8,128)(2,1)S(1)} %collective-permute-done.5.refs_4_), channel_id=1, source_target_pairs={{0,16},{1,17},{2,18},{3,19},{4,20},{5,21},{6,22},{7,23},{8,24},{9,... | collective-permute-start | bytes 1474568 | tf_op jit(solution)/shard_map/ppermute | solution.py:57
  34.7 1.9 %collective-permute-start.14 = (bf16[320,768]{1,0:T(8,128)(2,1)S(1)}, bf16[320,768]{1,0:T(8,128)(2,1)S(1)}, u32[]{:S(2)}, u32[]{:S(2)}) collective-permute-start(bf16[320,768]{1,0:T(8,128)(2,1)S(1)} %collective-permute-done.7.refs_6_), channel_id=1, source_target_pairs={{0,16},{1,17},{2,18},{3,19},{4,20},{5,21},{6,22},{7,23},{8,24},{9,... | collective-permute-start | bytes 1474568 | tf_op jit(solution)/shard_map/ppermute | solution.py:57
  54.7 1.3 %collective-permute-start.15 = (f32[8,320]{1,0:T(8,128)S(1)}, f32[8,320]{1,0:T(8,128)S(1)}, u32[]{:S(2)}, u32[]{:S(2)}) collective-permute-start(f32[8,320]{1,0:T(8,128)S(1)} %get-tuple-element.47), channel_id=1, source_target_pairs={{0,16},{1,17},{2,18},{3,19},{4,20},{5,21},{6,22},{7,23},{8,24},{9,... | collective-permute-start | bytes 30728 | tf_op jit(solution)/shard_map/ppermute | solution.py:57
  56.0 3.8 %collective-permute-start.16 = (f32[8,320]{1,0:T(8,128)S(1)}, f32[8,320]{1,0:T(8,128)S(1)}, u32[]{:S(2)}, u32[]{:S(2)}) collective-permute-start(f32[8,320]{1,0:T(8,128)S(1)} %merge.4.mine_ref), channel_id=1, source_target_pairs={{0,4},{1,5},{2,6},{3,7},{4,0},{5,1},{6,2},{7,3},{8,12},{9,13},{10,... | collective-permute-start | bytes 30728 | tf_op jit(solution)/shard_map/ppermute | solution.py:53
  59.8 2.6 %collective-permute-start.17 = (f32[8,320]{1,0:T(8,128)S(1)}, f32[8,320]{1,0:T(8,128)S(1)}, u32[]{:S(2)}, u32[]{:S(2)}) collective-permute-start(f32[8,320]{1,0:T(8,128)S(1)} %merge.5.mine_ref), channel_id=1, source_target_pairs={{0,96},{1,97},{2,98},{3,99},{4,100},{5,101},{6,102},{7,103},{8,104... | collective-permute-start | bytes 30728 | tf_op jit(solution)/shard_map/ppermute | solution.py:53
  62.5 3.8 %collective-permute-start.18 = (f32[8,320]{1,0:T(8,128)S(1)}, f32[8,320]{1,0:T(8,128)S(1)}, u32[]{:S(2)}, u32[]{:S(2)}) collective-permute-start(f32[8,320]{1,0:T(8,128)S(1)} %merge.6.mine_ref), channel_id=1, source_target_pairs={{0,1},{1,0},{2,3},{3,2},{4,5},{5,4},{6,7},{7,6},{8,9},{9,8},{10,11... | collective-permute-start | bytes 30728 | tf_op jit(solution)/shard_map/ppermute | solution.py:53
  66.4 3.3 %collective-permute-start.19 = (f32[8,320]{1,0:T(8,128)S(1)}, f32[8,320]{1,0:T(8,128)S(1)}, u32[]{:S(2)}, u32[]{:S(2)}) collective-permute-start(f32[8,320]{1,0:T(8,128)S(1)} %merge.7.a_lse), channel_id=1, source_target_pairs={{0,16},{1,17},{2,18},{3,19},{4,20},{5,21},{6,22},{7,23},{8,24},{9,... | collective-permute-start | bytes 30728 | tf_op jit(solution)/shard_map/ppermute | solution.py:57
  77.4 6.2 %collective-permute-start.21 = (bf16[1280,768]{1,0:T(8,128)(2,1)S(1)}, bf16[1280,768]{1,0:T(8,128)(2,1)S(1)}, u32[]{:S(2)}, u32[]{:S(2)}) collective-permute-start(bf16[1280,768]{1,0:T(8,128)(2,1)S(1)} %get-tuple-element.51), channel_id=1, source_target_pairs={{0,16},{1,17},{2,18},{3,19},{4,20},{5,21},{6,22},{7,23},{8,24},{9,... | collective-permute-start | bytes 5898248 | tf_op jit(solution)/shard_map/ppermute | solution.py:57
  83.4 11.9 %collective-permute-start.20 = (bf16[1600,768]{1,0:T(8,128)(2,1)S(1)}, bf16[1600,768]{1,0:T(8,128)(2,1)S(1)}, u32[]{:S(2)}, u32[]{:S(2)}) collective-permute-start(bf16[1600,768]{1,0:T(8,128)(2,1)S(1)} %get-tuple-element.49), channel_id=1, source_target_pairs={{0,16},{1,17},{2,18},{3,19},{4,20},{5,21},{6,22},{7,23},{8,24},{9,... | collective-permute-start | bytes 7372808 | tf_op jit(solution)/shard_map/ppermute | solution.py:57
  83.9 9.3 %collective-permute-start.22 = (bf16[320,768]{1,0:T(8,128)(2,1)S(1)}, bf16[320,768]{1,0:T(8,128)(2,1)S(1)}, u32[]{:S(2)}, u32[]{:S(2)}) collective-permute-start(bf16[320,768]{1,0:T(8,128)(2,1)S(1)} %get-tuple-element.52), channel_id=1, source_target_pairs={{0,4},{1,5},{2,6},{3,7},{4,0},{5,1},{6,2},{7,3},{8,12},{9,13},{10,... | collective-permute-start | bytes 1474568 | tf_op jit(solution)/shard_map/ppermute | solution.py:53
  86.0 8.0 %collective-permute-start.23 = (bf16[320,768]{1,0:T(8,128)(2,1)S(1)}, bf16[320,768]{1,0:T(8,128)(2,1)S(1)}, u32[]{:S(2)}, u32[]{:S(2)}) collective-permute-start(bf16[320,768]{1,0:T(8,128)(2,1)S(1)} %get-tuple-element.53), channel_id=1, source_target_pairs={{0,96},{1,97},{2,98},{3,99},{4,100},{5,101},{6,102},{7,103},{8,104... | collective-permute-start | bytes 1474568 | tf_op jit(solution)/shard_map/ppermute | solution.py:53
  86.0 9.2 %collective-permute-start.24 = (bf16[320,768]{1,0:T(8,128)(2,1)S(1)}, bf16[320,768]{1,0:T(8,128)(2,1)S(1)}, u32[]{:S(2)}, u32[]{:S(2)}) collective-permute-start(bf16[320,768]{1,0:T(8,128)(2,1)S(1)} %get-tuple-element.54), channel_id=1, source_target_pairs={{0,1},{1,0},{2,3},{3,2},{4,5},{5,4},{6,7},{7,6},{8,9},{9,8},{10,11... | collective-permute-start | bytes 1474568 | tf_op jit(solution)/shard_map/ppermute | solution.py:53
  91.9 12.1 %collective-permute-start.25 = (bf16[320,768]{1,0:T(8,128)(2,1)S(1)}, bf16[320,768]{1,0:T(8,128)(2,1)S(1)}, u32[]{:S(2)}, u32[]{:S(2)}) collective-permute-start(bf16[320,768]{1,0:T(8,128)(2,1)S(1)} %get-tuple-element.56), channel_id=1, source_target_pairs={{0,101},{1,100},{2,103},{3,102},{4,97},{5,96},{6,99},{7,98},{8,109... | collective-permute-start | bytes 1474568 | tf_op jit(solution)/shard_map/ppermute | solution.py:53
  95.8 15.6 %copy-start = (bf16[160,768]{1,0:T(8,128)(2,1)S(1)}, bf16[160,768]{1,0:T(8,128)(2,1)}, u32[]{:S(2)}) copy-start(bf16[160,768]{1,0:T(8,128)(2,1)} %images.1) | copy-start | bytes 737284
  95.8 15.6 %copy-start.1 = (bf16[160,768]{1,0:T(8,128)(2,1)S(1)}, bf16[160,768]{1,0:T(8,128)(2,1)}, u32[]{:S(2)}) copy-start(bf16[160,768]{1,0:T(8,128)(2,1)} %texts.1) | copy-start | bytes 737284
  95.8 11.5 %collective-permute-start.26 = (bf16[320,768]{1,0:T(8,128)(2,1)S(1)}, bf16[320,768]{1,0:T(8,128)(2,1)S(1)}, u32[]{:S(2)}, u32[]{:S(2)}) collective-permute-start(bf16[320,768]{1,0:T(8,128)(2,1)S(1)} %get-tuple-element.57), channel_id=1, source_target_pairs={{0,4},{1,5},{2,6},{3,7},{4,0},{5,1},{6,2},{7,3},{8,12},{9,13},{10,... | collective-permute-start | bytes 1474568 | tf_op jit(solution)/shard_map/ppermute | solution.py:53
  96.5 10.8 %collective-permute-start.27 = (bf16[320,768]{1,0:T(8,128)(2,1)S(1)}, bf16[320,768]{1,0:T(8,128)(2,1)S(1)}, u32[]{:S(2)}, u32[]{:S(2)}) collective-permute-start(bf16[320,768]{1,0:T(8,128)(2,1)S(1)} %get-tuple-element.58), channel_id=1, source_target_pairs={{0,96},{1,97},{2,98},{3,99},{4,100},{5,101},{6,102},{7,103},{8,104... | collective-permute-start | bytes 1474568 | tf_op jit(solution)/shard_map/ppermute | solution.py:53
  98.0 11.2 %collective-permute-start.28 = (bf16[320,768]{1,0:T(8,128)(2,1)S(1)}, bf16[320,768]{1,0:T(8,128)(2,1)S(1)}, u32[]{:S(2)}, u32[]{:S(2)}) collective-permute-start(bf16[320,768]{1,0:T(8,128)(2,1)S(1)} %get-tuple-element.59), channel_id=1, source_target_pairs={{0,1},{1,0},{2,3},{3,2},{4,5},{5,4},{6,7},{7,6},{8,9},{9,8},{10,11... | collective-permute-start | bytes 1474568 | tf_op jit(solution)/shard_map/ppermute | solution.py:53
  109.5 1.9 %collective-permute-start.29 = (f32[160,768]{1,0:T(8,128)S(1)}, f32[160,768]{1,0:T(8,128)S(1)}, u32[]{:S(2)}, u32[]{:S(2)}) collective-permute-start(f32[160,768]{1,0:T(8,128)S(1)} %slice.9), channel_id=1, source_target_pairs={{0,16},{1,17},{2,18},{3,19},{4,20},{5,21},{6,22},{7,23},{8,24},{9,... | collective-permute-start | bytes 1474568 | tf_op jit(solution)/shard_map/ppermute | solution.py:57

commit v12 on v11

--- a/solution.py
+++ b/solution.py
@@ -99,8 +99,8 @@
     return lax.dot_general(a, b, (((0,), (0,)), ((), ())), preferred_element_type=jnp.float32)
 
 
-def load_kernel(core_ref, images, texts, mine, yours, sem):
-    core = core_ref[0]
+def load_kernel(images, texts, mine, yours, sem):
+    core = lax.axis_index("core")
     for c, order in enumerate(((mine, yours), (yours, mine))):
 
         @pl.when(core == c)
@@ -112,44 +112,44 @@
                 copy.wait()
 
 
-def load_call(core, images, texts):
+def load_call(images, texts):
     block = pltpu.VMEM(images.shape, images.dtype)
     return pl.pallas_call(
         load_kernel,
-        in_specs=[smem_spec()] + [pl.BlockSpec(memory_space=pl.ANY)] * 2,
+        in_specs=[pl.BlockSpec(memory_space=pl.ANY)] * 2,
         out_specs=[vmem_spec()] * 2,
         out_shape=[block, block],
         scratch_shapes=[pltpu.SemaphoreType.DMA((2,))],
         compiler_params=params(),
         cost_estimate=cost(0, images.shape[0], images.shape[1], 1, 32),
         name="load",
-    )(core, images, texts)
-
-
-def own_kernel(core_ref, mine, yours, got_images, got_texts, own, other):
+    )(images, texts)
+
+
+def own_kernel(mine, yours, got_images, got_texts, own, other):
     rows = mine.shape[0]
     own[:rows] = mine[...]
     other[rows:] = yours[...]
     for c, (low, top) in enumerate(((got_images, got_texts), (got_texts, got_images))):
 
-        @pl.when(core_ref[0] == c)
+        @pl.when(lax.axis_index("core") == c)
         def _():
             own[rows:] = low[...]
             other[:rows] = top[...]
 
 
-def own_call(core, *parts):
+def own_call(*parts):
     rows, features = parts[0].shape
     block = pltpu.VMEM((2 * rows, features), parts[0].dtype)
     return pl.pallas_call(
         own_kernel,
-        in_specs=[smem_spec()] + [vmem_spec()] * 4,
+        in_specs=[vmem_spec()] * 4,
         out_specs=[vmem_spec()] * 2,
         out_shape=[block, block],
         compiler_params=params(),
         cost_estimate=cost(0, rows, features, 1, 16),
         name="own",
-    )(core, *parts)
+    )(*parts)
 
 
 def join_kernel(b0, b1, b2, out0, out1):
@@ -194,12 +194,12 @@
     return refs[:3], refs[3:7]
 
 
-def scores_kernel(scale, core_ref, *refs):
+def scores_kernel(scale, *refs):
     a_refs, b_refs = refs[:8], b_halves(refs[8:15])
     e_ref, a_stat, b_stat, flags, a_cat, b_cat, col_m, col_s = refs[15:]
     rows = a_refs[0].shape[0]
     half = 4 * rows
-    core = core_ref[0]
+    core = lax.axis_index("core")
     for q in range(2):
         take_half(core, b_refs, q, b_cat.at[q])
 
@@ -249,6 +249,7 @@
 
     bad = jnp.logical_not(jnp.max(jnp.maximum(quadrant(0), quadrant(1))) <= RANGE)
     flags[0] = bad.astype(jnp.int32)
+    flags[1] = bad.astype(jnp.int32)
 
     @pl.when(bad)
     def _():
@@ -256,19 +257,19 @@
         by_maxima(1)
 
 
-def scores_call(core, a_blocks, b_blocks, scale):
+def scores_call(a_blocks, b_blocks, scale):
     rows, features = a_blocks[0].shape
     half = 4 * rows
     stat = jax.ShapeDtypeStruct((8, rows), jnp.float32)
     return pl.pallas_call(
         functools.partial(scores_kernel, scale),
-        in_specs=[smem_spec()] + [vmem_spec()] * 15,
+        in_specs=[vmem_spec()] * 15,
         out_specs=[vmem_spec()] * 3 + [smem_spec()],
         out_shape=[
             pltpu.VMEM((2, half, half), jnp.float32),
             stat,
             stat,
-            jax.ShapeDtypeStruct((1,), jnp.int32),
+            jax.ShapeDtypeStruct((2,), jnp.int32),
         ],
         scratch_shapes=[
             pltpu.VMEM((half, features), jnp.bfloat16),
@@ -279,7 +280,7 @@
         compiler_params=params(),
         cost_estimate=cost(2, half, half, features),
         name="scores",
-    )(core, *a_blocks, *b_blocks)
+    )(*a_blocks, *b_blocks)
 
 
 def merge_kernel(m, mine_ref, got_ref, out_ref):
@@ -301,17 +302,17 @@
     )(mine, got)
 
 
-def weights_kernel(core_ref, flags, e_ref, a_lse, b_lse, *refs):
+def weights_kernel(flags, e_ref, a_lse, b_lse, *refs):
     a_refs, (w_ref, gb_hi, a_half) = refs[:8], refs[8:]
     rows = a_lse.shape[1]
     half = 4 * rows
-    core = core_ref[0]
+    core = lax.axis_index("core")
     take_half(core, a_halves(a_refs), 1, a_half)
     for q in range(2):
         a_row = jnp.concatenate([a_lse[4 * q + j : 4 * q + j + 1, :] for j in range(4)], axis=1)
         b_row = jnp.concatenate([b_lse[pl.ds((q ^ core) * 4 + j, 1), :] for j in range(4)], axis=1)
 
-        @pl.when(flags[0] == 0)
+        @pl.when(flags[q] == 0)
         def _():
             a_col = column_of(jnp.exp2(-a_row), half)
             b_exp = jnp.exp2(-b_row)
@@ -319,7 +320,7 @@
                 sl = slice(r * rows, (r + 1) * rows)
                 w_ref[q, sl, :] = (e_ref[q, sl, :] * (a_col[sl, :] + b_exp)).astype(jnp.bfloat16)
 
-        @pl.when(flags[0] != 0)
+        @pl.when(flags[q] != 0)
         def _():
             a_col = column_of(a_row, half)
             for r in range(4):
@@ -330,12 +331,12 @@
     gb_hi[...] = (0.5 * dot_tn(w_ref[1 - core], a_half[...])).astype(jnp.bfloat16)
 
 
-def weights_call(core, flags, e, a_lse, b_lse, a_blocks):
+def weights_call(flags, e, a_lse, b_lse, a_blocks):
     rows, features = a_blocks[0].shape
     half = 4 * rows
     return pl.pallas_call(
         weights_kernel,
-        in_specs=[smem_spec()] * 2 + [vmem_spec()] * 11,
+        in_specs=[smem_spec()] + [vmem_spec()] * 11,
         out_specs=[vmem_spec()] * 2,
         out_shape=[
             pltpu.VMEM((2, half, half), jnp.bfloat16),
@@ -345,14 +346,14 @@
         compiler_params=params(),
         cost_estimate=cost(1, half, half, features, 12),
         name="weights",
-    )(core, flags, e, a_lse, b_lse, *a_blocks)
-
-
-def middle_kernel(core_ref, w_ref, *refs):
+    )(flags, e, a_lse, b_lse, *a_blocks)
+
+
+def middle_kernel(w_ref, *refs):
     a_refs, b_refs = refs[:8], b_halves(refs[8:15])
     ga_hi, gb_lo, a_half, b_half = refs[15:]
     rows = a_refs[0].shape[0]
-    core = core_ref[0]
+    core = lax.axis_index("core")
     take_half(core, a_halves(a_refs), 0, a_half)
     take_half(core, b_refs, 1, b_half)
     g = 0.5 * dot_tn(w_ref[core], a_half[...])
@@ -363,12 +364,12 @@
     ga_hi[...] = 0.5 * jnp.dot(w_ref[1], b_half[...], preferred_element_type=jnp.float32)
 
 
-def middle_call(core, w, a_blocks, b_blocks):
+def middle_call(w, a_blocks, b_blocks):
     rows, features = a_blocks[0].shape
     half = 4 * rows
     return pl.pallas_call(
         middle_kernel,
-        in_specs=[smem_spec()] + [vmem_spec()] * 16,
+        in_specs=[vmem_spec()] * 16,
         out_specs=[vmem_spec()] * 2,
         out_shape=[
             pltpu.VMEM((half, features), jnp.float32),
@@ -378,7 +379,7 @@
         compiler_params=params(),
         cost_estimate=cost(2, half, half, features),
         name="middle",
-    )(core, w, *a_blocks, *b_blocks)
+    )(w, *a_blocks, *b_blocks)
 
 
 def far_kernel(ga_hi, got, *outs):
@@ -402,25 +403,25 @@
     )(ga_hi, got)
 
 
-def last_kernel(core_ref, w_ref, *refs):
+def last_kernel(w_ref, *refs):
     b_refs, (ga_lo, b_half) = b_halves(refs[:7]), refs[7:]
-    take_half(core_ref[0], b_refs, 0, b_half)
+    take_half(lax.axis_index("core"), b_refs, 0, b_half)
     ga_lo[...] = 0.5 * jnp.dot(w_ref[0], b_half[...], preferred_element_type=jnp.float32)
 
 
-def last_call(core, w, b_blocks):
+def last_call(w, b_blocks):
     rows, features = b_blocks[0].shape
     half = 4 * rows
     return pl.pallas_call(
         last_kernel,
-        in_specs=[smem_spec()] + [vmem_spec()] * 8,
+        in_specs=[vmem_spec()] * 8,
         out_specs=vmem_spec(),
         out_shape=pltpu.VMEM((half, features), jnp.float32),
         scratch_shapes=[pltpu.VMEM((half, features), jnp.bfloat16)],
         compiler_params=params(),
         cost_estimate=cost(1, half, half, features),
         name="last",
-    )(core, w, *b_blocks)
+    )(w, *b_blocks)
 
 
 def near_kernel(ga_lo, got_lo, r_xy, r_yz, r_xz, p0, p1, p2, p4):
@@ -452,10 +453,9 @@
     scale = 4.0 / math.sqrt(features) * LOG2E
     core = lax.axis_index("core")
     first = core == 0
-    core_arr = core.astype(jnp.int32).reshape(1)
     in_hbm = lambda a: pltpu.with_memory_space_constraint(a, pltpu.HBM)
     got = swap(images), swap(texts)
-    own, other = own_call(core_arr, *load_call(core_arr, in_hbm(images), in_hbm(texts)), *got)
+    own, other = own_call(*load_call(in_hbm(images), in_hbm(texts)), *got)
     near = {m: to_cube(own, m) for m in (4, 2, 1)}
     late = lax.optimization_barrier((own, near[1]))[0]
     far = {7: to_cube(late, 7), 5: to_cube(near[1], 4), 3: to_cube(near[2], 1), 6: to_cube(near[4], 2)}
@@ -470,22 +470,22 @@
     b_blocks = [other] + held[3:] + [swapped[m] for m in ORDER[4:]]
     b_blocks = [in_vmem(b) for b in b_blocks]
 
-    e, a_stat, b_stat, flags = scores_call(core_arr, a_blocks, b_blocks, scale)
+    e, a_stat, b_stat, flags = scores_call(a_blocks, b_blocks, scale)
     a_lse = merge_call(a_stat, swap(b_stat), 0)
     for m in (1, 2, 4):
         a_lse = merge_call(a_lse, to_cube(a_lse, m), m)
     b_lse = swap(a_lse)
 
-    w, gb_hi = weights_call(core_arr, flags, e, a_lse, b_lse, a_blocks)
+    w, gb_hi = weights_call(flags, e, a_lse, b_lse, a_blocks)
     got_hi = swap(gb_hi)
-    ga_hi, gb_lo = middle_call(core_arr, w, a_blocks, b_blocks)
+    ga_hi, gb_lo = middle_call(w, a_blocks, b_blocks)
     got_lo = swap(gb_lo)
     p = dict(zip(ORDER[4:], far_call(ga_hi, got_hi)))
     from_xy = to_cube(p[3], 1)
     from_yz = to_cube(p[6], 2)
     from_xz = to_cube(p[5], 4)
     from_xyz = to_cube(p[7], 7)
-    ga_lo = last_call(core_arr, w, b_blocks)
+    ga_lo = last_call(w, b_blocks)
     p0, p1, p2, p4 = near_call(ga_lo, got_lo, from_xy, from_yz, from_xz)
     wide = lambda a: a.astype(jnp.float32)
     total = p0 + wide(from_xyz) + wide(to_cube(p1, 1)) + wide(to_cube(p2, 2)) + wide(to_cube(p4, 4))

time: 113 us -> 114 us (level)
  no operation moved by 1% of the time
where the time goes in v12:
time: 114 us; the launch traced here: 113 us
  starting transfers between devices  37.6 us (33%)
  Pallas kernels  36.8 us (32%)
  waiting for transfers between devices  36.4 us (32%)
  other arithmetic  1.34 us (1%)
    ppermute x17, starting transfers between devices, to_cube(): return lax.ppermute(a, AXES, across(m))  31.8 us
    ppermute x17, waiting for transfers between devices, to_cube(): return lax.ppermute(a, AXES, across(m))  27.9 us
    pallas_call x1, Pallas kernels, scores_call(): pl.pallas_call(functools.partial(scores_kernel, scale), in_specs=[vmem_sp...  18.4 us
    ppermute x13, waiting for transfers between devices, swap(): return lax.ppermute(a, AXES, SWAP)  8.5 us
    pallas_call x1, Pallas kernels, weights_call(): pl.pallas_call(weights_kernel, in_specs=[smem_spec()] + [vmem_spec()] * 1...  7.64 us
    ppermute x13, starting transfers between devices, swap(): return lax.ppermute(a, AXES, SWAP)  5.79 us
    pallas_call x1, Pallas kernels, middle_call(): pl.pallas_call(middle_kernel, in_specs=[vmem_spec()] * 16, out_specs=[vme...  5.61 us
    pallas_call x1, Pallas kernels, last_call(): pl.pallas_call(last_kernel, in_specs=[vmem_spec()] * 8, out_specs=vmem_sp...  2.87 us
  transfers between devices with their start and end apart: 30, of which 21 were waited for; matrix products, arithmetic and copies ran while one was open for 0% of the time, Pallas kernels for 9%

profile of v12, /device:TPU:1, one launch (start us, length us, event | category | flops | bytes accessed | tf_op | source)
XLA Modules:
  0.0 112.9 jit_solution(16144429742902335809)
XLA Ops:
  0.6 1.5 %collective-permute-start = (bf16[160,768]{1,0:T(8,128)(2,1)}, bf16[160,768]{1,0:T(8,128)(2,1)S(1)}, u32[]{:S(2)}, u32[]{:S(2)}) collective-permute-start(bf16[160,768]{1,0:T(8,128)(2,1)} %images.1), channel_id=1, source_target_pairs={{0,16},{1,17},{2,18},{3,19},{4,20},{5,21},{6,22},{7,23},{8,24},{9,... | collective-permute-start | bytes 737288 | tf_op jit(solution)/shard_map/ppermute | solution.py:57
  2.1 0.1 collective-permute-start.1
  2.2 1.1 load.1
  3.3 0.2 collective-permute-done.got_images
  3.5 0.4 collective-permute-done.1.got_texts
  3.9 0.1 own.1
  3.9 2.6 %collective-permute-start.2 = (bf16[320,768]{1,0:T(8,128)(2,1)S(1)}, bf16[320,768]{1,0:T(8,128)(2,1)S(1)}, u32[]{:S(2)}, u32[]{:S(2)}) collective-permute-start(bf16[320,768]{1,0:T(8,128)(2,1)S(1)} %get-tuple-element.34.refs_0_), channel_id=1, source_target_pairs={{0,4},{1,5},{2,6},{3,7},{4,0},{5,1},{6,2},{7,3},{8,12},{9,13},{10,... | collective-permute-start | bytes 1474568 | tf_op jit(solution)/shard_map/ppermute | solution.py:53
  6.6 1.3 %collective-permute-start.3 = (bf16[320,768]{1,0:T(8,128)(2,1)S(1)}, bf16[320,768]{1,0:T(8,128)(2,1)S(1)}, u32[]{:S(2)}, u32[]{:S(2)}) collective-permute-start(bf16[320,768]{1,0:T(8,128)(2,1)S(1)} %get-tuple-element.34.refs_0_), channel_id=1, source_target_pairs={{0,96},{1,97},{2,98},{3,99},{4,100},{5,101},{6,102},{7,103},{8,104... | collective-permute-start | bytes 1474568 | tf_op jit(solution)/shard_map/ppermute | solution.py:53
  7.9 3.8 %collective-permute-start.4 = (bf16[320,768]{1,0:T(8,128)(2,1)S(1)}, bf16[320,768]{1,0:T(8,128)(2,1)S(1)}, u32[]{:S(2)}, u32[]{:S(2)}) collective-permute-start(bf16[320,768]{1,0:T(8,128)(2,1)S(1)} %get-tuple-element.34.refs_0_), channel_id=1, source_target_pairs={{0,1},{1,0},{2,3},{3,2},{4,5},{5,4},{6,7},{7,6},{8,9},{9,8},{10,11... | collective-permute-start | bytes 1474568 | tf_op jit(solution)/shard_map/ppermute | solution.py:53
  11.6 1.6 %collective-permute-done.2.b0.refs_1_ = bf16[320,768]{1,0:T(8,128)(2,1)S(1)} collective-permute-done((bf16[320,768]{1,0:T(8,128)(2,1)S(1)}, bf16[320,768]{1,0:T(8,128)(2,1)S(1)}, u32[]{:S(2)}, u32[]{:S(2)}) %collective-permute-start.2) | collective-permute-done | bytes 491552 | tf_op jit(solution)/shard_map/ppermute | solution.py:53
  13.2 6.8 %collective-permute-start.8 = (bf16[320,768]{1,0:T(8,128)(2,1)S(1)}, bf16[320,768]{1,0:T(8,128)(2,1)S(1)}, u32[]{:S(2)}, u32[]{:S(2)}) collective-permute-start(bf16[320,768]{1,0:T(8,128)(2,1)S(1)} %get-tuple-element.34.refs_0_), channel_id=1, source_target_pairs={{0,101},{1,100},{2,103},{3,102},{4,97},{5,96},{6,99},{7,98},{8,109... | collective-permute-start | bytes 1474568 | tf_op jit(solution)/shard_map/ppermute | solution.py:53
  19.9 0.0 collective-permute-done.3.b1.refs_2_
  19.9 0.2 collective-permute-start.5
  20.1 0.0 collective-permute-done.4.b2.refs_3_
  20.2 0.5 collective-permute-start.7
  20.6 0.1 join.1
  20.7 0.1 collective-permute-start.12
  20.8 5.5 %collective-permute-done.8.refs_7_ = bf16[320,768]{1,0:T(8,128)(2,1)S(1)} collective-permute-done((bf16[320,768]{1,0:T(8,128)(2,1)S(1)}, bf16[320,768]{1,0:T(8,128)(2,1)S(1)}, u32[]{:S(2)}, u32[]{:S(2)}) %collective-permute-start.8) | collective-permute-done | bytes 491552 | tf_op jit(solution)/shard_map/ppermute | solution.py:53
  26.3 5.1 %collective-permute-done.6.refs_5_ = bf16[320,768]{1,0:T(8,128)(2,1)S(1)} collective-permute-done((bf16[320,768]{1,0:T(8,128)(2,1)S(1)}, bf16[320,768]{1,0:T(8,128)(2,1)S(1)}, u32[]{:S(2)}, u32[]{:S(2)}) %collective-permute-start.6) | collective-permute-done | bytes 491552 | tf_op jit(solution)/shard_map/ppermute | solution.py:53
  31.4 0.0 collective-permute-start.9
  31.4 0.2 collective-permute-done.5.refs_4_
  31.7 0.3 collective-permute-start.10
  31.9 0.0 collective-permute-done.7.refs_6_
  31.9 0.2 collective-permute-start.11
  32.2 1.1 collective-permute-done.9.refs_14_.refs_6_
  33.3 0.7 collective-permute-done.10.refs_12_.refs_4_
  34.0 0.7 collective-permute-done.11.refs_11_.refs_3_
  34.7 0.1 collective-permute-start.14
  34.8 1.7 %collective-permute-done.14.refs_13_.refs_5_ = bf16[320,768]{1,0:T(8,128)(2,1)S(1)} collective-permute-done((bf16[320,768]{1,0:T(8,128)(2,1)S(1)}, bf16[320,768]{1,0:T(8,128)(2,1)S(1)}, u32[]{:S(2)}, u32[]{:S(2)}) %collective-permute-start.14) | collective-permute-done | bytes 491552 | tf_op jit(solution)/shard_map/ppermute | solution.py:57
  36.6 18.4 %scores.1 = (f32[2,1280,1280]{2,1,0:T(8,128)S(1)}, f32[8,320]{1,0:T(8,128)S(1)}, f32[8,320]{1,0:T(8,128)S(1)}, s32[2]{0:T(128)S(1)}) custom-call(bf16[320,768]{1,0:T(8,128)(2,1)S(1)} %get-tuple-element.34.refs_0_, bf16[320,768]{1,0:T(8,128)(2,1)S(1)} %collective-permute-done.2.b0.refs_1_, bf16[320,768]{1,0:T(8,128)(2,1)S(1)} %collective-permute-done.3.b1.refs_2_, ...), custom_call_target="tpu_custom_call" | custom-call | flops 5033164800 | tf_op jit(solution)/shard_map/scores/pallas_call | solution.py:264
  55.0 0.2 collective-permute-start.15
  55.2 1.0 collective-permute-done.15.got_ref
  56.3 2.1 %collective-permute-start.16 = (f32[8,320]{1,0:T(8,128)S(1)}, f32[8,320]{1,0:T(8,128)S(1)}, u32[]{:S(2)}, u32[]{:S(2)}) collective-permute-start(f32[8,320]{1,0:T(8,128)S(1)} %merge.4.mine_ref), channel_id=1, source_target_pairs={{0,4},{1,5},{2,6},{3,7},{4,0},{5,1},{6,2},{7,3},{8,12},{9,13},{10,... | collective-permute-start | bytes 30728 | tf_op jit(solution)/shard_map/ppermute | solution.py:53
  58.4 1.7 %collective-permute-done.16.got_ref = f32[8,320]{1,0:T(8,128)S(1)} collective-permute-done((f32[8,320]{1,0:T(8,128)S(1)}, f32[8,320]{1,0:T(8,128)S(1)}, u32[]{:S(2)}, u32[]{:S(2)}) %collective-permute-start.16) | collective-permute-done | bytes 10272 | tf_op jit(solution)/shard_map/ppermute | solution.py:53
  60.2 0.6 collective-permute-start.17
  60.7 2.1 %collective-permute-done.17.got_ref = f32[8,320]{1,0:T(8,128)S(1)} collective-permute-done((f32[8,320]{1,0:T(8,128)S(1)}, f32[8,320]{1,0:T(8,128)S(1)}, u32[]{:S(2)}, u32[]{:S(2)}) %collective-permute-start.17) | collective-permute-done | bytes 10272 | tf_op jit(solution)/shard_map/ppermute | solution.py:53
  62.8 2.8 %collective-permute-start.18 = (f32[8,320]{1,0:T(8,128)S(1)}, f32[8,320]{1,0:T(8,128)S(1)}, u32[]{:S(2)}, u32[]{:S(2)}) collective-permute-start(f32[8,320]{1,0:T(8,128)S(1)} %merge.6.mine_ref), channel_id=1, source_target_pairs={{0,1},{1,0},{2,3},{3,2},{4,5},{5,4},{6,7},{7,6},{8,9},{9,8},{10,11... | collective-permute-start | bytes 30728 | tf_op jit(solution)/shard_map/ppermute | solution.py:53
  65.6 1.1 collective-permute-done.18.got_ref
  66.7 2.5 %collective-permute-start.19 = (f32[8,320]{1,0:T(8,128)S(1)}, f32[8,320]{1,0:T(8,128)S(1)}, u32[]{:S(2)}, u32[]{:S(2)}) collective-permute-start(f32[8,320]{1,0:T(8,128)S(1)} %merge.7.a_lse), channel_id=1, source_target_pairs={{0,16},{1,17},{2,18},{3,19},{4,20},{5,21},{6,22},{7,23},{8,24},{9,... | collective-permute-start | bytes 30728 | tf_op jit(solution)/shard_map/ppermute | solution.py:57
  69.2 0.8 collective-permute-done.19.b_lse
  70.0 7.6 %weights.1 = (bf16[2,1280,1280]{2,1,0:T(8,128)(2,1)S(1)}, bf16[1280,768]{1,0:T(8,128)(2,1)S(1)}) custom-call(s32[2]{0:T(128)S(1)} %get-tuple-element.44.flags, f32[2,1280,1280]{2,1,0:T(8,128)S(1)} %get-tuple-element.45.e_ref, f32[8,320]{1,0:T(8,128)S(1)} %merge.7.a_lse, f32[8,320]{1,0:T(8,128)S(1)} %collective-permute-done.19.b_lse, ...), custom_call_target="tpu_custom_call" | custom-call | flops 2516582400 | bytes 19660800 | tf_op jit(solution)/shard_map/weights/pallas_call | solution.py:337
  77.6 0.4 collective-permute-start.21
  78.1 5.6 %middle.1 = (f32[1280,768]{1,0:T(8,128)S(1)}, bf16[1600,768]{1,0:T(8,128)(2,1)S(1)}) custom-call(bf16[2,1280,1280]{2,1,0:T(8,128)(2,1)S(1)} %get-tuple-element.48.w_ref, bf16[320,768]{1,0:T(8,128)(2,1)S(1)} %get-tuple-element.34.refs_0_, bf16[320,768]{1,0:T(8,128)(2,1)S(1)} %collective-permute-done.2.b0.refs_1_, ...), custom_call_target="tpu_custom_call" | custom-call | flops 5033164800 | tf_op jit(solution)/shard_map/middle/pallas_call | solution.py:370
  83.7 0.2 collective-permute-start.20
  83.9 0.3 far.1
  84.3 2.1 %collective-permute-start.22 = (bf16[320,768]{1,0:T(8,128)(2,1)S(1)}, bf16[320,768]{1,0:T(8,128)(2,1)S(1)}, u32[]{:S(2)}, u32[]{:S(2)}) collective-permute-start(bf16[320,768]{1,0:T(8,128)(2,1)S(1)} %get-tuple-element.52), channel_id=1, source_target_pairs={{0,4},{1,5},{2,6},{3,7},{4,0},{5,1},{6,2},{7,3},{8,12},{9,13},{10,... | collective-permute-start | bytes 1474568 | tf_op jit(solution)/shard_map/ppermute | solution.py:53
  86.4 3.0 %collective-permute-start.24 = (bf16[320,768]{1,0:T(8,128)(2,1)S(1)}, bf16[320,768]{1,0:T(8,128)(2,1)S(1)}, u32[]{:S(2)}, u32[]{:S(2)}) collective-permute-start(bf16[320,768]{1,0:T(8,128)(2,1)S(1)} %get-tuple-element.54), channel_id=1, source_target_pairs={{0,1},{1,0},{2,3},{3,2},{4,5},{5,4},{6,7},{7,6},{8,9},{9,8},{10,11... | collective-permute-start | bytes 1474568 | tf_op jit(solution)/shard_map/ppermute | solution.py:53
  89.4 2.9 %last.1.ga_lo = f32[1280,768]{1,0:T(8,128)S(1)} custom-call(bf16[2,1280,1280]{2,1,0:T(8,128)(2,1)S(1)} %get-tuple-element.48.w_ref, bf16[320,768]{1,0:T(8,128)(2,1)S(1)} %get-tuple-element.35.refs_8_.refs_0_, bf16[480,768]{1,0:T(8,128)(2,1)S(1)} %collective-permute-done.12.refs_9_.refs_1_, bf16[480,768]{1,0:T(8,128)(2,1)S(1)} %collective-permute-done.13.refs_10_.refs_2_, ...), custom_call_target="tpu_custom_call" | custom-call | flops 2516582400 | tf_op jit(solution)/shard_map/last/pallas_call | solution.py:415
  92.3 1.3 %collective-permute-start.25 = (bf16[320,768]{1,0:T(8,128)(2,1)S(1)}, bf16[320,768]{1,0:T(8,128)(2,1)S(1)}, u32[]{:S(2)}, u32[]{:S(2)}) collective-permute-start(bf16[320,768]{1,0:T(8,128)(2,1)S(1)} %get-tuple-element.56), channel_id=1, source_target_pairs={{0,101},{1,100},{2,103},{3,102},{4,97},{5,96},{6,99},{7,98},{8,109... | collective-permute-start | bytes 1474568 | tf_op jit(solution)/shard_map/ppermute | solution.py:53
  93.6 0.8 collective-permute-done.23.r_yz
  94.3 1.3 %collective-permute-done.24.r_xz = bf16[320,768]{1,0:T(8,128)(2,1)S(1)} collective-permute-done((bf16[320,768]{1,0:T(8,128)(2,1)S(1)}, bf16[320,768]{1,0:T(8,128)(2,1)S(1)}, u32[]{:S(2)}, u32[]{:S(2)}) %collective-permute-start.24) | collective-permute-done | bytes 491552 | tf_op jit(solution)/shard_map/ppermute | solution.py:53
  95.6 0.6 near.1
  96.2 0.0 copy-start
  96.2 0.0 copy-start.1
  96.2 0.7 collective-permute-start.26
  96.9 1.5 %collective-permute-start.27 = (bf16[320,768]{1,0:T(8,128)(2,1)S(1)}, bf16[320,768]{1,0:T(8,128)(2,1)S(1)}, u32[]{:S(2)}, u32[]{:S(2)}) collective-permute-start(bf16[320,768]{1,0:T(8,128)(2,1)S(1)} %get-tuple-element.58), channel_id=1, source_target_pairs={{0,96},{1,97},{2,98},{3,99},{4,100},{5,101},{6,102},{7,103},{8,104... | collective-permute-start | bytes 1474568 | tf_op jit(solution)/shard_map/ppermute | solution.py:53
  98.3 2.7 %collective-permute-start.28 = (bf16[320,768]{1,0:T(8,128)(2,1)S(1)}, bf16[320,768]{1,0:T(8,128)(2,1)S(1)}, u32[]{:S(2)}, u32[]{:S(2)}) collective-permute-start(bf16[320,768]{1,0:T(8,128)(2,1)S(1)} %get-tuple-element.59), channel_id=1, source_target_pairs={{0,1},{1,0},{2,3},{3,2},{4,5},{5,4},{6,7},{7,6},{8,9},{9,8},{10,11... | collective-permute-start | bytes 1474568 | tf_op jit(solution)/shard_map/ppermute | solution.py:53
  101.0 3.4 %collective-permute-done.25 = bf16[320,768]{1,0:T(8,128)(2,1)S(1)} collective-permute-done((bf16[320,768]{1,0:T(8,128)(2,1)S(1)}, bf16[320,768]{1,0:T(8,128)(2,1)S(1)}, u32[]{:S(2)}, u32[]{:S(2)}) %collective-permute-start.25) | collective-permute-done | bytes 491552 | tf_op jit(solution)/shard_map/ppermute | solution.py:53
  104.4 3.3 %collective-permute-done.26 = bf16[320,768]{1,0:T(8,128)(2,1)S(1)} collective-permute-done((bf16[320,768]{1,0:T(8,128)(2,1)S(1)}, bf16[320,768]{1,0:T(8,128)(2,1)S(1)}, u32[]{:S(2)}, u32[]{:S(2)}) %collective-permute-start.26) | collective-permute-done | bytes 491552 | tf_op jit(solution)/shard_map/ppermute | solution.py:53
  107.7 1.8 %collective-permute-done.28 = bf16[320,768]{1,0:T(8,128)(2,1)S(1)} collective-permute-done((bf16[320,768]{1,0:T(8,128)(2,1)S(1)}, bf16[320,768]{1,0:T(8,128)(2,1)S(1)}, u32[]{:S(2)}, u32[]{:S(2)}) %collective-permute-start.28) | collective-permute-done | bytes 491552 | tf_op jit(solution)/shard_map/ppermute | solution.py:53
  109.5 0.3 convert_add_fusion
  109.9 0.1 collective-permute-start.29
  110.0 1.8 %collective-permute-done.29 = f32[160,768]{1,0:T(8,128)S(1)} collective-permute-done((f32[160,768]{1,0:T(8,128)S(1)}, f32[160,768]{1,0:T(8,128)S(1)}, u32[]{:S(2)}, u32[]{:S(2)}) %collective-permute-start.29) | collective-permute-done | bytes 491552 | tf_op jit(solution)/shard_map/ppermute | solution.py:57
  111.8 1.0 convert_subtract_fusion
  (16 shorter events, 0.2 us)
Async XLA Ops:
  0.6 2.9 %collective-permute-start = (bf16[160,768]{1,0:T(8,128)(2,1)}, bf16[160,768]{1,0:T(8,128)(2,1)S(1)}, u32[]{:S(2)}, u32[]{:S(2)}) collective-permute-start(bf16[160,768]{1,0:T(8,128)(2,1)} %images.1), channel_id=1, source_target_pairs={{0,16},{1,17},{2,18},{3,19},{4,20},{5,21},{6,22},{7,23},{8,24},{9,... | collective-permute-start | bytes 737288 | tf_op jit(solution)/shard_map/ppermute | solution.py:57
  2.1 1.7 %collective-permute-start.1 = (bf16[160,768]{1,0:T(8,128)(2,1)}, bf16[160,768]{1,0:T(8,128)(2,1)S(1)}, u32[]{:S(2)}, u32[]{:S(2)}) collective-permute-start(bf16[160,768]{1,0:T(8,128)(2,1)} %texts.1), channel_id=1, source_target_pairs={{0,16},{1,17},{2,18},{3,19},{4,20},{5,21},{6,22},{7,23},{8,24},{9,... | collective-permute-start | bytes 737288 | tf_op jit(solution)/shard_map/ppermute | solution.py:57
  3.9 9.3 %collective-permute-start.2 = (bf16[320,768]{1,0:T(8,128)(2,1)S(1)}, bf16[320,768]{1,0:T(8,128)(2,1)S(1)}, u32[]{:S(2)}, u32[]{:S(2)}) collective-permute-start(bf16[320,768]{1,0:T(8,128)(2,1)S(1)} %get-tuple-element.34.refs_0_), channel_id=1, source_target_pairs={{0,4},{1,5},{2,6},{3,7},{4,0},{5,1},{6,2},{7,3},{8,12},{9,13},{10,... | collective-permute-start | bytes 1474568 | tf_op jit(solution)/shard_map/ppermute | solution.py:53
  6.6 13.4 %collective-permute-start.3 = (bf16[320,768]{1,0:T(8,128)(2,1)S(1)}, bf16[320,768]{1,0:T(8,128)(2,1)S(1)}, u32[]{:S(2)}, u32[]{:S(2)}) collective-permute-start(bf16[320,768]{1,0:T(8,128)(2,1)S(1)} %get-tuple-element.34.refs_0_), channel_id=1, source_target_pairs={{0,96},{1,97},{2,98},{3,99},{4,100},{5,101},{6,102},{7,103},{8,104... | collective-permute-start | bytes 1474568 | tf_op jit(solution)/shard_map/ppermute | solution.py:53
  7.9 12.3 %collective-permute-start.4 = (bf16[320,768]{1,0:T(8,128)(2,1)S(1)}, bf16[320,768]{1,0:T(8,128)(2,1)S(1)}, u32[]{:S(2)}, u32[]{:S(2)}) collective-permute-start(bf16[320,768]{1,0:T(8,128)(2,1)S(1)} %get-tuple-element.34.refs_0_), channel_id=1, source_target_pairs={{0,1},{1,0},{2,3},{3,2},{4,5},{5,4},{6,7},{7,6},{8,9},{9,8},{10,11... | collective-permute-start | bytes 1474568 | tf_op jit(solution)/shard_map/ppermute | solution.py:53
  13.2 13.1 %collective-permute-start.8 = (bf16[320,768]{1,0:T(8,128)(2,1)S(1)}, bf16[320,768]{1,0:T(8,128)(2,1)S(1)}, u32[]{:S(2)}, u32[]{:S(2)}) collective-permute-start(bf16[320,768]{1,0:T(8,128)(2,1)S(1)} %get-tuple-element.34.refs_0_), channel_id=1, source_target_pairs={{0,101},{1,100},{2,103},{3,102},{4,97},{5,96},{6,99},{7,98},{8,109... | collective-permute-start | bytes 1474568 | tf_op jit(solution)/shard_map/ppermute | solution.py:53
  19.9 11.5 %collective-permute-start.6 = (bf16[320,768]{1,0:T(8,128)(2,1)S(1)}, bf16[320,768]{1,0:T(8,128)(2,1)S(1)}, u32[]{:S(2)}, u32[]{:S(2)}) collective-permute-start(bf16[320,768]{1,0:T(8,128)(2,1)S(1)} %collective-permute-done.2.b0.refs_1_), channel_id=1, source_target_pairs={{0,1},{1,0},{2,3},{3,2},{4,5},{5,4},{6,7},{7,6},{8,9},{9,8},{10,11... | collective-permute-start | bytes 1474568 | tf_op jit(solution)/shard_map/ppermute | solution.py:53
  19.9 11.7 %collective-permute-start.5 = (bf16[320,768]{1,0:T(8,128)(2,1)S(1)}, bf16[320,768]{1,0:T(8,128)(2,1)S(1)}, u32[]{:S(2)}, u32[]{:S(2)}) collective-permute-start(bf16[320,768]{1,0:T(8,128)(2,1)S(1)} %collective-permute-done.3.b1.refs_2_), channel_id=1, source_target_pairs={{0,4},{1,5},{2,6},{3,7},{4,0},{5,1},{6,2},{7,3},{8,12},{9,13},{10,... | collective-permute-start | bytes 1474568 | tf_op jit(solution)/shard_map/ppermute | solution.py:53
  20.2 11.8 %collective-permute-start.7 = (bf16[320,768]{1,0:T(8,128)(2,1)S(1)}, bf16[320,768]{1,0:T(8,128)(2,1)S(1)}, u32[]{:S(2)}, u32[]{:S(2)}) collective-permute-start(bf16[320,768]{1,0:T(8,128)(2,1)S(1)} %collective-permute-done.4.b2.refs_3_), channel_id=1, source_target_pairs={{0,96},{1,97},{2,98},{3,99},{4,100},{5,101},{6,102},{7,103},{8,104... | collective-permute-start | bytes 1474568 | tf_op jit(solution)/shard_map/ppermute | solution.py:53
  20.7 11.5 %collective-permute-start.12 = (bf16[480,768]{1,0:T(8,128)(2,1)S(1)}, bf16[480,768]{1,0:T(8,128)(2,1)S(1)}, u32[]{:S(2)}, u32[]{:S(2)}) collective-permute-start(bf16[480,768]{1,0:T(8,128)(2,1)S(1)} %get-tuple-element.36), channel_id=1, source_target_pairs={{0,16},{1,17},{2,18},{3,19},{4,20},{5,21},{6,22},{7,23},{8,24},{9,... | collective-permute-start | bytes 2211848 | tf_op jit(solution)/shard_map/ppermute | solution.py:57
  26.3 5.9 %collective-permute-start.13 = (bf16[480,768]{1,0:T(8,128)(2,1)S(1)}, bf16[480,768]{1,0:T(8,128)(2,1)S(1)}, u32[]{:S(2)}, u32[]{:S(2)}) collective-permute-start(bf16[480,768]{1,0:T(8,128)(2,1)S(1)} %get-tuple-element.37), channel_id=1, source_target_pairs={{0,16},{1,17},{2,18},{3,19},{4,20},{5,21},{6,22},{7,23},{8,24},{9,... | collective-permute-start | bytes 2211848 | tf_op jit(solution)/shard_map/ppermute | solution.py:57
  31.4 1.9 %collective-permute-start.9 = (bf16[320,768]{1,0:T(8,128)(2,1)S(1)}, bf16[320,768]{1,0:T(8,128)(2,1)S(1)}, u32[]{:S(2)}, u32[]{:S(2)}) collective-permute-start(bf16[320,768]{1,0:T(8,128)(2,1)S(1)} %collective-permute-done.8.refs_7_), channel_id=1, source_target_pairs={{0,16},{1,17},{2,18},{3,19},{4,20},{5,21},{6,22},{7,23},{8,24},{9,... | collective-permute-start | bytes 1474568 | tf_op jit(solution)/shard_map/ppermute | solution.py:57
  31.7 2.3 %collective-permute-start.10 = (bf16[320,768]{1,0:T(8,128)(2,1)S(1)}, bf16[320,768]{1,0:T(8,128)(2,1)S(1)}, u32[]{:S(2)}, u32[]{:S(2)}) collective-permute-start(bf16[320,768]{1,0:T(8,128)(2,1)S(1)} %collective-permute-done.6.refs_5_), channel_id=1, source_target_pairs={{0,16},{1,17},{2,18},{3,19},{4,20},{5,21},{6,22},{7,23},{8,24},{9,... | collective-permute-start | bytes 1474568 | tf_op jit(solution)/shard_map/ppermute | solution.py:57
  31.9 2.8 %collective-permute-start.11 = (bf16[320,768]{1,0:T(8,128)(2,1)S(1)}, bf16[320,768]{1,0:T(8,128)(2,1)S(1)}, u32[]{:S(2)}, u32[]{:S(2)}) collective-permute-start(bf16[320,768]{1,0:T(8,128)(2,1)S(1)} %collective-permute-done.5.refs_4_), channel_id=1, source_target_pairs={{0,16},{1,17},{2,18},{3,19},{4,20},{5,21},{6,22},{7,23},{8,24},{9,... | collective-permute-start | bytes 1474568 | tf_op jit(solution)/shard_map/ppermute | solution.py:57
  34.7 1.9 %collective-permute-start.14 = (bf16[320,768]{1,0:T(8,128)(2,1)S(1)}, bf16[320,768]{1,0:T(8,128)(2,1)S(1)}, u32[]{:S(2)}, u32[]{:S(2)}) collective-permute-start(bf16[320,768]{1,0:T(8,128)(2,1)S(1)} %collective-permute-done.7.refs_6_), channel_id=1, source_target_pairs={{0,16},{1,17},{2,18},{3,19},{4,20},{5,21},{6,22},{7,23},{8,24},{9,... | collective-permute-start | bytes 1474568 | tf_op jit(solution)/shard_map/ppermute | solution.py:57
  55.0 1.3 %collective-permute-start.15 = (f32[8,320]{1,0:T(8,128)S(1)}, f32[8,320]{1,0:T(8,128)S(1)}, u32[]{:S(2)}, u32[]{:S(2)}) collective-permute-start(f32[8,320]{1,0:T(8,128)S(1)} %get-tuple-element.47), channel_id=1, source_target_pairs={{0,16},{1,17},{2,18},{3,19},{4,20},{5,21},{6,22},{7,23},{8,24},{9,... | collective-permute-start | bytes 30728 | tf_op jit(solution)/shard_map/ppermute | solution.py:57
  56.3 3.8 %collective-permute-start.16 = (f32[8,320]{1,0:T(8,128)S(1)}, f32[8,320]{1,0:T(8,128)S(1)}, u32[]{:S(2)}, u32[]{:S(2)}) collective-permute-start(f32[8,320]{1,0:T(8,128)S(1)} %merge.4.mine_ref), channel_id=1, source_target_pairs={{0,4},{1,5},{2,6},{3,7},{4,0},{5,1},{6,2},{7,3},{8,12},{9,13},{10,... | collective-permute-start | bytes 30728 | tf_op jit(solution)/shard_map/ppermute | solution.py:53
  60.2 2.6 %collective-permute-start.17 = (f32[8,320]{1,0:T(8,128)S(1)}, f32[8,320]{1,0:T(8,128)S(1)}, u32[]{:S(2)}, u32[]{:S(2)}) collective-permute-start(f32[8,320]{1,0:T(8,128)S(1)} %merge.5.mine_ref), channel_id=1, source_target_pairs={{0,96},{1,97},{2,98},{3,99},{4,100},{5,101},{6,102},{7,103},{8,104... | collective-permute-start | bytes 30728 | tf_op jit(solution)/shard_map/ppermute | solution.py:53
  62.8 3.8 %collective-permute-start.18 = (f32[8,320]{1,0:T(8,128)S(1)}, f32[8,320]{1,0:T(8,128)S(1)}, u32[]{:S(2)}, u32[]{:S(2)}) collective-permute-start(f32[8,320]{1,0:T(8,128)S(1)} %merge.6.mine_ref), channel_id=1, source_target_pairs={{0,1},{1,0},{2,3},{3,2},{4,5},{5,4},{6,7},{7,6},{8,9},{9,8},{10,11... | collective-permute-start | bytes 30728 | tf_op jit(solution)/shard_map/ppermute | solution.py:53
  66.7 3.3 %collective-permute-start.19 = (f32[8,320]{1,0:T(8,128)S(1)}, f32[8,320]{1,0:T(8,128)S(1)}, u32[]{:S(2)}, u32[]{:S(2)}) collective-permute-start(f32[8,320]{1,0:T(8,128)S(1)} %merge.7.a_lse), channel_id=1, source_target_pairs={{0,16},{1,17},{2,18},{3,19},{4,20},{5,21},{6,22},{7,23},{8,24},{9,... | collective-permute-start | bytes 30728 | tf_op jit(solution)/shard_map/ppermute | solution.py:57
  77.6 6.3 %collective-permute-start.21 = (bf16[1280,768]{1,0:T(8,128)(2,1)S(1)}, bf16[1280,768]{1,0:T(8,128)(2,1)S(1)}, u32[]{:S(2)}, u32[]{:S(2)}) collective-permute-start(bf16[1280,768]{1,0:T(8,128)(2,1)S(1)} %get-tuple-element.51), channel_id=1, source_target_pairs={{0,16},{1,17},{2,18},{3,19},{4,20},{5,21},{6,22},{7,23},{8,24},{9,... | collective-permute-start | bytes 5898248 | tf_op jit(solution)/shard_map/ppermute | solution.py:57
  83.7 11.9 %collective-permute-start.20 = (bf16[1600,768]{1,0:T(8,128)(2,1)S(1)}, bf16[1600,768]{1,0:T(8,128)(2,1)S(1)}, u32[]{:S(2)}, u32[]{:S(2)}) collective-permute-start(bf16[1600,768]{1,0:T(8,128)(2,1)S(1)} %get-tuple-element.49), channel_id=1, source_target_pairs={{0,16},{1,17},{2,18},{3,19},{4,20},{5,21},{6,22},{7,23},{8,24},{9,... | collective-permute-start | bytes 7372808 | tf_op jit(solution)/shard_map/ppermute | solution.py:57
  84.3 9.3 %collective-permute-start.22 = (bf16[320,768]{1,0:T(8,128)(2,1)S(1)}, bf16[320,768]{1,0:T(8,128)(2,1)S(1)}, u32[]{:S(2)}, u32[]{:S(2)}) collective-permute-start(bf16[320,768]{1,0:T(8,128)(2,1)S(1)} %get-tuple-element.52), channel_id=1, source_target_pairs={{0,4},{1,5},{2,6},{3,7},{4,0},{5,1},{6,2},{7,3},{8,12},{9,13},{10,... | collective-permute-start | bytes 1474568 | tf_op jit(solution)/shard_map/ppermute | solution.py:53
  86.4 8.0 %collective-permute-start.23 = (bf16[320,768]{1,0:T(8,128)(2,1)S(1)}, bf16[320,768]{1,0:T(8,128)(2,1)S(1)}, u32[]{:S(2)}, u32[]{:S(2)}) collective-permute-start(bf16[320,768]{1,0:T(8,128)(2,1)S(1)} %get-tuple-element.53), channel_id=1, source_target_pairs={{0,96},{1,97},{2,98},{3,99},{4,100},{5,101},{6,102},{7,103},{8,104... | collective-permute-start | bytes 1474568 | tf_op jit(solution)/shard_map/ppermute | solution.py:53
  86.4 9.2 %collective-permute-start.24 = (bf16[320,768]{1,0:T(8,128)(2,1)S(1)}, bf16[320,768]{1,0:T(8,128)(2,1)S(1)}, u32[]{:S(2)}, u32[]{:S(2)}) collective-permute-start(bf16[320,768]{1,0:T(8,128)(2,1)S(1)} %get-tuple-element.54), channel_id=1, source_target_pairs={{0,1},{1,0},{2,3},{3,2},{4,5},{5,4},{6,7},{7,6},{8,9},{9,8},{10,11... | collective-permute-start | bytes 1474568 | tf_op jit(solution)/shard_map/ppermute | solution.py:53
  92.3 12.1 %collective-permute-start.25 = (bf16[320,768]{1,0:T(8,128)(2,1)S(1)}, bf16[320,768]{1,0:T(8,128)(2,1)S(1)}, u32[]{:S(2)}, u32[]{:S(2)}) collective-permute-start(bf16[320,768]{1,0:T(8,128)(2,1)S(1)} %get-tuple-element.56), channel_id=1, source_target_pairs={{0,101},{1,100},{2,103},{3,102},{4,97},{5,96},{6,99},{7,98},{8,109... | collective-permute-start | bytes 1474568 | tf_op jit(solution)/shard_map/ppermute | solution.py:53
  96.2 15.7 %copy-start = (bf16[160,768]{1,0:T(8,128)(2,1)S(1)}, bf16[160,768]{1,0:T(8,128)(2,1)}, u32[]{:S(2)}) copy-start(bf16[160,768]{1,0:T(8,128)(2,1)} %images.1) | copy-start | bytes 737284
  96.2 15.6 %copy-start.1 = (bf16[160,768]{1,0:T(8,128)(2,1)S(1)}, bf16[160,768]{1,0:T(8,128)(2,1)}, u32[]{:S(2)}) copy-start(bf16[160,768]{1,0:T(8,128)(2,1)} %texts.1) | copy-start | bytes 737284
  96.2 11.5 %collective-permute-start.26 = (bf16[320,768]{1,0:T(8,128)(2,1)S(1)}, bf16[320,768]{1,0:T(8,128)(2,1)S(1)}, u32[]{:S(2)}, u32[]{:S(2)}) collective-permute-start(bf16[320,768]{1,0:T(8,128)(2,1)S(1)} %get-tuple-element.57), channel_id=1, source_target_pairs={{0,4},{1,5},{2,6},{3,7},{4,0},{5,1},{6,2},{7,3},{8,12},{9,13},{10,... | collective-permute-start | bytes 1474568 | tf_op jit(solution)/shard_map/ppermute | solution.py:53
  96.9 10.8 %collective-permute-start.27 = (bf16[320,768]{1,0:T(8,128)(2,1)S(1)}, bf16[320,768]{1,0:T(8,128)(2,1)S(1)}, u32[]{:S(2)}, u32[]{:S(2)}) collective-permute-start(bf16[320,768]{1,0:T(8,128)(2,1)S(1)} %get-tuple-element.58), channel_id=1, source_target_pairs={{0,96},{1,97},{2,98},{3,99},{4,100},{5,101},{6,102},{7,103},{8,104... | collective-permute-start | bytes 1474568 | tf_op jit(solution)/shard_map/ppermute | solution.py:53
  98.3 11.2 %collective-permute-start.28 = (bf16[320,768]{1,0:T(8,128)(2,1)S(1)}, bf16[320,768]{1,0:T(8,128)(2,1)S(1)}, u32[]{:S(2)}, u32[]{:S(2)}) collective-permute-start(bf16[320,768]{1,0:T(8,128)(2,1)S(1)} %get-tuple-element.59), channel_id=1, source_target_pairs={{0,1},{1,0},{2,3},{3,2},{4,5},{5,4},{6,7},{7,6},{8,9},{9,8},{10,11... | collective-permute-start | bytes 1474568 | tf_op jit(solution)/shard_map/ppermute | solution.py:53
  109.9 1.9 %collective-permute-start.29 = (f32[160,768]{1,0:T(8,128)S(1)}, f32[160,768]{1,0:T(8,128)S(1)}, u32[]{:S(2)}, u32[]{:S(2)}) collective-permute-start(f32[160,768]{1,0:T(8,128)S(1)} %slice.9), channel_id=1, source_target_pairs={{0,16},{1,17},{2,18},{3,19},{4,20},{5,21},{6,22},{7,23},{8,24},{9,... | collective-permute-start | bytes 1474568 | tf_op jit(solution)/shard_map/ppermute | solution.py:57

commit v13 on v12

--- a/solution.py
+++ b/solution.py
@@ -37,9 +37,9 @@
     pairs = []
     for y, c, x, z in coords():
         target = (
-            partner(y, c == 0) if m & 2 else y,
+            partner(y, c == 1) if m & 2 else y,
             c,
-            partner(x, c == 1) if m & 1 else x,
+            partner(x, c == 0) if m & 1 else x,
             partner(z, c == 1) if m & 4 else z,
         )
         pairs.append((flat(y, c, x, z), flat(*target)))

time: 114 us -> 115 us (level)
  starting transfers between devices: 37.6 us -> 42.6 us
  waiting for transfers between devices: 36.4 us -> 32.6 us
    ppermute x17, waiting for transfers between devices: 27.9 us -> 24.8 us  [to_cube(): return lax.ppermute(a, AXES, across(m))]
    ppermute x17, starting transfers between devices: 31.8 us -> 34.3 us  [to_cube(): return lax.ppermute(a, AXES, across(m))]
    ppermute x13, starting transfers between devices: 5.79 us -> 8.27 us  [swap(): return lax.ppermute(a, AXES, SWAP)]
  transfers between devices with their start and end apart: 30 -> 30, of which waited for: 21 -> 20; matrix products, arithmetic and copies ran while one was open for 0% -> 0% of each run, Pallas kernels for 9% -> 9%
where the time goes in v13:
time: 115 us; the launch traced here: 114 us
  starting transfers between devices  42.6 us (37%)
  Pallas kernels  36.8 us (32%)
  waiting for transfers between devices  32.6 us (28%)
  other arithmetic  1.34 us (1%)
    ppermute x17, starting transfers between devices, to_cube(): return lax.ppermute(a, AXES, across(m))  34.3 us
    ppermute x17, waiting for transfers between devices, to_cube(): return lax.ppermute(a, AXES, across(m))  24.8 us
    pallas_call x1, Pallas kernels, scores_call(): pl.pallas_call(functools.partial(scores_kernel, scale), in_specs=[vmem_sp...  18.4 us
    ppermute x13, starting transfers between devices, swap(): return lax.ppermute(a, AXES, SWAP)  8.27 us
    ppermute x13, waiting for transfers between devices, swap(): return lax.ppermute(a, AXES, SWAP)  7.86 us
    pallas_call x1, Pallas kernels, weights_call(): pl.pallas_call(weights_kernel, in_specs=[smem_spec()] + [vmem_spec()] * 1...  7.64 us
    pallas_call x1, Pallas kernels, middle_call(): pl.pallas_call(middle_kernel, in_specs=[vmem_spec()] * 16, out_specs=[vme...  5.61 us
    pallas_call x1, Pallas kernels, last_call(): pl.pallas_call(last_kernel, in_specs=[vmem_spec()] * 8, out_specs=vmem_sp...  2.87 us
  transfers between devices with their start and end apart: 30, of which 20 were waited for; matrix products, arithmetic and copies ran while one was open for 0% of the time, Pallas kernels for 9%

profile of v13, /device:TPU:1, one launch (start us, length us, event | category | flops | bytes accessed | tf_op | source)
XLA Modules:
  0.0 114.2 jit_solution(9468318828877217017)
XLA Ops:
  0.6 1.5 %collective-permute-start = (bf16[160,768]{1,0:T(8,128)(2,1)}, bf16[160,768]{1,0:T(8,128)(2,1)S(1)}, u32[]{:S(2)}, u32[]{:S(2)}) collective-permute-start(bf16[160,768]{1,0:T(8,128)(2,1)} %images.1), channel_id=1, source_target_pairs={{0,16},{1,17},{2,18},{3,19},{4,20},{5,21},{6,22},{7,23},{8,24},{9,... | collective-permute-start | bytes 737288 | tf_op jit(solution)/shard_map/ppermute | solution.py:57
  2.1 0.1 collective-permute-start.1
  2.2 1.1 load.1
  3.3 0.2 collective-permute-done.got_images
  3.5 0.4 collective-permute-done.1.got_texts
  3.9 0.1 own.1
  3.9 1.4 %collective-permute-start.2 = (bf16[320,768]{1,0:T(8,128)(2,1)S(1)}, bf16[320,768]{1,0:T(8,128)(2,1)S(1)}, u32[]{:S(2)}, u32[]{:S(2)}) collective-permute-start(bf16[320,768]{1,0:T(8,128)(2,1)S(1)} %get-tuple-element.34.refs_0_), channel_id=1, source_target_pairs={{0,12},{1,13},{2,14},{3,15},{4,8},{5,9},{6,10},{7,11},{8,4},{9,5},... | collective-permute-start | bytes 1474568 | tf_op jit(solution)/shard_map/ppermute | solution.py:53
  5.3 2.7 %collective-permute-start.3 = (bf16[320,768]{1,0:T(8,128)(2,1)S(1)}, bf16[320,768]{1,0:T(8,128)(2,1)S(1)}, u32[]{:S(2)}, u32[]{:S(2)}) collective-permute-start(bf16[320,768]{1,0:T(8,128)(2,1)S(1)} %get-tuple-element.34.refs_0_), channel_id=1, source_target_pairs={{0,32},{1,33},{2,34},{3,35},{4,36},{5,37},{6,38},{7,39},{8,40},{9,... | collective-permute-start | bytes 1474568 | tf_op jit(solution)/shard_map/ppermute | solution.py:53
  8.0 3.8 %collective-permute-start.4 = (bf16[320,768]{1,0:T(8,128)(2,1)S(1)}, bf16[320,768]{1,0:T(8,128)(2,1)S(1)}, u32[]{:S(2)}, u32[]{:S(2)}) collective-permute-start(bf16[320,768]{1,0:T(8,128)(2,1)S(1)} %get-tuple-element.34.refs_0_), channel_id=1, source_target_pairs={{0,1},{1,0},{2,3},{3,2},{4,5},{5,4},{6,7},{7,6},{8,9},{9,8},{10,11... | collective-permute-start | bytes 1474568 | tf_op jit(solution)/shard_map/ppermute | solution.py:53
  11.8 0.2 collective-permute-done.2.b0.refs_1_
  12.0 7.2 %collective-permute-start.8 = (bf16[320,768]{1,0:T(8,128)(2,1)S(1)}, bf16[320,768]{1,0:T(8,128)(2,1)S(1)}, u32[]{:S(2)}, u32[]{:S(2)}) collective-permute-start(bf16[320,768]{1,0:T(8,128)(2,1)S(1)} %get-tuple-element.34.refs_0_), channel_id=1, source_target_pairs={{0,45},{1,44},{2,47},{3,46},{4,41},{5,40},{6,43},{7,42},{8,37},{9,... | collective-permute-start | bytes 1474568 | tf_op jit(solution)/shard_map/ppermute | solution.py:53
  19.2 0.0 collective-permute-start.6
  19.2 0.0 collective-permute-done.3.b1.refs_2_
  19.2 0.3 collective-permute-start.5
  19.5 0.3 collective-permute-start.7
  19.8 0.1 join.1
  19.9 1.0 collective-permute-start.12
  20.9 4.6 %collective-permute-done.8.refs_7_ = bf16[320,768]{1,0:T(8,128)(2,1)S(1)} collective-permute-done((bf16[320,768]{1,0:T(8,128)(2,1)S(1)}, bf16[320,768]{1,0:T(8,128)(2,1)S(1)}, u32[]{:S(2)}, u32[]{:S(2)}) %collective-permute-start.8) | collective-permute-done | bytes 491552 | tf_op jit(solution)/shard_map/ppermute | solution.py:53
  25.5 1.1 collective-permute-start.13
  26.6 4.4 %collective-permute-done.6.refs_5_ = bf16[320,768]{1,0:T(8,128)(2,1)S(1)} collective-permute-done((bf16[320,768]{1,0:T(8,128)(2,1)S(1)}, bf16[320,768]{1,0:T(8,128)(2,1)S(1)}, u32[]{:S(2)}, u32[]{:S(2)}) %collective-permute-start.6) | collective-permute-done | bytes 491552 | tf_op jit(solution)/shard_map/ppermute | solution.py:53
  31.0 0.7 collective-permute-start.9
  31.7 0.6 collective-permute-start.10
  32.2 0.0 collective-permute-start.11
  32.3 0.9 collective-permute-done.9.refs_14_.refs_6_
  33.2 0.7 collective-permute-done.10.refs_12_.refs_4_
  33.9 0.7 collective-permute-done.11.refs_11_.refs_3_
  34.6 0.4 collective-permute-start.14
  35.0 1.5 %collective-permute-done.14.refs_13_.refs_5_ = bf16[320,768]{1,0:T(8,128)(2,1)S(1)} collective-permute-done((bf16[320,768]{1,0:T(8,128)(2,1)S(1)}, bf16[320,768]{1,0:T(8,128)(2,1)S(1)}, u32[]{:S(2)}, u32[]{:S(2)}) %collective-permute-start.14) | collective-permute-done | bytes 491552 | tf_op jit(solution)/shard_map/ppermute | solution.py:57
  36.4 18.4 %scores.1 = (f32[2,1280,1280]{2,1,0:T(8,128)S(1)}, f32[8,320]{1,0:T(8,128)S(1)}, f32[8,320]{1,0:T(8,128)S(1)}, s32[2]{0:T(128)S(1)}) custom-call(bf16[320,768]{1,0:T(8,128)(2,1)S(1)} %get-tuple-element.34.refs_0_, bf16[320,768]{1,0:T(8,128)(2,1)S(1)} %collective-permute-done.2.b0.refs_1_, bf16[320,768]{1,0:T(8,128)(2,1)S(1)} %collective-permute-done.3.b1.refs_2_, ...), custom_call_target="tpu_custom_call" | custom-call | flops 5033164800 | tf_op jit(solution)/shard_map/scores/pallas_call | solution.py:264
  54.9 0.5 collective-permute-start.15
  55.3 0.8 collective-permute-done.15.got_ref
  56.2 0.2 collective-permute-start.16
  56.4 2.4 %collective-permute-done.16.got_ref = f32[8,320]{1,0:T(8,128)S(1)} collective-permute-done((f32[8,320]{1,0:T(8,128)S(1)}, f32[8,320]{1,0:T(8,128)S(1)}, u32[]{:S(2)}, u32[]{:S(2)}) %collective-permute-start.16) | collective-permute-done | bytes 10272 | tf_op jit(solution)/shard_map/ppermute | solution.py:53
  58.9 2.7 %collective-permute-start.17 = (f32[8,320]{1,0:T(8,128)S(1)}, f32[8,320]{1,0:T(8,128)S(1)}, u32[]{:S(2)}, u32[]{:S(2)}) collective-permute-start(f32[8,320]{1,0:T(8,128)S(1)} %merge.5.mine_ref), channel_id=1, source_target_pairs={{0,32},{1,33},{2,34},{3,35},{4,36},{5,37},{6,38},{7,39},{8,40},{9,... | collective-permute-start | bytes 30728 | tf_op jit(solution)/shard_map/ppermute | solution.py:53
  61.6 1.1 collective-permute-done.17.got_ref
  62.7 3.7 %collective-permute-start.18 = (f32[8,320]{1,0:T(8,128)S(1)}, f32[8,320]{1,0:T(8,128)S(1)}, u32[]{:S(2)}, u32[]{:S(2)}) collective-permute-start(f32[8,320]{1,0:T(8,128)S(1)} %merge.6.mine_ref), channel_id=1, source_target_pairs={{0,1},{1,0},{2,3},{3,2},{4,5},{5,4},{6,7},{7,6},{8,9},{9,8},{10,11... | collective-permute-start | bytes 30728 | tf_op jit(solution)/shard_map/ppermute | solution.py:53
  66.5 1.1 collective-permute-done.18.got_ref
  67.6 1.7 %collective-permute-start.19 = (f32[8,320]{1,0:T(8,128)S(1)}, f32[8,320]{1,0:T(8,128)S(1)}, u32[]{:S(2)}, u32[]{:S(2)}) collective-permute-start(f32[8,320]{1,0:T(8,128)S(1)} %merge.7.a_lse), channel_id=1, source_target_pairs={{0,16},{1,17},{2,18},{3,19},{4,20},{5,21},{6,22},{7,23},{8,24},{9,... | collective-permute-start | bytes 30728 | tf_op jit(solution)/shard_map/ppermute | solution.py:57
  69.3 0.8 collective-permute-done.19.b_lse
  70.1 7.6 %weights.1 = (bf16[2,1280,1280]{2,1,0:T(8,128)(2,1)S(1)}, bf16[1280,768]{1,0:T(8,128)(2,1)S(1)}) custom-call(s32[2]{0:T(128)S(1)} %get-tuple-element.44.flags, f32[2,1280,1280]{2,1,0:T(8,128)S(1)} %get-tuple-element.45.e_ref, f32[8,320]{1,0:T(8,128)S(1)} %merge.7.a_lse, f32[8,320]{1,0:T(8,128)S(1)} %collective-permute-done.19.b_lse, ...), custom_call_target="tpu_custom_call" | custom-call | flops 2516582400 | bytes 19660800 | tf_op jit(solution)/shard_map/weights/pallas_call | solution.py:337
  77.7 0.4 collective-permute-start.21
  78.2 5.6 %middle.1 = (f32[1280,768]{1,0:T(8,128)S(1)}, bf16[1600,768]{1,0:T(8,128)(2,1)S(1)}) custom-call(bf16[2,1280,1280]{2,1,0:T(8,128)(2,1)S(1)} %get-tuple-element.48.w_ref, bf16[320,768]{1,0:T(8,128)(2,1)S(1)} %get-tuple-element.34.refs_0_, bf16[320,768]{1,0:T(8,128)(2,1)S(1)} %collective-permute-done.2.b0.refs_1_, ...), custom_call_target="tpu_custom_call" | custom-call | flops 5033164800 | tf_op jit(solution)/shard_map/middle/pallas_call | solution.py:370
  83.8 0.3 collective-permute-start.20
  84.0 0.3 far.1
  84.4 0.1 collective-permute-start.22
  84.5 2.7 %collective-permute-start.23 = (bf16[320,768]{1,0:T(8,128)(2,1)S(1)}, bf16[320,768]{1,0:T(8,128)(2,1)S(1)}, u32[]{:S(2)}, u32[]{:S(2)}) collective-permute-start(bf16[320,768]{1,0:T(8,128)(2,1)S(1)} %get-tuple-element.53), channel_id=1, source_target_pairs={{0,32},{1,33},{2,34},{3,35},{4,36},{5,37},{6,38},{7,39},{8,40},{9,... | collective-permute-start | bytes 1474568 | tf_op jit(solution)/shard_map/ppermute | solution.py:53
  87.2 3.5 %collective-permute-start.24 = (bf16[320,768]{1,0:T(8,128)(2,1)S(1)}, bf16[320,768]{1,0:T(8,128)(2,1)S(1)}, u32[]{:S(2)}, u32[]{:S(2)}) collective-permute-start(bf16[320,768]{1,0:T(8,128)(2,1)S(1)} %get-tuple-element.54), channel_id=1, source_target_pairs={{0,1},{1,0},{2,3},{3,2},{4,5},{5,4},{6,7},{7,6},{8,9},{9,8},{10,11... | collective-permute-start | bytes 1474568 | tf_op jit(solution)/shard_map/ppermute | solution.py:53
  90.7 2.9 %last.1.ga_lo = f32[1280,768]{1,0:T(8,128)S(1)} custom-call(bf16[2,1280,1280]{2,1,0:T(8,128)(2,1)S(1)} %get-tuple-element.48.w_ref, bf16[320,768]{1,0:T(8,128)(2,1)S(1)} %get-tuple-element.35.refs_8_.refs_0_, bf16[480,768]{1,0:T(8,128)(2,1)S(1)} %collective-permute-done.12.refs_9_.refs_1_, bf16[480,768]{1,0:T(8,128)(2,1)S(1)} %collective-permute-done.13.refs_10_.refs_2_, ...), custom_call_target="tpu_custom_call" | custom-call | flops 2516582400 | tf_op jit(solution)/shard_map/last/pallas_call | solution.py:415
  93.6 1.1 collective-permute-start.25
  94.6 2.3 %collective-permute-done.24.r_xz = bf16[320,768]{1,0:T(8,128)(2,1)S(1)} collective-permute-done((bf16[320,768]{1,0:T(8,128)(2,1)S(1)}, bf16[320,768]{1,0:T(8,128)(2,1)S(1)}, u32[]{:S(2)}, u32[]{:S(2)}) %collective-permute-start.24) | collective-permute-done | bytes 491552 | tf_op jit(solution)/shard_map/ppermute | solution.py:53
  96.9 0.6 near.1
  97.5 0.0 copy-start
  97.5 0.0 copy-start.1
  97.5 1.7 %collective-permute-start.26 = (bf16[320,768]{1,0:T(8,128)(2,1)S(1)}, bf16[320,768]{1,0:T(8,128)(2,1)S(1)}, u32[]{:S(2)}, u32[]{:S(2)}) collective-permute-start(bf16[320,768]{1,0:T(8,128)(2,1)S(1)} %get-tuple-element.57), channel_id=1, source_target_pairs={{0,12},{1,13},{2,14},{3,15},{4,8},{5,9},{6,10},{7,11},{8,4},{9,5},... | collective-permute-start | bytes 1474568 | tf_op jit(solution)/shard_map/ppermute | solution.py:53
  99.3 0.2 collective-permute-start.27
  99.4 2.7 %collective-permute-start.28 = (bf16[320,768]{1,0:T(8,128)(2,1)S(1)}, bf16[320,768]{1,0:T(8,128)(2,1)S(1)}, u32[]{:S(2)}, u32[]{:S(2)}) collective-permute-start(bf16[320,768]{1,0:T(8,128)(2,1)S(1)} %get-tuple-element.59), channel_id=1, source_target_pairs={{0,1},{1,0},{2,3},{3,2},{4,5},{5,4},{6,7},{7,6},{8,9},{9,8},{10,11... | collective-permute-start | bytes 1474568 | tf_op jit(solution)/shard_map/ppermute | solution.py:53
  102.1 3.6 %collective-permute-done.25 = bf16[320,768]{1,0:T(8,128)(2,1)S(1)} collective-permute-done((bf16[320,768]{1,0:T(8,128)(2,1)S(1)}, bf16[320,768]{1,0:T(8,128)(2,1)S(1)}, u32[]{:S(2)}, u32[]{:S(2)}) %collective-permute-start.25) | collective-permute-done | bytes 491552 | tf_op jit(solution)/shard_map/ppermute | solution.py:53
  105.7 1.2 %collective-permute-done.26 = bf16[320,768]{1,0:T(8,128)(2,1)S(1)} collective-permute-done((bf16[320,768]{1,0:T(8,128)(2,1)S(1)}, bf16[320,768]{1,0:T(8,128)(2,1)S(1)}, u32[]{:S(2)}, u32[]{:S(2)}) %collective-permute-start.26) | collective-permute-done | bytes 491552 | tf_op jit(solution)/shard_map/ppermute | solution.py:53
  106.8 1.6 %collective-permute-done.27 = bf16[320,768]{1,0:T(8,128)(2,1)S(1)} collective-permute-done((bf16[320,768]{1,0:T(8,128)(2,1)S(1)}, bf16[320,768]{1,0:T(8,128)(2,1)S(1)}, u32[]{:S(2)}, u32[]{:S(2)}) %collective-permute-start.27) | collective-permute-done | bytes 491552 | tf_op jit(solution)/shard_map/ppermute | solution.py:53
  108.4 2.4 %collective-permute-done.28 = bf16[320,768]{1,0:T(8,128)(2,1)S(1)} collective-permute-done((bf16[320,768]{1,0:T(8,128)(2,1)S(1)}, bf16[320,768]{1,0:T(8,128)(2,1)S(1)}, u32[]{:S(2)}, u32[]{:S(2)}) %collective-permute-start.28) | collective-permute-done | bytes 491552 | tf_op jit(solution)/shard_map/ppermute | solution.py:53
  110.8 0.3 convert_add_fusion
  111.2 0.1 collective-permute-start.29
  111.3 1.8 %collective-permute-done.29 = f32[160,768]{1,0:T(8,128)S(1)} collective-permute-done((f32[160,768]{1,0:T(8,128)S(1)}, f32[160,768]{1,0:T(8,128)S(1)}, u32[]{:S(2)}, u32[]{:S(2)}) %collective-permute-start.29) | collective-permute-done | bytes 491552 | tf_op jit(solution)/shard_map/ppermute | solution.py:57
  113.1 1.0 convert_subtract_fusion
  (16 shorter events, 0.2 us)
Async XLA Ops:
  0.6 2.9 %collective-permute-start = (bf16[160,768]{1,0:T(8,128)(2,1)}, bf16[160,768]{1,0:T(8,128)(2,1)S(1)}, u32[]{:S(2)}, u32[]{:S(2)}) collective-permute-start(bf16[160,768]{1,0:T(8,128)(2,1)} %images.1), channel_id=1, source_target_pairs={{0,16},{1,17},{2,18},{3,19},{4,20},{5,21},{6,22},{7,23},{8,24},{9,... | collective-permute-start | bytes 737288 | tf_op jit(solution)/shard_map/ppermute | solution.py:57
  2.1 1.7 %collective-permute-start.1 = (bf16[160,768]{1,0:T(8,128)(2,1)}, bf16[160,768]{1,0:T(8,128)(2,1)S(1)}, u32[]{:S(2)}, u32[]{:S(2)}) collective-permute-start(bf16[160,768]{1,0:T(8,128)(2,1)} %texts.1), channel_id=1, source_target_pairs={{0,16},{1,17},{2,18},{3,19},{4,20},{5,21},{6,22},{7,23},{8,24},{9,... | collective-permute-start | bytes 737288 | tf_op jit(solution)/shard_map/ppermute | solution.py:57
  3.9 8.1 %collective-permute-start.2 = (bf16[320,768]{1,0:T(8,128)(2,1)S(1)}, bf16[320,768]{1,0:T(8,128)(2,1)S(1)}, u32[]{:S(2)}, u32[]{:S(2)}) collective-permute-start(bf16[320,768]{1,0:T(8,128)(2,1)S(1)} %get-tuple-element.34.refs_0_), channel_id=1, source_target_pairs={{0,12},{1,13},{2,14},{3,15},{4,8},{5,9},{6,10},{7,11},{8,4},{9,5},... | collective-permute-start | bytes 1474568 | tf_op jit(solution)/shard_map/ppermute | solution.py:53
  5.3 13.9 %collective-permute-start.3 = (bf16[320,768]{1,0:T(8,128)(2,1)S(1)}, bf16[320,768]{1,0:T(8,128)(2,1)S(1)}, u32[]{:S(2)}, u32[]{:S(2)}) collective-permute-start(bf16[320,768]{1,0:T(8,128)(2,1)S(1)} %get-tuple-element.34.refs_0_), channel_id=1, source_target_pairs={{0,32},{1,33},{2,34},{3,35},{4,36},{5,37},{6,38},{7,39},{8,40},{9,... | collective-permute-start | bytes 1474568 | tf_op jit(solution)/shard_map/ppermute | solution.py:53
  8.0 11.4 %collective-permute-start.4 = (bf16[320,768]{1,0:T(8,128)(2,1)S(1)}, bf16[320,768]{1,0:T(8,128)(2,1)S(1)}, u32[]{:S(2)}, u32[]{:S(2)}) collective-permute-start(bf16[320,768]{1,0:T(8,128)(2,1)S(1)} %get-tuple-element.34.refs_0_), channel_id=1, source_target_pairs={{0,1},{1,0},{2,3},{3,2},{4,5},{5,4},{6,7},{7,6},{8,9},{9,8},{10,11... | collective-permute-start | bytes 1474568 | tf_op jit(solution)/shard_map/ppermute | solution.py:53
  12.0 13.5 %collective-permute-start.8 = (bf16[320,768]{1,0:T(8,128)(2,1)S(1)}, bf16[320,768]{1,0:T(8,128)(2,1)S(1)}, u32[]{:S(2)}, u32[]{:S(2)}) collective-permute-start(bf16[320,768]{1,0:T(8,128)(2,1)S(1)} %get-tuple-element.34.refs_0_), channel_id=1, source_target_pairs={{0,45},{1,44},{2,47},{3,46},{4,41},{5,40},{6,43},{7,42},{8,37},{9,... | collective-permute-start | bytes 1474568 | tf_op jit(solution)/shard_map/ppermute | solution.py:53
  19.2 11.8 %collective-permute-start.6 = (bf16[320,768]{1,0:T(8,128)(2,1)S(1)}, bf16[320,768]{1,0:T(8,128)(2,1)S(1)}, u32[]{:S(2)}, u32[]{:S(2)}) collective-permute-start(bf16[320,768]{1,0:T(8,128)(2,1)S(1)} %collective-permute-done.2.b0.refs_1_), channel_id=1, source_target_pairs={{0,1},{1,0},{2,3},{3,2},{4,5},{5,4},{6,7},{7,6},{8,9},{9,8},{10,11... | collective-permute-start | bytes 1474568 | tf_op jit(solution)/shard_map/ppermute | solution.py:53
  19.2 12.5 %collective-permute-start.5 = (bf16[320,768]{1,0:T(8,128)(2,1)S(1)}, bf16[320,768]{1,0:T(8,128)(2,1)S(1)}, u32[]{:S(2)}, u32[]{:S(2)}) collective-permute-start(bf16[320,768]{1,0:T(8,128)(2,1)S(1)} %collective-permute-done.3.b1.refs_2_), channel_id=1, source_target_pairs={{0,12},{1,13},{2,14},{3,15},{4,8},{5,9},{6,10},{7,11},{8,4},{9,5},... | collective-permute-start | bytes 1474568 | tf_op jit(solution)/shard_map/ppermute | solution.py:53
  19.5 12.8 %collective-permute-start.7 = (bf16[320,768]{1,0:T(8,128)(2,1)S(1)}, bf16[320,768]{1,0:T(8,128)(2,1)S(1)}, u32[]{:S(2)}, u32[]{:S(2)}) collective-permute-start(bf16[320,768]{1,0:T(8,128)(2,1)S(1)} %collective-permute-done.4.b2.refs_3_), channel_id=1, source_target_pairs={{0,32},{1,33},{2,34},{3,35},{4,36},{5,37},{6,38},{7,39},{8,40},{9,... | collective-permute-start | bytes 1474568 | tf_op jit(solution)/shard_map/ppermute | solution.py:53
  19.9 12.4 %collective-permute-start.12 = (bf16[480,768]{1,0:T(8,128)(2,1)S(1)}, bf16[480,768]{1,0:T(8,128)(2,1)S(1)}, u32[]{:S(2)}, u32[]{:S(2)}) collective-permute-start(bf16[480,768]{1,0:T(8,128)(2,1)S(1)} %get-tuple-element.36), channel_id=1, source_target_pairs={{0,16},{1,17},{2,18},{3,19},{4,20},{5,21},{6,22},{7,23},{8,24},{9,... | collective-permute-start | bytes 2211848 | tf_op jit(solution)/shard_map/ppermute | solution.py:57
  25.5 6.7 %collective-permute-start.13 = (bf16[480,768]{1,0:T(8,128)(2,1)S(1)}, bf16[480,768]{1,0:T(8,128)(2,1)S(1)}, u32[]{:S(2)}, u32[]{:S(2)}) collective-permute-start(bf16[480,768]{1,0:T(8,128)(2,1)S(1)} %get-tuple-element.37), channel_id=1, source_target_pairs={{0,16},{1,17},{2,18},{3,19},{4,20},{5,21},{6,22},{7,23},{8,24},{9,... | collective-permute-start | bytes 2211848 | tf_op jit(solution)/shard_map/ppermute | solution.py:57
  31.0 2.2 %collective-permute-start.9 = (bf16[320,768]{1,0:T(8,128)(2,1)S(1)}, bf16[320,768]{1,0:T(8,128)(2,1)S(1)}, u32[]{:S(2)}, u32[]{:S(2)}) collective-permute-start(bf16[320,768]{1,0:T(8,128)(2,1)S(1)} %collective-permute-done.8.refs_7_), channel_id=1, source_target_pairs={{0,16},{1,17},{2,18},{3,19},{4,20},{5,21},{6,22},{7,23},{8,24},{9,... | collective-permute-start | bytes 1474568 | tf_op jit(solution)/shard_map/ppermute | solution.py:57
  31.7 2.2 %collective-permute-start.10 = (bf16[320,768]{1,0:T(8,128)(2,1)S(1)}, bf16[320,768]{1,0:T(8,128)(2,1)S(1)}, u32[]{:S(2)}, u32[]{:S(2)}) collective-permute-start(bf16[320,768]{1,0:T(8,128)(2,1)S(1)} %collective-permute-done.6.refs_5_), channel_id=1, source_target_pairs={{0,16},{1,17},{2,18},{3,19},{4,20},{5,21},{6,22},{7,23},{8,24},{9,... | collective-permute-start | bytes 1474568 | tf_op jit(solution)/shard_map/ppermute | solution.py:57
  32.2 2.3 %collective-permute-start.11 = (bf16[320,768]{1,0:T(8,128)(2,1)S(1)}, bf16[320,768]{1,0:T(8,128)(2,1)S(1)}, u32[]{:S(2)}, u32[]{:S(2)}) collective-permute-start(bf16[320,768]{1,0:T(8,128)(2,1)S(1)} %collective-permute-done.5.refs_4_), channel_id=1, source_target_pairs={{0,16},{1,17},{2,18},{3,19},{4,20},{5,21},{6,22},{7,23},{8,24},{9,... | collective-permute-start | bytes 1474568 | tf_op jit(solution)/shard_map/ppermute | solution.py:57
  34.6 1.9 %collective-permute-start.14 = (bf16[320,768]{1,0:T(8,128)(2,1)S(1)}, bf16[320,768]{1,0:T(8,128)(2,1)S(1)}, u32[]{:S(2)}, u32[]{:S(2)}) collective-permute-start(bf16[320,768]{1,0:T(8,128)(2,1)S(1)} %collective-permute-done.7.refs_6_), channel_id=1, source_target_pairs={{0,16},{1,17},{2,18},{3,19},{4,20},{5,21},{6,22},{7,23},{8,24},{9,... | collective-permute-start | bytes 1474568 | tf_op jit(solution)/shard_map/ppermute | solution.py:57
  54.9 1.3 %collective-permute-start.15 = (f32[8,320]{1,0:T(8,128)S(1)}, f32[8,320]{1,0:T(8,128)S(1)}, u32[]{:S(2)}, u32[]{:S(2)}) collective-permute-start(f32[8,320]{1,0:T(8,128)S(1)} %get-tuple-element.47), channel_id=1, source_target_pairs={{0,16},{1,17},{2,18},{3,19},{4,20},{5,21},{6,22},{7,23},{8,24},{9,... | collective-permute-start | bytes 30728 | tf_op jit(solution)/shard_map/ppermute | solution.py:57
  56.2 2.6 %collective-permute-start.16 = (f32[8,320]{1,0:T(8,128)S(1)}, f32[8,320]{1,0:T(8,128)S(1)}, u32[]{:S(2)}, u32[]{:S(2)}) collective-permute-start(f32[8,320]{1,0:T(8,128)S(1)} %merge.4.mine_ref), channel_id=1, source_target_pairs={{0,12},{1,13},{2,14},{3,15},{4,8},{5,9},{6,10},{7,11},{8,4},{9,5},... | collective-permute-start | bytes 30728 | tf_op jit(solution)/shard_map/ppermute | solution.py:53
  58.9 3.8 %collective-permute-start.17 = (f32[8,320]{1,0:T(8,128)S(1)}, f32[8,320]{1,0:T(8,128)S(1)}, u32[]{:S(2)}, u32[]{:S(2)}) collective-permute-start(f32[8,320]{1,0:T(8,128)S(1)} %merge.5.mine_ref), channel_id=1, source_target_pairs={{0,32},{1,33},{2,34},{3,35},{4,36},{5,37},{6,38},{7,39},{8,40},{9,... | collective-permute-start | bytes 30728 | tf_op jit(solution)/shard_map/ppermute | solution.py:53
  62.7 4.8 %collective-permute-start.18 = (f32[8,320]{1,0:T(8,128)S(1)}, f32[8,320]{1,0:T(8,128)S(1)}, u32[]{:S(2)}, u32[]{:S(2)}) collective-permute-start(f32[8,320]{1,0:T(8,128)S(1)} %merge.6.mine_ref), channel_id=1, source_target_pairs={{0,1},{1,0},{2,3},{3,2},{4,5},{5,4},{6,7},{7,6},{8,9},{9,8},{10,11... | collective-permute-start | bytes 30728 | tf_op jit(solution)/shard_map/ppermute | solution.py:53
  67.6 2.5 %collective-permute-start.19 = (f32[8,320]{1,0:T(8,128)S(1)}, f32[8,320]{1,0:T(8,128)S(1)}, u32[]{:S(2)}, u32[]{:S(2)}) collective-permute-start(f32[8,320]{1,0:T(8,128)S(1)} %merge.7.a_lse), channel_id=1, source_target_pairs={{0,16},{1,17},{2,18},{3,19},{4,20},{5,21},{6,22},{7,23},{8,24},{9,... | collective-permute-start | bytes 30728 | tf_op jit(solution)/shard_map/ppermute | solution.py:57
  77.7 6.3 %collective-permute-start.21 = (bf16[1280,768]{1,0:T(8,128)(2,1)S(1)}, bf16[1280,768]{1,0:T(8,128)(2,1)S(1)}, u32[]{:S(2)}, u32[]{:S(2)}) collective-permute-start(bf16[1280,768]{1,0:T(8,128)(2,1)S(1)} %get-tuple-element.51), channel_id=1, source_target_pairs={{0,16},{1,17},{2,18},{3,19},{4,20},{5,21},{6,22},{7,23},{8,24},{9,... | collective-permute-start | bytes 5898248 | tf_op jit(solution)/shard_map/ppermute | solution.py:57
  83.8 13.1 %collective-permute-start.20 = (bf16[1600,768]{1,0:T(8,128)(2,1)S(1)}, bf16[1600,768]{1,0:T(8,128)(2,1)S(1)}, u32[]{:S(2)}, u32[]{:S(2)}) collective-permute-start(bf16[1600,768]{1,0:T(8,128)(2,1)S(1)} %get-tuple-element.49), channel_id=1, source_target_pairs={{0,16},{1,17},{2,18},{3,19},{4,20},{5,21},{6,22},{7,23},{8,24},{9,... | collective-permute-start | bytes 7372808 | tf_op jit(solution)/shard_map/ppermute | solution.py:57
  84.4 10.3 %collective-permute-start.22 = (bf16[320,768]{1,0:T(8,128)(2,1)S(1)}, bf16[320,768]{1,0:T(8,128)(2,1)S(1)}, u32[]{:S(2)}, u32[]{:S(2)}) collective-permute-start(bf16[320,768]{1,0:T(8,128)(2,1)S(1)} %get-tuple-element.52), channel_id=1, source_target_pairs={{0,12},{1,13},{2,14},{3,15},{4,8},{5,9},{6,10},{7,11},{8,4},{9,5},... | collective-permute-start | bytes 1474568 | tf_op jit(solution)/shard_map/ppermute | solution.py:53
  84.5 10.2 %collective-permute-start.23 = (bf16[320,768]{1,0:T(8,128)(2,1)S(1)}, bf16[320,768]{1,0:T(8,128)(2,1)S(1)}, u32[]{:S(2)}, u32[]{:S(2)}) collective-permute-start(bf16[320,768]{1,0:T(8,128)(2,1)S(1)} %get-tuple-element.53), channel_id=1, source_target_pairs={{0,32},{1,33},{2,34},{3,35},{4,36},{5,37},{6,38},{7,39},{8,40},{9,... | collective-permute-start | bytes 1474568 | tf_op jit(solution)/shard_map/ppermute | solution.py:53
  87.2 9.7 %collective-permute-start.24 = (bf16[320,768]{1,0:T(8,128)(2,1)S(1)}, bf16[320,768]{1,0:T(8,128)(2,1)S(1)}, u32[]{:S(2)}, u32[]{:S(2)}) collective-permute-start(bf16[320,768]{1,0:T(8,128)(2,1)S(1)} %get-tuple-element.54), channel_id=1, source_target_pairs={{0,1},{1,0},{2,3},{3,2},{4,5},{5,4},{6,7},{7,6},{8,9},{9,8},{10,11... | collective-permute-start | bytes 1474568 | tf_op jit(solution)/shard_map/ppermute | solution.py:53
  93.6 12.1 %collective-permute-start.25 = (bf16[320,768]{1,0:T(8,128)(2,1)S(1)}, bf16[320,768]{1,0:T(8,128)(2,1)S(1)}, u32[]{:S(2)}, u32[]{:S(2)}) collective-permute-start(bf16[320,768]{1,0:T(8,128)(2,1)S(1)} %get-tuple-element.56), channel_id=1, source_target_pairs={{0,45},{1,44},{2,47},{3,46},{4,41},{5,40},{6,43},{7,42},{8,37},{9,... | collective-permute-start | bytes 1474568 | tf_op jit(solution)/shard_map/ppermute | solution.py:53
  97.5 15.6 %copy-start = (bf16[160,768]{1,0:T(8,128)(2,1)S(1)}, bf16[160,768]{1,0:T(8,128)(2,1)}, u32[]{:S(2)}) copy-start(bf16[160,768]{1,0:T(8,128)(2,1)} %images.1) | copy-start | bytes 737284
  97.5 15.6 %copy-start.1 = (bf16[160,768]{1,0:T(8,128)(2,1)S(1)}, bf16[160,768]{1,0:T(8,128)(2,1)}, u32[]{:S(2)}) copy-start(bf16[160,768]{1,0:T(8,128)(2,1)} %texts.1) | copy-start | bytes 737284
  97.5 9.3 %collective-permute-start.26 = (bf16[320,768]{1,0:T(8,128)(2,1)S(1)}, bf16[320,768]{1,0:T(8,128)(2,1)S(1)}, u32[]{:S(2)}, u32[]{:S(2)}) collective-permute-start(bf16[320,768]{1,0:T(8,128)(2,1)S(1)} %get-tuple-element.57), channel_id=1, source_target_pairs={{0,12},{1,13},{2,14},{3,15},{4,8},{5,9},{6,10},{7,11},{8,4},{9,5},... | collective-permute-start | bytes 1474568 | tf_op jit(solution)/shard_map/ppermute | solution.py:53
  99.3 9.2 %collective-permute-start.27 = (bf16[320,768]{1,0:T(8,128)(2,1)S(1)}, bf16[320,768]{1,0:T(8,128)(2,1)S(1)}, u32[]{:S(2)}, u32[]{:S(2)}) collective-permute-start(bf16[320,768]{1,0:T(8,128)(2,1)S(1)} %get-tuple-element.58), channel_id=1, source_target_pairs={{0,32},{1,33},{2,34},{3,35},{4,36},{5,37},{6,38},{7,39},{8,40},{9,... | collective-permute-start | bytes 1474568 | tf_op jit(solution)/shard_map/ppermute | solution.py:53
  99.4 11.4 %collective-permute-start.28 = (bf16[320,768]{1,0:T(8,128)(2,1)S(1)}, bf16[320,768]{1,0:T(8,128)(2,1)S(1)}, u32[]{:S(2)}, u32[]{:S(2)}) collective-permute-start(bf16[320,768]{1,0:T(8,128)(2,1)S(1)} %get-tuple-element.59), channel_id=1, source_target_pairs={{0,1},{1,0},{2,3},{3,2},{4,5},{5,4},{6,7},{7,6},{8,9},{9,8},{10,11... | collective-permute-start | bytes 1474568 | tf_op jit(solution)/shard_map/ppermute | solution.py:53
  111.2 1.9 %collective-permute-start.29 = (f32[160,768]{1,0:T(8,128)S(1)}, f32[160,768]{1,0:T(8,128)S(1)}, u32[]{:S(2)}, u32[]{:S(2)}) collective-permute-start(f32[160,768]{1,0:T(8,128)S(1)} %slice.9), channel_id=1, source_target_pairs={{0,16},{1,17},{2,18},{3,19},{4,20},{5,21},{6,22},{7,23},{8,24},{9,... | collective-permute-start | bytes 1474568 | tf_op jit(solution)/shard_map/ppermute | solution.py:57

commit v14 on v13

--- a/solution.py
+++ b/solution.py
@@ -39,8 +39,8 @@
         target = (
             partner(y, c == 1) if m & 2 else y,
             c,
-            partner(x, c == 0) if m & 1 else x,
-            partner(z, c == 1) if m & 4 else z,
+            partner(x, c == 1) if m & 1 else x,
+            partner(z, c == 0) if m & 4 else z,
         )
         pairs.append((flat(y, c, x, z), flat(*target)))
     return pairs

time: 115 us -> 118 us (1.026)
  waiting for transfers between devices: 32.6 us -> 38.4 us
  starting transfers between devices: 42.6 us -> 40.2 us
    ppermute x17, starting transfers between devices: 34.3 us -> 27 us  [to_cube(): return lax.ppermute(a, AXES, across(m))]
    ppermute x17, waiting for transfers between devices: 24.8 us -> 30.7 us  [to_cube(): return lax.ppermute(a, AXES, across(m))]
    ppermute x13, starting transfers between devices: 8.27 us -> 13.2 us  [swap(): return lax.ppermute(a, AXES, SWAP)]
where the time goes in v14:
time: 118 us
  starting transfers between devices  40.2 us (34%)
  waiting for transfers between devices  38.4 us (33%)
  Pallas kernels  36.8 us (31%)
  other arithmetic  1.33 us (1%)
    ppermute x17, waiting for transfers between devices, to_cube(): return lax.ppermute(a, AXES, across(m))  30.7 us
    ppermute x17, starting transfers between devices, to_cube(): return lax.ppermute(a, AXES, across(m))  27 us
    pallas_call x1, Pallas kernels, scores_call(): pl.pallas_call(functools.partial(scores_kernel, scale), in_specs=[vmem_sp...  18.4 us
    ppermute x13, starting transfers between devices, swap(): return lax.ppermute(a, AXES, SWAP)  13.2 us
    ppermute x13, waiting for transfers between devices, swap(): return lax.ppermute(a, AXES, SWAP)  7.69 us
    pallas_call x1, Pallas kernels, weights_call(): pl.pallas_call(weights_kernel, in_specs=[smem_spec()] + [vmem_spec()] * 1...  7.64 us
    pallas_call x1, Pallas kernels, middle_call(): pl.pallas_call(middle_kernel, in_specs=[vmem_spec()] * 16, out_specs=[vme...  5.61 us
    pallas_call x1, Pallas kernels, last_call(): pl.pallas_call(last_kernel, in_specs=[vmem_spec()] * 8, out_specs=vmem_sp...  2.87 us
  transfers between devices with their start and end apart: 30, of which 20 were waited for; matrix products, arithmetic and copies ran while one was open for 0% of the time, Pallas kernels for 9%

profile of v14, /device:TPU:1, one launch (start us, length us, event | category | flops | bytes accessed | tf_op | source)
XLA Modules:
  0.0 117.5 jit_solution(3583900691677761599)
XLA Ops:
  0.6 1.5 %collective-permute-start = (bf16[160,768]{1,0:T(8,128)(2,1)}, bf16[160,768]{1,0:T(8,128)(2,1)S(1)}, u32[]{:S(2)}, u32[]{:S(2)}) collective-permute-start(bf16[160,768]{1,0:T(8,128)(2,1)} %images.1), channel_id=1, source_target_pairs={{0,16},{1,17},{2,18},{3,19},{4,20},{5,21},{6,22},{7,23},{8,24},{9,... | collective-permute-start | bytes 737288 | tf_op jit(solution)/shard_map/ppermute | solution.py:57
  2.1 0.1 collective-permute-start.1
  2.2 1.1 load.1
  3.3 0.2 collective-permute-done.got_images
  3.5 0.4 collective-permute-done.1.got_texts
  3.9 0.1 own.1
  3.9 2.6 %collective-permute-start.2 = (bf16[320,768]{1,0:T(8,128)(2,1)S(1)}, bf16[320,768]{1,0:T(8,128)(2,1)S(1)}, u32[]{:S(2)}, u32[]{:S(2)}) collective-permute-start(bf16[320,768]{1,0:T(8,128)(2,1)S(1)} %get-tuple-element.34.refs_0_), channel_id=1, source_target_pairs={{0,4},{1,5},{2,6},{3,7},{4,0},{5,1},{6,2},{7,3},{8,12},{9,13},{10,... | collective-permute-start | bytes 1474568 | tf_op jit(solution)/shard_map/ppermute | solution.py:53
  6.6 2.7 %collective-permute-start.3 = (bf16[320,768]{1,0:T(8,128)(2,1)S(1)}, bf16[320,768]{1,0:T(8,128)(2,1)S(1)}, u32[]{:S(2)}, u32[]{:S(2)}) collective-permute-start(bf16[320,768]{1,0:T(8,128)(2,1)S(1)} %get-tuple-element.34.refs_0_), channel_id=1, source_target_pairs={{0,32},{1,33},{2,34},{3,35},{4,36},{5,37},{6,38},{7,39},{8,40},{9,... | collective-permute-start | bytes 1474568 | tf_op jit(solution)/shard_map/ppermute | solution.py:53
  9.3 1.6 %collective-permute-start.4 = (bf16[320,768]{1,0:T(8,128)(2,1)S(1)}, bf16[320,768]{1,0:T(8,128)(2,1)S(1)}, u32[]{:S(2)}, u32[]{:S(2)}) collective-permute-start(bf16[320,768]{1,0:T(8,128)(2,1)S(1)} %get-tuple-element.34.refs_0_), channel_id=1, source_target_pairs={{0,3},{1,2},{2,1},{3,0},{4,7},{5,6},{6,5},{7,4},{8,11},{9,10},{10,... | collective-permute-start | bytes 1474568 | tf_op jit(solution)/shard_map/ppermute | solution.py:53
  10.9 2.3 %collective-permute-done.2.b0.refs_1_ = bf16[320,768]{1,0:T(8,128)(2,1)S(1)} collective-permute-done((bf16[320,768]{1,0:T(8,128)(2,1)S(1)}, bf16[320,768]{1,0:T(8,128)(2,1)S(1)}, u32[]{:S(2)}, u32[]{:S(2)}) %collective-permute-start.2) | collective-permute-done | bytes 491552 | tf_op jit(solution)/shard_map/ppermute | solution.py:53
  13.2 6.1 %collective-permute-start.8 = (bf16[320,768]{1,0:T(8,128)(2,1)S(1)}, bf16[320,768]{1,0:T(8,128)(2,1)S(1)}, u32[]{:S(2)}, u32[]{:S(2)}) collective-permute-start(bf16[320,768]{1,0:T(8,128)(2,1)S(1)} %get-tuple-element.34.refs_0_), channel_id=1, source_target_pairs={{0,39},{1,38},{2,37},{3,36},{4,35},{5,34},{6,33},{7,32},{8,47},{9,... | collective-permute-start | bytes 1474568 | tf_op jit(solution)/shard_map/ppermute | solution.py:53
  19.3 0.1 collective-permute-start.6
  19.4 0.0 collective-permute-done.3.b1.refs_2_
  19.4 0.2 collective-permute-start.5
  19.6 0.2 collective-permute-start.7
  19.8 0.1 join.1
  19.9 0.6 collective-permute-start.12
  20.6 5.1 %collective-permute-done.8.refs_7_ = bf16[320,768]{1,0:T(8,128)(2,1)S(1)} collective-permute-done((bf16[320,768]{1,0:T(8,128)(2,1)S(1)}, bf16[320,768]{1,0:T(8,128)(2,1)S(1)}, u32[]{:S(2)}, u32[]{:S(2)}) %collective-permute-start.8) | collective-permute-done | bytes 491552 | tf_op jit(solution)/shard_map/ppermute | solution.py:53
  25.6 0.5 collective-permute-start.13
  26.2 4.9 %collective-permute-done.6.refs_5_ = bf16[320,768]{1,0:T(8,128)(2,1)S(1)} collective-permute-done((bf16[320,768]{1,0:T(8,128)(2,1)S(1)}, bf16[320,768]{1,0:T(8,128)(2,1)S(1)}, u32[]{:S(2)}, u32[]{:S(2)}) %collective-permute-start.6) | collective-permute-done | bytes 491552 | tf_op jit(solution)/shard_map/ppermute | solution.py:53
  31.0 0.3 collective-permute-start.9
  31.3 0.6 collective-permute-start.10
  31.9 0.0 collective-permute-done.7.refs_6_
  31.9 0.0 collective-permute-start.11
  32.0 0.0 collective-permute-done.13.refs_10_.refs_2_
  32.0 0.9 collective-permute-done.9.refs_14_.refs_6_
  32.9 0.7 collective-permute-done.10.refs_12_.refs_4_
  33.6 0.7 collective-permute-done.11.refs_11_.refs_3_
  34.3 0.3 collective-permute-start.14
  34.6 1.6 %collective-permute-done.14.refs_13_.refs_5_ = bf16[320,768]{1,0:T(8,128)(2,1)S(1)} collective-permute-done((bf16[320,768]{1,0:T(8,128)(2,1)S(1)}, bf16[320,768]{1,0:T(8,128)(2,1)S(1)}, u32[]{:S(2)}, u32[]{:S(2)}) %collective-permute-start.14) | collective-permute-done | bytes 491552 | tf_op jit(solution)/shard_map/ppermute | solution.py:57
  36.2 18.4 %scores.1 = (f32[2,1280,1280]{2,1,0:T(8,128)S(1)}, f32[8,320]{1,0:T(8,128)S(1)}, f32[8,320]{1,0:T(8,128)S(1)}, s32[2]{0:T(128)S(1)}) custom-call(bf16[320,768]{1,0:T(8,128)(2,1)S(1)} %get-tuple-element.34.refs_0_, bf16[320,768]{1,0:T(8,128)(2,1)S(1)} %collective-permute-done.2.b0.refs_1_, bf16[320,768]{1,0:T(8,128)(2,1)S(1)} %collective-permute-done.3.b1.refs_2_, ...), custom_call_target="tpu_custom_call" | custom-call | flops 5033164800 | tf_op jit(solution)/shard_map/scores/pallas_call | solution.py:264
  54.6 0.4 collective-permute-start.15
  55.0 0.9 collective-permute-done.15.got_ref
  55.9 2.4 %collective-permute-start.16 = (f32[8,320]{1,0:T(8,128)S(1)}, f32[8,320]{1,0:T(8,128)S(1)}, u32[]{:S(2)}, u32[]{:S(2)}) collective-permute-start(f32[8,320]{1,0:T(8,128)S(1)} %merge.4.mine_ref), channel_id=1, source_target_pairs={{0,4},{1,5},{2,6},{3,7},{4,0},{5,1},{6,2},{7,3},{8,12},{9,13},{10,... | collective-permute-start | bytes 30728 | tf_op jit(solution)/shard_map/ppermute | solution.py:53
  58.3 1.4 %collective-permute-done.16.got_ref = f32[8,320]{1,0:T(8,128)S(1)} collective-permute-done((f32[8,320]{1,0:T(8,128)S(1)}, f32[8,320]{1,0:T(8,128)S(1)}, u32[]{:S(2)}, u32[]{:S(2)}) %collective-permute-start.16) | collective-permute-done | bytes 10272 | tf_op jit(solution)/shard_map/ppermute | solution.py:53
  59.8 1.9 %collective-permute-start.17 = (f32[8,320]{1,0:T(8,128)S(1)}, f32[8,320]{1,0:T(8,128)S(1)}, u32[]{:S(2)}, u32[]{:S(2)}) collective-permute-start(f32[8,320]{1,0:T(8,128)S(1)} %merge.5.mine_ref), channel_id=1, source_target_pairs={{0,32},{1,33},{2,34},{3,35},{4,36},{5,37},{6,38},{7,39},{8,40},{9,... | collective-permute-start | bytes 30728 | tf_op jit(solution)/shard_map/ppermute | solution.py:53
  61.7 1.9 %collective-permute-done.17.got_ref = f32[8,320]{1,0:T(8,128)S(1)} collective-permute-done((f32[8,320]{1,0:T(8,128)S(1)}, f32[8,320]{1,0:T(8,128)S(1)}, u32[]{:S(2)}, u32[]{:S(2)}) %collective-permute-start.17) | collective-permute-done | bytes 10272 | tf_op jit(solution)/shard_map/ppermute | solution.py:53
  63.6 0.8 collective-permute-start.18
  64.5 1.8 %collective-permute-done.18.got_ref = f32[8,320]{1,0:T(8,128)S(1)} collective-permute-done((f32[8,320]{1,0:T(8,128)S(1)}, f32[8,320]{1,0:T(8,128)S(1)}, u32[]{:S(2)}, u32[]{:S(2)}) %collective-permute-start.18) | collective-permute-done | bytes 10272 | tf_op jit(solution)/shard_map/ppermute | solution.py:53
  66.3 2.7 %collective-permute-start.19 = (f32[8,320]{1,0:T(8,128)S(1)}, f32[8,320]{1,0:T(8,128)S(1)}, u32[]{:S(2)}, u32[]{:S(2)}) collective-permute-start(f32[8,320]{1,0:T(8,128)S(1)} %merge.7.a_lse), channel_id=1, source_target_pairs={{0,16},{1,17},{2,18},{3,19},{4,20},{5,21},{6,22},{7,23},{8,24},{9,... | collective-permute-start | bytes 30728 | tf_op jit(solution)/shard_map/ppermute | solution.py:57
  69.0 0.8 collective-permute-done.19.b_lse
  69.8 7.6 %weights.1 = (bf16[2,1280,1280]{2,1,0:T(8,128)(2,1)S(1)}, bf16[1280,768]{1,0:T(8,128)(2,1)S(1)}) custom-call(s32[2]{0:T(128)S(1)} %get-tuple-element.44.flags, f32[2,1280,1280]{2,1,0:T(8,128)S(1)} %get-tuple-element.45.e_ref, f32[8,320]{1,0:T(8,128)S(1)} %merge.7.a_lse, f32[8,320]{1,0:T(8,128)S(1)} %collective-permute-done.19.b_lse, ...), custom_call_target="tpu_custom_call" | custom-call | flops 2516582400 | bytes 19660800 | tf_op jit(solution)/shard_map/weights/pallas_call | solution.py:337
  77.5 0.4 collective-permute-start.21
  77.9 5.6 %middle.1 = (f32[1280,768]{1,0:T(8,128)S(1)}, bf16[1600,768]{1,0:T(8,128)(2,1)S(1)}) custom-call(bf16[2,1280,1280]{2,1,0:T(8,128)(2,1)S(1)} %get-tuple-element.48.w_ref, bf16[320,768]{1,0:T(8,128)(2,1)S(1)} %get-tuple-element.34.refs_0_, bf16[320,768]{1,0:T(8,128)(2,1)S(1)} %collective-permute-done.2.b0.refs_1_, ...), custom_call_target="tpu_custom_call" | custom-call | flops 5033164800 | tf_op jit(solution)/shard_map/middle/pallas_call | solution.py:370
  83.5 0.2 collective-permute-start.20
  83.8 0.3 far.1
  84.1 2.4 %collective-permute-start.22 = (bf16[320,768]{1,0:T(8,128)(2,1)S(1)}, bf16[320,768]{1,0:T(8,128)(2,1)S(1)}, u32[]{:S(2)}, u32[]{:S(2)}) collective-permute-start(bf16[320,768]{1,0:T(8,128)(2,1)S(1)} %get-tuple-element.52), channel_id=1, source_target_pairs={{0,4},{1,5},{2,6},{3,7},{4,0},{5,1},{6,2},{7,3},{8,12},{9,13},{10,... | collective-permute-start | bytes 1474568 | tf_op jit(solution)/shard_map/ppermute | solution.py:53
  86.5 1.9 %collective-permute-start.23 = (bf16[320,768]{1,0:T(8,128)(2,1)S(1)}, bf16[320,768]{1,0:T(8,128)(2,1)S(1)}, u32[]{:S(2)}, u32[]{:S(2)}) collective-permute-start(bf16[320,768]{1,0:T(8,128)(2,1)S(1)} %get-tuple-element.53), channel_id=1, source_target_pairs={{0,32},{1,33},{2,34},{3,35},{4,36},{5,37},{6,38},{7,39},{8,40},{9,... | collective-permute-start | bytes 1474568 | tf_op jit(solution)/shard_map/ppermute | solution.py:53
  88.4 2.9 %last.1.ga_lo = f32[1280,768]{1,0:T(8,128)S(1)} custom-call(bf16[2,1280,1280]{2,1,0:T(8,128)(2,1)S(1)} %get-tuple-element.48.w_ref, bf16[320,768]{1,0:T(8,128)(2,1)S(1)} %get-tuple-element.35.refs_8_.refs_0_, bf16[480,768]{1,0:T(8,128)(2,1)S(1)} %collective-permute-done.12.refs_9_.refs_1_, bf16[480,768]{1,0:T(8,128)(2,1)S(1)} %collective-permute-done.13.refs_10_.refs_2_, ...), custom_call_target="tpu_custom_call" | custom-call | flops 2516582400 | tf_op jit(solution)/shard_map/last/pallas_call | solution.py:415
  91.3 2.1 %collective-permute-start.25 = (bf16[320,768]{1,0:T(8,128)(2,1)S(1)}, bf16[320,768]{1,0:T(8,128)(2,1)S(1)}, u32[]{:S(2)}, u32[]{:S(2)}) collective-permute-start(bf16[320,768]{1,0:T(8,128)(2,1)S(1)} %get-tuple-element.56), channel_id=1, source_target_pairs={{0,39},{1,38},{2,37},{3,36},{4,35},{5,34},{6,33},{7,32},{8,47},{9,... | collective-permute-start | bytes 1474568 | tf_op jit(solution)/shard_map/ppermute | solution.py:53
  93.4 2.3 %collective-permute-done.23.r_yz = bf16[320,768]{1,0:T(8,128)(2,1)S(1)} collective-permute-done((bf16[320,768]{1,0:T(8,128)(2,1)S(1)}, bf16[320,768]{1,0:T(8,128)(2,1)S(1)}, u32[]{:S(2)}, u32[]{:S(2)}) %collective-permute-start.23) | collective-permute-done | bytes 491552 | tf_op jit(solution)/shard_map/ppermute | solution.py:53
  95.7 0.5 collective-permute-done.24.r_xz
  96.2 0.6 near.1
  96.8 0.0 copy-start
  96.8 0.0 copy-start.1
  96.8 0.5 collective-permute-start.26
  97.3 1.2 %collective-permute-start.27 = (bf16[320,768]{1,0:T(8,128)(2,1)S(1)}, bf16[320,768]{1,0:T(8,128)(2,1)S(1)}, u32[]{:S(2)}, u32[]{:S(2)}) collective-permute-start(bf16[320,768]{1,0:T(8,128)(2,1)S(1)} %get-tuple-element.58), channel_id=1, source_target_pairs={{0,32},{1,33},{2,34},{3,35},{4,36},{5,37},{6,38},{7,39},{8,40},{9,... | collective-permute-start | bytes 1474568 | tf_op jit(solution)/shard_map/ppermute | solution.py:53
  98.5 4.9 %collective-permute-done.25 = bf16[320,768]{1,0:T(8,128)(2,1)S(1)} collective-permute-done((bf16[320,768]{1,0:T(8,128)(2,1)S(1)}, bf16[320,768]{1,0:T(8,128)(2,1)S(1)}, u32[]{:S(2)}, u32[]{:S(2)}) %collective-permute-start.25) | collective-permute-done | bytes 491552 | tf_op jit(solution)/shard_map/ppermute | solution.py:53
  103.4 3.8 %collective-permute-done.26 = bf16[320,768]{1,0:T(8,128)(2,1)S(1)} collective-permute-done((bf16[320,768]{1,0:T(8,128)(2,1)S(1)}, bf16[320,768]{1,0:T(8,128)(2,1)S(1)}, u32[]{:S(2)}, u32[]{:S(2)}) %collective-permute-start.26) | collective-permute-done | bytes 491552 | tf_op jit(solution)/shard_map/ppermute | solution.py:53
  107.2 1.9 %collective-permute-done.27 = bf16[320,768]{1,0:T(8,128)(2,1)S(1)} collective-permute-done((bf16[320,768]{1,0:T(8,128)(2,1)S(1)}, bf16[320,768]{1,0:T(8,128)(2,1)S(1)}, u32[]{:S(2)}, u32[]{:S(2)}) %collective-permute-start.27) | collective-permute-done | bytes 491552 | tf_op jit(solution)/shard_map/ppermute | solution.py:53
  109.1 0.3 convert_add_fusion
  109.4 5.6 %collective-permute-start.29 = (f32[160,768]{1,0:T(8,128)S(1)}, f32[160,768]{1,0:T(8,128)S(1)}, u32[]{:S(2)}, u32[]{:S(2)}) collective-permute-start(f32[160,768]{1,0:T(8,128)S(1)} %slice.9), channel_id=1, source_target_pairs={{0,16},{1,17},{2,18},{3,19},{4,20},{5,21},{6,22},{7,23},{8,24},{9,... | collective-permute-start | bytes 1474568 | tf_op jit(solution)/shard_map/ppermute | solution.py:57
  115.0 1.5 %collective-permute-done.29 = f32[160,768]{1,0:T(8,128)S(1)} collective-permute-done((f32[160,768]{1,0:T(8,128)S(1)}, f32[160,768]{1,0:T(8,128)S(1)}, u32[]{:S(2)}, u32[]{:S(2)}) %collective-permute-start.29) | collective-permute-done | bytes 491552 | tf_op jit(solution)/shard_map/ppermute | solution.py:57
  116.5 1.0 convert_subtract_fusion
  (16 shorter events, 0.2 us)
Async XLA Ops:
  0.6 2.9 %collective-permute-start = (bf16[160,768]{1,0:T(8,128)(2,1)}, bf16[160,768]{1,0:T(8,128)(2,1)S(1)}, u32[]{:S(2)}, u32[]{:S(2)}) collective-permute-start(bf16[160,768]{1,0:T(8,128)(2,1)} %images.1), channel_id=1, source_target_pairs={{0,16},{1,17},{2,18},{3,19},{4,20},{5,21},{6,22},{7,23},{8,24},{9,... | collective-permute-start | bytes 737288 | tf_op jit(solution)/shard_map/ppermute | solution.py:57
  2.1 1.7 %collective-permute-start.1 = (bf16[160,768]{1,0:T(8,128)(2,1)}, bf16[160,768]{1,0:T(8,128)(2,1)S(1)}, u32[]{:S(2)}, u32[]{:S(2)}) collective-permute-start(bf16[160,768]{1,0:T(8,128)(2,1)} %texts.1), channel_id=1, source_target_pairs={{0,16},{1,17},{2,18},{3,19},{4,20},{5,21},{6,22},{7,23},{8,24},{9,... | collective-permute-start | bytes 737288 | tf_op jit(solution)/shard_map/ppermute | solution.py:57
  3.9 9.3 %collective-permute-start.2 = (bf16[320,768]{1,0:T(8,128)(2,1)S(1)}, bf16[320,768]{1,0:T(8,128)(2,1)S(1)}, u32[]{:S(2)}, u32[]{:S(2)}) collective-permute-start(bf16[320,768]{1,0:T(8,128)(2,1)S(1)} %get-tuple-element.34.refs_0_), channel_id=1, source_target_pairs={{0,4},{1,5},{2,6},{3,7},{4,0},{5,1},{6,2},{7,3},{8,12},{9,13},{10,... | collective-permute-start | bytes 1474568 | tf_op jit(solution)/shard_map/ppermute | solution.py:53
  6.6 12.8 %collective-permute-start.3 = (bf16[320,768]{1,0:T(8,128)(2,1)S(1)}, bf16[320,768]{1,0:T(8,128)(2,1)S(1)}, u32[]{:S(2)}, u32[]{:S(2)}) collective-permute-start(bf16[320,768]{1,0:T(8,128)(2,1)S(1)} %get-tuple-element.34.refs_0_), channel_id=1, source_target_pairs={{0,32},{1,33},{2,34},{3,35},{4,36},{5,37},{6,38},{7,39},{8,40},{9,... | collective-permute-start | bytes 1474568 | tf_op jit(solution)/shard_map/ppermute | solution.py:53
  9.3 10.3 %collective-permute-start.4 = (bf16[320,768]{1,0:T(8,128)(2,1)S(1)}, bf16[320,768]{1,0:T(8,128)(2,1)S(1)}, u32[]{:S(2)}, u32[]{:S(2)}) collective-permute-start(bf16[320,768]{1,0:T(8,128)(2,1)S(1)} %get-tuple-element.34.refs_0_), channel_id=1, source_target_pairs={{0,3},{1,2},{2,1},{3,0},{4,7},{5,6},{6,5},{7,4},{8,11},{9,10},{10,... | collective-permute-start | bytes 1474568 | tf_op jit(solution)/shard_map/ppermute | solution.py:53
  13.2 12.4 %collective-permute-start.8 = (bf16[320,768]{1,0:T(8,128)(2,1)S(1)}, bf16[320,768]{1,0:T(8,128)(2,1)S(1)}, u32[]{:S(2)}, u32[]{:S(2)}) collective-permute-start(bf16[320,768]{1,0:T(8,128)(2,1)S(1)} %get-tuple-element.34.refs_0_), channel_id=1, source_target_pairs={{0,39},{1,38},{2,37},{3,36},{4,35},{5,34},{6,33},{7,32},{8,47},{9,... | collective-permute-start | bytes 1474568 | tf_op jit(solution)/shard_map/ppermute | solution.py:53
  19.3 11.8 %collective-permute-start.6 = (bf16[320,768]{1,0:T(8,128)(2,1)S(1)}, bf16[320,768]{1,0:T(8,128)(2,1)S(1)}, u32[]{:S(2)}, u32[]{:S(2)}) collective-permute-start(bf16[320,768]{1,0:T(8,128)(2,1)S(1)} %collective-permute-done.2.b0.refs_1_), channel_id=1, source_target_pairs={{0,3},{1,2},{2,1},{3,0},{4,7},{5,6},{6,5},{7,4},{8,11},{9,10},{10,... | collective-permute-start | bytes 1474568 | tf_op jit(solution)/shard_map/ppermute | solution.py:53
  19.4 11.9 %collective-permute-start.5 = (bf16[320,768]{1,0:T(8,128)(2,1)S(1)}, bf16[320,768]{1,0:T(8,128)(2,1)S(1)}, u32[]{:S(2)}, u32[]{:S(2)}) collective-permute-start(bf16[320,768]{1,0:T(8,128)(2,1)S(1)} %collective-permute-done.3.b1.refs_2_), channel_id=1, source_target_pairs={{0,4},{1,5},{2,6},{3,7},{4,0},{5,1},{6,2},{7,3},{8,12},{9,13},{10,... | collective-permute-start | bytes 1474568 | tf_op jit(solution)/shard_map/ppermute | solution.py:53
  19.6 12.4 %collective-permute-start.7 = (bf16[320,768]{1,0:T(8,128)(2,1)S(1)}, bf16[320,768]{1,0:T(8,128)(2,1)S(1)}, u32[]{:S(2)}, u32[]{:S(2)}) collective-permute-start(bf16[320,768]{1,0:T(8,128)(2,1)S(1)} %collective-permute-done.4.b2.refs_3_), channel_id=1, source_target_pairs={{0,32},{1,33},{2,34},{3,35},{4,36},{5,37},{6,38},{7,39},{8,40},{9,... | collective-permute-start | bytes 1474568 | tf_op jit(solution)/shard_map/ppermute | solution.py:53
  19.9 12.0 %collective-permute-start.12 = (bf16[480,768]{1,0:T(8,128)(2,1)S(1)}, bf16[480,768]{1,0:T(8,128)(2,1)S(1)}, u32[]{:S(2)}, u32[]{:S(2)}) collective-permute-start(bf16[480,768]{1,0:T(8,128)(2,1)S(1)} %get-tuple-element.36), channel_id=1, source_target_pairs={{0,16},{1,17},{2,18},{3,19},{4,20},{5,21},{6,22},{7,23},{8,24},{9,... | collective-permute-start | bytes 2211848 | tf_op jit(solution)/shard_map/ppermute | solution.py:57
  25.6 6.3 %collective-permute-start.13 = (bf16[480,768]{1,0:T(8,128)(2,1)S(1)}, bf16[480,768]{1,0:T(8,128)(2,1)S(1)}, u32[]{:S(2)}, u32[]{:S(2)}) collective-permute-start(bf16[480,768]{1,0:T(8,128)(2,1)S(1)} %get-tuple-element.37), channel_id=1, source_target_pairs={{0,16},{1,17},{2,18},{3,19},{4,20},{5,21},{6,22},{7,23},{8,24},{9,... | collective-permute-start | bytes 2211848 | tf_op jit(solution)/shard_map/ppermute | solution.py:57
  31.0 1.9 %collective-permute-start.9 = (bf16[320,768]{1,0:T(8,128)(2,1)S(1)}, bf16[320,768]{1,0:T(8,128)(2,1)S(1)}, u32[]{:S(2)}, u32[]{:S(2)}) collective-permute-start(bf16[320,768]{1,0:T(8,128)(2,1)S(1)} %collective-permute-done.8.refs_7_), channel_id=1, source_target_pairs={{0,16},{1,17},{2,18},{3,19},{4,20},{5,21},{6,22},{7,23},{8,24},{9,... | collective-permute-start | bytes 1474568 | tf_op jit(solution)/shard_map/ppermute | solution.py:57
  31.3 2.3 %collective-permute-start.10 = (bf16[320,768]{1,0:T(8,128)(2,1)S(1)}, bf16[320,768]{1,0:T(8,128)(2,1)S(1)}, u32[]{:S(2)}, u32[]{:S(2)}) collective-permute-start(bf16[320,768]{1,0:T(8,128)(2,1)S(1)} %collective-permute-done.6.refs_5_), channel_id=1, source_target_pairs={{0,16},{1,17},{2,18},{3,19},{4,20},{5,21},{6,22},{7,23},{8,24},{9,... | collective-permute-start | bytes 1474568 | tf_op jit(solution)/shard_map/ppermute | solution.py:57
  31.9 2.4 %collective-permute-start.11 = (bf16[320,768]{1,0:T(8,128)(2,1)S(1)}, bf16[320,768]{1,0:T(8,128)(2,1)S(1)}, u32[]{:S(2)}, u32[]{:S(2)}) collective-permute-start(bf16[320,768]{1,0:T(8,128)(2,1)S(1)} %collective-permute-done.5.refs_4_), channel_id=1, source_target_pairs={{0,16},{1,17},{2,18},{3,19},{4,20},{5,21},{6,22},{7,23},{8,24},{9,... | collective-permute-start | bytes 1474568 | tf_op jit(solution)/shard_map/ppermute | solution.py:57
  34.3 1.9 %collective-permute-start.14 = (bf16[320,768]{1,0:T(8,128)(2,1)S(1)}, bf16[320,768]{1,0:T(8,128)(2,1)S(1)}, u32[]{:S(2)}, u32[]{:S(2)}) collective-permute-start(bf16[320,768]{1,0:T(8,128)(2,1)S(1)} %collective-permute-done.7.refs_6_), channel_id=1, source_target_pairs={{0,16},{1,17},{2,18},{3,19},{4,20},{5,21},{6,22},{7,23},{8,24},{9,... | collective-permute-start | bytes 1474568 | tf_op jit(solution)/shard_map/ppermute | solution.py:57
  54.6 1.3 %collective-permute-start.15 = (f32[8,320]{1,0:T(8,128)S(1)}, f32[8,320]{1,0:T(8,128)S(1)}, u32[]{:S(2)}, u32[]{:S(2)}) collective-permute-start(f32[8,320]{1,0:T(8,128)S(1)} %get-tuple-element.47), channel_id=1, source_target_pairs={{0,16},{1,17},{2,18},{3,19},{4,20},{5,21},{6,22},{7,23},{8,24},{9,... | collective-permute-start | bytes 30728 | tf_op jit(solution)/shard_map/ppermute | solution.py:57
  55.9 3.8 %collective-permute-start.16 = (f32[8,320]{1,0:T(8,128)S(1)}, f32[8,320]{1,0:T(8,128)S(1)}, u32[]{:S(2)}, u32[]{:S(2)}) collective-permute-start(f32[8,320]{1,0:T(8,128)S(1)} %merge.4.mine_ref), channel_id=1, source_target_pairs={{0,4},{1,5},{2,6},{3,7},{4,0},{5,1},{6,2},{7,3},{8,12},{9,13},{10,... | collective-permute-start | bytes 30728 | tf_op jit(solution)/shard_map/ppermute | solution.py:53
  59.8 3.8 %collective-permute-start.17 = (f32[8,320]{1,0:T(8,128)S(1)}, f32[8,320]{1,0:T(8,128)S(1)}, u32[]{:S(2)}, u32[]{:S(2)}) collective-permute-start(f32[8,320]{1,0:T(8,128)S(1)} %merge.5.mine_ref), channel_id=1, source_target_pairs={{0,32},{1,33},{2,34},{3,35},{4,36},{5,37},{6,38},{7,39},{8,40},{9,... | collective-permute-start | bytes 30728 | tf_op jit(solution)/shard_map/ppermute | solution.py:53
  63.6 2.6 %collective-permute-start.18 = (f32[8,320]{1,0:T(8,128)S(1)}, f32[8,320]{1,0:T(8,128)S(1)}, u32[]{:S(2)}, u32[]{:S(2)}) collective-permute-start(f32[8,320]{1,0:T(8,128)S(1)} %merge.6.mine_ref), channel_id=1, source_target_pairs={{0,3},{1,2},{2,1},{3,0},{4,7},{5,6},{6,5},{7,4},{8,11},{9,10},{10,... | collective-permute-start | bytes 30728 | tf_op jit(solution)/shard_map/ppermute | solution.py:53
  66.3 3.5 %collective-permute-start.19 = (f32[8,320]{1,0:T(8,128)S(1)}, f32[8,320]{1,0:T(8,128)S(1)}, u32[]{:S(2)}, u32[]{:S(2)}) collective-permute-start(f32[8,320]{1,0:T(8,128)S(1)} %merge.7.a_lse), channel_id=1, source_target_pairs={{0,16},{1,17},{2,18},{3,19},{4,20},{5,21},{6,22},{7,23},{8,24},{9,... | collective-permute-start | bytes 30728 | tf_op jit(solution)/shard_map/ppermute | solution.py:57
  77.5 6.3 %collective-permute-start.21 = (bf16[1280,768]{1,0:T(8,128)(2,1)S(1)}, bf16[1280,768]{1,0:T(8,128)(2,1)S(1)}, u32[]{:S(2)}, u32[]{:S(2)}) collective-permute-start(bf16[1280,768]{1,0:T(8,128)(2,1)S(1)} %get-tuple-element.51), channel_id=1, source_target_pairs={{0,16},{1,17},{2,18},{3,19},{4,20},{5,21},{6,22},{7,23},{8,24},{9,... | collective-permute-start | bytes 5898248 | tf_op jit(solution)/shard_map/ppermute | solution.py:57
  83.5 12.7 %collective-permute-start.20 = (bf16[1600,768]{1,0:T(8,128)(2,1)S(1)}, bf16[1600,768]{1,0:T(8,128)(2,1)S(1)}, u32[]{:S(2)}, u32[]{:S(2)}) collective-permute-start(bf16[1600,768]{1,0:T(8,128)(2,1)S(1)} %get-tuple-element.49), channel_id=1, source_target_pairs={{0,16},{1,17},{2,18},{3,19},{4,20},{5,21},{6,22},{7,23},{8,24},{9,... | collective-permute-start | bytes 7372808 | tf_op jit(solution)/shard_map/ppermute | solution.py:57
  84.1 9.3 %collective-permute-start.22 = (bf16[320,768]{1,0:T(8,128)(2,1)S(1)}, bf16[320,768]{1,0:T(8,128)(2,1)S(1)}, u32[]{:S(2)}, u32[]{:S(2)}) collective-permute-start(bf16[320,768]{1,0:T(8,128)(2,1)S(1)} %get-tuple-element.52), channel_id=1, source_target_pairs={{0,4},{1,5},{2,6},{3,7},{4,0},{5,1},{6,2},{7,3},{8,12},{9,13},{10,... | collective-permute-start | bytes 1474568 | tf_op jit(solution)/shard_map/ppermute | solution.py:53
  86.5 9.2 %collective-permute-start.23 = (bf16[320,768]{1,0:T(8,128)(2,1)S(1)}, bf16[320,768]{1,0:T(8,128)(2,1)S(1)}, u32[]{:S(2)}, u32[]{:S(2)}) collective-permute-start(bf16[320,768]{1,0:T(8,128)(2,1)S(1)} %get-tuple-element.53), channel_id=1, source_target_pairs={{0,32},{1,33},{2,34},{3,35},{4,36},{5,37},{6,38},{7,39},{8,40},{9,... | collective-permute-start | bytes 1474568 | tf_op jit(solution)/shard_map/ppermute | solution.py:53
  88.4 7.8 %collective-permute-start.24 = (bf16[320,768]{1,0:T(8,128)(2,1)S(1)}, bf16[320,768]{1,0:T(8,128)(2,1)S(1)}, u32[]{:S(2)}, u32[]{:S(2)}) collective-permute-start(bf16[320,768]{1,0:T(8,128)(2,1)S(1)} %get-tuple-element.54), channel_id=1, source_target_pairs={{0,3},{1,2},{2,1},{3,0},{4,7},{5,6},{6,5},{7,4},{8,11},{9,10},{10,... | collective-permute-start | bytes 1474568 | tf_op jit(solution)/shard_map/ppermute | solution.py:53
  91.3 12.1 %collective-permute-start.25 = (bf16[320,768]{1,0:T(8,128)(2,1)S(1)}, bf16[320,768]{1,0:T(8,128)(2,1)S(1)}, u32[]{:S(2)}, u32[]{:S(2)}) collective-permute-start(bf16[320,768]{1,0:T(8,128)(2,1)S(1)} %get-tuple-element.56), channel_id=1, source_target_pairs={{0,39},{1,38},{2,37},{3,36},{4,35},{5,34},{6,33},{7,32},{8,47},{9,... | collective-permute-start | bytes 1474568 | tf_op jit(solution)/shard_map/ppermute | solution.py:53
  96.8 19.7 %copy-start = (bf16[160,768]{1,0:T(8,128)(2,1)S(1)}, bf16[160,768]{1,0:T(8,128)(2,1)}, u32[]{:S(2)}) copy-start(bf16[160,768]{1,0:T(8,128)(2,1)} %images.1) | copy-start | bytes 737284
  96.8 19.7 %copy-start.1 = (bf16[160,768]{1,0:T(8,128)(2,1)S(1)}, bf16[160,768]{1,0:T(8,128)(2,1)}, u32[]{:S(2)}) copy-start(bf16[160,768]{1,0:T(8,128)(2,1)} %texts.1) | copy-start | bytes 737284
  96.8 10.4 %collective-permute-start.26 = (bf16[320,768]{1,0:T(8,128)(2,1)S(1)}, bf16[320,768]{1,0:T(8,128)(2,1)S(1)}, u32[]{:S(2)}, u32[]{:S(2)}) collective-permute-start(bf16[320,768]{1,0:T(8,128)(2,1)S(1)} %get-tuple-element.57), channel_id=1, source_target_pairs={{0,4},{1,5},{2,6},{3,7},{4,0},{5,1},{6,2},{7,3},{8,12},{9,13},{10,... | collective-permute-start | bytes 1474568 | tf_op jit(solution)/shard_map/ppermute | solution.py:53
  97.3 11.8 %collective-permute-start.27 = (bf16[320,768]{1,0:T(8,128)(2,1)S(1)}, bf16[320,768]{1,0:T(8,128)(2,1)S(1)}, u32[]{:S(2)}, u32[]{:S(2)}) collective-permute-start(bf16[320,768]{1,0:T(8,128)(2,1)S(1)} %get-tuple-element.58), channel_id=1, source_target_pairs={{0,32},{1,33},{2,34},{3,35},{4,36},{5,37},{6,38},{7,39},{8,40},{9,... | collective-permute-start | bytes 1474568 | tf_op jit(solution)/shard_map/ppermute | solution.py:53
  98.5 10.6 %collective-permute-start.28 = (bf16[320,768]{1,0:T(8,128)(2,1)S(1)}, bf16[320,768]{1,0:T(8,128)(2,1)S(1)}, u32[]{:S(2)}, u32[]{:S(2)}) collective-permute-start(bf16[320,768]{1,0:T(8,128)(2,1)S(1)} %get-tuple-element.59), channel_id=1, source_target_pairs={{0,3},{1,2},{2,1},{3,0},{4,7},{5,6},{6,5},{7,4},{8,11},{9,10},{10,... | collective-permute-start | bytes 1474568 | tf_op jit(solution)/shard_map/ppermute | solution.py:53
  109.4 7.1 %collective-permute-start.29 = (f32[160,768]{1,0:T(8,128)S(1)}, f32[160,768]{1,0:T(8,128)S(1)}, u32[]{:S(2)}, u32[]{:S(2)}) collective-permute-start(f32[160,768]{1,0:T(8,128)S(1)} %slice.9), channel_id=1, source_target_pairs={{0,16},{1,17},{2,18},{3,19},{4,20},{5,21},{6,22},{7,23},{8,24},{9,... | collective-permute-start | bytes 1474568 | tf_op jit(solution)/shard_map/ppermute | solution.py:57

commit v15 on v12

--- a/solution.py
+++ b/solution.py
@@ -488,8 +488,9 @@
     ga_lo = last_call(w, b_blocks)
     p0, p1, p2, p4 = near_call(ga_lo, got_lo, from_xy, from_yz, from_xz)
     wide = lambda a: a.astype(jnp.float32)
-    total = p0 + wide(from_xyz) + wide(to_cube(p1, 1)) + wide(to_cube(p2, 2)) + wide(to_cube(p4, 4))
-    kept, sent = total[:rows], total[rows:]
+    parts = (p0, from_xyz, to_cube(p1, 1), to_cube(p2, 2), to_cube(p4, 4))
+    add = lambda cut: functools.reduce(jnp.add, [wide(a[cut]) for a in parts])
+    sent, kept = add(slice(rows, None)), add(slice(rows))
     got_sum = swap(sent)
     image_sum = jnp.where(first, kept, got_sum)
     text_sum = jnp.where(first, got_sum, kept)

time: 114 us -> 116 us (1.018)
  other arithmetic: 1.34 us -> 3.11 us
where the time goes in v15:
time: 116 us; the launch traced here: 115 us
  starting transfers between devices  37.5 us (32%)
  Pallas kernels  36.8 us (32%)
  waiting for transfers between devices  36.7 us (32%)
  other arithmetic  3.11 us (3%)
    ppermute x17, starting transfers between devices, to_cube(): return lax.ppermute(a, AXES, across(m))  31.8 us
    ppermute x17, waiting for transfers between devices, to_cube(): return lax.ppermute(a, AXES, across(m))  27.9 us
    pallas_call x1, Pallas kernels, scores_call(): pl.pallas_call(functools.partial(scores_kernel, scale), in_specs=[vmem_sp...  18.4 us
    ppermute x13, waiting for transfers between devices, swap(): return lax.ppermute(a, AXES, SWAP)  8.86 us
    pallas_call x1, Pallas kernels, weights_call(): pl.pallas_call(weights_kernel, in_specs=[smem_spec()] + [vmem_spec()] * 1...  7.64 us
    ppermute x13, starting transfers between devices, swap(): return lax.ppermute(a, AXES, SWAP)  5.71 us
    pallas_call x1, Pallas kernels, middle_call(): pl.pallas_call(middle_kernel, in_specs=[vmem_spec()] * 16, out_specs=[vme...  5.61 us
    pallas_call x1, Pallas kernels, last_call(): pl.pallas_call(last_kernel, in_specs=[vmem_spec()] * 8, out_specs=vmem_sp...  2.87 us
  transfers between devices with their start and end apart: 30, of which 21 were waited for; matrix products, arithmetic and copies ran while one was open for 0% of the time, Pallas kernels for 9%

profile of v15, /device:TPU:1, one launch (start us, length us, event | category | flops | bytes accessed | tf_op | source)
XLA Modules:
  0.0 114.9 jit_solution(6067287289535398061)
XLA Ops:
  0.6 1.5 %collective-permute-start = (bf16[160,768]{1,0:T(8,128)(2,1)}, bf16[160,768]{1,0:T(8,128)(2,1)S(1)}, u32[]{:S(2)}, u32[]{:S(2)}) collective-permute-start(bf16[160,768]{1,0:T(8,128)(2,1)} %images.1), channel_id=1, source_target_pairs={{0,16},{1,17},{2,18},{3,19},{4,20},{5,21},{6,22},{7,23},{8,24},{9,... | collective-permute-start | bytes 737288 | tf_op jit(solution)/shard_map/ppermute | solution.py:57
  2.1 0.1 collective-permute-start.1
  2.2 1.1 load.1
  3.3 0.2 collective-permute-done.got_images
  3.5 0.4 collective-permute-done.1.got_texts
  3.9 0.1 own.1
  3.9 2.6 %collective-permute-start.2 = (bf16[320,768]{1,0:T(8,128)(2,1)S(1)}, bf16[320,768]{1,0:T(8,128)(2,1)S(1)}, u32[]{:S(2)}, u32[]{:S(2)}) collective-permute-start(bf16[320,768]{1,0:T(8,128)(2,1)S(1)} %get-tuple-element.34.refs_0_), channel_id=1, source_target_pairs={{0,4},{1,5},{2,6},{3,7},{4,0},{5,1},{6,2},{7,3},{8,12},{9,13},{10,... | collective-permute-start | bytes 1474568 | tf_op jit(solution)/shard_map/ppermute | solution.py:53
  6.6 1.3 %collective-permute-start.3 = (bf16[320,768]{1,0:T(8,128)(2,1)S(1)}, bf16[320,768]{1,0:T(8,128)(2,1)S(1)}, u32[]{:S(2)}, u32[]{:S(2)}) collective-permute-start(bf16[320,768]{1,0:T(8,128)(2,1)S(1)} %get-tuple-element.34.refs_0_), channel_id=1, source_target_pairs={{0,96},{1,97},{2,98},{3,99},{4,100},{5,101},{6,102},{7,103},{8,104... | collective-permute-start | bytes 1474568 | tf_op jit(solution)/shard_map/ppermute | solution.py:53
  7.9 3.8 %collective-permute-start.4 = (bf16[320,768]{1,0:T(8,128)(2,1)S(1)}, bf16[320,768]{1,0:T(8,128)(2,1)S(1)}, u32[]{:S(2)}, u32[]{:S(2)}) collective-permute-start(bf16[320,768]{1,0:T(8,128)(2,1)S(1)} %get-tuple-element.34.refs_0_), channel_id=1, source_target_pairs={{0,1},{1,0},{2,3},{3,2},{4,5},{5,4},{6,7},{7,6},{8,9},{9,8},{10,11... | collective-permute-start | bytes 1474568 | tf_op jit(solution)/shard_map/ppermute | solution.py:53
  11.6 1.6 %collective-permute-done.2.b0.refs_1_ = bf16[320,768]{1,0:T(8,128)(2,1)S(1)} collective-permute-done((bf16[320,768]{1,0:T(8,128)(2,1)S(1)}, bf16[320,768]{1,0:T(8,128)(2,1)S(1)}, u32[]{:S(2)}, u32[]{:S(2)}) %collective-permute-start.2) | collective-permute-done | bytes 491552 | tf_op jit(solution)/shard_map/ppermute | solution.py:53
  13.2 6.8 %collective-permute-start.8 = (bf16[320,768]{1,0:T(8,128)(2,1)S(1)}, bf16[320,768]{1,0:T(8,128)(2,1)S(1)}, u32[]{:S(2)}, u32[]{:S(2)}) collective-permute-start(bf16[320,768]{1,0:T(8,128)(2,1)S(1)} %get-tuple-element.34.refs_0_), channel_id=1, source_target_pairs={{0,101},{1,100},{2,103},{3,102},{4,97},{5,96},{6,99},{7,98},{8,109... | collective-permute-start | bytes 1474568 | tf_op jit(solution)/shard_map/ppermute | solution.py:53
  19.9 0.0 collective-permute-start.6
  19.9 0.0 collective-permute-done.3.b1.refs_2_
  19.9 0.2 collective-permute-start.5
  20.1 0.0 collective-permute-done.4.b2.refs_3_
  20.2 0.5 collective-permute-start.7
  20.6 0.1 join.1
  20.7 0.1 collective-permute-start.12
  20.8 5.5 %collective-permute-done.8.refs_7_ = bf16[320,768]{1,0:T(8,128)(2,1)S(1)} collective-permute-done((bf16[320,768]{1,0:T(8,128)(2,1)S(1)}, bf16[320,768]{1,0:T(8,128)(2,1)S(1)}, u32[]{:S(2)}, u32[]{:S(2)}) %collective-permute-start.8) | collective-permute-done | bytes 491552 | tf_op jit(solution)/shard_map/ppermute | solution.py:53
  26.3 5.1 %collective-permute-done.6.refs_5_ = bf16[320,768]{1,0:T(8,128)(2,1)S(1)} collective-permute-done((bf16[320,768]{1,0:T(8,128)(2,1)S(1)}, bf16[320,768]{1,0:T(8,128)(2,1)S(1)}, u32[]{:S(2)}, u32[]{:S(2)}) %collective-permute-start.6) | collective-permute-done | bytes 491552 | tf_op jit(solution)/shard_map/ppermute | solution.py:53
  31.4 0.0 collective-permute-start.9
  31.4 0.2 collective-permute-done.5.refs_4_
  31.7 0.3 collective-permute-start.10
  31.9 0.0 collective-permute-done.7.refs_6_
  31.9 0.2 collective-permute-start.11
  32.2 1.1 collective-permute-done.9.refs_14_.refs_6_
  33.3 0.7 collective-permute-done.10.refs_12_.refs_4_
  34.0 0.7 collective-permute-done.11.refs_11_.refs_3_
  34.7 0.1 collective-permute-start.14
  34.8 1.7 %collective-permute-done.14.refs_13_.refs_5_ = bf16[320,768]{1,0:T(8,128)(2,1)S(1)} collective-permute-done((bf16[320,768]{1,0:T(8,128)(2,1)S(1)}, bf16[320,768]{1,0:T(8,128)(2,1)S(1)}, u32[]{:S(2)}, u32[]{:S(2)}) %collective-permute-start.14) | collective-permute-done | bytes 491552 | tf_op jit(solution)/shard_map/ppermute | solution.py:57
  36.6 18.4 %scores.1 = (f32[2,1280,1280]{2,1,0:T(8,128)S(1)}, f32[8,320]{1,0:T(8,128)S(1)}, f32[8,320]{1,0:T(8,128)S(1)}, s32[2]{0:T(128)S(1)}) custom-call(bf16[320,768]{1,0:T(8,128)(2,1)S(1)} %get-tuple-element.34.refs_0_, bf16[320,768]{1,0:T(8,128)(2,1)S(1)} %collective-permute-done.2.b0.refs_1_, bf16[320,768]{1,0:T(8,128)(2,1)S(1)} %collective-permute-done.3.b1.refs_2_, ...), custom_call_target="tpu_custom_call" | custom-call | flops 5033164800 | tf_op jit(solution)/shard_map/scores/pallas_call | solution.py:264
  55.0 0.2 collective-permute-start.15
  55.2 1.0 collective-permute-done.15.got_ref
  56.3 2.1 %collective-permute-start.16 = (f32[8,320]{1,0:T(8,128)S(1)}, f32[8,320]{1,0:T(8,128)S(1)}, u32[]{:S(2)}, u32[]{:S(2)}) collective-permute-start(f32[8,320]{1,0:T(8,128)S(1)} %merge.4.mine_ref), channel_id=1, source_target_pairs={{0,4},{1,5},{2,6},{3,7},{4,0},{5,1},{6,2},{7,3},{8,12},{9,13},{10,... | collective-permute-start | bytes 30728 | tf_op jit(solution)/shard_map/ppermute | solution.py:53
  58.4 1.7 %collective-permute-done.16.got_ref = f32[8,320]{1,0:T(8,128)S(1)} collective-permute-done((f32[8,320]{1,0:T(8,128)S(1)}, f32[8,320]{1,0:T(8,128)S(1)}, u32[]{:S(2)}, u32[]{:S(2)}) %collective-permute-start.16) | collective-permute-done | bytes 10272 | tf_op jit(solution)/shard_map/ppermute | solution.py:53
  60.2 0.6 collective-permute-start.17
  60.7 2.1 %collective-permute-done.17.got_ref = f32[8,320]{1,0:T(8,128)S(1)} collective-permute-done((f32[8,320]{1,0:T(8,128)S(1)}, f32[8,320]{1,0:T(8,128)S(1)}, u32[]{:S(2)}, u32[]{:S(2)}) %collective-permute-start.17) | collective-permute-done | bytes 10272 | tf_op jit(solution)/shard_map/ppermute | solution.py:53
  62.8 2.8 %collective-permute-start.18 = (f32[8,320]{1,0:T(8,128)S(1)}, f32[8,320]{1,0:T(8,128)S(1)}, u32[]{:S(2)}, u32[]{:S(2)}) collective-permute-start(f32[8,320]{1,0:T(8,128)S(1)} %merge.6.mine_ref), channel_id=1, source_target_pairs={{0,1},{1,0},{2,3},{3,2},{4,5},{5,4},{6,7},{7,6},{8,9},{9,8},{10,11... | collective-permute-start | bytes 30728 | tf_op jit(solution)/shard_map/ppermute | solution.py:53
  65.6 1.1 collective-permute-done.18.got_ref
  66.7 2.5 %collective-permute-start.19 = (f32[8,320]{1,0:T(8,128)S(1)}, f32[8,320]{1,0:T(8,128)S(1)}, u32[]{:S(2)}, u32[]{:S(2)}) collective-permute-start(f32[8,320]{1,0:T(8,128)S(1)} %merge.7.a_lse), channel_id=1, source_target_pairs={{0,16},{1,17},{2,18},{3,19},{4,20},{5,21},{6,22},{7,23},{8,24},{9,... | collective-permute-start | bytes 30728 | tf_op jit(solution)/shard_map/ppermute | solution.py:57
  69.2 0.8 collective-permute-done.19.b_lse
  70.0 7.6 %weights.1 = (bf16[2,1280,1280]{2,1,0:T(8,128)(2,1)S(1)}, bf16[1280,768]{1,0:T(8,128)(2,1)S(1)}) custom-call(s32[2]{0:T(128)S(1)} %get-tuple-element.44.flags, f32[2,1280,1280]{2,1,0:T(8,128)S(1)} %get-tuple-element.45.e_ref, f32[8,320]{1,0:T(8,128)S(1)} %merge.7.a_lse, f32[8,320]{1,0:T(8,128)S(1)} %collective-permute-done.19.b_lse, ...), custom_call_target="tpu_custom_call" | custom-call | flops 2516582400 | bytes 19660800 | tf_op jit(solution)/shard_map/weights/pallas_call | solution.py:337
  77.6 0.4 collective-permute-start.21
  78.1 5.6 %middle.1 = (f32[1280,768]{1,0:T(8,128)S(1)}, bf16[1600,768]{1,0:T(8,128)(2,1)S(1)}) custom-call(bf16[2,1280,1280]{2,1,0:T(8,128)(2,1)S(1)} %get-tuple-element.48.w_ref, bf16[320,768]{1,0:T(8,128)(2,1)S(1)} %get-tuple-element.34.refs_0_, bf16[320,768]{1,0:T(8,128)(2,1)S(1)} %collective-permute-done.2.b0.refs_1_, ...), custom_call_target="tpu_custom_call" | custom-call | flops 5033164800 | tf_op jit(solution)/shard_map/middle/pallas_call | solution.py:370
  83.7 0.2 collective-permute-start.20
  83.9 0.3 far.1
  84.3 2.1 %collective-permute-start.22 = (bf16[320,768]{1,0:T(8,128)(2,1)S(1)}, bf16[320,768]{1,0:T(8,128)(2,1)S(1)}, u32[]{:S(2)}, u32[]{:S(2)}) collective-permute-start(bf16[320,768]{1,0:T(8,128)(2,1)S(1)} %get-tuple-element.52), channel_id=1, source_target_pairs={{0,4},{1,5},{2,6},{3,7},{4,0},{5,1},{6,2},{7,3},{8,12},{9,13},{10,... | collective-permute-start | bytes 1474568 | tf_op jit(solution)/shard_map/ppermute | solution.py:53
  86.4 3.0 %collective-permute-start.24 = (bf16[320,768]{1,0:T(8,128)(2,1)S(1)}, bf16[320,768]{1,0:T(8,128)(2,1)S(1)}, u32[]{:S(2)}, u32[]{:S(2)}) collective-permute-start(bf16[320,768]{1,0:T(8,128)(2,1)S(1)} %get-tuple-element.54), channel_id=1, source_target_pairs={{0,1},{1,0},{2,3},{3,2},{4,5},{5,4},{6,7},{7,6},{8,9},{9,8},{10,11... | collective-permute-start | bytes 1474568 | tf_op jit(solution)/shard_map/ppermute | solution.py:53
  89.4 2.9 %last.1.ga_lo = f32[1280,768]{1,0:T(8,128)S(1)} custom-call(bf16[2,1280,1280]{2,1,0:T(8,128)(2,1)S(1)} %get-tuple-element.48.w_ref, bf16[320,768]{1,0:T(8,128)(2,1)S(1)} %get-tuple-element.35.refs_8_.refs_0_, bf16[480,768]{1,0:T(8,128)(2,1)S(1)} %collective-permute-done.12.refs_9_.refs_1_, bf16[480,768]{1,0:T(8,128)(2,1)S(1)} %collective-permute-done.13.refs_10_.refs_2_, ...), custom_call_target="tpu_custom_call" | custom-call | flops 2516582400 | tf_op jit(solution)/shard_map/last/pallas_call | solution.py:415
  92.3 0.0 copy-start
  92.3 0.0 copy-start.1
  92.3 1.3 %collective-permute-start.25 = (bf16[320,768]{1,0:T(8,128)(2,1)S(1)}, bf16[320,768]{1,0:T(8,128)(2,1)S(1)}, u32[]{:S(2)}, u32[]{:S(2)}) collective-permute-start(bf16[320,768]{1,0:T(8,128)(2,1)S(1)} %get-tuple-element.56), channel_id=1, source_target_pairs={{0,101},{1,100},{2,103},{3,102},{4,97},{5,96},{6,99},{7,98},{8,109... | collective-permute-start | bytes 1474568 | tf_op jit(solution)/shard_map/ppermute | solution.py:53
  93.6 0.8 collective-permute-done.23.r_yz
  94.3 1.3 %collective-permute-done.24.r_xz = bf16[320,768]{1,0:T(8,128)(2,1)S(1)} collective-permute-done((bf16[320,768]{1,0:T(8,128)(2,1)S(1)}, bf16[320,768]{1,0:T(8,128)(2,1)S(1)}, u32[]{:S(2)}, u32[]{:S(2)}) %collective-permute-start.24) | collective-permute-done | bytes 491552 | tf_op jit(solution)/shard_map/ppermute | solution.py:53
  95.6 0.6 near.1
  96.2 0.7 collective-permute-start.26
  96.9 1.5 %collective-permute-start.27 = (bf16[320,768]{1,0:T(8,128)(2,1)S(1)}, bf16[320,768]{1,0:T(8,128)(2,1)S(1)}, u32[]{:S(2)}, u32[]{:S(2)}) collective-permute-start(bf16[320,768]{1,0:T(8,128)(2,1)S(1)} %get-tuple-element.58), channel_id=1, source_target_pairs={{0,96},{1,97},{2,98},{3,99},{4,100},{5,101},{6,102},{7,103},{8,104... | collective-permute-start | bytes 1474568 | tf_op jit(solution)/shard_map/ppermute | solution.py:53
  98.3 2.7 %collective-permute-start.28 = (bf16[320,768]{1,0:T(8,128)(2,1)S(1)}, bf16[320,768]{1,0:T(8,128)(2,1)S(1)}, u32[]{:S(2)}, u32[]{:S(2)}) collective-permute-start(bf16[320,768]{1,0:T(8,128)(2,1)S(1)} %get-tuple-element.59), channel_id=1, source_target_pairs={{0,1},{1,0},{2,3},{3,2},{4,5},{5,4},{6,7},{7,6},{8,9},{9,8},{10,11... | collective-permute-start | bytes 1474568 | tf_op jit(solution)/shard_map/ppermute | solution.py:53
  101.0 3.4 %collective-permute-done.25 = bf16[320,768]{1,0:T(8,128)(2,1)S(1)} collective-permute-done((bf16[320,768]{1,0:T(8,128)(2,1)S(1)}, bf16[320,768]{1,0:T(8,128)(2,1)S(1)}, u32[]{:S(2)}, u32[]{:S(2)}) %collective-permute-start.25) | collective-permute-done | bytes 491552 | tf_op jit(solution)/shard_map/ppermute | solution.py:53
  104.4 3.3 %collective-permute-done.26 = bf16[320,768]{1,0:T(8,128)(2,1)S(1)} collective-permute-done((bf16[320,768]{1,0:T(8,128)(2,1)S(1)}, bf16[320,768]{1,0:T(8,128)(2,1)S(1)}, u32[]{:S(2)}, u32[]{:S(2)}) %collective-permute-start.26) | collective-permute-done | bytes 491552 | tf_op jit(solution)/shard_map/ppermute | solution.py:53
  107.7 1.8 %collective-permute-done.28 = bf16[320,768]{1,0:T(8,128)(2,1)S(1)} collective-permute-done((bf16[320,768]{1,0:T(8,128)(2,1)S(1)}, bf16[320,768]{1,0:T(8,128)(2,1)S(1)}, u32[]{:S(2)}, u32[]{:S(2)}) %collective-permute-start.28) | collective-permute-done | bytes 491552 | tf_op jit(solution)/shard_map/ppermute | solution.py:53
  109.5 0.9 convert_add_fusion
  110.5 2.2 %collective-permute-done.29 = f32[160,768]{1,0:T(8,128)} collective-permute-done((f32[160,768]{1,0:T(8,128)}, f32[160,768]{1,0:T(8,128)}, u32[]{:S(2)}, u32[]{:S(2)}) %collective-permute-start.29) | collective-permute-done | bytes 491552 | tf_op jit(solution)/shard_map/ppermute | solution.py:57
  112.7 2.2 %convert_subtract_fusion = (f32[160,768]{1,0:T(8,128)}, f32[160,768]{1,0:T(8,128)}) fusion(bf16[160,768]{1,0:T(8,128)(2,1)S(1)} %copy-done, f32[160,768]{1,0:T(8,128)} %collective-permute-done.29, pred[]{:T(512)S(6)} %eq.3, bf16[320,768]{1,0:T(8,128)(2,1)S(1)} %collective-permute-done.28, bf16[320,768]{1,0:T(8,128)(2,1)S(1)} %collective-permute-done.27, ...), kind=kLoop, calls=%fused_computation | loop fusion | flops 1720320 | bytes 3440641 | tf_op jit(solution)/shard_map/sub | solution.py:497
  (15 shorter events, 0.1 us)
Async XLA Ops:
  0.6 2.9 %collective-permute-start = (bf16[160,768]{1,0:T(8,128)(2,1)}, bf16[160,768]{1,0:T(8,128)(2,1)S(1)}, u32[]{:S(2)}, u32[]{:S(2)}) collective-permute-start(bf16[160,768]{1,0:T(8,128)(2,1)} %images.1), channel_id=1, source_target_pairs={{0,16},{1,17},{2,18},{3,19},{4,20},{5,21},{6,22},{7,23},{8,24},{9,... | collective-permute-start | bytes 737288 | tf_op jit(solution)/shard_map/ppermute | solution.py:57
  2.1 1.7 %collective-permute-start.1 = (bf16[160,768]{1,0:T(8,128)(2,1)}, bf16[160,768]{1,0:T(8,128)(2,1)S(1)}, u32[]{:S(2)}, u32[]{:S(2)}) collective-permute-start(bf16[160,768]{1,0:T(8,128)(2,1)} %texts.1), channel_id=1, source_target_pairs={{0,16},{1,17},{2,18},{3,19},{4,20},{5,21},{6,22},{7,23},{8,24},{9,... | collective-permute-start | bytes 737288 | tf_op jit(solution)/shard_map/ppermute | solution.py:57
  3.9 9.3 %collective-permute-start.2 = (bf16[320,768]{1,0:T(8,128)(2,1)S(1)}, bf16[320,768]{1,0:T(8,128)(2,1)S(1)}, u32[]{:S(2)}, u32[]{:S(2)}) collective-permute-start(bf16[320,768]{1,0:T(8,128)(2,1)S(1)} %get-tuple-element.34.refs_0_), channel_id=1, source_target_pairs={{0,4},{1,5},{2,6},{3,7},{4,0},{5,1},{6,2},{7,3},{8,12},{9,13},{10,... | collective-permute-start | bytes 1474568 | tf_op jit(solution)/shard_map/ppermute | solution.py:53
  6.6 13.4 %collective-permute-start.3 = (bf16[320,768]{1,0:T(8,128)(2,1)S(1)}, bf16[320,768]{1,0:T(8,128)(2,1)S(1)}, u32[]{:S(2)}, u32[]{:S(2)}) collective-permute-start(bf16[320,768]{1,0:T(8,128)(2,1)S(1)} %get-tuple-element.34.refs_0_), channel_id=1, source_target_pairs={{0,96},{1,97},{2,98},{3,99},{4,100},{5,101},{6,102},{7,103},{8,104... | collective-permute-start | bytes 1474568 | tf_op jit(solution)/shard_map/ppermute | solution.py:53
  7.9 12.3 %collective-permute-start.4 = (bf16[320,768]{1,0:T(8,128)(2,1)S(1)}, bf16[320,768]{1,0:T(8,128)(2,1)S(1)}, u32[]{:S(2)}, u32[]{:S(2)}) collective-permute-start(bf16[320,768]{1,0:T(8,128)(2,1)S(1)} %get-tuple-element.34.refs_0_), channel_id=1, source_target_pairs={{0,1},{1,0},{2,3},{3,2},{4,5},{5,4},{6,7},{7,6},{8,9},{9,8},{10,11... | collective-permute-start | bytes 1474568 | tf_op jit(solution)/shard_map/ppermute | solution.py:53
  13.2 13.1 %collective-permute-start.8 = (bf16[320,768]{1,0:T(8,128)(2,1)S(1)}, bf16[320,768]{1,0:T(8,128)(2,1)S(1)}, u32[]{:S(2)}, u32[]{:S(2)}) collective-permute-start(bf16[320,768]{1,0:T(8,128)(2,1)S(1)} %get-tuple-element.34.refs_0_), channel_id=1, source_target_pairs={{0,101},{1,100},{2,103},{3,102},{4,97},{5,96},{6,99},{7,98},{8,109... | collective-permute-start | bytes 1474568 | tf_op jit(solution)/shard_map/ppermute | solution.py:53
  19.9 11.5 %collective-permute-start.6 = (bf16[320,768]{1,0:T(8,128)(2,1)S(1)}, bf16[320,768]{1,0:T(8,128)(2,1)S(1)}, u32[]{:S(2)}, u32[]{:S(2)}) collective-permute-start(bf16[320,768]{1,0:T(8,128)(2,1)S(1)} %collective-permute-done.2.b0.refs_1_), channel_id=1, source_target_pairs={{0,1},{1,0},{2,3},{3,2},{4,5},{5,4},{6,7},{7,6},{8,9},{9,8},{10,11... | collective-permute-start | bytes 1474568 | tf_op jit(solution)/shard_map/ppermute | solution.py:53
  19.9 11.7 %collective-permute-start.5 = (bf16[320,768]{1,0:T(8,128)(2,1)S(1)}, bf16[320,768]{1,0:T(8,128)(2,1)S(1)}, u32[]{:S(2)}, u32[]{:S(2)}) collective-permute-start(bf16[320,768]{1,0:T(8,128)(2,1)S(1)} %collective-permute-done.3.b1.refs_2_), channel_id=1, source_target_pairs={{0,4},{1,5},{2,6},{3,7},{4,0},{5,1},{6,2},{7,3},{8,12},{9,13},{10,... | collective-permute-start | bytes 1474568 | tf_op jit(solution)/shard_map/ppermute | solution.py:53
  20.2 11.8 %collective-permute-start.7 = (bf16[320,768]{1,0:T(8,128)(2,1)S(1)}, bf16[320,768]{1,0:T(8,128)(2,1)S(1)}, u32[]{:S(2)}, u32[]{:S(2)}) collective-permute-start(bf16[320,768]{1,0:T(8,128)(2,1)S(1)} %collective-permute-done.4.b2.refs_3_), channel_id=1, source_target_pairs={{0,96},{1,97},{2,98},{3,99},{4,100},{5,101},{6,102},{7,103},{8,104... | collective-permute-start | bytes 1474568 | tf_op jit(solution)/shard_map/ppermute | solution.py:53
  20.7 11.5 %collective-permute-start.12 = (bf16[480,768]{1,0:T(8,128)(2,1)S(1)}, bf16[480,768]{1,0:T(8,128)(2,1)S(1)}, u32[]{:S(2)}, u32[]{:S(2)}) collective-permute-start(bf16[480,768]{1,0:T(8,128)(2,1)S(1)} %get-tuple-element.36), channel_id=1, source_target_pairs={{0,16},{1,17},{2,18},{3,19},{4,20},{5,21},{6,22},{7,23},{8,24},{9,... | collective-permute-start | bytes 2211848 | tf_op jit(solution)/shard_map/ppermute | solution.py:57
  26.3 5.9 %collective-permute-start.13 = (bf16[480,768]{1,0:T(8,128)(2,1)S(1)}, bf16[480,768]{1,0:T(8,128)(2,1)S(1)}, u32[]{:S(2)}, u32[]{:S(2)}) collective-permute-start(bf16[480,768]{1,0:T(8,128)(2,1)S(1)} %get-tuple-element.37), channel_id=1, source_target_pairs={{0,16},{1,17},{2,18},{3,19},{4,20},{5,21},{6,22},{7,23},{8,24},{9,... | collective-permute-start | bytes 2211848 | tf_op jit(solution)/shard_map/ppermute | solution.py:57
  31.4 1.9 %collective-permute-start.9 = (bf16[320,768]{1,0:T(8,128)(2,1)S(1)}, bf16[320,768]{1,0:T(8,128)(2,1)S(1)}, u32[]{:S(2)}, u32[]{:S(2)}) collective-permute-start(bf16[320,768]{1,0:T(8,128)(2,1)S(1)} %collective-permute-done.8.refs_7_), channel_id=1, source_target_pairs={{0,16},{1,17},{2,18},{3,19},{4,20},{5,21},{6,22},{7,23},{8,24},{9,... | collective-permute-start | bytes 1474568 | tf_op jit(solution)/shard_map/ppermute | solution.py:57
  31.7 2.3 %collective-permute-start.10 = (bf16[320,768]{1,0:T(8,128)(2,1)S(1)}, bf16[320,768]{1,0:T(8,128)(2,1)S(1)}, u32[]{:S(2)}, u32[]{:S(2)}) collective-permute-start(bf16[320,768]{1,0:T(8,128)(2,1)S(1)} %collective-permute-done.6.refs_5_), channel_id=1, source_target_pairs={{0,16},{1,17},{2,18},{3,19},{4,20},{5,21},{6,22},{7,23},{8,24},{9,... | collective-permute-start | bytes 1474568 | tf_op jit(solution)/shard_map/ppermute | solution.py:57
  31.9 2.8 %collective-permute-start.11 = (bf16[320,768]{1,0:T(8,128)(2,1)S(1)}, bf16[320,768]{1,0:T(8,128)(2,1)S(1)}, u32[]{:S(2)}, u32[]{:S(2)}) collective-permute-start(bf16[320,768]{1,0:T(8,128)(2,1)S(1)} %collective-permute-done.5.refs_4_), channel_id=1, source_target_pairs={{0,16},{1,17},{2,18},{3,19},{4,20},{5,21},{6,22},{7,23},{8,24},{9,... | collective-permute-start | bytes 1474568 | tf_op jit(solution)/shard_map/ppermute | solution.py:57
  34.7 1.9 %collective-permute-start.14 = (bf16[320,768]{1,0:T(8,128)(2,1)S(1)}, bf16[320,768]{1,0:T(8,128)(2,1)S(1)}, u32[]{:S(2)}, u32[]{:S(2)}) collective-permute-start(bf16[320,768]{1,0:T(8,128)(2,1)S(1)} %collective-permute-done.7.refs_6_), channel_id=1, source_target_pairs={{0,16},{1,17},{2,18},{3,19},{4,20},{5,21},{6,22},{7,23},{8,24},{9,... | collective-permute-start | bytes 1474568 | tf_op jit(solution)/shard_map/ppermute | solution.py:57
  55.0 1.3 %collective-permute-start.15 = (f32[8,320]{1,0:T(8,128)S(1)}, f32[8,320]{1,0:T(8,128)S(1)}, u32[]{:S(2)}, u32[]{:S(2)}) collective-permute-start(f32[8,320]{1,0:T(8,128)S(1)} %get-tuple-element.47), channel_id=1, source_target_pairs={{0,16},{1,17},{2,18},{3,19},{4,20},{5,21},{6,22},{7,23},{8,24},{9,... | collective-permute-start | bytes 30728 | tf_op jit(solution)/shard_map/ppermute | solution.py:57
  56.3 3.8 %collective-permute-start.16 = (f32[8,320]{1,0:T(8,128)S(1)}, f32[8,320]{1,0:T(8,128)S(1)}, u32[]{:S(2)}, u32[]{:S(2)}) collective-permute-start(f32[8,320]{1,0:T(8,128)S(1)} %merge.4.mine_ref), channel_id=1, source_target_pairs={{0,4},{1,5},{2,6},{3,7},{4,0},{5,1},{6,2},{7,3},{8,12},{9,13},{10,... | collective-permute-start | bytes 30728 | tf_op jit(solution)/shard_map/ppermute | solution.py:53
  60.2 2.6 %collective-permute-start.17 = (f32[8,320]{1,0:T(8,128)S(1)}, f32[8,320]{1,0:T(8,128)S(1)}, u32[]{:S(2)}, u32[]{:S(2)}) collective-permute-start(f32[8,320]{1,0:T(8,128)S(1)} %merge.5.mine_ref), channel_id=1, source_target_pairs={{0,96},{1,97},{2,98},{3,99},{4,100},{5,101},{6,102},{7,103},{8,104... | collective-permute-start | bytes 30728 | tf_op jit(solution)/shard_map/ppermute | solution.py:53
  62.8 3.8 %collective-permute-start.18 = (f32[8,320]{1,0:T(8,128)S(1)}, f32[8,320]{1,0:T(8,128)S(1)}, u32[]{:S(2)}, u32[]{:S(2)}) collective-permute-start(f32[8,320]{1,0:T(8,128)S(1)} %merge.6.mine_ref), channel_id=1, source_target_pairs={{0,1},{1,0},{2,3},{3,2},{4,5},{5,4},{6,7},{7,6},{8,9},{9,8},{10,11... | collective-permute-start | bytes 30728 | tf_op jit(solution)/shard_map/ppermute | solution.py:53
  66.7 3.3 %collective-permute-start.19 = (f32[8,320]{1,0:T(8,128)S(1)}, f32[8,320]{1,0:T(8,128)S(1)}, u32[]{:S(2)}, u32[]{:S(2)}) collective-permute-start(f32[8,320]{1,0:T(8,128)S(1)} %merge.7.a_lse), channel_id=1, source_target_pairs={{0,16},{1,17},{2,18},{3,19},{4,20},{5,21},{6,22},{7,23},{8,24},{9,... | collective-permute-start | bytes 30728 | tf_op jit(solution)/shard_map/ppermute | solution.py:57
  77.6 6.3 %collective-permute-start.21 = (bf16[1280,768]{1,0:T(8,128)(2,1)S(1)}, bf16[1280,768]{1,0:T(8,128)(2,1)S(1)}, u32[]{:S(2)}, u32[]{:S(2)}) collective-permute-start(bf16[1280,768]{1,0:T(8,128)(2,1)S(1)} %get-tuple-element.51), channel_id=1, source_target_pairs={{0,16},{1,17},{2,18},{3,19},{4,20},{5,21},{6,22},{7,23},{8,24},{9,... | collective-permute-start | bytes 5898248 | tf_op jit(solution)/shard_map/ppermute | solution.py:57
  83.7 11.9 %collective-permute-start.20 = (bf16[1600,768]{1,0:T(8,128)(2,1)S(1)}, bf16[1600,768]{1,0:T(8,128)(2,1)S(1)}, u32[]{:S(2)}, u32[]{:S(2)}) collective-permute-start(bf16[1600,768]{1,0:T(8,128)(2,1)S(1)} %get-tuple-element.49), channel_id=1, source_target_pairs={{0,16},{1,17},{2,18},{3,19},{4,20},{5,21},{6,22},{7,23},{8,24},{9,... | collective-permute-start | bytes 7372808 | tf_op jit(solution)/shard_map/ppermute | solution.py:57
  84.3 9.3 %collective-permute-start.22 = (bf16[320,768]{1,0:T(8,128)(2,1)S(1)}, bf16[320,768]{1,0:T(8,128)(2,1)S(1)}, u32[]{:S(2)}, u32[]{:S(2)}) collective-permute-start(bf16[320,768]{1,0:T(8,128)(2,1)S(1)} %get-tuple-element.52), channel_id=1, source_target_pairs={{0,4},{1,5},{2,6},{3,7},{4,0},{5,1},{6,2},{7,3},{8,12},{9,13},{10,... | collective-permute-start | bytes 1474568 | tf_op jit(solution)/shard_map/ppermute | solution.py:53
  86.4 8.0 %collective-permute-start.23 = (bf16[320,768]{1,0:T(8,128)(2,1)S(1)}, bf16[320,768]{1,0:T(8,128)(2,1)S(1)}, u32[]{:S(2)}, u32[]{:S(2)}) collective-permute-start(bf16[320,768]{1,0:T(8,128)(2,1)S(1)} %get-tuple-element.53), channel_id=1, source_target_pairs={{0,96},{1,97},{2,98},{3,99},{4,100},{5,101},{6,102},{7,103},{8,104... | collective-permute-start | bytes 1474568 | tf_op jit(solution)/shard_map/ppermute | solution.py:53
  86.4 9.2 %collective-permute-start.24 = (bf16[320,768]{1,0:T(8,128)(2,1)S(1)}, bf16[320,768]{1,0:T(8,128)(2,1)S(1)}, u32[]{:S(2)}, u32[]{:S(2)}) collective-permute-start(bf16[320,768]{1,0:T(8,128)(2,1)S(1)} %get-tuple-element.54), channel_id=1, source_target_pairs={{0,1},{1,0},{2,3},{3,2},{4,5},{5,4},{6,7},{7,6},{8,9},{9,8},{10,11... | collective-permute-start | bytes 1474568 | tf_op jit(solution)/shard_map/ppermute | solution.py:53
  92.3 20.4 %copy-start = (bf16[160,768]{1,0:T(8,128)(2,1)S(1)}, bf16[160,768]{1,0:T(8,128)(2,1)}, u32[]{:S(2)}) copy-start(bf16[160,768]{1,0:T(8,128)(2,1)} %images.1) | copy-start | bytes 737284
  92.3 20.4 %copy-start.1 = (bf16[160,768]{1,0:T(8,128)(2,1)S(1)}, bf16[160,768]{1,0:T(8,128)(2,1)}, u32[]{:S(2)}) copy-start(bf16[160,768]{1,0:T(8,128)(2,1)} %texts.1) | copy-start | bytes 737284
  92.3 12.1 %collective-permute-start.25 = (bf16[320,768]{1,0:T(8,128)(2,1)S(1)}, bf16[320,768]{1,0:T(8,128)(2,1)S(1)}, u32[]{:S(2)}, u32[]{:S(2)}) collective-permute-start(bf16[320,768]{1,0:T(8,128)(2,1)S(1)} %get-tuple-element.56), channel_id=1, source_target_pairs={{0,101},{1,100},{2,103},{3,102},{4,97},{5,96},{6,99},{7,98},{8,109... | collective-permute-start | bytes 1474568 | tf_op jit(solution)/shard_map/ppermute | solution.py:53
  96.2 11.6 %collective-permute-start.26 = (bf16[320,768]{1,0:T(8,128)(2,1)S(1)}, bf16[320,768]{1,0:T(8,128)(2,1)S(1)}, u32[]{:S(2)}, u32[]{:S(2)}) collective-permute-start(bf16[320,768]{1,0:T(8,128)(2,1)S(1)} %get-tuple-element.57), channel_id=1, source_target_pairs={{0,4},{1,5},{2,6},{3,7},{4,0},{5,1},{6,2},{7,3},{8,12},{9,13},{10,... | collective-permute-start | bytes 1474568 | tf_op jit(solution)/shard_map/ppermute | solution.py:53
  96.9 10.9 %collective-permute-start.27 = (bf16[320,768]{1,0:T(8,128)(2,1)S(1)}, bf16[320,768]{1,0:T(8,128)(2,1)S(1)}, u32[]{:S(2)}, u32[]{:S(2)}) collective-permute-start(bf16[320,768]{1,0:T(8,128)(2,1)S(1)} %get-tuple-element.58), channel_id=1, source_target_pairs={{0,96},{1,97},{2,98},{3,99},{4,100},{5,101},{6,102},{7,103},{8,104... | collective-permute-start | bytes 1474568 | tf_op jit(solution)/shard_map/ppermute | solution.py:53
  98.3 11.2 %collective-permute-start.28 = (bf16[320,768]{1,0:T(8,128)(2,1)S(1)}, bf16[320,768]{1,0:T(8,128)(2,1)S(1)}, u32[]{:S(2)}, u32[]{:S(2)}) collective-permute-start(bf16[320,768]{1,0:T(8,128)(2,1)S(1)} %get-tuple-element.59), channel_id=1, source_target_pairs={{0,1},{1,0},{2,3},{3,2},{4,5},{5,4},{6,7},{7,6},{8,9},{9,8},{10,11... | collective-permute-start | bytes 1474568 | tf_op jit(solution)/shard_map/ppermute | solution.py:53
  110.5 2.2 %collective-permute-start.29 = (f32[160,768]{1,0:T(8,128)}, f32[160,768]{1,0:T(8,128)}, u32[]{:S(2)}, u32[]{:S(2)}) collective-permute-start(f32[160,768]{1,0:T(8,128)} %convert_add_fusion), channel_id=1, source_target_pairs={{0,16},{1,17},{2,18},{3,19},{4,20},{5,21},{6,22},{7,23},{8,24},{9,... | collective-permute-start | bytes 1474568 | tf_op jit(solution)/shard_map/ppermute | solution.py:57
